TPU v7x, 32 devices: a whole 2x2x4 slice. The times are simulated.
32 devices in a mesh: dp: 8 (over z, x), mp: 4 (over y, core).
Axes of the slice: x: 2, y: 2, z: 4, core: 2. Of those that a mesh axis runs over, the one named last changes fastest.
Arguments:
- pixels: bfloat16 [256, 196, 768], P(('dp', 'mp')), may hold values from -6 to 6
- token_mask: int32 [256, 196], P('dp'), may hold values from 0 to 1, as said below
- counts: int32 [8], P('dp'), may hold values from 8 to 32, as said below
- labels: int32 [256], P(('dp', 'mp')), may hold values from 0 to 999
- pairs: int32 [256], P(('dp', 'mp')), may hold values from 0 to 255, as said below
- attn_in: float32 [2, 384, 3, 384], P(None, None, None, 'mp'), may hold values from -0.3125 to 0.3125
- attn_in_mean: float32 [2, 384, 3, 384], P(None, None, None, 'mp'), may hold values from -6.67572e-06 to 6.67572e-06
- attn_in_square: float32 [2, 384, 3, 384], P(None, None, None, 'mp'), may hold values from 9.300319e-14 to 3.7201275e-13
- attn_out: float32 [2, 384, 384], P(None, 'mp'), may hold values from -1 to 1
- attn_out_mean: float32 [2, 384, 384], P(None, 'mp'), may hold values from -6.67572e-06 to 6.67572e-06
- attn_out_square: float32 [2, 384, 384], P(None, 'mp'), may hold values from 9.300319e-14 to 3.7201275e-13
- mlp_in: float32 [2, 384, 1536], P(None, None, 'mp'), may hold values from -0.3125 to 0.3125
- mlp_in_mean: float32 [2, 384, 1536], P(None, None, 'mp'), may hold values from -6.67572e-06 to 6.67572e-06
- mlp_in_square: float32 [2, 384, 1536], P(None, None, 'mp'), may hold values from 9.300319e-14 to 3.7201275e-13
- mlp_out: float32 [2, 1536, 384], P(None, 'mp'), may hold values from -0.15625 to 0.15625
- mlp_out_mean: float32 [2, 1536, 384], P(None, 'mp'), may hold values from -6.67572e-06 to 6.67572e-06
- mlp_out_square: float32 [2, 1536, 384], P(None, 'mp'), may hold values from 9.300319e-14 to 3.7201275e-13
- tables: float32 [1964, 384], replicated, may hold values from -5 to 5
- tables_mean: float32 [1964, 384], replicated, may hold values from -6.67572e-06 to 6.67572e-06
- tables_square: float32 [1964, 384], replicated, may hold values from 9.300319e-14 to 3.7201275e-13
- vectors: float32 [20, 384], replicated, may hold values from -8 to 8
- vectors_mean: float32 [20, 384], replicated, may hold values from -3.0517578e-05 to 3.0517578e-05
- vectors_square: float32 [20, 384], replicated, may hold values from 2.3250796e-12 to 9.300318e-12
- talking: float32 [2, 8, 8], replicated, may hold values from -2 to 2
- talking_mean: float32 [2, 8, 8], replicated, may hold values from -6.67572e-06 to 6.67572e-06
- talking_square: float32 [2, 8, 8], replicated, may hold values from 9.300319e-14 to 3.7201275e-13
Outputs:
- attn_in_new: float32 [2, 384, 3, 384], P(None, None, None, 'mp')
- attn_in_mean_new: float32 [2, 384, 3, 384], P(None, None, None, 'mp')
- attn_in_square_new: float32 [2, 384, 3, 384], P(None, None, None, 'mp')
- attn_out_new: float32 [2, 384, 384], P(None, 'mp')
- attn_out_mean_new: float32 [2, 384, 384], P(None, 'mp')
- attn_out_square_new: float32 [2, 384, 384], P(None, 'mp')
- mlp_in_new: float32 [2, 384, 1536], P(None, None, 'mp')
- mlp_in_mean_new: float32 [2, 384, 1536], P(None, None, 'mp')
- mlp_in_square_new: float32 [2, 384, 1536], P(None, None, 'mp')
- mlp_out_new: float32 [2, 1536, 384], P(None, 'mp')
- mlp_out_mean_new: float32 [2, 1536, 384], P(None, 'mp')
- mlp_out_square_new: float32 [2, 1536, 384], P(None, 'mp')
- tables_new: float32 [1964, 384], replicated
- tables_mean_new: float32 [1964, 384], replicated
- tables_square_new: float32 [1964, 384], replicated
- vectors_new: float32 [20, 384], replicated
- vectors_mean_new: float32 [20, 384], replicated
- vectors_square_new: float32 [20, 384], replicated
- talking_new: float32 [2, 8, 8], replicated
- talking_mean_new: float32 [2, 8, 8], replicated
- talking_square_new: float32 [2, 8, 8], replicated
- attn_in_copy: bfloat16 [2, 384, 3, 384], P(None, None, None, 'mp')
- attn_out_copy: bfloat16 [2, 384, 384], P(None, 'mp')
- mlp_in_copy: bfloat16 [2, 384, 1536], P(None, None, 'mp')
- mlp_out_copy: bfloat16 [2, 1536, 384], P(None, 'mp')
- statistics: float32 [12], replicated
- clip_norm: float32 [], replicated
- norms: float32 [2, 13], replicated
Inputs may be any that keep to these rules, and one draw needn't show every extreme that they name: The valid images of dp index d are the last counts[d] of its 32 slots; some index has all 32. `token_mask`: the first patch of every image is 1. `pairs`: each entry names a valid image other than its own row.
All inputs are finite; a program needn't handle non-finite values.
Results may differ from a plain program's by a relative error of at most 0.028.
Values may be sent and summed in bfloat16 or wider, within the bound.
A program may use at most 320 MiB of HBM per device.

v0:
```python
import jax
import jax.numpy as jnp
from jax import lax
from jax.sharding import PartitionSpec as P

PIX = 768
P_SIZE = 196
STEP = 10
HEAD = 48


HIGH_PRECISION = lax.Precision.HIGHEST
BETA_ONE = 0.9
BETA_TWO = 0.999
ADAM_EPS = 1e-08
DECAY = 0.01
RATE = 0.5
RATE_VECTOR = 0.5
CLIP = 0.02
SIMILARITY_TEMP = 0.05
MASKED = -1000000000.0
NORM_EPS = 1e-06
LAYER_BOUNDS = ((0, 1), (1, 2))


def norm_rows(inputs, gain, bias):
    center = inputs - jnp.mean(inputs, -1, keepdims=True)
    spread = jnp.mean(center * center, -1, keepdims=True)
    return center * lax.rsqrt(spread + NORM_EPS) * gain + bias


def norm_back(inputs, gain, bias, incoming):
    unused, pullback = jax.vjp(norm_rows, inputs, gain, bias)
    return pullback(incoming)


def gelu_exact(values):
    return jax.nn.gelu(values, approximate=False)


def gelu_back(inner, incoming):
    unused, pullback = jax.vjp(gelu_exact, inner)
    return pullback(incoming)[0]


def unit_rows(feature):
    return feature * lax.rsqrt(jnp.sum(feature * feature, -1, keepdims=True) + NORM_EPS)


def matmul(left, right):
    return lax.dot_general(
        left, right, (((left.ndim - 1,), (0,)), ((), ())), preferred_element_type=jnp.float32
    )


def outer_sum(left, incoming, lead):
    dims = tuple(range(lead))
    return lax.dot_general(
        left, incoming, ((dims, dims), ((), ())), preferred_element_type=jnp.float32
    )


def back_input(incoming, weight, trailing):
    left_dims = tuple(range(incoming.ndim - trailing, incoming.ndim))
    right_dims = tuple(range(1, 1 + trailing))
    return lax.dot_general(
        incoming, weight, ((left_dims, right_dims), ((), ())), preferred_element_type=jnp.float32
    )


def self_scores(packed, keep, talking):
    count, patches, unused, width = packed.shape
    heads = talking.shape[1]
    parts = packed.reshape(count, patches, 3, heads, width // heads)
    query, keys, values = (parts[:, :, 0], parts[:, :, 1], parts[:, :, 2])
    scores = jnp.einsum(
        "nqhd,nkhd->nhqk", query, keys, preferred_element_type=jnp.float32
    ) * HEAD ** (-0.5)
    mixed = jnp.einsum("gh,nhqk->ngqk", talking[0], scores, precision=HIGH_PRECISION)
    mixed = jnp.where(keep[:, None, None, :], mixed, MASKED)
    probs = jax.nn.softmax(mixed, axis=-1)
    weights = jnp.einsum("hg,ngqk->nhqk", talking[1], probs, precision=HIGH_PRECISION).astype(
        jnp.bfloat16
    )
    return (query, keys, values, scores, probs, weights)


def self_attend(packed, keep, talking):
    query, keys, values, scores, probs, weights = self_scores(packed, keep, talking)
    result = jnp.einsum("nhqk,nkhd->nqhd", weights, values, preferred_element_type=jnp.float32)
    return result.reshape(packed.shape[0], packed.shape[1], packed.shape[3]).astype(jnp.bfloat16)


def self_attend_back(packed, keep, talking, incoming):
    count, patches, unused, width = packed.shape
    query, keys, values, scores, probs, weights = self_scores(packed, keep, talking)
    incoming_heads = incoming.reshape(query.shape)
    grad_weights = jnp.einsum(
        "nqhd,nkhd->nhqk", incoming_heads, values, preferred_element_type=jnp.float32
    )
    grad_values = jnp.einsum(
        "nhqk,nqhd->nkhd", weights, incoming_heads, preferred_element_type=jnp.float32
    )
    grad_probs = jnp.einsum("hg,nhqk->ngqk", talking[1], grad_weights, precision=HIGH_PRECISION)
    grad_post = jnp.einsum("nhqk,ngqk->hg", grad_weights, probs, precision=HIGH_PRECISION)
    grad_mixed = probs * (grad_probs - jnp.sum(grad_probs * probs, -1, keepdims=True))
    grad_scores = jnp.einsum("gh,ngqk->nhqk", talking[0], grad_mixed, precision=HIGH_PRECISION)
    grad_pre = jnp.einsum("ngqk,nhqk->gh", grad_mixed, scores, precision=HIGH_PRECISION)
    rounded = grad_scores.astype(jnp.bfloat16)
    grad_query = jnp.einsum(
        "nhqk,nkhd->nqhd", rounded, keys, preferred_element_type=jnp.float32
    ) * HEAD ** (-0.5)
    grad_keys = jnp.einsum(
        "nhqk,nqhd->nkhd", rounded, query, preferred_element_type=jnp.float32
    ) * HEAD ** (-0.5)
    grad_packed = jnp.stack([grad_query, grad_keys, grad_values], axis=2).reshape(
        count, patches, 3, width
    )
    return (grad_packed.astype(jnp.bfloat16), jnp.stack([grad_pre, grad_post]))


def mlp_forward(middle, vectors, base, weight_up, weight_down):
    normed = norm_rows(middle, vectors[base + 4], vectors[base + 5]).astype(jnp.bfloat16)
    inner = matmul(normed, weight_up)
    active = gelu_exact(inner).astype(jnp.bfloat16)
    down_part = matmul(active, weight_down)
    mlp_branch = vectors[base + 7] * (down_part + vectors[base + 6])
    return (middle + mlp_branch, mlp_branch, (normed, inner, active, down_part))


def mlp_backward(incoming, middle, saved, vectors, base, weight_up, weight_down):
    rows, inner, active, down_raw = saved
    axes = tuple(range(incoming.ndim - 1))
    lead = rows.ndim - 1
    grad_scale = jnp.sum(incoming * (down_raw + vectors[base + 6]), axes)
    grad_bias = jnp.sum(incoming * vectors[base + 7], axes)
    grad_down = (incoming * vectors[base + 7]).astype(jnp.bfloat16)
    grad_weight_down = outer_sum(active, grad_down, lead)
    grad_inner = gelu_back(inner, back_input(grad_down, weight_down, 1)).astype(jnp.bfloat16)
    grad_weight_up = outer_sum(rows, grad_inner, lead)
    grad_rows = back_input(grad_inner, weight_up, 1)
    grad_norm_in, grad_gain, grad_beta = norm_back(
        middle, vectors[base + 4], vectors[base + 5], grad_rows
    )
    return (
        incoming + grad_norm_in,
        grad_weight_up,
        grad_weight_down,
        (grad_gain, grad_beta, grad_bias, grad_scale),
    )


def self_forward(resid, keep, vectors, weights, talking):
    weight_in, weight_out, weight_up, weight_down = weights
    normed = norm_rows(resid, vectors[0], vectors[1]).astype(jnp.bfloat16)
    grouped = matmul(normed, weight_in).astype(jnp.bfloat16)
    heads_out = self_attend(grouped, keep, talking)
    branch_raw = matmul(heads_out, weight_out)
    branch = vectors[3] * (branch_raw + vectors[2])
    middle = resid + branch
    final, mlp_branch, mlp_saved = mlp_forward(middle, vectors, 0, weight_up, weight_down)
    return (
        final,
        (branch, middle, mlp_branch, final),
        (normed, grouped, heads_out, branch_raw, middle, mlp_saved),
    )


def self_backward(incoming, resid, saved, keep, vectors, weights, talking):
    weight_in, weight_out, weight_up, weight_down = weights
    rows, grouped, heads_out, branch_raw, middle, mlp_saved = saved
    grad_middle, grad_weight_up, grad_weight_down, mlp_vectors = mlp_backward(
        incoming, middle, mlp_saved, vectors, 0, weight_up, weight_down
    )
    grad_scale = jnp.sum(grad_middle * (branch_raw + vectors[2]), (0, 1))
    grad_bias = jnp.sum(grad_middle * vectors[3], (0, 1))
    grad_branch = (grad_middle * vectors[3]).astype(jnp.bfloat16)
    grad_weight_out = outer_sum(heads_out, grad_branch, 2)
    grad_heads = back_input(grad_branch, weight_out, 1).astype(jnp.bfloat16)
    grad_packed, grad_talking = self_attend_back(grouped, keep, talking, grad_heads)
    grad_normed = back_input(grad_packed, weight_in, 2)
    grad_weight_in = outer_sum(rows, grad_packed, 2)
    grad_resid, grad_gain, grad_beta = norm_back(resid, vectors[0], vectors[1], grad_normed)
    vector_rows = jnp.stack(
        [
            grad_gain,
            grad_beta,
            grad_bias,
            grad_scale,
            mlp_vectors[0],
            mlp_vectors[1],
            mlp_vectors[2],
            mlp_vectors[3],
        ]
    )
    return (
        grad_middle + grad_resid,
        (grad_weight_in, grad_weight_out, grad_weight_up, grad_weight_down),
        vector_rows,
        grad_talking,
    )


def class_probs(query, keyval, allowed):
    count, width = query.shape
    heads = width // HEAD
    keys_count = keyval.shape[1]
    q = query.reshape(count, heads, HEAD)
    k = keyval[:, :, 0].reshape(count, keys_count, heads, HEAD)
    v = keyval[:, :, 1].reshape(count, keys_count, heads, HEAD)
    scores = jnp.einsum("nhd,nkhd->nhk", q, k, preferred_element_type=jnp.float32) * HEAD ** (-0.5)
    probs = jax.nn.softmax(jnp.where(allowed[:, None, :], scores, MASKED), axis=-1)
    return (q, k, v, probs)


def class_forward(patches, class_keep, vectors, weights):
    weight_in, weight_out, weight_up, weight_down = weights
    count = patches.shape[0]
    token = jnp.broadcast_to(vectors[17], (count, 1, patches.shape[2]))
    joined = jnp.concatenate([token, patches], 1)
    normed = norm_rows(joined, vectors[8], vectors[9]).astype(jnp.bfloat16)
    query = matmul(normed[:, 0], weight_in[:, 0]).astype(jnp.bfloat16)
    keyval = matmul(normed, weight_in[:, 1:]).astype(jnp.bfloat16)
    allowed = jnp.concatenate([jnp.ones((class_keep.shape[0], 1), bool), class_keep], 1)
    q, k, v, probs = class_probs(query, keyval, allowed)
    result = jnp.einsum(
        "nhk,nkhd->nhd", probs.astype(jnp.bfloat16), v, preferred_element_type=jnp.float32
    )
    heads_out = result.reshape(query.shape).astype(jnp.bfloat16)
    branch_part = matmul(heads_out, weight_out)
    branch = vectors[11] * (branch_part + vectors[10])
    middle = vectors[17] + branch
    final, mlp_branch, mlp_saved = mlp_forward(middle, vectors, 8, weight_up, weight_down)
    return (
        final,
        (branch, middle, mlp_branch, final),
        (joined, normed, query, keyval, allowed, heads_out, branch_part, middle, mlp_saved),
    )


def class_backward(incoming, saved, vectors, weights):
    weight_in, weight_out, weight_up, weight_down = weights
    joined, rows, query, keyval, allowed, heads_out, branch_raw, middle, mlp_saved = saved
    grad_middle, grad_weight_up, grad_weight_down, mlp_vectors = mlp_backward(
        incoming, middle, mlp_saved, vectors, 8, weight_up, weight_down
    )
    grad_scale = jnp.sum(grad_middle * (branch_raw + vectors[10]), 0)
    grad_bias = jnp.sum(grad_middle * vectors[11], 0)
    grad_branch = (grad_middle * vectors[11]).astype(jnp.bfloat16)
    grad_weight_out = outer_sum(heads_out, grad_branch, 1)
    count, width = query.shape
    grad_heads = (
        back_input(grad_branch, weight_out, 1)
        .astype(jnp.bfloat16)
        .reshape(count, width // HEAD, HEAD)
    )
    q, k, v, probs = class_probs(query, keyval, allowed)
    grad_probs = jnp.einsum("nhd,nkhd->nhk", grad_heads, v, preferred_element_type=jnp.float32)
    grad_values = jnp.einsum(
        "nhk,nhd->nkhd", probs.astype(jnp.bfloat16), grad_heads, preferred_element_type=jnp.float32
    )
    grad_scores = (probs * (grad_probs - jnp.sum(grad_probs * probs, -1, keepdims=True))).astype(
        jnp.bfloat16
    )
    grad_query = jnp.einsum(
        "nhk,nkhd->nhd", grad_scores, k, preferred_element_type=jnp.float32
    ) * HEAD ** (-0.5)
    grad_query = grad_query.reshape(count, width).astype(jnp.bfloat16)
    grad_keys = jnp.einsum(
        "nhk,nhd->nkhd", grad_scores, q, preferred_element_type=jnp.float32
    ) * HEAD ** (-0.5)
    keys_count = keyval.shape[1]
    grad_keyval = jnp.stack(
        [
            grad_keys.reshape(count, keys_count, width),
            grad_values.reshape(count, keys_count, width),
        ],
        2,
    ).astype(jnp.bfloat16)
    grad_weight_in = jnp.concatenate(
        [outer_sum(rows[:, 0], grad_query, 1)[:, None], outer_sum(rows, grad_keyval, 2)], 1
    )
    grad_rows = back_input(grad_keyval, weight_in[:, 1:], 2)
    first_row = grad_rows[:, :1] + back_input(grad_query, weight_in[:, 0], 1)[:, None]
    grad_rows = jnp.concatenate([first_row, grad_rows[:, 1:]], 1)
    grad_joined, grad_gain, grad_beta = norm_back(joined, vectors[8], vectors[9], grad_rows)
    grad_token = jnp.sum(grad_middle, 0) + jnp.sum(grad_joined[:, 0], 0)
    vector_rows = jnp.stack(
        [
            grad_gain,
            grad_beta,
            grad_bias,
            grad_scale,
            mlp_vectors[0],
            mlp_vectors[1],
            mlp_vectors[2],
            mlp_vectors[3],
        ]
    )
    return (
        grad_joined[:, 1:],
        (grad_weight_in, grad_weight_out, grad_weight_up, grad_weight_down),
        vector_rows,
        grad_token,
    )


def adam_parts(gradient, mean, square, factor):
    clipped = gradient * factor
    mean_new = BETA_ONE * mean + (1.0 - BETA_ONE) * clipped
    square_new = BETA_TWO * square + (1.0 - BETA_TWO) * clipped * clipped
    direction = (
        mean_new
        / (1.0 - BETA_ONE**STEP)
        / (jnp.sqrt(square_new / (1.0 - BETA_TWO**STEP)) + ADAM_EPS)
    )
    return (mean_new, square_new, direction)


def segment_squares(values, bounds):
    return jnp.stack(
        [jnp.sum(values[lower:upper] * values[lower:upper]) for lower, upper in bounds]
    )


def apply_trust(weight, update, bounds, weight_sq, update_sq):
    trust = jnp.sqrt(weight_sq / (update_sq + 1e-12))
    pieces = [
        weight[lower:upper] - RATE * trust[place] * update[lower:upper]
        for place, (lower, upper) in enumerate(bounds)
    ]
    return jnp.concatenate(pieces, 0)


def shards(
    pixels,
    token_mask,
    counts,
    labels,
    pairs,
    attn_in,
    attn_in_mean,
    attn_in_square,
    attn_out,
    attn_out_mean,
    attn_out_square,
    mlp_in,
    mlp_in_mean,
    mlp_in_square,
    mlp_out,
    mlp_out_mean,
    mlp_out_square,
    tables,
    tables_mean,
    tables_square,
    vectors,
    vectors_mean,
    vectors_square,
    talking,
    talking_mean,
    talking_square,
):
    local = pixels.shape[0]
    group = token_mask.shape[0]
    place_mp = lax.axis_index("mp")
    okay_group = (jnp.arange(group) >= group - counts[0]).astype(jnp.float32)
    okay = lax.dynamic_slice_in_dim(okay_group, place_mp * local, local, 0)
    keep_group = token_mask > 0
    keep = lax.dynamic_slice_in_dim(keep_group, place_mp * local, local, 0)
    token_weight = keep.astype(jnp.float32) * okay[:, None]
    low_weights = (
        attn_in.astype(jnp.bfloat16),
        attn_out.astype(jnp.bfloat16),
        mlp_in.astype(jnp.bfloat16),
        mlp_out.astype(jnp.bfloat16),
    )
    low_weights = (
        lax.all_gather(low_weights[0], "mp", axis=3, tiled=True),
        lax.all_gather(low_weights[1], "mp", axis=1, tiled=True),
        lax.all_gather(low_weights[2], "mp", axis=2, tiled=True),
        lax.all_gather(low_weights[3], "mp", axis=1, tiled=True),
    )
    self_weights = tuple((item[0] for item in low_weights))
    class_weights = tuple((item[1] for item in low_weights))
    head = tables[PIX + P_SIZE :].astype(jnp.bfloat16)
    embed = (
        matmul(pixels, tables[:PIX].astype(jnp.bfloat16)) + vectors[16] + tables[PIX : PIX + P_SIZE]
    )
    patches, self_parts, self_saved = self_forward(embed, keep, vectors, self_weights, talking)
    token, class_parts, class_saved = class_forward(patches, keep, vectors, class_weights)
    feature = norm_rows(token, vectors[18], vectors[19])
    feature_low = feature.astype(jnp.bfloat16)
    logits = lax.dot_general(
        feature_low, head, (((1,), (1,)), ((), ())), preferred_element_type=jnp.float32
    )
    cross = jax.nn.logsumexp(logits, -1) - jnp.take_along_axis(logits, labels[:, None], 1)[:, 0]
    unit_embeddings = unit_rows(feature).astype(jnp.bfloat16)
    everyone, valid_all = (
        lax.all_gather(unit_embeddings, ("dp", "mp"), axis=0, tiled=True),
        lax.all_gather(okay.astype(jnp.bfloat16), ("dp", "mp"), axis=0, tiled=True),
    )
    unit_values = unit_embeddings.astype(jnp.float32)
    gathered_values = everyone.astype(jnp.float32)
    similarity_scores = (
        lax.dot_general(
            unit_values, gathered_values, (((1,), (1,)), ((), ())), precision=HIGH_PRECISION
        )
        / SIMILARITY_TEMP
    )
    columns = jnp.arange(everyone.shape[0])
    owned = lax.axis_index(("dp", "mp")) * local + jnp.arange(local)
    allowed = (valid_all[None, :] > 0) & (owned[:, None] != columns[None, :])
    similarity_scores = jnp.where(allowed, similarity_scores, MASKED)
    contrast = (
        jax.nn.logsumexp(similarity_scores, -1)
        - jnp.take_along_axis(similarity_scores, pairs[:, None], 1)[:, 0]
    )
    self_sums = jnp.stack(
        [jnp.sum(jnp.mean(part * part, -1) * token_weight) for part in self_parts]
    )
    class_sums = jnp.stack([jnp.sum(jnp.mean(part * part, -1) * okay) for part in class_parts])
    local_sums = jnp.concatenate(
        [
            jnp.stack(
                [
                    jnp.sum(okay * cross),
                    jnp.sum(okay * contrast),
                    jnp.sum(okay),
                    jnp.sum(token_weight),
                ]
            ),
            self_sums,
            class_sums,
        ]
    )
    totals = lax.psum(local_sums, ("dp", "mp"))
    statistics = jnp.concatenate(
        [totals[:4], jnp.sqrt(totals[4:8] / totals[3]), jnp.sqrt(totals[8:] / totals[2])]
    )
    share = okay / totals[2]
    label_hot = (jnp.arange(logits.shape[1])[None, :] == labels[:, None]).astype(jnp.float32)
    grad_logits = (share[:, None] * (jax.nn.softmax(logits, -1) - label_hot)).astype(jnp.bfloat16)
    grad_head = lax.dot_general(
        grad_logits, feature_low, (((0,), (0,)), ((), ())), preferred_element_type=jnp.float32
    )
    grad_feature = matmul(grad_logits, head)
    pair_hot = (columns[None, :] == pairs[:, None]).astype(jnp.float32)
    grad_similarity = share[:, None] * (jax.nn.softmax(similarity_scores, -1) - pair_hot)
    grad_unit_vectors = (
        jnp.dot(grad_similarity, gathered_values, precision=HIGH_PRECISION) / SIMILARITY_TEMP
    )
    grad_everyone = (
        lax.dot_general(
            grad_similarity, unit_values, (((0,), (0,)), ((), ())), precision=HIGH_PRECISION
        )
        / SIMILARITY_TEMP
    )
    grad_unit_vectors = grad_unit_vectors + lax.psum_scatter(
        grad_everyone, ("dp", "mp"), scatter_dimension=0, tiled=True
    )
    unused, pullback = jax.vjp(unit_rows, feature)
    grad_feature = grad_feature + pullback(grad_unit_vectors)[0]
    grad_token, grad_final_gain, grad_final_bias = norm_back(
        token, vectors[18], vectors[19], grad_feature
    )
    grad_patches, class_grads, class_vectors, grad_class_token = class_backward(
        grad_token, class_saved, vectors, class_weights
    )
    grad_embed, self_grads, self_vectors, grad_talking = self_backward(
        grad_patches, embed, self_saved, keep, vectors, self_weights, talking
    )
    grad_patch_weight = outer_sum(pixels, grad_embed.astype(jnp.bfloat16), 2)
    grad_tables = jnp.concatenate([grad_patch_weight, jnp.sum(grad_embed, 0), grad_head], 0)
    closing = jnp.stack(
        [jnp.sum(grad_embed, (0, 1)), grad_class_token, grad_final_gain, grad_final_bias]
    )
    grad_vectors = jnp.concatenate([self_vectors, class_vectors, closing], 0)
    stacked = tuple((jnp.stack([first, second]) for first, second in zip(self_grads, class_grads)))
    stacked = (
        lax.psum_scatter(stacked[0], "mp", scatter_dimension=3, tiled=True),
        lax.psum_scatter(stacked[1], "mp", scatter_dimension=1, tiled=True),
        lax.psum_scatter(stacked[2], "mp", scatter_dimension=2, tiled=True),
        lax.psum_scatter(stacked[3], "mp", scatter_dimension=1, tiled=True),
    )
    stacked = lax.psum((stacked[0], stacked[1], stacked[2], stacked[3]), "dp")
    shard_sq = sum((jnp.sum(item * item) for item in stacked))
    grad_tables, grad_vectors, grad_talking, shard_sq = lax.psum(
        (grad_tables, grad_vectors, grad_talking, shard_sq), ("dp", "mp")
    )
    total_sq = (
        shard_sq / lax.axis_size("dp")
        + jnp.sum(grad_tables * grad_tables)
        + jnp.sum(grad_vectors * grad_vectors)
        + jnp.sum(grad_talking * grad_talking)
    )
    grad_norm = jnp.sqrt(total_sq)
    factor = CLIP / jnp.maximum(grad_norm, CLIP)
    sharded = (attn_in, attn_out, mlp_in, mlp_out)
    sharded_means = (attn_in_mean, attn_out_mean, mlp_in_mean, mlp_out_mean)
    sharded_squares = (attn_in_square, attn_out_square, mlp_in_square, mlp_out_square)
    moved = [
        adam_parts(stacked[place], sharded_means[place], sharded_squares[place], factor)
        for place in range(4)
    ]
    updates = [moved[place][2] + DECAY * sharded[place] for place in range(4)]
    weight_sq = jnp.concatenate(
        [segment_squares(sharded[place], LAYER_BOUNDS) for place in range(4)]
    )
    update_sq = jnp.concatenate(
        [segment_squares(updates[place], LAYER_BOUNDS) for place in range(4)]
    )
    weight_sq, update_sq = lax.psum((weight_sq, update_sq), "mp")
    renewed = [
        apply_trust(
            sharded[place],
            updates[place],
            LAYER_BOUNDS,
            weight_sq[2 * place : 2 * place + 2],
            update_sq[2 * place : 2 * place + 2],
        )
        for place in range(4)
    ]
    table_bounds = ((0, PIX), (PIX, PIX + P_SIZE), (PIX + P_SIZE, tables.shape[0]))
    table_mean, table_square, table_direction = adam_parts(
        grad_tables, tables_mean, tables_square, factor
    )
    table_update = table_direction + DECAY * tables
    table_weight_sq = segment_squares(tables, table_bounds)
    table_update_sq = segment_squares(table_update, table_bounds)
    tables_new = apply_trust(tables, table_update, table_bounds, table_weight_sq, table_update_sq)
    vector_mean, vector_square, vector_direction = adam_parts(
        grad_vectors, vectors_mean, vectors_square, factor
    )
    vectors_new = vectors - RATE_VECTOR * vector_direction
    mixing_mean, mixing_square, mixing_direction = adam_parts(
        grad_talking, talking_mean, talking_square, factor
    )
    mixing_update = mixing_direction + DECAY * talking
    mixing_weight_sq = segment_squares(talking, LAYER_BOUNDS)
    mixing_update_sq = segment_squares(mixing_update, LAYER_BOUNDS)
    talking_new = apply_trust(
        talking, mixing_update, LAYER_BOUNDS, mixing_weight_sq, mixing_update_sq
    )
    norms = jnp.stack(
        [
            jnp.sqrt(jnp.concatenate([weight_sq, table_weight_sq, mixing_weight_sq])),
            jnp.sqrt(jnp.concatenate([update_sq, table_update_sq, mixing_update_sq])),
        ]
    )
    return (
        renewed[0],
        moved[0][0],
        moved[0][1],
        renewed[1],
        moved[1][0],
        moved[1][1],
        renewed[2],
        moved[2][0],
        moved[2][1],
        renewed[3],
        moved[3][0],
        moved[3][1],
        tables_new,
        table_mean,
        table_square,
        vectors_new,
        vector_mean,
        vector_square,
        talking_new,
        mixing_mean,
        mixing_square,
        renewed[0].astype(jnp.bfloat16),
        renewed[1].astype(jnp.bfloat16),
        renewed[2].astype(jnp.bfloat16),
        renewed[3].astype(jnp.bfloat16),
        statistics,
        grad_norm,
        norms,
    )


def solution(mesh):
    return jax.shard_map(
        shards,
        mesh=mesh,
        in_specs=(
            P(("dp", "mp"), None, None),
            P("dp", None),
            P("dp"),
            P(("dp", "mp")),
            P(("dp", "mp")),
            P(None, None, None, "mp"),
            P(None, None, None, "mp"),
            P(None, None, None, "mp"),
            P(None, "mp", None),
            P(None, "mp", None),
            P(None, "mp", None),
            P(None, None, "mp"),
            P(None, None, "mp"),
            P(None, None, "mp"),
            P(None, "mp", None),
            P(None, "mp", None),
            P(None, "mp", None),
            P(),
            P(),
            P(),
            P(),
            P(),
            P(),
            P(),
            P(),
            P(),
        ),
        out_specs=(
            P(None, None, None, "mp"),
            P(None, None, None, "mp"),
            P(None, None, None, "mp"),
            P(None, "mp", None),
            P(None, "mp", None),
            P(None, "mp", None),
            P(None, None, "mp"),
            P(None, None, "mp"),
            P(None, None, "mp"),
            P(None, "mp", None),
            P(None, "mp", None),
            P(None, "mp", None),
            P(),
            P(),
            P(),
            P(),
            P(),
            P(),
            P(),
            P(),
            P(),
            P(None, None, None, "mp"),
            P(None, "mp", None),
            P(None, None, "mp"),
            P(None, "mp", None),
            P(),
            P(),
            P(),
        ),
        check_vma=False,
    )
```

profile of v0, /device:TPU:0, one launch (start us, length us, event | category | flops | bytes accessed | tf_op | source)
XLA Modules:
  0.0 1262.3 jit_solution(7485409648742090070)
XLA Ops:
  15.5 42.4 %all-reduce.1 = bf16[256]{0:T(256)(128)(2,1)S(1)} all-reduce(bf16[256]{0:T(256)(128)(2,1)S(1)} %dynamic-update-slice), channel_id=1, replica_groups=mesh['dp'=8,'mp'=4] {'dp','mp'}, use_global_device_ids=true, to_apply=%add.1 | all-reduce | flops 256 | bytes 1024
  60.7 8.5 all_gather.19
  106.5 8.5 fusion.62
  114.9 23.6 %bitcast_reduce_fusion = (f32[8,8,196]{1,2,0:T(8,128)S(1)}, f32[8,196,196,8]{2,3,1,0:T(8,128)S(1)}) fusion(pred[8,196]{1,0:T(8,128)(4,1)S(1)} %dynamic-slice_compare_fusion, f32[2,8,8]{2,1,0:T(8,128)S(1)} %copy-done.83, f32[8,8,196,196]{3,2,1,0:T(8,128)} %fusion.62), kind=kOutput, calls=%fused_computation.11 | convolution fusion | flops 243391232 | bytes 19725312 | tf_op jit(solution)/shard_map/gh,nhqk->ngqk/dot_general | solution.py:79
  144.8 18.8 %fusion.30 = bf16[8,8,196,196]{3,1,2,0:T(8,128)(2,1)S(1)} fusion(f32[2,8,8]{2,1,0:T(8,128)S(1)} %copy-done.83, f32[8,196,196,8]{2,3,1,0:T(8,128)S(1)} %get-tuple-element.321, f32[8,8,196]{1,2,0:T(8,128)S(1)} %fusion.13, f32[8,8,196]{1,2,0:T(8,128)} %copy-done.38, pred[8,196]{1,0:T(8,128)(4,1)S(1)} %dynamic-slice_compare_fusion), kind=kOutput, calls=%fused_computation.54 | convolution fusion | flops 245862400 | bytes 18637824 | tf_op jit(solution)/shard_map/hg,ngqk->nhqk/dot_general | solution.py:82
  183.7 23.3 %multiply_convert_fusion = (bf16[8,196,1536]{2,1,0:T(8,128)(2,1)}, f32[8,196,1536]{2,1,0:T(8,128)}) fusion(f32[8,196,1536]{2,1,0:T(8,128)S(1)} %get-tuple-element.323, u8[196,1536]{1,0:T(8,128)(4,1)S(1)} %get-tuple-element.113, u8[196,1536]{1,0:T(8,128)(4,1)S(1)} %get-tuple-element.112), kind=kLoop, calls=%fused_computation.29 | loop fusion | flops 168591360 | bytes 24686592 | tf_op jit(solution)/shard_map/convert_element_type | solution.py:125
  207.0 8.8 multiply_reduce_fusion.8
  244.8 39.6 %all_gather.23 = bf16[256,384]{1,0:T(8,128)(2,1)S(1)} all-gather(bf16[8,384]{1,0:T(8,128)(2,1)S(1)} %multiply_convert_fusion.14), channel_id=1, replica_groups=mesh['dp'=8,'mp'=4] {'dp','mp'}, dimensions={0}, use_global_device_ids=true | all-gather | bytes 202752 | tf_op jit(solution)/shard_map/all_gather | solution.py:399
  296.3 36.9 %psum.78 = f32[12]{0:T(128)S(1)} all-reduce(f32[12]{0:T(128)S(1)} %concatenate.99), channel_id=1, replica_groups=mesh['dp'=8,'mp'=4] {'dp','mp'}, use_global_device_ids=true, to_apply=%region_48.49 | all-reduce | flops 12 | bytes 96 | tf_op jit(solution)/shard_map/psum | solution.py:436
  335.8 127.8 %all-reduce.14.cloned.1.call-done = f32[256,384]{1,0:T(8,128)} async-done(((f32[256,384]{1,0:T(8,128)}), f32[256,384]{1,0:T(8,128)}) %all-reduce.14.cloned.1.call-update) | async-done | bytes 393232
  497.7 9.4 add_convert_fusion
  529.0 8.7 fusion.63
  537.8 44.9 %fusion.3 = (f32[8,8,196]{1,2,0:T(8,128)S(1)}, f32[8,196,196,8]{2,3,1,0:T(8,128)}) fusion(f32[8,8,196]{1,2,0:T(8,128)S(1)} %copy-done.53, f32[8,8,196]{1,2,0:T(8,128)S(1)} %copy-done.39, f32[8,196,196,8]{2,3,1,0:T(8,128)S(1)} %bitcast.387, pred[8,196]{1,0:T(8,128)(4,1)S(1)} %copy-done.106, f32[2,8,8]{2,1,0:T(8,128)S(1)} %copy-done.84, ...), kind=kOutput, calls=%fused_computation.8 | convolution fusion | flops 248308480 | bytes 34208768 | tf_op jit(solution)/shard_map/hg,nhqk->ngqk/dot_general | solution.py:104
  582.7 18.6 %fusion.31 = bf16[8,8,196,196]{3,1,2,0:T(8,128)(2,1)S(1)} fusion(f32[8,196,196,8]{2,3,1,0:T(8,128)} %get-tuple-element.339, f32[8,8,196]{1,2,0:T(8,128)S(1)} %get-tuple-element.338, f32[2,8,8]{2,1,0:T(8,128)S(1)} %copy-done.84, f32[8,196,196,8]{2,3,1,0:T(8,128)S(1)} %bitcast.387, f32[8,8,196]{1,2,0:T(8,128)S(1)} %copy-done.53, ...), kind=kOutput, calls=%fused_computation.55 | convolution fusion | flops 250779648 | bytes 30060544 | tf_op jit(solution)/shard_map/gh,ngqk->nhqk/dot_general | solution.py:107
  692.2 8.7 concatenate.102
  700.9 32.0 %fusion.82 = f32[1,8,8]{2,1,0:T(8,128)S(1)} fusion(f32[8,8,196,196]{3,2,1,0:T(8,128)} %fusion.63, f32[8,196,196,8]{2,3,1,0:T(8,128)} %copy-done, f32[8,8,196]{1,2,0:T(8,128)S(1)} %copy-done.54, f32[8,8,196]{1,2,0:T(8,128)S(1)} %copy-done.40, pred[8,196]{1,0:T(8,128)(4,1)S(1)} %copy-done.106), kind=kOutput, calls=%fused_computation.187 | convolution fusion | flops 243403776 | bytes 19771168 | tf_op jit(solution)/shard_map/nhqk,ngqk->hg/dot_general | solution.py:105
  735.4 49.3 %reduce-scatter.8.cloned.1.call-done = f32[2,384,384]{2,1,0:T(8,128)} async-done(((f32[2,1536,384]{2,1,0:T(8,128)}), f32[2,384,384]{2,1,0:T(8,128)}) %reduce-scatter.8.cloned.1.call-update) | async-done | bytes 1179664 | tf_op jit(solution)/shard_map/reduce_scatter | solution.py:483
  784.6 50.6 %reduce-scatter.6.cloned.1.call-done = f32[2,384,384]{2,1,0:T(8,128)} async-done(((f32[2,384,1536]{2,1,0:T(8,128)}), f32[2,384,384]{2,1,0:T(8,128)}) %reduce-scatter.6.cloned.1.call-update) | async-done | bytes 1179664 | tf_op jit(solution)/shard_map/reduce_scatter | solution.py:482
  835.3 14.7 %fusion.243 = f32[8,8,196,196]{3,1,2,0:T(8,128)} fusion(f32[8,196,196,8]{2,3,1,0:T(8,128)} %get-tuple-element.339, f32[8,8,196]{1,2,0:T(8,128)S(1)} %copy-done.74, f32[8,8,196]{1,2,0:T(8,128)S(1)} %copy-done.54, f32[8,8,196]{1,2,0:T(8,128)S(1)} %copy-done.40, f32[8,196,196,8]{2,3,1,0:T(8,128)} %copy-done, ...), kind=kLoop, calls=%fused_computation.9.clone.clone.clone.clone.2 | loop fusion | flops 12293120 | bytes 29655584 | tf_op jit(solution)/shard_map/ngqk,nhqk->gh/dot_general | solution.py:108
  850.9 32.2 %fusion.79 = f32[1,8,8]{2,1,0:T(8,128)S(1)} fusion(f32[8,8,196,196]{3,2,1,0:T(8,128)} %fusion.62, f32[8,8,196,196]{3,1,2,0:T(8,128)} %fusion.243), kind=kOutput, calls=%fused_computation.186 | convolution fusion | flops 238486528 | bytes 19669248 | tf_op jit(solution)/shard_map/ngqk,nhqk->gh/dot_general | solution.py:108
  883.2 97.1 %all-reduce.18.cloned.1.call-done = (f32[2,384,3,96]{1,3,2,0:T(8,128)}, f32[2,96,384]{2,1,0:T(8,128)}, f32[2,384,384]{2,1,0:T(8,128)}, f32[2,384,384]{2,1,0:T(8,128)}) async-done(((f32[2,384,3,96]{1,3,2,0:T(8,128)}, f32[2,96,384]{2,1,0:T(8,128)}, f32[2,384,384]{2,1,0:T(8,128)}, f32[2,384,384]{2,1,0:T(8,128)}), (f32[2,384,3,96]{1,3,2,0:T(8,128)}, f32[2,96,384]{2,1,0:T(8,128)}, f32[2,384,384]{2,1,0:T(8,128)}, ...) | async-done | bytes 3538960 | tf_op jit(solution)/shard_map/psum | solution.py:485
  991.0 131.8 %all-reduce.12.cloned.1.call-done = f32[1964,384]{1,0:T(8,128)} async-done(((f32[1964,384]{1,0:T(8,128)}), f32[1964,384]{1,0:T(8,128)}) %all-reduce.12.cloned.1.call-update) | async-done | bytes 3016720 | tf_op jit(solution)/shard_map/psum | solution.py:487
  1126.1 41.1 %all-reduce.4 = (f32[]{:T(128)}, f32[20,384]{1,0:T(8,128)S(1)}, f32[2,8,8]{2,1,0:T(8,128)S(1)}) all-reduce(f32[]{:T(128)S(6)} %add.493, f32[20,384]{1,0:T(8,128)S(1)} %concatenate.103, f32[2,8,8]{2,1,0:T(8,128)S(1)} %pad_maximum_fusion.18), channel_id=1, replica_groups=mesh['dp'=8,'mp'=4] {'dp','mp'}, use_global_device_ids=true, to_apply=%region_75.76 | all-reduce | flops 7809 | bytes 62472 | tf_op jit(solution)/shard_map/psum | solution.py:487
  1171.0 8.4 multiply_add_fusion
  (636 shorter events, 344.0 us)
Async XLA Ops:
  7.2 68.3 %all-gather.4.cloned.1.call-start = ((), (), s32[]{:S(2)}) async-start(), calls=%async_computation.3 | async-start | bytes 2211840 | tf_op jit(solution)/shard_map/all_gather | solution.py:378
  10.1 163.3 %all-gather.6.cloned.1.call-start = ((), (), s32[]{:S(2)}) async-start(), calls=%async_computation.4 | async-start | bytes 2949120 | tf_op jit(solution)/shard_map/all_gather | solution.py:380
  11.1 195.9 %all-gather.8.cloned.1.call-start = ((), (), s32[]{:S(2)}) async-start(), calls=%async_computation.5 | async-start | bytes 2949120 | tf_op jit(solution)/shard_map/all_gather | solution.py:381
  12.0 451.5 %all-reduce.14.cloned.1.call-start = ((), (), s32[]{:S(2)}) async-start(), calls=%async_computation.10 | async-start | bytes 786432
  13.4 155.1 %copy-start.122 = (f32[384]{0:T(512)}, f32[384]{0:T(512)S(1)}, u32[]{:S(2)}) copy-start(f32[384]{0:T(512)S(1)} %get-tuple-element.161) | copy-start | bytes 4612
  13.4 160.0 %copy-start.103 = (f32[384]{0:T(512)}, f32[384]{0:T(512)S(1)}, u32[]{:S(2)}) copy-start(f32[384]{0:T(512)S(1)} %get-tuple-element.159) | copy-start | bytes 4612
  13.4 160.0 %copy-start.124 = (f32[384]{0:T(512)}, f32[384]{0:T(512)S(1)}, u32[]{:S(2)}) copy-start(f32[384]{0:T(512)S(1)} %get-tuple-element.158) | copy-start | bytes 4612
  13.4 193.6 %copy-start.128 = (f32[384]{0:T(512)}, f32[384]{0:T(512)S(1)}, u32[]{:S(2)}) copy-start(f32[384]{0:T(512)S(1)} %get-tuple-element.160) | copy-start | bytes 4612
  13.4 193.6 %copy-start.130 = (f32[384]{0:T(512)}, f32[384]{0:T(512)S(1)}, u32[]{:S(2)}) copy-start(f32[384]{0:T(512)S(1)} %get-tuple-element.157) | copy-start | bytes 4612
  13.4 202.4 %copy-start.118 = (f32[384]{0:T(512)}, f32[384]{0:T(512)S(1)}, u32[]{:S(2)}) copy-start(f32[384]{0:T(512)S(1)} %get-tuple-element.163) | copy-start | bytes 4612
  60.7 556.0 %copy-start.36 = (f32[196,384]{1,0:T(8,128)}, f32[196,384]{1,0:T(8,128)S(1)}, u32[]{:S(2)}) copy-start(f32[196,384]{1,0:T(8,128)S(1)} %get-tuple-element.264) | copy-start | bytes 903172
  69.2 167.9 %copy-start.43 = (bf16[2,384,384]{2,1,0:T(8,128)(2,1)}, bf16[2,384,384]{2,1,0:T(8,128)(2,1)S(1)}, u32[]{:S(2)}) copy-start(bf16[2,384,384]{2,1,0:T(8,128)(2,1)S(1)} %all_gather.19) | copy-start | bytes 1769476
  243.1 221.7 %copy-start.117 = (f32[384]{0:T(512)S(1)}, f32[384]{0:T(512)}, u32[]{:S(2)}) copy-start(f32[384]{0:T(512)} %get-tuple-element.148) | copy-start | bytes 4612
  244.2 223.0 %copy-start.81 = (f32[8,384]{1,0:T(8,128)}, f32[8,384]{1,0:T(8,128)S(1)}, u32[]{:S(2)}) copy-start(f32[8,384]{1,0:T(8,128)S(1)} %get-tuple-element.254) | copy-start | bytes 36868
  244.7 222.5 %copy-start.134 = (f32[8]{0:T(128)}, f32[8]{0:T(128)S(1)}, u32[]{:S(2)}) copy-start(f32[8]{0:T(128)S(1)} %get-tuple-element.329) | copy-start | bytes 100
  284.4 183.0 %copy-start.116 = (f32[384]{0:T(512)S(1)}, f32[384]{0:T(512)}, u32[]{:S(2)}) copy-start(f32[384]{0:T(512)} %get-tuple-element.152) | copy-start | bytes 4612
  286.5 182.7 %copy-start.156 = (f32[8]{0:T(128)}, f32[8]{0:T(128)S(1)}, u32[]{:S(2)}) copy-start(f32[8]{0:T(128)S(1)} %get-tuple-element.167) | copy-start | bytes 100
  335.6 397.3 %all-reduce.16.cloned.1.call-start = ((), (), s32[]{:S(2)}) async-start(), calls=%async_computation.11 | async-start | bytes 7077888
  631.2 104.2 %reduce-scatter.4.cloned.1.call-start = ((), (), s32[]{:S(2)}) async-start(), calls=%async_computation.6 | async-start | bytes 1474560 | tf_op jit(solution)/shard_map/reduce_scatter | solution.py:481
  636.3 148.3 %reduce-scatter.8.cloned.1.call-start = ((), (), s32[]{:S(2)}) async-start(), calls=%async_computation.8 | async-start | bytes 5898240 | tf_op jit(solution)/shard_map/reduce_scatter | solution.py:483
  645.0 190.2 %reduce-scatter.6.cloned.1.call-start = ((), (), s32[]{:S(2)}) async-start(), calls=%async_computation.7 | async-start | bytes 5898240 | tf_op jit(solution)/shard_map/reduce_scatter | solution.py:482
  653.7 326.6 %all-reduce.18.cloned.1.call-start = ((), (), s32[]{:S(2)}) async-start(), calls=%async_computation.12 | async-start | bytes 7077888 | tf_op jit(solution)/shard_map/psum | solution.py:485
  835.3 287.6 %all-reduce.12.cloned.1.call-start = ((), (), s32[]{:S(2)}) async-start(), calls=%async_computation.9 | async-start | bytes 6045696 | tf_op jit(solution)/shard_map/psum | solution.py:487
  985.2 185.8 %copy-start.10 = (f32[1964,384]{1,0:T(8,128)S(1)}, f32[1964,384]{1,0:T(8,128)}, u32[]{:S(2)}) copy-start(f32[1964,384]{1,0:T(8,128)} %param.43) | copy-start | bytes 9050116
  (170 other events, 2589.7 us)
Sparse Core Ops, SparseCore 0:
  10.2 24.0 all-gather.3
  36.5 24.5 all-gather.5
  63.2 24.0 all-gather.7
  335.7 127.7 all-reduce.13
  631.3 73.8 all-reduce.15
  708.3 25.9 reduce-scatter.3
  736.8 47.7 reduce-scatter.7
  787.3 47.8 reduce-scatter.5
  839.8 140.4 all-reduce.17
  987.1 135.6 all-reduce.11
where the time goes:
time: 1270 us; the launch traced here: 1260 us
  waiting for transfers between devices  457 us (36%)
  matrix products  311 us (24%)
  blocking collectives  174 us (14%)
  other arithmetic  152 us (12%)
  local copies, waits for them, and re-layouts  136 us (11%)
  between operations  32.8 us (3%)
    psum x1, waiting for transfers between devices, shards(): lax.psum((grad_tables, grad_vectors, grad_talking, shard_sq), ('dp', 'mp'))  132 us
    unnamed x12, waiting for transfers between devices  128 us
    psum x1, waiting for transfers between devices, shards(): stacked = lax.psum((stacked[0], stacked[1], stacked[2], stacked[3]), 'dp')  97.1 us
    reduce_scatter x1, waiting for transfers between devices, shards(): lax.psum_scatter(stacked[2], 'mp', scatter_dimension=2, tiled=True)  50.6 us
    reduce_scatter x1, waiting for transfers between devices, shards(): lax.psum_scatter(stacked[3], 'mp', scatter_dimension=1, tiled=True)  49.3 us
    dot_general x1, matrix products, self_attend_back(): jnp.einsum('hg,nhqk->ngqk', talking[1], grad_weights, precision=HIGH_PREC...  44.9 us
    unnamed x1, blocking collectives  42.4 us
    psum x1, blocking collectives, shards(): lax.psum((grad_tables, grad_vectors, grad_talking, shard_sq), ('dp', 'mp'))  41.1 us
  transfers between devices with their start and end apart: 10, of which 5 were waited for; matrix products, arithmetic and copies ran while one was open for 23% of the time, Pallas kernels for 0%

commit v1 on v0

v1 whole, which is shorter than its diff:
```python
import functools

import jax
import jax.numpy as jnp
from jax import lax
from jax.experimental import pallas as pl
from jax.experimental.pallas import tpu as pltpu
from jax.sharding import PartitionSpec as P

D = 384
HEADS = 8
HEAD = 48
PIX = 768
P_SIZE = 196
STEP = 10
SCALE = HEAD**-0.5
BETA_ONE = 0.9
BETA_TWO = 0.999
ADAM_EPS = 1e-08
DECAY = 0.01
RATE = 0.5
RATE_VECTOR = 0.5
CLIP = 0.02
TEMP = 0.05
MASKED = -1000000000.0
NORM_EPS = 1e-06
F32 = jnp.float32
BF = jnp.bfloat16
VMEM_LIMIT = 58 * 2**20
ANY = pl.BlockSpec(memory_space=pl.ANY)
MESH = pl.DeviceIdType.MESH
WHOLE = pl.BlockSpec(memory_space=pltpu.VMEM)


def nn(left, right):
    return lax.dot_general(left, right, (((1,), (0,)), ((), ())), preferred_element_type=F32)


def nt(left, right):
    return lax.dot_general(left, right, (((1,), (1,)), ((), ())), preferred_element_type=F32)


def tn(left, right):
    return lax.dot_general(left, right, (((0,), (0,)), ((), ())), preferred_element_type=F32)


def colsum(values):
    return jnp.sum(values, 0, keepdims=True)


def normalize(inputs):
    center = inputs - jnp.mean(inputs, -1, keepdims=True)
    spread = jnp.mean(center * center, -1, keepdims=True)
    inverse = lax.rsqrt(spread + NORM_EPS)
    return center * inverse, inverse


def normalize_back(unit, inverse, gain, incoming):
    scaled = incoming * gain
    return inverse * (
        scaled
        - jnp.mean(scaled, -1, keepdims=True)
        - unit * jnp.mean(scaled * unit, -1, keepdims=True)
    )


def gelu_parts(inner):
    size = jnp.abs(inner)
    t = 1.0 / (1.0 + (0.3275911 * 0.5**0.5) * size)
    bell = jnp.exp(-0.5 * inner * inner)
    poly = t * (
        0.5 * 0.254829592
        + t
        * (
            0.5 * -0.284496736
            + t * (0.5 * 1.421413741 + t * (0.5 * -1.453152027 + t * (0.5 * 1.061405429)))
        )
    )
    tail = poly * bell
    cumulative = jnp.where(inner >= 0, 1.0 - tail, tail)
    return inner * cumulative, cumulative + inner * bell * 0.3989422804014327


def head_mask():
    row = lax.broadcasted_iota(jnp.int32, (HEADS, D), 0)
    column = lax.broadcasted_iota(jnp.int32, (HEADS, D), 1)
    return ((column >= row * HEAD) & (column < row * HEAD + HEAD)).astype(F32)


def stat_lanes(parts, weight, first):
    lane = lax.broadcasted_iota(jnp.int32, (1, 128), 1)
    row = jnp.zeros((1, 128), F32)
    for place, values in enumerate(parts):
        total = jnp.sum(colsum(values * values * weight), keepdims=True)
        high = total.astype(BF).astype(F32)
        row = jnp.where(lane == first + 2 * place, high, row)
        row = jnp.where(lane == first + 2 * place + 1, total - high, row)
    return row


def part(ref, first, rows):
    shards_count = ref.shape[0]
    return ref[:, first : first + rows, :].reshape(shards_count * rows, ref.shape[2])


def self_attend_kernel(
    pixels, cols, vec, pos, wp, wattn, t1row, t2col,
    embed_out, q_out, k_out, v_out, prob_out, ho_out, raw_out, mid_out, stat_out,
):
    shard = wattn.shape[1] // 4
    x = nn(pixels[0], wp[...]) + vec[16:17, :] + pos[...]
    embed_out[0] = x
    unit, _ = normalize(x)
    normed = (unit * vec[0:1, :] + vec[1:2, :]).astype(BF)
    wv = part(wattn, 2 * shard, shard)
    q = nt(normed, part(wattn, 0, shard)).astype(BF)
    k = nt(normed, part(wattn, shard, shard)).astype(BF)
    q_out[0] = q
    k_out[0] = k
    v_out[0] = nt(normed, wv).astype(BF)
    v_flip = nt(wv, normed).astype(BF).astype(F32)
    bias = cols[0][:, 0:1]
    q_wide = q.astype(F32)
    heads_out = jnp.zeros((D, x.shape[0]), F32)
    for g in range(HEADS):
        mixed = nt(k, (q_wide * t1row[g : g + 1, :]).astype(BF)) + bias
        grown = jnp.exp(mixed - jnp.max(mixed, 0, keepdims=True))
        prob = (grown * (1.0 / jnp.sum(grown, 0, keepdims=True))).astype(BF)
        prob_out[0, g] = prob
        heads_out += nn((v_flip * t2col[:, g : g + 1]).astype(BF), prob)
    heads_out = heads_out.astype(BF)
    ho_out[0] = heads_out
    raw = tn(heads_out, part(wattn, 3 * shard, shard))
    raw_out[0] = raw.astype(BF)
    branch = vec[3:4, :] * (raw + vec[2:3, :])
    middle = x + branch
    mid_out[0] = middle
    stat_out[0] = stat_lanes((branch, middle), cols[0][:, 1:2], 8)


def feed_kernel(
    mid, cols, bias_row, base, stat, vec, wmlp, wcls,
    patch_out, act_out, slope_out, raw_out, cprob_out, cprob0_out, z_out, card_out, aux_out,
):
    hidden = wmlp.shape[1] // 2
    shard = wcls.shape[1] // 4
    mask = head_mask()

    @pl.when(pl.program_id(0) == 0)
    def _():
        unit, _ = normalize(jnp.broadcast_to(vec[17:18, :], (HEADS, D)))
        token = (unit * vec[8:9, :] + vec[9:10, :]).astype(BF)
        query = nt(token, part(wcls, 0, shard)).astype(BF).astype(F32)
        keys = nn((query * mask).astype(BF), part(wcls, shard, shard)) * SCALE
        aux_out[0:8, :] = keys
        aux_out[8:16, :] = token.astype(F32)
        aux_out[16:24, :] = query

    middle = mid[0]
    unit, _ = normalize(middle)
    normed = (unit * vec[4:5, :] + vec[5:6, :]).astype(BF)
    inner = nt(normed, part(wmlp, 0, hidden))
    active, slope = gelu_parts(inner)
    active = active.astype(BF)
    act_out[0] = active
    slope_out[0] = slope.astype(BF)
    raw = nn(active, part(wmlp, hidden, hidden))
    raw_out[0] = raw.astype(BF)
    branch = vec[7:8, :] * (raw + vec[6:7, :])
    patches = middle + branch
    patch_out[0] = patches
    first = 4 * pl.program_id(0)
    card_out[pl.ds(first + 3, 1), :] = (
        base[0] + stat[0] + stat_lanes((branch, patches), cols[0][:, 1:2], 12)
    )
    unit, _ = normalize(patches)
    normed = (unit * vec[8:9, :] + vec[9:10, :]).astype(BF)
    keys = aux_out[0:8, :]
    token = aux_out[8:16, :]
    scores = nt(keys.astype(BF), normed) + bias_row[0]
    score0 = jnp.sum(keys * token, -1, keepdims=True)
    top = jnp.maximum(jnp.max(scores, -1, keepdims=True), score0)
    grown = jnp.exp(scores - top)
    grown0 = jnp.exp(score0 - top)
    scale = 1.0 / (jnp.sum(grown, -1, keepdims=True) + grown0)
    cprob = grown * scale
    cprob0 = grown0 * scale
    cprob_out[0] = cprob
    cprob0_out[0] = jnp.broadcast_to(cprob0, (HEADS, 128))
    z = (nn(cprob.astype(BF), normed) + cprob0 * token).astype(BF)
    z_out[0] = z
    cheads = colsum(nt(z, part(wcls, 2 * shard, shard)) * mask)
    for piece in range(3):
        card_out[pl.ds(first + piece, 1), :] = cheads[:, 128 * piece : 128 * piece + 128]


def token_kernel(
    group, cards, vec, wcls, wmlp, head,
    dch_out, gout_out, gup_out, gdown_out, ghead_out, rows_out, stat_out,
):
    hidden = wmlp.shape[1] // 2
    shard = wcls.shape[1] // 4
    images = cards.shape[0] // 4
    cheads = jnp.concatenate(
        [cards[pl.ds(piece, images, stride=4), :] for piece in range(3)], 1
    ).astype(BF)
    card = cards[pl.ds(3, images, stride=4), :]
    labels = (card[:, 0:1] * 32.0 + card[:, 1:2]).astype(jnp.int32)
    pairs = (card[:, 2:3] * 32.0 + card[:, 3:4]).astype(jnp.int32)
    column = lax.broadcasted_iota(jnp.int32, (images, images), 1)
    row = lax.broadcasted_iota(jnp.int32, (images, images), 0)
    slot = lax.rem(lax.broadcasted_iota(jnp.int32, (images, 1), 0), group).astype(F32)
    okay = (slot >= group - card[:, 4:5]).astype(F32)
    okay_row = colsum(jnp.where(row == column, okay, 0.0))
    wo = part(wcls, 3 * shard, shard)
    wup = part(wmlp, 0, hidden)
    wdown = part(wmlp, hidden, hidden)
    count = jnp.sum(okay, keepdims=True)
    raw = nn(cheads, wo) + vec[10:11, :]
    branch = vec[11:12, :] * raw
    middle = vec[17:18, :] + branch
    unit2, inverse2 = normalize(middle)
    normed = (unit2 * vec[12:13, :] + vec[13:14, :]).astype(BF)
    inner = nt(normed, wup)
    active, slope = gelu_parts(inner)
    active = active.astype(BF)
    down = nn(active, wdown) + vec[14:15, :]
    mlp_branch = vec[15:16, :] * down
    token = middle + mlp_branch
    unit3, inverse3 = normalize(token)
    feature = unit3 * vec[18:19, :] + vec[19:20, :]
    feature_low = feature.astype(BF)
    logits = nt(feature_low, head[...])
    top = jnp.max(logits, -1, keepdims=True)
    grown = jnp.exp(logits - top)
    total = jnp.sum(grown, -1, keepdims=True)
    hot = lax.broadcasted_iota(jnp.int32, logits.shape, 1) == labels
    cross = jnp.log(total) + top - jnp.sum(jnp.where(hot, logits, 0.0), -1, keepdims=True)
    share = okay / count
    dlogits = (share * (grown / total - hot.astype(F32))).astype(BF)
    ghead_out[...] = tn(dlogits, feature_low)
    dfeature = nn(dlogits, head[...])

    length = lax.rsqrt(jnp.sum(feature * feature, -1, keepdims=True) + NORM_EPS)
    embed = (feature * length).astype(BF)
    sims = nt(embed, embed) / TEMP
    sims = jnp.where((okay_row > 0) & (row != column), sims, MASKED)
    top = jnp.max(sims, -1, keepdims=True)
    grown = jnp.exp(sims - top)
    total = jnp.sum(grown, -1, keepdims=True)
    hot = column == pairs
    contrast = jnp.log(total) + top - jnp.sum(jnp.where(hot, sims, 0.0), -1, keepdims=True)
    dsims = share * (grown / total - hot.astype(F32))
    high = dsims.astype(BF)
    low = (dsims - high.astype(F32)).astype(BF)
    dembed = (nn(high, embed) + nn(low, embed) + tn(high, embed) + tn(low, embed)) / TEMP
    dfeature += length * dembed - feature * (
        length * length * length * jnp.sum(dembed * feature, -1, keepdims=True)
    )

    dtoken = normalize_back(unit3, inverse3, vec[18:19, :], dfeature)
    rows_out[0:1, :] = jnp.zeros((1, D), F32)
    rows_out[1:2, :] = jnp.zeros((1, D), F32)
    rows_out[7:8, :] = colsum(dtoken * down)
    rows_out[6:7, :] = vec[15:16, :] * colsum(dtoken)
    ddown = (dtoken * vec[15:16, :]).astype(BF)
    gdown_out[...] = tn(active, ddown)
    dinner = (nt(ddown, wdown) * slope).astype(BF)
    gup_out[...] = tn(dinner, normed)
    dnormed = nn(dinner, wup)
    rows_out[4:5, :] = colsum(dnormed * unit2)
    rows_out[5:6, :] = colsum(dnormed)
    dmiddle = dtoken + normalize_back(unit2, inverse2, vec[12:13, :], dnormed)
    rows_out[3:4, :] = colsum(dmiddle * raw)
    rows_out[2:3, :] = vec[11:12, :] * colsum(dmiddle)
    rows_out[8:9, :] = colsum(dmiddle)
    rows_out[9:10, :] = colsum(dfeature * unit3)
    rows_out[10:11, :] = colsum(dfeature)
    dbranch = (dmiddle * vec[11:12, :]).astype(BF)
    gout_out[...] = tn(cheads, dbranch)
    dch_out[...] = nt(dbranch, wo).astype(BF)
    lane = lax.broadcasted_iota(jnp.int32, (1, 128), 1)
    self_sums = colsum(card)
    count_tokens = self_sums[:, 5:6]

    def squares(values):
        return jnp.sum(colsum(values * values * okay), keepdims=True)

    entries = [jnp.sum(okay * cross, keepdims=True), jnp.sum(okay * contrast, keepdims=True)]
    entries += [count, count_tokens]
    entries += [
        jnp.sqrt((self_sums[:, i : i + 1] + self_sums[:, i + 1 : i + 2]) / D / count_tokens)
        for i in (8, 10, 12, 14)
    ]
    entries += [
        jnp.sqrt(squares(item) / D / count) for item in (branch, middle, mlp_branch, token)
    ]
    line = jnp.zeros((1, 128), F32)
    for i, entry in enumerate(entries):
        line = jnp.where(lane == i, entry, line)
    stat_out[...] = jnp.broadcast_to(line, (8, 128))


def feed_back_kernel(
    dch, patch, mid, raw, act, slope, cprob, cprob0, z, aux, vec, wcls, wmlp,
    dmid_out, gmlp_out, gv_out, rows_out,
):
    hidden = wmlp.shape[1] // 2
    shard = wcls.shape[1] // 4
    count = wmlp.shape[0]
    mask = head_mask()

    @pl.when(pl.program_id(0) == 0)
    def _():
        gmlp_out[...] = jnp.zeros_like(gmlp_out)
        gv_out[...] = jnp.zeros_like(gv_out)
        rows_out[...] = jnp.zeros_like(rows_out)

    keys = aux[0:8, :]
    token = aux[8:16, :]
    unit, inverse = normalize(patch[0])
    normed = (unit * vec[8:9, :] + vec[9:10, :]).astype(BF)
    spread = (mask * dch[0].astype(F32)).astype(BF)
    dz = nn(spread, part(wcls, 2 * shard, shard))
    dz_low = dz.astype(BF)
    probs = cprob[0]
    prob0 = cprob0[0][:, 0:1]
    dprobs = nt(dz_low, normed)
    dprob0 = jnp.sum(dz * token, -1, keepdims=True)
    inside = jnp.sum(dprobs * probs, -1, keepdims=True) + dprob0 * prob0
    dscores = (probs * (dprobs - inside)).astype(BF)
    dscore0 = prob0 * (dprob0 - inside)
    dnormed = tn(
        jnp.concatenate([probs.astype(BF), dscores], 0),
        jnp.concatenate([dz_low, keys.astype(BF)], 0),
    )
    rows_out[8:16, :] += nn(dscores, normed) + dscore0 * token
    rows_out[6:7, :] += colsum(prob0 * dz + dscore0 * keys)
    gv_out[...] += tn(spread, z[0])
    rows_out[4:5, :] += colsum(dnormed * unit)
    rows_out[5:6, :] += colsum(dnormed)
    incoming = normalize_back(unit, inverse, vec[8:9, :], dnormed)

    unit, inverse = normalize(mid[0])
    normed = (unit * vec[4:5, :] + vec[5:6, :]).astype(BF)
    rows_out[3:4, :] += colsum(incoming * (raw[0].astype(F32) + vec[6:7, :]))
    rows_out[2:3, :] += vec[7:8, :] * colsum(incoming)
    ddown = (incoming * vec[7:8, :]).astype(BF)
    gmlp_out[:, hidden:, :] += tn(act[0], ddown).reshape(count, hidden, D)
    dinner = (nt(ddown, part(wmlp, hidden, hidden)) * slope[0].astype(F32)).astype(BF)
    gmlp_out[:, :hidden, :] += tn(dinner, normed).reshape(count, hidden, D)
    dnormed = nn(dinner, part(wmlp, 0, hidden))
    rows_out[0:1, :] += colsum(dnormed * unit)
    rows_out[1:2, :] += colsum(dnormed)
    dmid_out[0] = incoming + normalize_back(unit, inverse, vec[4:5, :], dnormed)


def self_back_kernel(
    dmid, pixels, embed, q, k, v, prob, ho, raw, vec, wattn, t1row, t1col, t2row,
    gattn_out, gpix_out, gpos_out, rows_out,
):
    shard = wattn.shape[1] // 4
    count = wattn.shape[0]

    @pl.when(pl.program_id(0) == 0)
    def _():
        gattn_out[...] = jnp.zeros_like(gattn_out)
        gpix_out[...] = jnp.zeros_like(gpix_out)
        gpos_out[...] = jnp.zeros_like(gpos_out)
        rows_out[...] = jnp.zeros_like(rows_out)

    wq = part(wattn, 0, shard)
    wk = part(wattn, shard, shard)
    wv = part(wattn, 2 * shard, shard)
    wo = part(wattn, 3 * shard, shard)
    incoming = dmid[0]
    rows_out[3:4, :] += colsum(incoming * (raw[0].astype(F32) + vec[2:3, :]))
    rows_out[2:3, :] += vec[3:4, :] * colsum(incoming)
    dbranch = (incoming * vec[3:4, :]).astype(BF)
    gattn_out[:, 3 * shard :, :] += nn(ho[0], dbranch).reshape(count, shard, D)
    dheads = nt(dbranch, wo).astype(BF)

    unit, inverse = normalize(embed[0])
    normed = (unit * vec[0:1, :] + vec[1:2, :]).astype(BF)
    q_low = q[0]
    k_wide = k[0].astype(F32)
    v_wide = v[0].astype(F32)
    k_flip = nt(wk, normed).astype(BF).astype(F32)
    dq = jnp.zeros((D, normed.shape[0]), F32)
    dk = jnp.zeros(normed.shape, F32)
    dv = jnp.zeros(normed.shape, F32)
    for g in range(HEADS):
        one = t1row[g : g + 1, :]
        two = t2row[g : g + 1, :]
        chance = prob[0, g]
        chance_wide = chance.astype(F32)
        dprob = nt((v_wide * two).astype(BF), dheads)
        dmixed = (chance_wide * (dprob - colsum(dprob * chance_wide))).astype(BF)
        dpost = nn(chance, dheads)
        dv += two * dpost
        rows_out[16 + g : 17 + g, :] += colsum(v_wide * dpost)
        dpre = nn(dmixed, q_low)
        dk += one * dpre
        rows_out[8 + g : 9 + g, :] += colsum(k_wide * dpre)
        dq += nn((k_flip * t1col[:, g : g + 1]).astype(BF), dmixed)
    dq = dq.astype(BF)
    dk = dk.astype(BF)
    dv = dv.astype(BF)
    gattn_out[:, :shard, :] += nn(dq, normed).reshape(count, shard, D)
    gattn_out[:, shard : 2 * shard, :] += tn(dk, normed).reshape(count, shard, D)
    gattn_out[:, 2 * shard : 3 * shard, :] += tn(dv, normed).reshape(count, shard, D)
    dnormed = tn(dq, wq) + nn(dk, wk) + nn(dv, wv)
    rows_out[0:1, :] += colsum(dnormed * unit)
    rows_out[1:2, :] += colsum(dnormed)
    dx = incoming + normalize_back(unit, inverse, vec[0:1, :], dnormed)
    gpos_out[...] += dx
    gpix_out[...] += tn(pixels[0], dx.astype(BF))


def per_image(*tail):
    return pl.BlockSpec((1, *tail), lambda n: (n, *(0 for _ in tail)))


def constant(*shape):
    return pl.BlockSpec(shape, lambda n: tuple(0 for _ in shape))


def shaped(*shape, dtype=F32):
    return jax.ShapeDtypeStruct(shape, dtype)


def params():
    return pltpu.CompilerParams(vmem_limit_bytes=VMEM_LIMIT, dimension_semantics=("arbitrary",))


def run_self_attend(pixels, cols, vec, pos, wp, wattn, t1row, t2col):
    count = pixels.shape[0]
    return pl.pallas_call(
        self_attend_kernel,
        grid=(count,),
        in_specs=[
            per_image(P_SIZE, PIX), per_image(P_SIZE, 2), constant(*vec.shape), constant(P_SIZE, D),
            constant(PIX, D), constant(*wattn.shape), constant(HEADS, D), constant(D, HEADS),
        ],
        out_specs=[
            per_image(P_SIZE, D), per_image(P_SIZE, D), per_image(P_SIZE, D), per_image(P_SIZE, D),
            per_image(HEADS, P_SIZE, P_SIZE), per_image(D, P_SIZE), per_image(P_SIZE, D),
            per_image(P_SIZE, D), per_image(1, 128),
        ],
        out_shape=[
            shaped(count, P_SIZE, D), shaped(count, P_SIZE, D, dtype=BF),
            shaped(count, P_SIZE, D, dtype=BF), shaped(count, P_SIZE, D, dtype=BF),
            shaped(count, HEADS, P_SIZE, P_SIZE, dtype=BF), shaped(count, D, P_SIZE, dtype=BF),
            shaped(count, P_SIZE, D, dtype=BF), shaped(count, P_SIZE, D), shaped(count, 1, 128),
        ],
        compiler_params=params(),
        name="self_attend",
    )(pixels, cols, vec, pos, wp, wattn, t1row, t2col)


def run_feed(mid, cols, bias_row, base, stat, vec, wmlp, wcls):
    count = mid.shape[0]
    wide = 2 * wmlp.shape[0] * wmlp.shape[1] // 4
    return pl.pallas_call(
        feed_kernel,
        grid=(count,),
        in_specs=[
            per_image(P_SIZE, D), per_image(P_SIZE, 2), per_image(1, P_SIZE), per_image(1, 128),
            per_image(1, 128), constant(*vec.shape), constant(*wmlp.shape), constant(*wcls.shape),
        ],
        out_specs=[
            per_image(P_SIZE, D), per_image(P_SIZE, wide), per_image(P_SIZE, wide),
            per_image(P_SIZE, D), per_image(HEADS, P_SIZE), per_image(HEADS, 128),
            per_image(HEADS, D), constant(4 * count, 128), constant(24, D),
        ],
        out_shape=[
            shaped(count, P_SIZE, D), shaped(count, P_SIZE, wide, dtype=BF),
            shaped(count, P_SIZE, wide, dtype=BF), shaped(count, P_SIZE, D, dtype=BF),
            shaped(count, HEADS, P_SIZE), shaped(count, HEADS, 128),
            shaped(count, HEADS, D, dtype=BF), shaped(4 * count, 128), shaped(24, D),
        ],
        compiler_params=params(),
        name="feed",
    )(mid, cols, bias_row, base, stat, vec, wmlp, wcls)


def run_token(group, cards, vec, wcls, wmlp, head):
    images = cards.shape[0] // 4
    wide = wmlp.shape[0] * wmlp.shape[1] // 2
    return pl.pallas_call(
        functools.partial(token_kernel, group),
        in_specs=[WHOLE] * 5,
        out_specs=[WHOLE] * 7,
        out_shape=[
            shaped(images, D, dtype=BF), shaped(D, D), shaped(wide, D), shaped(wide, D),
            shaped(*head.shape), shaped(16, D), shaped(8, 128),
        ],
        compiler_params=pltpu.CompilerParams(vmem_limit_bytes=VMEM_LIMIT),
        name="token_net",
    )(cards, vec, wcls, wmlp, head)


def run_feed_back(dch, patch, mid, raw, act, slope, cprob, cprob0, z, aux, vec, wcls, wmlp):
    count = mid.shape[0]
    wide = act.shape[2]
    return pl.pallas_call(
        feed_back_kernel,
        grid=(count,),
        in_specs=[
            per_image(1, D), per_image(P_SIZE, D), per_image(P_SIZE, D), per_image(P_SIZE, D),
            per_image(P_SIZE, wide), per_image(P_SIZE, wide), per_image(HEADS, P_SIZE),
            per_image(HEADS, 128), per_image(HEADS, D), constant(24, D), constant(*vec.shape),
            constant(*wcls.shape), constant(*wmlp.shape),
        ],
        out_specs=[
            per_image(P_SIZE, D), constant(*wmlp.shape), constant(D, D), constant(16, D),
        ],
        out_shape=[
            shaped(count, P_SIZE, D), shaped(*wmlp.shape), shaped(D, D), shaped(16, D),
        ],
        compiler_params=params(),
        name="feed_back",
    )(dch, patch, mid, raw, act, slope, cprob, cprob0, z, aux, vec, wcls, wmlp)


def run_self_back(dmid, pixels, embed, q, k, v, prob, ho, raw, vec, wattn, t1row, t1col, t2row):
    count = dmid.shape[0]
    return pl.pallas_call(
        self_back_kernel,
        grid=(count,),
        in_specs=[
            per_image(P_SIZE, D), per_image(P_SIZE, PIX), per_image(P_SIZE, D),
            per_image(P_SIZE, D), per_image(P_SIZE, D), per_image(P_SIZE, D),
            per_image(HEADS, P_SIZE, P_SIZE), per_image(D, P_SIZE), per_image(P_SIZE, D),
            constant(*vec.shape), constant(*wattn.shape), constant(HEADS, D), constant(D, HEADS),
            constant(HEADS, D),
        ],
        out_specs=[
            constant(*wattn.shape), constant(PIX, D), constant(P_SIZE, D), constant(24, D),
        ],
        out_shape=[shaped(*wattn.shape), shaped(PIX, D), shaped(P_SIZE, D), shaped(24, D)],
        compiler_params=params(),
        name="self_back",
    )(dmid, pixels, embed, q, k, v, prob, ho, raw, vec, wattn, t1row, t1col, t2row)


def peer_at(index, n_mp):
    return (lax.div(index, n_mp), lax.rem(index, n_mp))


def greet_all(me, n, n_mp):
    barrier = pltpu.get_barrier_semaphore()

    @pl.loop(1, n)
    def _(step):
        pl.semaphore_signal(
            barrier, inc=1, device_id=peer_at(lax.rem(me + step, n), n_mp), device_id_type=MESH
        )

    pl.semaphore_wait(barrier, n - 1)


def remote(src, dst, send_sem, recv_sem, device):
    return pltpu.make_async_remote_copy(
        src_ref=src, dst_ref=dst, send_sem=send_sem, recv_sem=recv_sem,
        device_id=device, device_id_type=MESH,
    )


def spread_to_all(me, n, n_mp, slots, rows, send_sem, recv_sem):
    def slot(index):
        return slots.at[pl.ds(pl.multiple_of(index * rows, rows), rows)]

    @pl.loop(1, n)
    def _(step):
        remote(
            slot(me), slot(me), send_sem.at[step], recv_sem.at[step],
            peer_at(lax.rem(me + step, n), n_mp),
        ).start()

    def finish():
        @pl.loop(1, n)
        def _(step):
            source = lax.rem(me + n - step, n)
            copy = remote(
                slot(me), slot(source), send_sem.at[step], recv_sem.at[step],
                peer_at(source, n_mp),
            )
            copy.wait_send()
            copy.wait_recv()

    return finish


def card_kernel(n_dp, n_mp, card, out, slots, send_sem, recv_sem):
    n = n_dp * n_mp
    me = lax.axis_index("dp") * n_mp + lax.axis_index("mp")
    rows = card.shape[0]
    greet_all(me, n, n_mp)
    slots[pl.ds(pl.multiple_of(me * rows, rows), rows), :] = card[...].astype(BF)
    spread_to_all(me, n, n_mp, slots, rows, send_sem, recv_sem)()
    out[...] = slots[...].astype(F32)


def run_cards(n_dp, n_mp, card):
    n = n_dp * n_mp
    return pl.pallas_call(
        functools.partial(card_kernel, n_dp, n_mp),
        in_specs=[WHOLE],
        out_specs=WHOLE,
        out_shape=shaped(n * card.shape[0], 128),
        scratch_shapes=[
            pltpu.VMEM((n * card.shape[0], 128), BF),
            pltpu.SemaphoreType.DMA((n,)),
            pltpu.SemaphoreType.DMA((n,)),
        ],
        compiler_params=pltpu.CompilerParams(
            vmem_limit_bytes=VMEM_LIMIT, collective_id=1, has_side_effects=True
        ),
        name="cards",
    )(card)


def weight_kernel(n_dp, n_mp, shard, out, near_send, near_recv, far_send, far_recv):
    dp = lax.axis_index("dp")
    mp = lax.axis_index("mp")
    n_y = n_mp // 2
    y = lax.div(mp, 2)
    core = lax.rem(mp, 2)
    sibling = (dp, y * 2 + 1 - core)
    barrier = pltpu.get_barrier_semaphore()
    pl.semaphore_signal(barrier, inc=1, device_id=sibling, device_id_type=MESH)
    for step in range(1, n_y):
        pl.semaphore_signal(
            barrier, inc=1, device_id=(dp, lax.rem(y + step, n_y) * 2 + core), device_id_type=MESH
        )
    pl.semaphore_wait(barrier, n_y)
    far = [
        remote(
            shard, out.at[mp], far_send.at[step], far_recv.at[step],
            (dp, lax.rem(y + step, n_y) * 2 + core),
        )
        for step in range(1, n_y)
    ]
    for copy in far:
        copy.start()
    near = [remote(shard, out.at[mp], near_send.at[0], near_recv.at[0], sibling)]
    near[0].start()
    out[pl.ds(mp, 1)] = shard[...][None]
    for step in range(1, n_y):
        source = lax.rem(y + n_y - step, n_y) * 2
        slot = source + core
        remote(
            shard, out.at[slot], far_send.at[step], far_recv.at[step], (dp, slot)
        ).wait_recv()
        copy = remote(
            out.at[slot], out.at[slot], near_send.at[step], near_recv.at[step], sibling
        )
        copy.start()
        near.append(copy)
    for copy in far:
        copy.wait_send()
    for step in range(n_y):
        slot = lax.rem(y + n_y - step, n_y) * 2 + 1 - core
        near[step].wait_send()
        remote(
            out.at[slot], out.at[slot], near_send.at[step], near_recv.at[step], sibling
        ).wait_recv()


def run_weights(n_dp, n_mp, rows):
    n_y = n_mp // 2
    return pl.pallas_call(
        functools.partial(weight_kernel, n_dp, n_mp),
        in_specs=[WHOLE],
        out_specs=WHOLE,
        out_shape=shaped(n_mp, *rows.shape, dtype=BF),
        scratch_shapes=[pltpu.SemaphoreType.DMA((n_y,))] * 4,
        compiler_params=pltpu.CompilerParams(
            vmem_limit_bytes=VMEM_LIMIT, collective_id=2, has_side_effects=True
        ),
        name="weights",
    )(rows)


def reduce_kernel(
    n_dp, n_mp, gattn, gmlp, gv, gpix, gpos, rows2, rows3,
    block_out, shared_out, square_out,
    blocks, commons, near_b, near_s, part_b, part_s, far_b, far_s, half_b, half_s, last_b, last_s,
    squares, near_sem, far_sem, last_sem, all_send, all_recv, block_sem, square_sem,
):
    n = n_dp * n_mp
    n_y = n_mp // 2
    dp = lax.axis_index("dp")
    mp = lax.axis_index("mp")
    me = dp * n_mp + mp
    y = lax.div(mp, 2)
    core = lax.rem(mp, 2)
    sibling = (dp, y * 2 + 1 - core)
    chunk_b = block_out.shape[0] // n_dp
    chunk_s = shared_out.shape[0] // n
    wide_s = chunk_s * n_dp

    greet_all(me, n, n_mp)

    first = 0
    for item in (gattn, gmlp, gv):
        size = item.shape[1]
        blocks[:, first : first + size, :] = item[...].astype(BF)
        first += size
    if first < blocks.shape[1]:
        blocks[:, first:, :] = jnp.zeros((n_mp, blocks.shape[1] - first, D), BF)
    commons[:PIX, :] = gpix[...].astype(BF)
    commons[PIX : PIX + P_SIZE + 12, :] = jnp.concatenate(
        [gpos[...], jnp.zeros((12, D), F32)], 0
    ).astype(BF)
    commons[PIX + 208 : PIX + 224, :] = rows2[...].astype(BF)
    commons[PIX + 224 : PIX + 256, :] = jnp.concatenate(
        [rows3[...], jnp.zeros((8, D), F32)], 0
    ).astype(BF)
    if commons.shape[0] > PIX + 256:
        commons[PIX + 256 :, :] = jnp.zeros((commons.shape[0] - PIX - 256, D), BF)

    def common(index, rows):
        return commons.at[pl.ds(pl.multiple_of(index * rows, rows), rows)]

    near = []
    for step in range(1, n_y + 1):
        place = lax.rem(y + step, n_y)
        give = place * 2 + 1 - core
        near.append(remote(blocks.at[give], near_b.at[place], near_sem.at[0, step], near_sem.at[1, step], sibling))
        near.append(remote(common(give, wide_s), near_s.at[place], near_sem.at[2, step], near_sem.at[3, step], sibling))
    for copy in near:
        copy.start()

    far = []
    for step in range(1, n_y + 1):
        place = lax.rem(y + step, n_y)
        near[2 * step - 2].wait_recv()
        near[2 * step - 1].wait_recv()
        keep = place * 2 + core
        part_b[pl.ds(place, 1)] = (
            blocks[pl.ds(keep, 1)].astype(F32) + near_b[pl.ds(place, 1)].astype(F32)
        ).astype(BF)
        part_s[pl.ds(place, 1)] = (
            commons[pl.ds(pl.multiple_of(keep * wide_s, wide_s), wide_s), :].astype(F32)[None]
            + near_s[pl.ds(place, 1)].astype(F32)
        ).astype(BF)
        if step < n_y:
            to = (dp, keep)
            far.append(remote(part_b.at[place], far_b.at[step - 1], far_sem.at[0, step], far_sem.at[1, step], to))
            far.append(remote(part_s.at[place], far_s.at[step - 1], far_sem.at[2, step], far_sem.at[3, step], to))
            far[-2].start()
            far[-1].start()
    total_b = part_b[pl.ds(y, 1)][0].astype(F32)
    total_s = part_s[pl.ds(y, 1)][0].astype(F32)
    for step in range(1, n_y):
        far[2 * step - 2].wait_recv()
        far[2 * step - 1].wait_recv()
        total_b += far_b[step - 1].astype(F32)
        total_s += far_s[step - 1].astype(F32)
    half_b[...] = total_b.astype(BF)
    half_s[...] = total_s.astype(BF)

    def rows_of(ref, index, rows):
        return ref.at[pl.ds(pl.multiple_of(index * rows, rows), rows)]

    last = []
    for step in range(1, n_dp):
        place = lax.rem(dp + step, n_dp)
        to = (place, mp)
        last.append(remote(rows_of(half_b, place, chunk_b), last_b.at[step - 1], last_sem.at[0, step], last_sem.at[1, step], to))
        last.append(remote(rows_of(half_s, place, chunk_s), last_s.at[step - 1], last_sem.at[2, step], last_sem.at[3, step], to))
    for copy in last:
        copy.start()
    total_b = half_b[pl.ds(pl.multiple_of(dp * chunk_b, chunk_b), chunk_b), :].astype(F32)
    total_s = half_s[pl.ds(pl.multiple_of(dp * chunk_s, chunk_s), chunk_s), :].astype(F32)
    for step in range(1, n_dp):
        last[2 * step - 2].wait_recv()
        last[2 * step - 1].wait_recv()
        total_b += last_b[step - 1].astype(F32)
        total_s += last_s[step - 1].astype(F32)
    block_out[pl.ds(pl.multiple_of(dp * chunk_b, chunk_b), chunk_b), :] = total_b.astype(BF)
    own = mp * n_dp + dp
    shared_out[pl.ds(pl.multiple_of(own * chunk_s, chunk_s), chunk_s), :] = total_s.astype(BF)

    back = []
    for step in range(1, n_dp):
        back.append(
            remote(
                rows_of(block_out, dp, chunk_b), rows_of(block_out, dp, chunk_b),
                block_sem.at[0, step], block_sem.at[1, step], (lax.rem(dp + step, n_dp), mp),
            )
        )
        back[-1].start()

    @pl.loop(1, n)
    def _(step):
        remote(
            rows_of(shared_out, own, chunk_s), rows_of(shared_out, own, chunk_s),
            all_send.at[step], all_recv.at[step], peer_at(lax.rem(me + step, n), n_mp),
        ).start()

    for step in range(1, n_dp):
        source = lax.rem(dp + n_dp - step, n_dp)
        remote(
            rows_of(block_out, dp, chunk_b), rows_of(block_out, source, chunk_b),
            block_sem.at[0, step], block_sem.at[1, step], (source, mp),
        ).wait_recv()

    sums = block_out[...].astype(F32)
    sums = colsum(sums * sums)
    squares[pl.ds(mp, 1)] = jnp.broadcast_to(
        sums[:, 0:128] + sums[:, 128:256] + sums[:, 256:384], (8, 128)
    )[None]
    tally = []
    for step in range(1, n_mp):
        tally.append(
            remote(
                squares.at[mp], squares.at[mp], square_sem.at[0, step], square_sem.at[1, step],
                (dp, lax.rem(mp + step, n_mp)),
            )
        )
        tally[-1].start()

    @pl.loop(1, n)
    def _(step):
        source = lax.rem(me + n - step, n)
        copy = remote(
            rows_of(shared_out, own, chunk_s),
            rows_of(shared_out, lax.rem(source, n_mp) * n_dp + lax.div(source, n_mp), chunk_s),
            all_send.at[step], all_recv.at[step], peer_at(source, n_mp),
        )
        copy.wait_send()
        copy.wait_recv()

    for step in range(1, n_mp):
        source = lax.rem(mp + n_mp - step, n_mp)
        tally[step - 1].wait_send()
        remote(
            squares.at[mp], squares.at[source], square_sem.at[0, step], square_sem.at[1, step],
            (dp, source),
        ).wait_recv()
    square_out[...] = jnp.sum(squares[...], 0)
    for copy in near + far + last + back:
        copy.wait_send()


def run_reduce(n_dp, n_mp, gattn, gmlp, gv, gpix, gpos, rows2, rows3):
    n = n_dp * n_mp
    n_y = n_mp // 2
    rows_b = gattn.shape[1] + gmlp.shape[1] + gv.shape[1]
    chunk_b = -(-rows_b // (16 * n_dp)) * 16
    rows_b = chunk_b * n_dp
    chunk_s = -(-(PIX + 256) // (16 * n)) * 16
    wide_s = chunk_s * n_dp
    y_less = max(n_y - 1, 1)
    dma = pltpu.SemaphoreType.DMA
    return pl.pallas_call(
        functools.partial(reduce_kernel, n_dp, n_mp),
        in_specs=[WHOLE] * 7,
        out_specs=[WHOLE] * 3,
        out_shape=[
            shaped(rows_b, D, dtype=BF), shaped(chunk_s * n, D, dtype=BF), shaped(8, 128),
        ],
        scratch_shapes=[
            pltpu.VMEM((n_mp, rows_b, D), BF), pltpu.VMEM((n * chunk_s, D), BF),
            pltpu.VMEM((n_y, rows_b, D), BF), pltpu.VMEM((n_y, wide_s, D), BF),
            pltpu.VMEM((n_y, rows_b, D), BF), pltpu.VMEM((n_y, wide_s, D), BF),
            pltpu.VMEM((y_less, rows_b, D), BF), pltpu.VMEM((y_less, wide_s, D), BF),
            pltpu.VMEM((rows_b, D), BF), pltpu.VMEM((wide_s, D), BF),
            pltpu.VMEM((n_dp - 1, chunk_b, D), BF), pltpu.VMEM((n_dp - 1, chunk_s, D), BF),
            pltpu.VMEM((n_mp, 8, 128), F32),
            dma((4, n_y + 1)), dma((4, n_y + 1)), dma((4, n_dp)), dma((n,)), dma((n,)),
            dma((2, n_dp)), dma((2, n_mp)),
        ],
        compiler_params=pltpu.CompilerParams(
            vmem_limit_bytes=VMEM_LIMIT, collective_id=3, has_side_effects=True
        ),
        name="reduce",
    )(gattn, gmlp, gv, gpix, gpos, rows2, rows3)


def adam_parts(gradient, mean, square, factor):
    clipped = gradient * factor
    mean_new = BETA_ONE * mean + (1.0 - BETA_ONE) * clipped
    square_new = BETA_TWO * square + (1.0 - BETA_TWO) * clipped * clipped
    direction = (
        mean_new
        / (1.0 - BETA_ONE**STEP)
        / (jnp.sqrt(square_new / (1.0 - BETA_TWO**STEP)) + ADAM_EPS)
    )
    return (mean_new, square_new, direction)


def layer_squares(values):
    return jnp.stack([jnp.sum(values[0] * values[0]), jnp.sum(values[1] * values[1])])


def trust_of(weight_sq, update_sq):
    return jnp.sqrt(weight_sq / (update_sq + 1e-12))


def per_layer(values, like):
    return values.reshape((2,) + (1,) * (like.ndim - 1))


def shards(
    pixels,
    token_mask,
    counts,
    labels,
    pairs,
    attn_in,
    attn_in_mean,
    attn_in_square,
    attn_out,
    attn_out_mean,
    attn_out_square,
    mlp_in,
    mlp_in_mean,
    mlp_in_square,
    mlp_out,
    mlp_out_mean,
    mlp_out_square,
    tables,
    tables_mean,
    tables_square,
    vectors,
    vectors_mean,
    vectors_square,
    talking,
    talking_mean,
    talking_square,
):
    local = pixels.shape[0]
    group = token_mask.shape[0]
    place_mp = lax.axis_index("mp")
    place_dp = lax.axis_index("dp")
    n_mp = lax.axis_size("mp")
    n_dp = lax.axis_size("dp")
    images = local * n_mp * n_dp
    place = place_dp * n_mp + place_mp
    hs = attn_in.shape[3]
    fs = mlp_in.shape[2]

    attn_rows = [
        jnp.concatenate(
            [attn_in[b].transpose(1, 2, 0).reshape(3 * hs, D), attn_out[b]], 0
        ).astype(BF)
        for b in range(2)
    ]
    mlp_rows = [jnp.concatenate([mlp_in[b].T, mlp_out[b]], 0).astype(BF) for b in range(2)]
    wattn = run_weights(n_dp, n_mp, attn_rows[0])
    wmlp = lax.all_gather(mlp_rows[0], "mp")
    wcls = lax.all_gather(attn_rows[1], "mp")
    wmlp_cls = lax.all_gather(mlp_rows[1], "mp")

    okay = lax.dynamic_slice_in_dim(
        (jnp.arange(group) >= group - counts[0]).astype(F32), place_mp * local, local, 0
    )
    keep = lax.dynamic_slice_in_dim(token_mask > 0, place_mp * local, local, 0)
    token_weight = keep.astype(F32) * okay[:, None]
    bias = jnp.where(keep, 0.0, MASKED).astype(F32)
    cols = jnp.stack([bias, token_weight], -1)
    digits = [labels // 32, labels % 32, pairs // 32, pairs % 32]
    digits = [item.astype(F32) for item in digits]
    digits += [jnp.broadcast_to(counts, (local,)).astype(F32), jnp.sum(token_weight, 1)]
    base = jnp.pad(jnp.stack(digits, 1), ((0, 0), (0, 128 - len(digits))))[:, None, :]

    spread_heads = functools.partial(jnp.repeat, repeats=HEAD, axis=1)
    t1row = spread_heads(talking[0]) * SCALE
    t1col = t1row.T
    t2row = spread_heads(talking[1].T)
    t2col = t2row.T
    wp = tables[:PIX].astype(BF)
    pos = tables[PIX : PIX + P_SIZE]
    head = tables[PIX + P_SIZE :].astype(BF)

    embed, q, k, v, prob, ho, raw0, middle, stat_a = run_self_attend(
        pixels, cols, vectors, pos, wp, wattn, t1row, t2col
    )
    patches, act, slope, raw1, cprob, cprob0, z, card, aux = run_feed(
        middle, cols, bias[:, None, :], base, stat_a, vectors, wmlp, wcls
    )
    cards = run_cards(n_dp, n_mp, card)
    dch, gout1, gup1, gdown1, ghead, rows1, stat = run_token(
        group, cards, vectors, wcls, wmlp_cls, head
    )
    dch = lax.dynamic_slice_in_dim(dch, place * local, local, 0).reshape(local, 1, D)
    dmid, gmlp, gv, rows2 = run_feed_back(
        dch, patches, middle, raw1, act, slope, cprob, cprob0, z, aux, vectors, wcls, wmlp
    )
    gattn, gpix, gpos, rows3 = run_self_back(
        dmid, pixels, embed, q, k, v, prob, ho, raw0, vectors, wattn, t1row, t1col, t2row
    )

    block, shared, block_sq = run_reduce(
        n_dp, n_mp, gattn, gmlp, gv.reshape(n_mp, hs, D), gpix, gpos, rows2, rows3
    )
    sharded = block.astype(F32)
    shared = shared[: PIX + 256].astype(F32)
    gpix = shared[:PIX]
    gpos = shared[PIX : PIX + P_SIZE]
    rows2 = shared[PIX + 208 : PIX + 224]
    rows3 = shared[PIX + 224 : PIX + 248]

    dkeys = rows2[8:16]
    token = aux[8:9]
    query = aux[16]
    wq1 = wcls[:, :hs].reshape(D, D)
    wk1 = wcls[:, hs : 2 * hs].reshape(D, D)
    dquery = SCALE * jnp.sum(wk1.astype(F32) * jnp.repeat(dkeys, HEAD, axis=0), 1)
    gq1 = dquery[:, None] * token
    gk1 = (SCALE * query)[:, None] * jnp.repeat(dkeys, HEAD, axis=0)
    dtoken = rows2[6] + jnp.sum(dquery[:, None] * wq1.astype(F32), 0)
    unit, inverse = normalize(vectors[17])
    grad_class_token = rows1[8] + normalize_back(unit, inverse, vectors[8], dtoken)
    grad_vectors = jnp.stack(
        [
            rows3[0], rows3[1], rows3[2], rows3[3], rows2[0], rows2[1], rows2[2], rows2[3],
            rows2[4] + dtoken * unit, rows2[5] + dtoken, rows1[2], rows1[3],
            rows1[4], rows1[5], rows1[6], rows1[7],
            jnp.sum(gpos, 0), grad_class_token, rows1[9], rows1[10],
        ]
    )
    by_head = rows3[8:24].reshape(2, HEADS, HEADS, HEAD).sum(-1)
    grad_talking = jnp.stack([by_head[0] * SCALE, by_head[1].T])

    def mine(rows, size):
        return lax.dynamic_slice_in_dim(rows, place_mp * size, size, 0)

    def unpack(rows):
        return rows.reshape(3, hs, D).transpose(2, 0, 1)

    class_rows = jnp.concatenate([mine(gq1, hs), mine(gk1, hs), sharded[4 * hs + 2 * fs : 5 * hs + 2 * fs]], 0)
    grads = (
        jnp.stack([unpack(sharded[: 3 * hs]), unpack(class_rows)]),
        jnp.stack([sharded[3 * hs : 4 * hs], mine(gout1, hs)]),
        jnp.stack([sharded[4 * hs : 4 * hs + fs].T, mine(gup1, fs).T]),
        jnp.stack([sharded[4 * hs + fs : 4 * hs + 2 * fs], mine(gdown1, fs)]),
    )
    grad_tables = jnp.concatenate([gpix, gpos, ghead], 0)

    weights = (attn_in, attn_out, mlp_in, mlp_out)
    means = (attn_in_mean, attn_out_mean, mlp_in_mean, mlp_out_mean)
    squares = (attn_in_square, attn_out_square, mlp_in_square, mlp_out_square)
    grad_norm = jnp.sqrt(
        jnp.sum(block_sq[0])
        + sum(jnp.sum(item * item) for item in (gq1, gk1, gout1, gup1, gdown1))
        + jnp.sum(grad_tables * grad_tables)
        + jnp.sum(grad_vectors * grad_vectors)
        + jnp.sum(grad_talking * grad_talking)
    )
    factor = CLIP / jnp.maximum(grad_norm, CLIP)
    moved = [adam_parts(grads[i], means[i], squares[i], factor) for i in range(4)]
    updates = [moved[i][2] + DECAY * weights[i] for i in range(4)]
    weight_sq, update_sq = lax.psum(
        (
            jnp.concatenate([layer_squares(item) for item in weights]),
            jnp.concatenate([layer_squares(item) for item in updates]),
        ),
        "mp",
    )
    trust = trust_of(weight_sq, update_sq)
    renewed = [
        weights[i] - RATE * per_layer(trust[2 * i : 2 * i + 2], weights[i]) * updates[i]
        for i in range(4)
    ]

    table_mean, table_square, table_direction = adam_parts(
        grad_tables, tables_mean, tables_square, factor
    )
    table_update = table_direction + DECAY * tables
    bounds = ((0, PIX), (PIX, PIX + P_SIZE), (PIX + P_SIZE, tables.shape[0]))

    def segments(values):
        by_row = jnp.sum(values * values, 1)
        return jnp.stack([jnp.sum(by_row[low:high]) for low, high in bounds])

    table_weight_sq = segments(tables)
    table_update_sq = segments(table_update)
    table_trust = trust_of(table_weight_sq, table_update_sq)
    row = jnp.arange(tables.shape[0])[:, None]
    row_trust = jnp.where(
        row < PIX, table_trust[0], jnp.where(row < PIX + P_SIZE, table_trust[1], table_trust[2])
    )
    tables_new = tables - RATE * row_trust * table_update

    vector_mean, vector_square, vector_direction = adam_parts(
        grad_vectors, vectors_mean, vectors_square, factor
    )
    vectors_new = vectors - RATE_VECTOR * vector_direction
    mixing_mean, mixing_square, mixing_direction = adam_parts(
        grad_talking, talking_mean, talking_square, factor
    )
    mixing_update = mixing_direction + DECAY * talking
    mixing_weight_sq = layer_squares(talking)
    mixing_update_sq = layer_squares(mixing_update)
    talking_new = talking - RATE * per_layer(
        trust_of(mixing_weight_sq, mixing_update_sq), talking
    ) * mixing_update
    norms = jnp.stack(
        [
            jnp.sqrt(jnp.concatenate([weight_sq, table_weight_sq, mixing_weight_sq])),
            jnp.sqrt(jnp.concatenate([update_sq, table_update_sq, mixing_update_sq])),
        ]
    )
    statistics = stat[0, :12]
    return (
        renewed[0],
        moved[0][0],
        moved[0][1],
        renewed[1],
        moved[1][0],
        moved[1][1],
        renewed[2],
        moved[2][0],
        moved[2][1],
        renewed[3],
        moved[3][0],
        moved[3][1],
        tables_new,
        table_mean,
        table_square,
        vectors_new,
        vector_mean,
        vector_square,
        talking_new,
        mixing_mean,
        mixing_square,
        renewed[0].astype(BF),
        renewed[1].astype(BF),
        renewed[2].astype(BF),
        renewed[3].astype(BF),
        statistics,
        grad_norm,
        norms,
    )


def solution(mesh):
    return jax.shard_map(
        shards,
        mesh=mesh,
        in_specs=(
            P(("dp", "mp"), None, None),
            P("dp", None),
            P("dp"),
            P(("dp", "mp")),
            P(("dp", "mp")),
            P(None, None, None, "mp"),
            P(None, None, None, "mp"),
            P(None, None, None, "mp"),
            P(None, "mp", None),
            P(None, "mp", None),
            P(None, "mp", None),
            P(None, None, "mp"),
            P(None, None, "mp"),
            P(None, None, "mp"),
            P(None, "mp", None),
            P(None, "mp", None),
            P(None, "mp", None),
            P(),
            P(),
            P(),
            P(),
            P(),
            P(),
            P(),
            P(),
            P(),
        ),
        out_specs=(
            P(None, None, None, "mp"),
            P(None, None, None, "mp"),
            P(None, None, None, "mp"),
            P(None, "mp", None),
            P(None, "mp", None),
            P(None, "mp", None),
            P(None, None, "mp"),
            P(None, None, "mp"),
            P(None, None, "mp"),
            P(None, "mp", None),
            P(None, "mp", None),
            P(None, "mp", None),
            P(),
            P(),
            P(),
            P(),
            P(),
            P(),
            P(),
            P(),
            P(),
            P(None, None, None, "mp"),
            P(None, "mp", None),
            P(None, None, "mp"),
            P(None, "mp", None),
            P(),
            P(),
            P(),
        ),
        check_vma=False,
    )
```

time: 1270 us -> 450 us (0.35)
  waiting for transfers between devices: 457 us -> 0.11 us
  matrix products: 311 us -> 0 us
  Pallas kernels: 0 us -> 260 us
  blocking collectives: 174 us -> 7.36 us
  local copies, waits for them, and re-layouts: 136 us -> 62.6 us
  other arithmetic: 152 us -> 85.9 us
    dot_general x51 -> x0, matrix products: 311 us -> none  [the longest x1 44.9 us: self_attend_back(): jnp.einsum('hg,nhqk->ngqk', talking[1], grad_weights, precision=HIGH_PREC...]
    pallas_call x0 -> x8, Pallas kernels: none -> 260 us  [the longest x1 102 us: run_reduce(): pl.pallas_call(functools.partial(reduce_kernel, n_dp, n_mp), in_specs=[WH...]
    psum x2 -> x0, waiting for transfers between devices: 229 us -> none  [the longest x1 132 us: shards(): lax.psum((grad_tables, grad_vectors, grad_talking, shard_sq), ('dp', 'mp'))]
    unnamed x12 -> x3, waiting for transfers between devices: 128 us -> 0.05 us
    reduce_scatter x3 -> x0, waiting for transfers between devices: 99.9 us -> none  [the longest x1 50.6 us: shards(): lax.psum_scatter(stacked[2], 'mp', scatter_dimension=2, tiled=True)]
    psum x3 -> x1, blocking collectives: 83.8 us -> 7.36 us  [shards(): lax.psum((jnp.concatenate([layer_squares(item) for item in weights]), jnp...]
    all_gather x2 -> x0, blocking collectives: 48.1 us -> none  [the longest x1 39.6 us: shards(): lax.all_gather(unit_embeddings, ('dp', 'mp'), axis=0, tiled=True)]
    unnamed x1 -> x0, blocking collectives: 42.4 us -> none
  transfers between devices with their start and end apart: 10 -> 3, of which waited for: 5 -> 0; matrix products, arithmetic and copies ran while one was open for 23% -> 8% of each run, Pallas kernels for 0% -> 17%
where the time goes in v1:
time: 450 us; the launch traced here: 441 us
  Pallas kernels  260 us (58%)
  other arithmetic  85.9 us (19%)
  local copies, waits for them, and re-layouts  62.6 us (14%)
  between operations  25.1 us (6%)
  blocking collectives  7.36 us (2%)
    pallas_call x1, Pallas kernels, run_reduce(): pl.pallas_call(functools.partial(reduce_kernel, n_dp, n_mp), in_specs=[WH...  102 us
    pallas_call x1, Pallas kernels, run_self_back(): pl.pallas_call(self_back_kernel, grid=(count,), in_specs=[per_image(P_SIZ...  42.2 us
    pallas_call x1, Pallas kernels, run_feed_back(): pl.pallas_call(feed_back_kernel, grid=(count,), in_specs=[per_image(1, D)...  28.9 us
    pallas_call x1, Pallas kernels, run_self_attend(): pl.pallas_call(self_attend_kernel, grid=(count,), in_specs=[per_image(P_S...  25.2 us
    pallas_call x1, Pallas kernels, run_feed(): pl.pallas_call(feed_kernel, grid=(count,), in_specs=[per_image(P_SIZE, D)...  24.4 us
    pallas_call x1, Pallas kernels, run_weights(): pl.pallas_call(functools.partial(weight_kernel, n_dp, n_mp), in_specs=[WH...  13.9 us
    unnamed x112, local copies, waits for them, and re-layouts  13.4 us
    pallas_call x1, Pallas kernels, run_cards(): pl.pallas_call(functools.partial(card_kernel, n_dp, n_mp), in_specs=[WHOL...  12.3 us
  transfers between devices with their start and end apart: 3, of which 0 were waited for; matrix products, arithmetic and copies ran while one was open for 8% of the time, Pallas kernels for 17%

profile of v1, /device:TPU:0, one launch (start us, length us, event | category | flops | bytes accessed | tf_op | source)
XLA Modules:
  0.0 441.5 jit_solution(13394676726654773602)
XLA Ops:
  28.0 13.9 %weights.1.wattn = bf16[4,384,384]{2,1,0:T(8,128)(2,1)} custom-call(bf16[384,384]{1,0:T(8,128)(2,1)} %pad_maximum_fusion.4.shard), custom_call_target="tpu_custom_call" | custom-call | tf_op jit(solution)/shard_map/weights/pallas_call | solution.py:673
  43.0 3.6 copy.97.pixels
  52.3 25.2 %self_attend.1 = (f32[8,196,384]{2,1,0:T(8,128)}, bf16[8,196,384]{2,1,0:T(8,128)(2,1)}, bf16[8,196,384]{2,1,0:T(8,128)(2,1)}, bf16[8,196,384]{2,1,0:T(8,128)(2,1...) custom-call(bf16[8,196,768]{2,1,0:T(8,128)(2,1)} %copy.97.pixels, ...), custom_call_target="tpu_custom_call" | custom-call | tf_op jit(solution)/shard_map/self_attend/pallas_call | solution.py:438
  79.7 5.7 %concatenate.110 = f32[8]{0:T(128)} concatenate(f32[1]{0:T(128)} %bitcast, f32[1]{0:T(128)} %bitcast.1, f32[1]{0:T(128)} %bitcast.2, f32[1]{0:T(128)} %bitcast.3, f32[1]{0:T(128)} %bitcast.4, f32[1]{0:T(128)} %bitcast.5, f32[1]{0:T(128)} %bitcast.6, f32[1]{0:T(128)} %bitcast.7), dimensions={0} | concatenate | bytes 64 | tf_op jit(solution)/shard_map/concatenate | solution.py:1060
  86.9 24.4 %feed.1 = (f32[8,196,384]{2,1,0:T(8,128)}, bf16[8,196,1536]{2,1,0:T(8,128)(2,1)}, bf16[8,196,1536]{2,1,0:T(8,128)(2,1)}, bf16[8,196,384]{2,1,0:T(8,128)(2,1)}, f...) custom-call(f32[8,196,384]{2,1,0:T(8,128)} %get-tuple-element.64.mid, ...), custom_call_target="tpu_custom_call" | custom-call | tf_op jit(solution)/shard_map/feed/pallas_call | solution.py:464
  111.3 12.3 %cards.1 = f32[1024,128]{1,0:T(8,128)} custom-call(f32[32,128]{1,0:T(8,128)} %get-tuple-element.66.card), custom_call_target="tpu_custom_call" | custom-call | tf_op jit(solution)/shard_map/cards/pallas_call | solution.py:607
  123.6 11.4 %token_net.1 = (bf16[256,384]{1,0:T(8,128)(2,1)}, f32[384,384]{1,0:T(8,128)}, f32[1536,384]{1,0:T(8,128)}, f32[1536,384]{1,0:T(8,128)}, f32[1000,384]{1,0:T(8,12...) custom-call(f32[1024,128]{1,0:T(8,128)} %cards.1, f32[20,384]{1,0:T(8,128)} %vec.9, ...), custom_call_target="tpu_custom_call" | custom-call | tf_op jit(solution)/shard_map/token_net/pallas_call | solution.py:490
  136.3 28.9 %feed_back.1 = (f32[8,196,384]{2,1,0:T(8,128)}, f32[4,768,384]{2,1,0:T(8,128)}, f32[384,384]{1,0:T(8,128)}, f32[16,384]{1,0:T(8,128)}) custom-call(bf16[8,1,384]{2,1,0:T(2,128)(2,1)} %copy.107.dch, f32[8,196,384]{2,1,0:T(8,128)} %get-tuple-element.68.patch, f32[8,196,384]{2,1,0:T(8,128)} %get-tuple-element.64.mid, ...), custom_call_target="tpu_custom_call" | custom-call | tf_op jit(solution)/shard_map/feed_back/pallas_call | solution.py:506
  165.2 42.2 %self_back.1 = (f32[4,384,384]{2,1,0:T(8,128)}, f32[768,384]{1,0:T(8,128)}, f32[196,384]{1,0:T(8,128)}, f32[24,384]{1,0:T(8,128)}) custom-call(f32[8,196,384]{2,1,0:T(8,128)} %get-tuple-element.76.dmid, bf16[8,196,768]{2,1,0:T(8,128)(2,1)} %copy.97.pixels, f32[8,196,384]{2,1,0:T(8,128)} %get-tuple-element.77.embed, ...), custom_call_target="tpu_custom_call" | custom-call | tf_op jit(solution)/shard_map/self_back/pallas_call | solution.py:528
  207.4 101.9 %reduce.38 = (bf16[1280,384]{1,0:T(8,128)(2,1)}, bf16[1024,384]{1,0:T(8,128)(2,1)}, f32[8,128]{1,0:T(8,128)}) custom-call(f32[4,384,384]{2,1,0:T(8,128)} %get-tuple-element.84.gattn, f32[4,768,384]{2,1,0:T(8,128)} %get-tuple-element.85.gmlp, f32[4,96,384]{2,1,0:T(8,128)} %bitcast.144, f32[768,384]{1,0:T(8,128)} %get-tuple-element.87.gpix, ...), custom_call_target="tpu_custom_call" | custom-call | tf_op jit(solution)/shard_map/reduce/pallas_call | solution.py:859
  324.8 3.0 multiply_reduce_fusion.4
  327.7 3.0 multiply_reduce_fusion.3
  341.5 9.7 %multiply_reduce_fusion.1 = (f32[1964]{0:T(1024)S(1)}, f32[1964]{0:T(1024)}, f32[1964,384]{1,0:T(8,128)}, f32[1964,384]{1,0:T(8,128)}) fusion(f32[1964,384]{1,0:T(8,128)S(1)} %copy-done, f32[]{:T(128)S(6)} %div.152, f32[1000,384]{1,0:T(8,128)} %get-tuple-element.97, f32[964,384]{1,0:T(8,128)} %slice.322, f32[1964,384]{1,0:T(8,128)} %param.44, ...), kind=kLoop, calls=%fused_computation.7 | loop fusion | flops 14325416 | bytes 18115940 | tf_op jit(solution)/shard_map/reduce_sum | solution.py:1078
  355.4 3.0 copy.112
  367.3 3.6 multiply_add_fusion.2
  376.3 4.1 multiply_add_fusion.4
  389.1 5.2 %concatenate.120 = f32[8]{0:T(128)S(1)} concatenate(f32[1]{0:T(128)} %bitcast.50, f32[1]{0:T(128)} %bitcast.51, f32[1]{0:T(128)} %bitcast.54, f32[1]{0:T(128)} %bitcast.55, f32[1]{0:T(128)} %bitcast.60, f32[1]{0:T(128)} %bitcast.61, f32[1]{0:T(128)} %bitcast.64, f32[1]{0:T(128)} %bitcast.65), dimensions={0} | concatenate | bytes 64 | tf_op jit(solution)/shard_map/concatenate | solution.py:1061
  395.0 7.4 %all-reduce.1 = (f32[8]{0:T(128)S(1)}, f32[8]{0:T(128)S(1)}) all-reduce(f32[8]{0:T(128)S(1)} %copy-done.51, f32[8]{0:T(128)S(1)} %concatenate.120), channel_id=1, replica_groups=mesh['dp'=8,'mp'=4] {'mp'}, use_global_device_ids=true, to_apply=%region_8.9 | all-reduce | flops 16 | bytes 128 | tf_op jit(solution)/shard_map/psum | solution.py:1058
  402.3 3.4 concatenate.127
  406.9 3.2 concatenate.134
  410.2 2.7 sqrt_multiply_fusion
  413.6 3.8 fusion.26
  418.1 3.2 fusion.29
  430.2 3.2 multiply_subtract_fusion
  (239 shorter events, 88.4 us)
Async XLA Ops:
  7.2 79.7 %all-gather.6.cloned.1.call-start = ((), (), s32[]{:S(2)}) async-start(), calls=%async_computation.1 | async-start | bytes 1474560 | tf_op jit(solution)/shard_map/all_gather | solution.py:956
  11.6 75.3 %all-gather.4.cloned.1.call-start = ((), (), s32[]{:S(2)}) async-start(), calls=%async_computation | async-start | bytes 2949120 | tf_op jit(solution)/shard_map/all_gather | solution.py:955
  14.8 108.7 %all-gather.8.cloned.1.call-start = ((), (), s32[]{:S(2)}) async-start(), calls=%async_computation.2 | async-start | bytes 2949120 | tf_op jit(solution)/shard_map/all_gather | solution.py:957
  14.9 5.2 %copy-start = (f32[1964,384]{1,0:T(8,128)S(1)}, f32[1964,384]{1,0:T(8,128)}, u32[]{:S(2)}) copy-start(f32[1964,384]{1,0:T(8,128)} %param.43) | copy-start | bytes 9050116
  21.8 5.4 %copy-start.31 = (bf16[1,384,3,96]{1,3,2,0:T(8,128)(2,1)S(1)}, bf16[1,384,3,96]{1,3,2,0:T(8,128)(2,1)}, u32[]{:S(2)}) copy-start(bf16[1,384,3,96]{1,3,2,0:T(8,128)(2,1)} %get-tuple-element.165) | copy-start | bytes 663556
  21.9 5.4 %copy-start.38 = (bf16[96,384]{1,0:T(8,128)(2,1)S(1)}, bf16[96,384]{1,0:T(8,128)(2,1)}, u32[]{:S(2)}) copy-start(bf16[96,384]{1,0:T(8,128)(2,1)} %get-tuple-element.173) | copy-start | bytes 221188
  26.5 16.4 %copy-start.27 = (f32[8,8,48]{0,2,1:T(8,128)}, f32[8,8,48]{0,2,1:T(8,128)S(1)}, u32[]{:S(2)}) copy-start(f32[8,8,48]{0,2,1:T(8,128)S(1)} %broadcast_in_dim.52) | copy-start | bytes 36868
  52.3 25.3 %copy-start.22 = (f32[2,96,384]{2,1,0:T(8,128)S(1)}, f32[2,96,384]{2,1,0:T(8,128)}, u32[]{:S(2)}) copy-start(f32[2,96,384]{2,1,0:T(8,128)} %param.34) | copy-start | bytes 884740
  52.3 25.9 %copy-start.7 = (f32[2,384,3,96]{1,3,2,0:T(8,128)S(1)}, f32[2,384,3,96]{1,3,2,0:T(8,128)}, u32[]{:S(2)}) copy-start(f32[2,384,3,96]{1,3,2,0:T(8,128)} %param.31) | copy-start | bytes 2654212
  313.1 6.7 %copy-start.29 = (f32[20,384]{1,0:T(8,128)S(1)}, f32[20,384]{1,0:T(8,128)}, u32[]{:S(2)}) copy-start(f32[20,384]{1,0:T(8,128)} %vec.9) | copy-start | bytes 92164
  314.5 7.5 %copy-start.49 = (f32[384]{0:T(512)S(1)}, f32[384]{0:T(512)}, u32[]{:S(2)}) copy-start(f32[384]{0:T(512)} %get-tuple-element.119) | copy-start | bytes 4612
  324.7 7.9 %copy-start.19 = (f32[1000,384]{1,0:T(8,128)S(1)}, f32[1000,384]{1,0:T(8,128)}, u32[]{:S(2)}) copy-start(f32[1000,384]{1,0:T(8,128)} %get-tuple-element.97) | copy-start | bytes 4608004
  327.7 4.9 %copy-start.4 = (f32[964,384]{1,0:T(8,128)S(1)}, f32[964,384]{1,0:T(8,128)}, u32[]{:S(2)}) copy-start(f32[964,384]{1,0:T(8,128)} %slice.322) | copy-start | bytes 4442116
  341.4 11.7 %copy-start.20 = (bf16[1280,384]{1,0:T(8,128)(2,1)S(1)}, bf16[1280,384]{1,0:T(8,128)(2,1)}, u32[]{:S(2)}) copy-start(bf16[1280,384]{1,0:T(8,128)(2,1)} %get-tuple-element.91) | copy-start | bytes 2949124
  358.5 5.1 %copy-start.21 = (bf16[1280,384]{1,0:T(8,128)(2,1)S(1)}, bf16[1280,384]{1,0:T(8,128)(2,1)}, u32[]{:S(2)}) copy-start(bf16[1280,384]{1,0:T(8,128)(2,1)} %get-tuple-element.91) | copy-start | bytes 2949124
  358.5 6.6 %copy-start.43 = (f32[1964]{0:T(1024)S(1)}, f32[1964]{0:T(1024)}, u32[]{:S(2)}) copy-start(f32[1964]{0:T(1024)} %get-tuple-element.101) | copy-start | bytes 23572
  362.2 5.2 %copy-start.3 = (f32[2,384,384]{2,1,0:T(8,128)S(1)}, f32[2,384,384]{2,1,0:T(8,128)}, u32[]{:S(2)}) copy-start(f32[2,384,384]{2,1,0:T(8,128)} %param.40) | copy-start | bytes 3538948
  362.2 5.2 %copy-start.30 = (f32[2,384,384]{2,1,0:T(8,128)S(1)}, f32[2,384,384]{2,1,0:T(8,128)}, u32[]{:S(2)}) copy-start(f32[2,384,384]{2,1,0:T(8,128)} %param.41) | copy-start | bytes 3538948
  385.6 8.7 %copy-start.44 = (f32[1964]{0:T(1024)S(1)}, f32[1964]{0:T(1024)}, u32[]{:S(2)}) copy-start(f32[1964]{0:T(1024)} %get-tuple-element.101) | copy-start | bytes 23572
  385.6 9.3 %copy-start.51 = (f32[8]{0:T(128)S(1)}, f32[8]{0:T(128)}, u32[]{:S(2)}) copy-start(f32[8]{0:T(128)} %concatenate.110) | copy-start | bytes 100
  385.6 20.0 %copy-start.47 = (f32[2,8,8]{2,1,0:T(8,128)S(1)}, f32[2,8,8]{2,1,0:T(8,128)}, u32[]{:S(2)}) copy-start(f32[2,8,8]{2,1,0:T(8,128)} %param.50) | copy-start | bytes 1540
  385.7 20.0 %copy-start.48 = (f32[2,8,8]{2,1,0:T(8,128)S(1)}, f32[2,8,8]{2,1,0:T(8,128)}, u32[]{:S(2)}) copy-start(f32[2,8,8]{2,1,0:T(8,128)} %param.51) | copy-start | bytes 1540
  421.3 8.9 %copy-start.6 = (f32[1964,384]{1,0:T(8,128)S(1)}, f32[1964,384]{1,0:T(8,128)}, u32[]{:S(2)}) copy-start(f32[1964,384]{1,0:T(8,128)} %get-tuple-element.141) | copy-start | bytes 9050116
  424.5 5.8 %copy-start.5 = (f32[1964,384]{1,0:T(8,128)S(1)}, f32[1964,384]{1,0:T(8,128)}, u32[]{:S(2)}) copy-start(f32[1964,384]{1,0:T(8,128)} %get-tuple-element.140) | copy-start | bytes 9050116
  (33 other events, 84.4 us)
Sparse Core Ops, SparseCore 0:
  11.8 20.1 all-gather.5
  34.1 24.0 all-gather.3
  60.4 24.0 all-gather.7

commit v2 on v1

--- a/solution.py
+++ b/solution.py
@@ -103,13 +103,134 @@
     return ref[:, first : first + rows, :].reshape(shards_count * rows, ref.shape[2])
 
 
+def pad_rows(rows, n_dp):
+    return -(-rows // (16 * n_dp)) * 16 * n_dp
+
+
+class Place:
+    def __init__(self, n_dp, n_mp):
+        self.n_dp, self.n_mp, self.n_y = n_dp, n_mp, n_mp // 2
+        self.dp = lax.axis_index("dp")
+        self.mp = lax.axis_index("mp")
+        self.y = lax.div(self.mp, 2)
+        self.core = lax.rem(self.mp, 2)
+        self.sibling = (self.dp, self.y * 2 + 1 - self.core)
+
+    def along_y(self, step):
+        return lax.rem(self.y + step, self.n_y)
+
+    def along_dp(self, step):
+        return lax.rem(self.dp + step, self.n_dp)
+
+    def greet(self):
+        barrier = pltpu.get_barrier_semaphore()
+        partners = [self.sibling]
+        partners += [(self.dp, self.along_y(step) * 2 + self.core) for step in range(1, self.n_y)]
+        partners += [(self.along_dp(step), self.mp) for step in range(1, self.n_dp)]
+        for partner in partners:
+            pl.semaphore_signal(barrier, inc=1, device_id=partner, device_id_type=MESH)
+        return lambda: pl.semaphore_wait(barrier, len(partners))
+
+
+class ShardSum:
+    def __init__(self, place, rows, near, far, half, last, near_sem, far_sem, last_sem):
+        self.place, self.rows, self.near, self.far = place, rows, near, far
+        self.half, self.last = half, last
+        self.near_sem, self.far_sem, self.last_sem = near_sem, far_sem, last_sem
+        self.chunk = half.shape[0] // place.n_dp
+
+    def near_copy(self, step):
+        p = self.place
+        y = p.along_y(step)
+        return remote(
+            self.rows.at[y * 2 + 1 - p.core], self.near.at[y],
+            self.near_sem.at[0, step], self.near_sem.at[1, step], p.sibling,
+        )
+
+    def far_copy(self, step):
+        p = self.place
+        y = p.along_y(step)
+        return remote(
+            self.near.at[y], self.far.at[step - 1],
+            self.far_sem.at[0, step], self.far_sem.at[1, step], (p.dp, y * 2 + p.core),
+        )
+
+    def last_copy(self, step):
+        p = self.place
+        to = p.along_dp(step)
+        return remote(
+            self.half.at[pl.ds(pl.multiple_of(to * self.chunk, self.chunk), self.chunk)],
+            self.last.at[step - 1],
+            self.last_sem.at[0, step], self.last_sem.at[1, step], (to, p.mp),
+        )
+
+    def start(self):
+        for step in range(1, self.place.n_y + 1):
+            self.near_copy(step).start()
+
+    def near_to_far(self):
+        p = self.place
+        for step in range(1, p.n_y + 1):
+            y = p.along_y(step)
+            self.near_copy(step).wait_recv()
+            self.near[pl.ds(y, 1)] = (
+                self.rows[pl.ds(y * 2 + p.core, 1)].astype(F32) + self.near[pl.ds(y, 1)].astype(F32)
+            ).astype(BF)
+            if step < p.n_y:
+                self.far_copy(step).start()
+
+    def far_to_last(self):
+        p = self.place
+        total_rows = self.near[pl.ds(p.y, 1)][0].astype(F32)
+        for step in range(1, p.n_y):
+            self.far_copy(step).wait_recv()
+            total_rows += self.far[step - 1].astype(F32)
+        self.half[...] = total_rows.astype(BF)
+        for step in range(1, p.n_dp):
+            self.last_copy(step).start()
+
+    def finish(self):
+        p = self.place
+        at = pl.ds(pl.multiple_of(p.dp * self.chunk, self.chunk), self.chunk)
+        total_rows = self.half[at, :].astype(F32)
+        for step in range(1, p.n_dp):
+            self.last_copy(step).wait_recv()
+            total_rows += self.last[step - 1].astype(F32)
+        return total_rows.astype(BF)
+
+    def wait_sends(self):
+        p = self.place
+        for step in range(1, p.n_y + 1):
+            self.near_copy(step).wait_send()
+            if step < p.n_y:
+                self.far_copy(step).wait_send()
+        for step in range(1, p.n_dp):
+            self.last_copy(step).wait_send()
+
+
+def sum_scratch(n_dp, n_mp, rows):
+    n_y = n_mp // 2
+    dma = pltpu.SemaphoreType.DMA
+    return [
+        pltpu.VMEM((n_y, rows, D), BF), pltpu.VMEM((max(n_y - 1, 1), rows, D), BF),
+        pltpu.VMEM((rows, D), BF), pltpu.VMEM((n_dp - 1, rows // n_dp, D), BF),
+        dma((2, n_y + 1)), dma((2, n_y + 1)), dma((2, n_dp)),
+    ]
+
+
+def remote(src, dst, send_sem, recv_sem, device):
+    return pltpu.make_async_remote_copy(
+        src_ref=src, dst_ref=dst, send_sem=send_sem, recv_sem=recv_sem,
+        device_id=device, device_id_type=MESH,
+    )
+
+
 def self_attend_kernel(
-    pixels, cols, vec, pos, wp, wattn, t1row, t2col,
-    embed_out, q_out, k_out, v_out, prob_out, ho_out, raw_out, mid_out, stat_out,
+    embed, cols, vec, wattn, t1row, t2col,
+    q_out, k_out, v_out, prob_out, ho_out, raw_out, mid_out, stat_out,
 ):
     shard = wattn.shape[1] // 4
-    x = nn(pixels[0], wp[...]) + vec[16:17, :] + pos[...]
-    embed_out[0] = x
+    x = embed[0]
     unit, _ = normalize(x)
     normed = (unit * vec[0:1, :] + vec[1:2, :]).astype(BF)
     wv = part(wattn, 2 * shard, shard)
@@ -196,7 +317,7 @@
 
 def token_kernel(
     group, cards, vec, wcls, wmlp, head,
-    dch_out, gout_out, gup_out, gdown_out, ghead_out, rows_out, stat_out,
+    dch_out, gout_out, gup_out, gdown_out, ghead_out, rows_out, stat_out, dch_all,
 ):
     hidden = wmlp.shape[1] // 2
     shard = wcls.shape[1] // 4
@@ -238,7 +359,12 @@
     cross = jnp.log(total) + top - jnp.sum(jnp.where(hot, logits, 0.0), -1, keepdims=True)
     share = okay / count
     dlogits = (share * (grown / total - hot.astype(F32))).astype(BF)
-    ghead_out[...] = tn(dlogits, feature_low)
+    classes = head.shape[0]
+    ghead = tn(dlogits, feature_low)
+    ghead_out[0:8, :] = jnp.zeros((8, D), F32)
+    ghead_out[classes:, :] = jnp.zeros((8, D), F32)
+    ghead_out[4 : classes + 4, :] = ghead
+    replicated_sq = colsum(ghead * ghead)
     dfeature = nn(dlogits, head[...])
 
     length = lax.rsqrt(jnp.sum(feature * feature, -1, keepdims=True) + NORM_EPS)
@@ -264,9 +390,13 @@
     rows_out[7:8, :] = colsum(dtoken * down)
     rows_out[6:7, :] = vec[15:16, :] * colsum(dtoken)
     ddown = (dtoken * vec[15:16, :]).astype(BF)
-    gdown_out[...] = tn(active, ddown)
+    gdown = tn(active, ddown)
+    gdown_out[...] = gdown
+    replicated_sq += colsum(gdown * gdown)
     dinner = (nt(ddown, wdown) * slope).astype(BF)
-    gup_out[...] = tn(dinner, normed)
+    gup = tn(dinner, normed)
+    gup_out[...] = gup
+    replicated_sq += colsum(gup * gup)
     dnormed = nn(dinner, wup)
     rows_out[4:5, :] = colsum(dnormed * unit2)
     rows_out[5:6, :] = colsum(dnormed)
@@ -277,8 +407,23 @@
     rows_out[9:10, :] = colsum(dfeature * unit3)
     rows_out[10:11, :] = colsum(dfeature)
     dbranch = (dmiddle * vec[11:12, :]).astype(BF)
-    gout_out[...] = tn(cheads, dbranch)
-    dch_out[...] = nt(dbranch, wo).astype(BF)
+    gout = tn(cheads, dbranch)
+    gout_out[...] = gout
+    replicated_sq += colsum(gout * gout)
+    dch_all[...] = nt(dbranch, wo)
+    local = dch_out.shape[0]
+    place = lax.axis_index("dp") * lax.axis_size("mp") + lax.axis_index("mp")
+    if local % 8 == 0:
+        dch_out[...] = dch_all[pl.ds(pl.multiple_of(place * local, local), local), :]
+    else:
+        share_of = 8 // local
+        start = pl.multiple_of(lax.div(place, share_of) * 8, 8)
+        window = dch_all[pl.ds(start, 8), :]
+        pick = lax.rem(place, share_of)
+        dch_out[...] = sum(
+            jnp.where(pick == i, window[i * local : (i + 1) * local, :], 0.0)
+            for i in range(share_of)
+        )
     lane = lax.broadcasted_iota(jnp.int32, (1, 128), 1)
     self_sums = colsum(card)
     count_tokens = self_sums[:, 5:6]
@@ -298,12 +443,15 @@
     line = jnp.zeros((1, 128), F32)
     for i, entry in enumerate(entries):
         line = jnp.where(lane == i, entry, line)
-    stat_out[...] = jnp.broadcast_to(line, (8, 128))
+    stat_out[0:1, :] = line
+    stat_out[1:8, :] = jnp.broadcast_to(
+        replicated_sq[:, 0:128] + replicated_sq[:, 128:256] + replicated_sq[:, 256:384], (7, 128)
+    )
 
 
 def feed_back_kernel(
     dch, patch, mid, raw, act, slope, cprob, cprob0, z, aux, vec, wcls, wmlp,
-    dmid_out, gmlp_out, gv_out, rows_out,
+    dmid_out, gfeed_out, rows_out, gmlp_out, gv_out,
 ):
     hidden = wmlp.shape[1] // 2
     shard = wcls.shape[1] // 4
@@ -320,7 +468,7 @@
     token = aux[8:16, :]
     unit, inverse = normalize(patch[0])
     normed = (unit * vec[8:9, :] + vec[9:10, :]).astype(BF)
-    spread = (mask * dch[0].astype(F32)).astype(BF)
+    spread = (mask * dch[pl.ds(pl.program_id(0), 1), :]).astype(BF)
     dz = nn(spread, part(wcls, 2 * shard, shard))
     dz_low = dz.astype(BF)
     probs = cprob[0]
@@ -354,20 +502,39 @@
     rows_out[1:2, :] += colsum(dnormed)
     dmid_out[0] = incoming + normalize_back(unit, inverse, vec[4:5, :], dnormed)
 
+    @pl.when(pl.program_id(0) == pl.num_programs(0) - 1)
+    def _():
+        used = 2 * hidden + shard
+        gfeed_out[:, : 2 * hidden, :] = gmlp_out[...].astype(BF)
+        gfeed_out[:, 2 * hidden : used, :] = gv_out[...].astype(BF).reshape(count, shard, D)
+        if used < gfeed_out.shape[1]:
+            gfeed_out[:, used:, :] = jnp.zeros((count, gfeed_out.shape[1] - used, D), BF)
+
 
 def self_back_kernel(
-    dmid, pixels, embed, q, k, v, prob, ho, raw, vec, wattn, t1row, t1col, t2row,
-    gattn_out, gpix_out, gpos_out, rows_out,
+    n_dp, n_mp, dmid, pixels, embed, q, k, v, prob, ho, raw, vec, wattn, t1row, t1col, t2row, gfeed,
+    gattn_out, gpix_out, gpos_out, rows_out, chunk_out, dx_all, dx_rows, *sum_buffers,
 ):
     shard = wattn.shape[1] // 4
     count = wattn.shape[0]
+    images = dx_all.shape[0]
+    feed = ShardSum(Place(n_dp, n_mp), gfeed, *sum_buffers)
 
     @pl.when(pl.program_id(0) == 0)
     def _():
         gattn_out[...] = jnp.zeros_like(gattn_out)
-        gpix_out[...] = jnp.zeros_like(gpix_out)
         gpos_out[...] = jnp.zeros_like(gpos_out)
         rows_out[...] = jnp.zeros_like(rows_out)
+        feed.place.greet()()
+        feed.start()
+
+    @pl.when(pl.program_id(0) == 1)
+    def _():
+        feed.near_to_far()
+
+    @pl.when(pl.program_id(0) == images // 2)
+    def _():
+        feed.far_to_last()
 
     wq = part(wattn, 0, shard)
     wk = part(wattn, shard, shard)
@@ -414,7 +581,15 @@
     rows_out[1:2, :] += colsum(dnormed)
     dx = incoming + normalize_back(unit, inverse, vec[0:1, :], dnormed)
     gpos_out[...] += dx
-    gpix_out[...] += tn(pixels[0], dx.astype(BF))
+    dx_all[pl.program_id(0)] = dx
+
+    @pl.when(pl.program_id(0) == pl.num_programs(0) - 1)
+    def _():
+        for n in range(images):
+            dx_rows[:, n, :] = dx_all[n]
+        gpix_out[...] = tn(pixels[...], dx_rows[...].reshape(pixels.shape[0], D).astype(BF))
+        chunk_out[...] = feed.finish()
+        feed.wait_sends()
 
 
 def per_image(*tail):
@@ -433,29 +608,29 @@
     return pltpu.CompilerParams(vmem_limit_bytes=VMEM_LIMIT, dimension_semantics=("arbitrary",))
 
 
-def run_self_attend(pixels, cols, vec, pos, wp, wattn, t1row, t2col):
-    count = pixels.shape[0]
+def run_self_attend(embed, cols, vec, wattn, t1row, t2col):
+    count = embed.shape[0]
     return pl.pallas_call(
         self_attend_kernel,
         grid=(count,),
         in_specs=[
-            per_image(P_SIZE, PIX), per_image(P_SIZE, 2), constant(*vec.shape), constant(P_SIZE, D),
-            constant(PIX, D), constant(*wattn.shape), constant(HEADS, D), constant(D, HEADS),
+            per_image(P_SIZE, D), per_image(P_SIZE, 2), constant(*vec.shape),
+            constant(*wattn.shape), constant(HEADS, D), constant(D, HEADS),
         ],
         out_specs=[
-            per_image(P_SIZE, D), per_image(P_SIZE, D), per_image(P_SIZE, D), per_image(P_SIZE, D),
+            per_image(P_SIZE, D), per_image(P_SIZE, D), per_image(P_SIZE, D),
             per_image(HEADS, P_SIZE, P_SIZE), per_image(D, P_SIZE), per_image(P_SIZE, D),
             per_image(P_SIZE, D), per_image(1, 128),
         ],
         out_shape=[
-            shaped(count, P_SIZE, D), shaped(count, P_SIZE, D, dtype=BF),
+            shaped(count, P_SIZE, D, dtype=BF),
             shaped(count, P_SIZE, D, dtype=BF), shaped(count, P_SIZE, D, dtype=BF),
             shaped(count, HEADS, P_SIZE, P_SIZE, dtype=BF), shaped(count, D, P_SIZE, dtype=BF),
             shaped(count, P_SIZE, D, dtype=BF), shaped(count, P_SIZE, D), shaped(count, 1, 128),
         ],
         compiler_params=params(),
         name="self_attend",
-    )(pixels, cols, vec, pos, wp, wattn, t1row, t2col)
+    )(embed, cols, vec, wattn, t1row, t2col)
 
 
 def run_feed(mid, cols, bias_row, base, stat, vec, wmlp, wcls):
@@ -484,7 +659,7 @@
     )(mid, cols, bias_row, base, stat, vec, wmlp, wcls)
 
 
-def run_token(group, cards, vec, wcls, wmlp, head):
+def run_token(group, local, cards, vec, wcls, wmlp, head):
     images = cards.shape[0] // 4
     wide = wmlp.shape[0] * wmlp.shape[1] // 2
     return pl.pallas_call(
@@ -492,56 +667,69 @@
         in_specs=[WHOLE] * 5,
         out_specs=[WHOLE] * 7,
         out_shape=[
-            shaped(images, D, dtype=BF), shaped(D, D), shaped(wide, D), shaped(wide, D),
-            shaped(*head.shape), shaped(16, D), shaped(8, 128),
-        ],
+            shaped(local, D), shaped(D, D), shaped(wide, D), shaped(wide, D),
+            shaped(head.shape[0] + 8, D), shaped(16, D), shaped(8, 128),
+        ],
+        scratch_shapes=[pltpu.VMEM((images, D), F32)],
         compiler_params=pltpu.CompilerParams(vmem_limit_bytes=VMEM_LIMIT),
         name="token_net",
     )(cards, vec, wcls, wmlp, head)
 
 
-def run_feed_back(dch, patch, mid, raw, act, slope, cprob, cprob0, z, aux, vec, wcls, wmlp):
+def run_feed_back(n_dp, dch, patch, mid, raw, act, slope, cprob, cprob0, z, aux, vec, wcls, wmlp):
     count = mid.shape[0]
     wide = act.shape[2]
+    feed = (wmlp.shape[0], pad_rows(wmlp.shape[1] + wcls.shape[1] // 4, n_dp), D)
     return pl.pallas_call(
         feed_back_kernel,
         grid=(count,),
         in_specs=[
-            per_image(1, D), per_image(P_SIZE, D), per_image(P_SIZE, D), per_image(P_SIZE, D),
+            constant(count, D), per_image(P_SIZE, D), per_image(P_SIZE, D), per_image(P_SIZE, D),
             per_image(P_SIZE, wide), per_image(P_SIZE, wide), per_image(HEADS, P_SIZE),
             per_image(HEADS, 128), per_image(HEADS, D), constant(24, D), constant(*vec.shape),
             constant(*wcls.shape), constant(*wmlp.shape),
         ],
         out_specs=[
-            per_image(P_SIZE, D), constant(*wmlp.shape), constant(D, D), constant(16, D),
-        ],
-        out_shape=[
-            shaped(count, P_SIZE, D), shaped(*wmlp.shape), shaped(D, D), shaped(16, D),
-        ],
+            per_image(P_SIZE, D), constant(*feed), constant(16, D),
+        ],
+        out_shape=[shaped(count, P_SIZE, D), shaped(*feed, dtype=BF), shaped(16, D)],
+        scratch_shapes=[pltpu.VMEM(wmlp.shape, F32), pltpu.VMEM((D, D), F32)],
         compiler_params=params(),
         name="feed_back",
     )(dch, patch, mid, raw, act, slope, cprob, cprob0, z, aux, vec, wcls, wmlp)
 
 
-def run_self_back(dmid, pixels, embed, q, k, v, prob, ho, raw, vec, wattn, t1row, t1col, t2row):
+def run_self_back(
+    n_dp, n_mp, dmid, pixels, embed, q, k, v, prob, ho, raw, vec, wattn, t1row, t1col, t2row, gfeed
+):
     count = dmid.shape[0]
+    rows = gfeed.shape[1]
     return pl.pallas_call(
-        self_back_kernel,
+        functools.partial(self_back_kernel, n_dp, n_mp),
         grid=(count,),
         in_specs=[
-            per_image(P_SIZE, D), per_image(P_SIZE, PIX), per_image(P_SIZE, D),
+            per_image(P_SIZE, D), constant(*pixels.shape), per_image(P_SIZE, D),
             per_image(P_SIZE, D), per_image(P_SIZE, D), per_image(P_SIZE, D),
             per_image(HEADS, P_SIZE, P_SIZE), per_image(D, P_SIZE), per_image(P_SIZE, D),
             constant(*vec.shape), constant(*wattn.shape), constant(HEADS, D), constant(D, HEADS),
-            constant(HEADS, D),
+            constant(HEADS, D), constant(*gfeed.shape),
         ],
         out_specs=[
             constant(*wattn.shape), constant(PIX, D), constant(P_SIZE, D), constant(24, D),
-        ],
-        out_shape=[shaped(*wattn.shape), shaped(PIX, D), shaped(P_SIZE, D), shaped(24, D)],
-        compiler_params=params(),
+            constant(rows // n_dp, D),
+        ],
+        out_shape=[
+            shaped(*wattn.shape), shaped(PIX, D), shaped(P_SIZE, D), shaped(24, D),
+            shaped(rows // n_dp, D, dtype=BF),
+        ],
+        scratch_shapes=[pltpu.VMEM((count, P_SIZE, D), F32), pltpu.VMEM((P_SIZE, count, D), F32)]
+        + sum_scratch(n_dp, n_mp, rows),
+        compiler_params=pltpu.CompilerParams(
+            vmem_limit_bytes=VMEM_LIMIT, dimension_semantics=("arbitrary",), collective_id=5,
+            has_side_effects=True,
+        ),
         name="self_back",
-    )(dmid, pixels, embed, q, k, v, prob, ho, raw, vec, wattn, t1row, t1col, t2row)
+    )(dmid, pixels, embed, q, k, v, prob, ho, raw, vec, wattn, t1row, t1col, t2row, gfeed)
 
 
 def peer_at(index, n_mp):
@@ -558,13 +746,6 @@
         )
 
     pl.semaphore_wait(barrier, n - 1)
-
-
-def remote(src, dst, send_sem, recv_sem, device):
-    return pltpu.make_async_remote_copy(
-        src_ref=src, dst_ref=dst, send_sem=send_sem, recv_sem=recv_sem,
-        device_id=device, device_id_type=MESH,
-    )
 
 
 def spread_to_all(me, n, n_mp, slots, rows, send_sem, recv_sem):
@@ -621,19 +802,36 @@
     )(card)
 
 
-def weight_kernel(n_dp, n_mp, shard, out, near_send, near_recv, far_send, far_recv):
+def start_kernel(
+    n_dp, n_mp, attn_in, attn_out, pixels, tables, vec,
+    out, embed_out,
+    shard, wide_in, wide_out, patch_rows, pos_rows, by_patch, near_send, near_recv, far_send, far_recv, load_sem,
+):
     dp = lax.axis_index("dp")
     mp = lax.axis_index("mp")
     n_y = n_mp // 2
     y = lax.div(mp, 2)
     core = lax.rem(mp, 2)
     sibling = (dp, y * 2 + 1 - core)
+    load_patch = pltpu.make_async_copy(tables.at[pl.ds(0, PIX)], patch_rows, load_sem.at[0])
+    load_pos = pltpu.make_async_copy(tables.at[pl.ds(PIX, 200)], pos_rows, load_sem.at[1])
+    load_in = pltpu.make_async_copy(attn_in.at[0], wide_in, load_sem.at[2])
+    load_out = pltpu.make_async_copy(attn_out.at[0], wide_out, load_sem.at[3])
+    load_in.start()
+    load_out.start()
+    load_patch.start()
+    load_pos.start()
     barrier = pltpu.get_barrier_semaphore()
     pl.semaphore_signal(barrier, inc=1, device_id=sibling, device_id_type=MESH)
     for step in range(1, n_y):
         pl.semaphore_signal(
             barrier, inc=1, device_id=(dp, lax.rem(y + step, n_y) * 2 + core), device_id_type=MESH
         )
+    third = attn_in.shape[1]
+    load_in.wait()
+    load_out.wait()
+    shard[:third, :] = wide_in[...].astype(BF)
+    shard[third:, :] = wide_out[...].astype(BF)
     pl.semaphore_wait(barrier, n_y)
     far = [
         remote(
@@ -647,6 +845,15 @@
     near = [remote(shard, out.at[mp], near_send.at[0], near_recv.at[0], sibling)]
     near[0].start()
     out[pl.ds(mp, 1)] = shard[...][None]
+
+    load_patch.wait()
+    wp = patch_rows[...].astype(BF)
+    local = embed_out.shape[0]
+    half = P_SIZE // 2
+    for place in range(2):
+        rows = slice(place * half * local, (place + 1) * half * local)
+        by_patch[place * half : (place + 1) * half] = nn(pixels[rows, :], wp).reshape(half, local, D)
+
     for step in range(1, n_y):
         source = lax.rem(y + n_y - step, n_y) * 2
         slot = source + core
@@ -658,6 +865,10 @@
         )
         copy.start()
         near.append(copy)
+    load_pos.wait()
+    offset = pos_rows[:P_SIZE, :] + vec[16:17, :]
+    for n in range(local):
+        embed_out[n] = by_patch[:, n, :] + offset
     for copy in far:
         copy.wait_send()
     for step in range(n_y):
@@ -668,217 +879,206 @@
         ).wait_recv()
 
 
-def run_weights(n_dp, n_mp, rows):
+def run_start(n_dp, n_mp, local, attn_in, attn_out, pixels, tables, vec):
     n_y = n_mp // 2
+    rows = attn_in.shape[1] + attn_out.shape[1]
+    dma = pltpu.SemaphoreType.DMA
     return pl.pallas_call(
-        functools.partial(weight_kernel, n_dp, n_mp),
-        in_specs=[WHOLE],
-        out_specs=WHOLE,
-        out_shape=shaped(n_mp, *rows.shape, dtype=BF),
-        scratch_shapes=[pltpu.SemaphoreType.DMA((n_y,))] * 4,
+        functools.partial(start_kernel, n_dp, n_mp),
+        in_specs=[ANY, ANY, WHOLE, ANY, WHOLE],
+        out_specs=[WHOLE, WHOLE],
+        out_shape=[shaped(n_mp, rows, D, dtype=BF), shaped(local, P_SIZE, D)],
+        scratch_shapes=[
+            pltpu.VMEM((rows, D), BF), pltpu.VMEM(attn_in.shape[1:], F32),
+            pltpu.VMEM(attn_out.shape[1:], F32), pltpu.VMEM((PIX, D), F32),
+            pltpu.VMEM((200, D), F32),
+            pltpu.VMEM((P_SIZE, local, D), F32),
+            dma((n_y,)), dma((n_y,)), dma((n_y,)), dma((n_y,)), dma((4,)),
+        ],
         compiler_params=pltpu.CompilerParams(
             vmem_limit_bytes=VMEM_LIMIT, collective_id=2, has_side_effects=True
         ),
-        name="weights",
-    )(rows)
+        name="start",
+    )(attn_in, attn_out, pixels, tables, vec)
 
 
 def reduce_kernel(
-    n_dp, n_mp, gattn, gmlp, gv, gpix, gpos, rows2, rows3,
+    n_dp, n_mp, gattn, chunk, gpix, gpos, rows2, rows3,
     block_out, shared_out, square_out,
-    blocks, commons, near_b, near_s, part_b, part_s, far_b, far_s, half_b, half_s, last_b, last_s,
-    squares, near_sem, far_sem, last_sem, all_send, all_recv, block_sem, square_sem,
+    blocks, commons, squares, feed_sem, attn_sem, shared_sem, slab_sem, hand_sem, square_sem,
+    *sum_buffers,
 ):
-    n = n_dp * n_mp
-    n_y = n_mp // 2
-    dp = lax.axis_index("dp")
-    mp = lax.axis_index("mp")
-    me = dp * n_mp + mp
-    y = lax.div(mp, 2)
-    core = lax.rem(mp, 2)
-    sibling = (dp, y * 2 + 1 - core)
-    chunk_b = block_out.shape[0] // n_dp
-    chunk_s = shared_out.shape[0] // n
-    wide_s = chunk_s * n_dp
-
-    greet_all(me, n, n_mp)
-
-    first = 0
-    for item in (gattn, gmlp, gv):
-        size = item.shape[1]
-        blocks[:, first : first + size, :] = item[...].astype(BF)
-        first += size
-    if first < blocks.shape[1]:
-        blocks[:, first:, :] = jnp.zeros((n_mp, blocks.shape[1] - first, D), BF)
-    commons[:PIX, :] = gpix[...].astype(BF)
-    commons[PIX : PIX + P_SIZE + 12, :] = jnp.concatenate(
-        [gpos[...], jnp.zeros((12, D), F32)], 0
+    p = Place(n_dp, n_mp)
+    attn = ShardSum(p, blocks, *sum_buffers[:7])
+    common = ShardSum(p, commons, *sum_buffers[7:])
+    feed_rows = chunk.shape[0]
+    rows_a = blocks.shape[1]
+    wide = commons.shape[1]
+    greeted = p.greet()
+
+    used = gattn.shape[1]
+    blocks[:, :used, :] = gattn[...].astype(BF)
+    if used < rows_a:
+        blocks[:, used:, :] = jnp.zeros((n_mp, rows_a - used, D), BF)
+    commons[:3] = gpix[...].astype(BF).reshape(3, wide, D)
+    commons[3] = jnp.concatenate(
+        [
+            gpos[...], jnp.zeros((12, D), F32), rows2[...], rows3[...], jnp.zeros((8, D), F32),
+        ],
+        0,
     ).astype(BF)
-    commons[PIX + 208 : PIX + 224, :] = rows2[...].astype(BF)
-    commons[PIX + 224 : PIX + 256, :] = jnp.concatenate(
-        [rows3[...], jnp.zeros((8, D), F32)], 0
-    ).astype(BF)
-    if commons.shape[0] > PIX + 256:
-        commons[PIX + 256 :, :] = jnp.zeros((commons.shape[0] - PIX - 256, D), BF)
-
-    def common(index, rows):
-        return commons.at[pl.ds(pl.multiple_of(index * rows, rows), rows)]
-
-    near = []
-    for step in range(1, n_y + 1):
-        place = lax.rem(y + step, n_y)
-        give = place * 2 + 1 - core
-        near.append(remote(blocks.at[give], near_b.at[place], near_sem.at[0, step], near_sem.at[1, step], sibling))
-        near.append(remote(common(give, wide_s), near_s.at[place], near_sem.at[2, step], near_sem.at[3, step], sibling))
-    for copy in near:
-        copy.start()
-
-    far = []
-    for step in range(1, n_y + 1):
-        place = lax.rem(y + step, n_y)
-        near[2 * step - 2].wait_recv()
-        near[2 * step - 1].wait_recv()
-        keep = place * 2 + core
-        part_b[pl.ds(place, 1)] = (
-            blocks[pl.ds(keep, 1)].astype(F32) + near_b[pl.ds(place, 1)].astype(F32)
-        ).astype(BF)
-        part_s[pl.ds(place, 1)] = (
-            commons[pl.ds(pl.multiple_of(keep * wide_s, wide_s), wide_s), :].astype(F32)[None]
-            + near_s[pl.ds(place, 1)].astype(F32)
-        ).astype(BF)
-        if step < n_y:
-            to = (dp, keep)
-            far.append(remote(part_b.at[place], far_b.at[step - 1], far_sem.at[0, step], far_sem.at[1, step], to))
-            far.append(remote(part_s.at[place], far_s.at[step - 1], far_sem.at[2, step], far_sem.at[3, step], to))
-            far[-2].start()
-            far[-1].start()
-    total_b = part_b[pl.ds(y, 1)][0].astype(F32)
-    total_s = part_s[pl.ds(y, 1)][0].astype(F32)
-    for step in range(1, n_y):
-        far[2 * step - 2].wait_recv()
-        far[2 * step - 1].wait_recv()
-        total_b += far_b[step - 1].astype(F32)
-        total_s += far_s[step - 1].astype(F32)
-    half_b[...] = total_b.astype(BF)
-    half_s[...] = total_s.astype(BF)
-
-    def rows_of(ref, index, rows):
-        return ref.at[pl.ds(pl.multiple_of(index * rows, rows), rows)]
-
-    last = []
-    for step in range(1, n_dp):
-        place = lax.rem(dp + step, n_dp)
-        to = (place, mp)
-        last.append(remote(rows_of(half_b, place, chunk_b), last_b.at[step - 1], last_sem.at[0, step], last_sem.at[1, step], to))
-        last.append(remote(rows_of(half_s, place, chunk_s), last_s.at[step - 1], last_sem.at[2, step], last_sem.at[3, step], to))
-    for copy in last:
-        copy.start()
-    total_b = half_b[pl.ds(pl.multiple_of(dp * chunk_b, chunk_b), chunk_b), :].astype(F32)
-    total_s = half_s[pl.ds(pl.multiple_of(dp * chunk_s, chunk_s), chunk_s), :].astype(F32)
-    for step in range(1, n_dp):
-        last[2 * step - 2].wait_recv()
-        last[2 * step - 1].wait_recv()
-        total_b += last_b[step - 1].astype(F32)
-        total_s += last_s[step - 1].astype(F32)
-    block_out[pl.ds(pl.multiple_of(dp * chunk_b, chunk_b), chunk_b), :] = total_b.astype(BF)
-    own = mp * n_dp + dp
-    shared_out[pl.ds(pl.multiple_of(own * chunk_s, chunk_s), chunk_s), :] = total_s.astype(BF)
-
-    back = []
-    for step in range(1, n_dp):
-        back.append(
+    if n_mp > 4:
+        commons[4:] = jnp.zeros((n_mp - 4, wide, D), BF)
+
+    def block_rows(index, first, rows):
+        return block_out.at[pl.ds(pl.multiple_of(first + index * rows, rows), rows)]
+
+    def shared_rows(index, rows):
+        return shared_out.at[pl.ds(pl.multiple_of(index * rows, rows), rows)]
+
+    def over_dp(view, sems):
+        sends = [
+            remote(view(p.dp), view(p.dp), sems.at[0, step], sems.at[1, step], (p.along_dp(step), p.mp))
+            for step in range(1, n_dp)
+        ]
+        for copy in sends:
+            copy.start()
+
+        def arrive():
+            for step in range(1, n_dp):
+                source = p.along_dp(n_dp - step)
+                remote(
+                    view(p.dp), view(source), sems.at[0, step], sems.at[1, step], (source, p.mp)
+                ).wait_recv()
+
+        return sends, arrive
+
+    greeted()
+    attn.start()
+    common.start()
+    block_out[pl.ds(pl.multiple_of(rows_a + p.dp * feed_rows, 16), feed_rows), :] = chunk[...]
+    sends, feed_arrive = over_dp(
+        lambda index: block_out.at[
+            pl.ds(pl.multiple_of(rows_a + index * feed_rows, 16), feed_rows)
+        ],
+        feed_sem,
+    )
+    attn.near_to_far()
+    common.near_to_far()
+    attn.far_to_last()
+    common.far_to_last()
+    size = attn.chunk
+    block_out[pl.ds(pl.multiple_of(p.dp * size, size), size), :] = attn.finish()
+    more, attn_arrive = over_dp(lambda index: block_rows(index, 0, size), attn_sem)
+    sends += more
+    size_s = common.chunk
+    own = p.mp * n_dp + p.dp
+    shared_out[pl.ds(pl.multiple_of(own * size_s, size_s), size_s), :] = common.finish()
+    more, shared_arrive = over_dp(
+        lambda index: shared_rows(p.mp * n_dp + index, size_s), shared_sem
+    )
+    sends += more
+    shared_arrive()
+
+    slab = shared_rows(p.mp, wide)
+    for step in range(1, p.n_y):
+        sends.append(
             remote(
-                rows_of(block_out, dp, chunk_b), rows_of(block_out, dp, chunk_b),
-                block_sem.at[0, step], block_sem.at[1, step], (lax.rem(dp + step, n_dp), mp),
+                slab, slab, slab_sem.at[0, step], slab_sem.at[1, step],
+                (p.dp, p.along_y(step) * 2 + p.core),
             )
         )
-        back[-1].start()
-
-    @pl.loop(1, n)
-    def _(step):
-        remote(
-            rows_of(shared_out, own, chunk_s), rows_of(shared_out, own, chunk_s),
-            all_send.at[step], all_recv.at[step], peer_at(lax.rem(me + step, n), n_mp),
-        ).start()
-
-    for step in range(1, n_dp):
-        source = lax.rem(dp + n_dp - step, n_dp)
-        remote(
-            rows_of(block_out, dp, chunk_b), rows_of(block_out, source, chunk_b),
-            block_sem.at[0, step], block_sem.at[1, step], (source, mp),
-        ).wait_recv()
-
+        sends[-1].start()
+    sends.append(remote(slab, slab, hand_sem.at[0, 0], hand_sem.at[1, 0], p.sibling))
+    sends[-1].start()
+
+    feed_arrive()
+    attn_arrive()
     sums = block_out[...].astype(F32)
     sums = colsum(sums * sums)
-    squares[pl.ds(mp, 1)] = jnp.broadcast_to(
+    squares[pl.ds(p.mp, 1)] = jnp.broadcast_to(
         sums[:, 0:128] + sums[:, 128:256] + sums[:, 256:384], (8, 128)
     )[None]
-    tally = []
-    for step in range(1, n_mp):
-        tally.append(
+
+    for step in range(1, p.n_y):
+        source = p.along_y(p.n_y - step) * 2 + p.core
+        theirs = shared_rows(source, wide)
+        remote(
+            slab, theirs, slab_sem.at[0, step], slab_sem.at[1, step], (p.dp, source)
+        ).wait_recv()
+        sends.append(
+            remote(theirs, theirs, hand_sem.at[0, step], hand_sem.at[1, step], p.sibling)
+        )
+        sends[-1].start()
+    for step in range(1, p.n_y):
+        sends.append(
             remote(
-                squares.at[mp], squares.at[mp], square_sem.at[0, step], square_sem.at[1, step],
-                (dp, lax.rem(mp + step, n_mp)),
+                squares.at[p.mp], squares.at[p.mp], square_sem.at[0, step],
+                square_sem.at[1, step], (p.dp, p.along_y(step) * 2 + p.core),
             )
         )
-        tally[-1].start()
-
-    @pl.loop(1, n)
-    def _(step):
-        source = lax.rem(me + n - step, n)
-        copy = remote(
-            rows_of(shared_out, own, chunk_s),
-            rows_of(shared_out, lax.rem(source, n_mp) * n_dp + lax.div(source, n_mp), chunk_s),
-            all_send.at[step], all_recv.at[step], peer_at(source, n_mp),
+        sends[-1].start()
+    for step in range(1, p.n_y):
+        source = p.along_y(p.n_y - step) * 2 + p.core
+        remote(
+            squares.at[p.mp], squares.at[source], square_sem.at[0, step], square_sem.at[1, step],
+            (p.dp, source),
+        ).wait_recv()
+    mine = squares[pl.ds(p.core, 1)]
+    for y in range(1, p.n_y):
+        mine += squares[pl.ds(2 * y + p.core, 1)]
+    squares[pl.ds(n_mp + p.core, 1)] = mine
+    sends.append(
+        remote(
+            squares.at[n_mp + p.core], squares.at[n_mp + p.core], square_sem.at[0, 0],
+            square_sem.at[1, 0], p.sibling,
         )
+    )
+    sends[-1].start()
+    for step in range(p.n_y):
+        theirs = shared_rows(p.along_y(p.n_y - step) * 2 + 1 - p.core, wide)
+        remote(
+            theirs, theirs, hand_sem.at[0, step], hand_sem.at[1, step], p.sibling
+        ).wait_recv()
+    remote(
+        squares.at[n_mp + p.core], squares.at[n_mp + 1 - p.core], square_sem.at[0, 0],
+        square_sem.at[1, 0], p.sibling,
+    ).wait_recv()
+    square_out[...] = squares[n_mp] + squares[n_mp + 1]
+    for copy in sends:
         copy.wait_send()
-        copy.wait_recv()
-
-    for step in range(1, n_mp):
-        source = lax.rem(mp + n_mp - step, n_mp)
-        tally[step - 1].wait_send()
-        remote(
-            squares.at[mp], squares.at[source], square_sem.at[0, step], square_sem.at[1, step],
-            (dp, source),
-        ).wait_recv()
-    square_out[...] = jnp.sum(squares[...], 0)
-    for copy in near + far + last + back:
-        copy.wait_send()
-
-
-def run_reduce(n_dp, n_mp, gattn, gmlp, gv, gpix, gpos, rows2, rows3):
+    attn.wait_sends()
+    common.wait_sends()
+
+
+def run_reduce(n_dp, n_mp, gattn, chunk, gpix, gpos, rows2, rows3):
     n = n_dp * n_mp
-    n_y = n_mp // 2
-    rows_b = gattn.shape[1] + gmlp.shape[1] + gv.shape[1]
-    chunk_b = -(-rows_b // (16 * n_dp)) * 16
-    rows_b = chunk_b * n_dp
+    rows_a = pad_rows(gattn.shape[1], n_dp)
     chunk_s = -(-(PIX + 256) // (16 * n)) * 16
-    wide_s = chunk_s * n_dp
-    y_less = max(n_y - 1, 1)
+    wide = chunk_s * n_dp
+    assert wide == 256
     dma = pltpu.SemaphoreType.DMA
     return pl.pallas_call(
         functools.partial(reduce_kernel, n_dp, n_mp),
-        in_specs=[WHOLE] * 7,
+        in_specs=[WHOLE] * 6,
         out_specs=[WHOLE] * 3,
         out_shape=[
-            shaped(rows_b, D, dtype=BF), shaped(chunk_s * n, D, dtype=BF), shaped(8, 128),
+            shaped(rows_a + chunk.shape[0] * n_dp, D, dtype=BF),
+            shaped(wide * n_mp, D, dtype=BF), shaped(8, 128),
         ],
         scratch_shapes=[
-            pltpu.VMEM((n_mp, rows_b, D), BF), pltpu.VMEM((n * chunk_s, D), BF),
-            pltpu.VMEM((n_y, rows_b, D), BF), pltpu.VMEM((n_y, wide_s, D), BF),
-            pltpu.VMEM((n_y, rows_b, D), BF), pltpu.VMEM((n_y, wide_s, D), BF),
-            pltpu.VMEM((y_less, rows_b, D), BF), pltpu.VMEM((y_less, wide_s, D), BF),
-            pltpu.VMEM((rows_b, D), BF), pltpu.VMEM((wide_s, D), BF),
-            pltpu.VMEM((n_dp - 1, chunk_b, D), BF), pltpu.VMEM((n_dp - 1, chunk_s, D), BF),
-            pltpu.VMEM((n_mp, 8, 128), F32),
-            dma((4, n_y + 1)), dma((4, n_y + 1)), dma((4, n_dp)), dma((n,)), dma((n,)),
-            dma((2, n_dp)), dma((2, n_mp)),
-        ],
+            pltpu.VMEM((n_mp, rows_a, D), BF), pltpu.VMEM((n_mp, wide, D), BF),
+            pltpu.VMEM((n_mp + 2, 8, 128), F32),
+            dma((2, n_dp)), dma((2, n_dp)), dma((2, n_dp)),
+            dma((2, n_mp)), dma((2, n_mp)), dma((2, n_mp)),
+        ]
+        + sum_scratch(n_dp, n_mp, rows_a)
+        + sum_scratch(n_dp, n_mp, wide),
         compiler_params=pltpu.CompilerParams(
             vmem_limit_bytes=VMEM_LIMIT, collective_id=3, has_side_effects=True
         ),
         name="reduce",
-    )(gattn, gmlp, gv, gpix, gpos, rows2, rows3)
+    )(gattn, chunk, gpix, gpos, rows2, rows3)
 
 
 def adam_parts(gradient, mean, square, factor):
@@ -887,22 +1087,388 @@
     square_new = BETA_TWO * square + (1.0 - BETA_TWO) * clipped * clipped
     direction = (
         mean_new
-        / (1.0 - BETA_ONE**STEP)
-        / (jnp.sqrt(square_new / (1.0 - BETA_TWO**STEP)) + ADAM_EPS)
+        * (1.0 / (1.0 - BETA_ONE**STEP))
+        / (jnp.sqrt(square_new * (1.0 / (1.0 - BETA_TWO**STEP))) + ADAM_EPS)
     )
     return (mean_new, square_new, direction)
 
 
-def layer_squares(values):
-    return jnp.stack([jnp.sum(values[0] * values[0]), jnp.sum(values[1] * values[1])])
-
-
-def trust_of(weight_sq, update_sq):
-    return jnp.sqrt(weight_sq / (update_sq + 1e-12))
-
-
-def per_layer(values, like):
-    return values.reshape((2,) + (1,) * (like.ndim - 1))
+def fold(values):
+    squares = (values * values).reshape(values.shape[0] // 8, 8, values.shape[1]).sum(0)
+    width = values.shape[1]
+    if width % 128:
+        return jnp.broadcast_to(jnp.sum(squares, 1, keepdims=True), (8, 128)) * (1.0 / 128)
+    return sum(squares[:, i : i + 128] for i in range(0, width, 128))
+
+
+def total(values):
+    return jnp.sum(jnp.sum(values, 0, keepdims=True), 1, keepdims=True)
+
+
+def moment_kernel(
+    n_dp, block, shared, block_sq, gout1, gup1, gdown1, ghead, rows1, stat, aux, wcls,
+    vec, vec_mean, vec_square, mix, mix_mean, mix_square, *rest,
+):
+    state = rest[:15]
+    outs = rest[15:30]
+    (
+        vec_out, vec_mean_out, vec_square_out, mix_out, mix_mean_out, mix_square_out,
+        misc_out, sums_out,
+    ) = rest[30:38]
+    held = rest[38:53]
+    updates = rest[53:57]
+    grad_q, grad_k, grad_flip, load_sem, save_sem, table_update = rest[57:]
+    loads = [pltpu.make_async_copy(state[i], held[i], load_sem.at[i]) for i in range(15)]
+    for copy in loads:
+        copy.start()
+    mp = lax.axis_index("mp")
+    hs = state[3].shape[1]
+    fs = state[9].shape[1]
+    feed = pad_rows(4 * hs, n_dp)
+
+    rows2 = shared[PIX + 208 : PIX + 224, :].astype(F32)
+    rows3 = shared[PIX + 224 : PIX + 256, :].astype(F32)
+    token = aux[8:9, :]
+    wq = part(wcls, 0, hs)
+    wk = part(wcls, hs, hs).astype(F32)
+    query = nt(wq, aux[8:16, :].astype(BF))[:, 0:1].astype(BF).astype(F32)
+    dkeys = jnp.concatenate(
+        [jnp.broadcast_to(rows2[8 + h : 9 + h, :], (HEAD, D)) for h in range(HEADS)], 0
+    )
+    dquery = SCALE * jnp.sum(wk * dkeys, 1, keepdims=True)
+    gq = dquery * token
+    gk = (SCALE * query) * dkeys
+    grad_q[...] = gq
+    grad_k[...] = gk
+    dtoken = rows2[6:7, :] + colsum(dquery * wq.astype(F32))
+    unit, inverse = normalize(jnp.broadcast_to(vec[17:18, :], (8, D)))
+    dcls = normalize_back(unit, inverse, vec[8:9, :], jnp.broadcast_to(dtoken, (8, D)))[0:1, :]
+    dgain = rows2[4:5, :] + dtoken * unit[0:1, :]
+    last = rows1[...]
+    positions = shared[PIX : PIX + 208, :].astype(F32)
+    grad_vec = jnp.concatenate(
+        [
+            rows3[0:4, :], rows2[0:4, :], dgain, rows2[5:6, :] + dtoken, last[2:8, :],
+            colsum(positions), last[8:9, :] + dcls, last[9:11, :],
+        ],
+        0,
+    )
+    mask = head_mask()
+    exact = functools.partial(
+        lax.dot_general, dimension_numbers=(((1,), (1,)), ((), ())),
+        preferred_element_type=F32, precision=lax.Precision.HIGHEST,
+    )
+    grad_mix = (exact(rows3[8:16, :], mask) * SCALE, exact(mask, rows3[16:24, :]))
+
+    square = total(block_sq[0:1, :]) + total(stat[1:2, :]) + total(colsum(gq * gq + gk * gk))
+    square += total(grad_vec * grad_vec)
+    square += total(grad_mix[0] * grad_mix[0]) + total(grad_mix[1] * grad_mix[1])
+
+    def square_rows(i, kept):
+        rows = shared[pl.ds(pl.multiple_of(i * 16, 16), 16), :].astype(F32)
+        return kept + fold(rows)
+
+    square += total(lax.fori_loop(0, (PIX + 208) // 16, square_rows, jnp.zeros((8, 128), F32)))
+    norm = jnp.sqrt(square)
+    factor = CLIP / jnp.maximum(norm, CLIP)
+
+    mean, second, direction = adam_parts(grad_vec, vec_mean[...], vec_square[...], factor)
+    vec_mean_out[...] = mean
+    vec_square_out[...] = second
+    vec_out[...] = vec[...] - RATE_VECTOR * direction
+    misc = [norm]
+    weight_sums = []
+    for b in range(2):
+        mean, second, direction = adam_parts(grad_mix[b], mix_mean[b], mix_square[b], factor)
+        mix_mean_out[b] = mean
+        mix_square_out[b] = second
+        update = direction + DECAY * mix[b]
+        weight_sq = total(mix[b] * mix[b])
+        update_sq = total(update * update)
+        mix_out[b] = mix[b] - RATE * jnp.sqrt(weight_sq / (update_sq + 1e-12)) * update
+        weight_sums.append(weight_sq)
+        misc.append(update_sq)
+
+    def sweep(grad, w, m, s, u, rows):
+        chunk = 32 if rows % 32 == 0 else 16
+
+        def step(i, kept):
+            at = pl.ds(pl.multiple_of(i * chunk, chunk), chunk)
+            weight = w[at, :]
+            mean, second, direction = adam_parts(grad(i, chunk), m[at, :], s[at, :], factor)
+            m[at, :] = mean
+            s[at, :] = second
+            update = direction + DECAY * weight
+            u[at, :] = update
+            return (kept[0] + fold(weight), kept[1] + fold(update))
+
+        zero = jnp.zeros((8, 128), F32)
+        return lax.fori_loop(0, rows // chunk, step, (zero, zero))
+
+    def rows_from(ref, first):
+        def read(i, chunk):
+            at = pl.ds(pl.multiple_of(first + i * chunk, 16), chunk)
+            return ref[at, :].astype(F32)
+
+        return read
+
+    saves = []
+
+    def save(i, source):
+        saves.append(pltpu.make_async_copy(source, outs[i], save_sem.at[i]))
+        saves[-1].start()
+
+    sums = []
+    own_h = pl.multiple_of(mp * hs, hs)
+    own_f = pl.multiple_of(mp * fs, fs)
+    for kind in range(4):
+        for copy in loads[3 * kind : 3 * kind + 3]:
+            copy.wait()
+        w, m, s = held[3 * kind : 3 * kind + 3]
+        u = updates[kind]
+        for b in range(2):
+            views = (w.at[b], m.at[b], s.at[b], u.at[b])
+            if kind == 0 and b == 0:
+                sums.append(sweep(rows_from(block, 0), *views, 3 * hs))
+            elif kind == 0:
+                pieces = []
+                for third, source in enumerate(
+                    (
+                        rows_from(grad_q, own_h),
+                        rows_from(grad_k, own_h),
+                        rows_from(block, feed + 2 * fs),
+                    )
+                ):
+                    pieces.append(
+                        sweep(
+                            source, *(view.at[pl.ds(third * hs, hs)] for view in views), hs
+                        )
+                    )
+                sums.append(
+                    tuple(pieces[0][i] + pieces[1][i] + pieces[2][i] for i in range(2))
+                )
+            elif kind == 1:
+                source = rows_from(gout1, own_h) if b else rows_from(block, 3 * hs)
+                sums.append(sweep(source, *views, hs))
+            elif kind == 2:
+                if b:
+                    grad_flip[...] = gup1[pl.ds(own_f, fs), :].T
+                else:
+                    grad_flip[...] = block[feed : feed + fs, :].astype(F32).T
+                sums.append(sweep(rows_from(grad_flip, 0), *views, D))
+            else:
+                source = rows_from(gdown1, own_f) if b else rows_from(block, feed + fs)
+                sums.append(sweep(source, *views, fs))
+        save(3 * kind, u)
+        save(3 * kind + 1, m)
+        save(3 * kind + 2, s)
+    for place, pair in enumerate(sums):
+        sums_out[place : place + 1, :] = colsum(pair[1])
+        sums_out[8 + place : 9 + place, :] = colsum(pair[0])
+
+    for copy in loads[12:]:
+        copy.wait()
+    w, m, s = held[12:15]
+    edge = PIX + P_SIZE - 4
+    rows_all = w.shape[0]
+
+    def slab(first, count, grad):
+        at = slice(first, first + count)
+        weight = w[at, :]
+        mean, second, direction = adam_parts(grad, m[at, :], s[at, :], factor)
+        m[at, :] = mean
+        s[at, :] = second
+        return weight, direction + DECAY * weight
+
+    def run(first, count, source, offset):
+        def step(i, kept):
+            at = pl.ds(pl.multiple_of(first + i * 32, 16), 32)
+            weight = w[at, :]
+            grad = source[pl.ds(pl.multiple_of(offset + i * 32, 16), 32), :].astype(F32)
+            mean, second, direction = adam_parts(grad, m[at, :], s[at, :], factor)
+            m[at, :] = mean
+            s[at, :] = second
+            update = direction + DECAY * weight
+            table_update[at, :] = update
+            return (kept[0] + fold(weight), kept[1] + fold(update))
+
+        zero = jnp.zeros((8, 128), F32)
+        return lax.fori_loop(0, count // 32, step, (zero, zero))
+
+    patch = run(0, PIX, shared, 0)
+    place_rows = run(PIX, P_SIZE - 4, shared, PIX)
+    body = (rows_all - edge - 16) // 32 * 32
+    heads = run(edge + 16, body, ghead, 16)
+    tile = lax.broadcasted_iota(jnp.int32, (16, 1), 0) < 4
+    weight, update = slab(
+        edge, 16, shared[edge : edge + 16, :].astype(F32) + ghead[0:16, :]
+    )
+    table_update[edge : edge + 16, :] = update
+    left = edge + 16 + body
+    tail_rows = rows_all - left
+    tail_weight, tail_update = slab(left, tail_rows, ghead[16 + body : 16 + body + tail_rows, :])
+    table_update[left:rows_all, :] = tail_update
+    save(13, m)
+    save(14, s)
+
+    def masked(values, mask):
+        return total(jnp.where(mask, values * values, 0.0))
+
+    sq_w = [
+        total(patch[0]), total(place_rows[0]) + masked(weight, tile),
+        total(heads[0]) + masked(weight, ~tile) + total(tail_weight * tail_weight),
+    ]
+    sq_u = [
+        total(patch[1]), total(place_rows[1]) + masked(update, tile),
+        total(heads[1]) + masked(update, ~tile) + total(tail_update * tail_update),
+    ]
+    rates = [RATE * jnp.sqrt(sq_w[i] / (sq_u[i] + 1e-12)) for i in range(3)]
+
+    def renew(first, count, rate):
+        def step(i, _):
+            at = pl.ds(pl.multiple_of(first + i * 32, 16), 32)
+            w[at, :] = w[at, :] - rate * table_update[at, :]
+            return 0
+
+        lax.fori_loop(0, count // 32, step, 0)
+
+    renew(0, PIX, rates[0])
+    renew(PIX, P_SIZE - 4, rates[1])
+    renew(edge + 16, body, rates[2])
+    w[edge : edge + 16, :] = weight - jnp.where(tile, rates[1], rates[2]) * update
+    w[left:rows_all, :] = tail_weight - rates[2] * tail_update
+    save(12, w)
+
+    lane = lax.broadcasted_iota(jnp.int32, (1, 128), 1)
+    line = jnp.where(lane == 0, norm, 0.0)
+    weight_line = jnp.zeros((1, 128), F32)
+    update_line = jnp.zeros((1, 128), F32)
+    for place, (first, second) in enumerate(
+        zip(sq_w + weight_sums, sq_u + misc[1:])
+    ):
+        weight_line = jnp.where(lane == 8 + place, first, weight_line)
+        update_line = jnp.where(lane == 8 + place, second, update_line)
+    misc_out[0:1, :] = line
+    misc_out[1:2, :] = weight_line
+    misc_out[2:3, :] = update_line
+    misc_out[3:8, :] = jnp.zeros((5, 128), F32)
+    for copy in saves:
+        copy.wait()
+
+
+def run_moments(n_dp, grads, smalls, state):
+    outs = []
+    for i, item in enumerate(state):
+        outs.append(jax.ShapeDtypeStruct(item.shape, F32))
+    hs, fs = state[3].shape[1], state[9].shape[1]
+    dma = pltpu.SemaphoreType.DMA
+    return pl.pallas_call(
+        functools.partial(moment_kernel, n_dp),
+        in_specs=[WHOLE] * (len(grads) + len(smalls)) + [ANY] * 15,
+        out_specs=[ANY] * 15 + [WHOLE] * 8,
+        out_shape=outs
+        + [jax.ShapeDtypeStruct(item.shape, F32) for item in smalls]
+        + [shaped(8, 128), shaped(16, 128)],
+        scratch_shapes=[pltpu.VMEM(item.shape, F32) for item in state]
+        + [pltpu.VMEM(state[3 * kind].shape, F32) for kind in range(4)]
+        + [
+            pltpu.VMEM((D, D), F32), pltpu.VMEM((D, D), F32), pltpu.VMEM((D, fs), F32),
+            dma((15,)), dma((15,)), pltpu.VMEM(state[12].shape, F32),
+        ],
+        compiler_params=pltpu.CompilerParams(vmem_limit_bytes=VMEM_LIMIT),
+        name="moments",
+    )(*grads, *smalls, *state)
+
+
+def sums_kernel(n_mp, sums, out, slots, send_sem, recv_sem):
+    dp = lax.axis_index("dp")
+    mp = lax.axis_index("mp")
+    barrier = pltpu.get_barrier_semaphore()
+    for step in range(1, n_mp):
+        pl.semaphore_signal(
+            barrier, inc=1, device_id=(dp, lax.rem(mp + step, n_mp)), device_id_type=MESH
+        )
+    slots[pl.ds(mp, 1)] = sums[...][None]
+    pl.semaphore_wait(barrier, n_mp - 1)
+    copies = [
+        remote(
+            slots.at[mp], slots.at[mp], send_sem.at[step], recv_sem.at[step],
+            (dp, lax.rem(mp + step, n_mp)),
+        )
+        for step in range(1, n_mp)
+    ]
+    for copy in copies:
+        copy.start()
+    for step in range(1, n_mp):
+        source = lax.rem(mp + n_mp - step, n_mp)
+        copies[step - 1].wait_send()
+        remote(
+            slots.at[mp], slots.at[source], send_sem.at[step], recv_sem.at[step], (dp, source)
+        ).wait_recv()
+    out[...] = jnp.sum(slots[...], 0)
+
+
+def run_sums(n_mp, sums):
+    return pl.pallas_call(
+        functools.partial(sums_kernel, n_mp),
+        in_specs=[WHOLE],
+        out_specs=WHOLE,
+        out_shape=shaped(*sums.shape),
+        scratch_shapes=[
+            pltpu.VMEM((n_mp, *sums.shape), F32),
+            pltpu.SemaphoreType.DMA((n_mp,)),
+            pltpu.SemaphoreType.DMA((n_mp,)),
+        ],
+        compiler_params=pltpu.CompilerParams(
+            vmem_limit_bytes=VMEM_LIMIT, collective_id=4, has_side_effects=True
+        ),
+        name="sums",
+    )(sums)
+
+
+def renew_kernel(sums, misc, *rest):
+    weights, updates = rest[:4], rest[4:8]
+    new, copies, norms = rest[8:12], rest[12:16], rest[16]
+    rates = []
+    lane = lax.broadcasted_iota(jnp.int32, (1, 128), 1)
+    weight_line, update_line = misc[1:2, :], misc[2:3, :]
+    for place in range(8):
+        update_sq = total(sums[place : place + 1, :])
+        weight_sq = total(sums[8 + place : 9 + place, :])
+        rates.append(RATE * jnp.sqrt(weight_sq / (update_sq + 1e-12)))
+        weight_line = jnp.where(lane == place, weight_sq, weight_line)
+        update_line = jnp.where(lane == place, update_sq, update_line)
+    norms[0:1, :] = jnp.sqrt(weight_line)
+    norms[1:2, :] = jnp.sqrt(update_line)
+    norms[2:8, :] = jnp.zeros((6, 128), F32)
+    for kind in range(4):
+        rows = weights[kind].shape[1]
+        chunk = 32 if rows % 32 == 0 else 16
+        for b in range(2):
+            w, u, out, low = weights[kind], updates[kind], new[kind], copies[kind]
+            rate = rates[2 * kind + b]
+
+            def step(i, _, b=b, w=w, u=u, out=out, low=low, rate=rate, chunk=chunk):
+                at = pl.ds(pl.multiple_of(i * chunk, chunk), chunk)
+                values = w[b, at, :] - rate * u[b, at, :]
+                out[b, at, :] = values
+                low[b, at, :] = values.astype(BF)
+                return 0
+
+            lax.fori_loop(0, rows // chunk, step, 0)
+
+
+def run_renew(sums, misc, weights, updates):
+    return pl.pallas_call(
+        renew_kernel,
+        in_specs=[WHOLE] * 10,
+        out_specs=[WHOLE] * 9,
+        out_shape=[shaped(*item.shape) for item in weights]
+        + [shaped(*item.shape, dtype=BF) for item in weights]
+        + [shaped(8, 128)],
+        compiler_params=pltpu.CompilerParams(vmem_limit_bytes=VMEM_LIMIT),
+        name="renew",
+    )(sums, misc, *weights, *updates)
 
 
 def shards(
@@ -936,25 +1502,27 @@
     local = pixels.shape[0]
     group = token_mask.shape[0]
     place_mp = lax.axis_index("mp")
-    place_dp = lax.axis_index("dp")
     n_mp = lax.axis_size("mp")
     n_dp = lax.axis_size("dp")
-    images = local * n_mp * n_dp
-    place = place_dp * n_mp + place_mp
     hs = attn_in.shape[3]
     fs = mlp_in.shape[2]
 
-    attn_rows = [
-        jnp.concatenate(
-            [attn_in[b].transpose(1, 2, 0).reshape(3 * hs, D), attn_out[b]], 0
-        ).astype(BF)
-        for b in range(2)
-    ]
+    def as_rows(item):
+        return item.transpose(0, 2, 3, 1).reshape(2, 3 * hs, D)
+
+    def from_rows(item):
+        return item.reshape(2, 3, hs, D).transpose(0, 3, 1, 2)
+
+    attn_in, attn_in_mean, attn_in_square = map(as_rows, (attn_in, attn_in_mean, attn_in_square))
     mlp_rows = [jnp.concatenate([mlp_in[b].T, mlp_out[b]], 0).astype(BF) for b in range(2)]
-    wattn = run_weights(n_dp, n_mp, attn_rows[0])
+    cls_rows = jnp.concatenate([attn_in[1], attn_out[1]], 0).astype(BF)
     wmlp = lax.all_gather(mlp_rows[0], "mp")
-    wcls = lax.all_gather(attn_rows[1], "mp")
+    wcls = lax.all_gather(cls_rows, "mp")
     wmlp_cls = lax.all_gather(mlp_rows[1], "mp")
+    pixel_rows = pixels.transpose(1, 0, 2).reshape(P_SIZE * local, PIX)
+    wattn, embed = run_start(
+        n_dp, n_mp, local, attn_in, attn_out, pixel_rows, tables, vectors
+    )
 
     okay = lax.dynamic_slice_in_dim(
         (jnp.arange(group) >= group - counts[0]).astype(F32), place_mp * local, local, 0
@@ -973,168 +1541,65 @@
     t1col = t1row.T
     t2row = spread_heads(talking[1].T)
     t2col = t2row.T
-    wp = tables[:PIX].astype(BF)
-    pos = tables[PIX : PIX + P_SIZE]
     head = tables[PIX + P_SIZE :].astype(BF)
 
-    embed, q, k, v, prob, ho, raw0, middle, stat_a = run_self_attend(
-        pixels, cols, vectors, pos, wp, wattn, t1row, t2col
+    q, k, v, prob, ho, raw0, middle, stat_a = run_self_attend(
+        embed, cols, vectors, wattn, t1row, t2col
     )
     patches, act, slope, raw1, cprob, cprob0, z, card, aux = run_feed(
         middle, cols, bias[:, None, :], base, stat_a, vectors, wmlp, wcls
     )
     cards = run_cards(n_dp, n_mp, card)
     dch, gout1, gup1, gdown1, ghead, rows1, stat = run_token(
-        group, cards, vectors, wcls, wmlp_cls, head
-    )
-    dch = lax.dynamic_slice_in_dim(dch, place * local, local, 0).reshape(local, 1, D)
-    dmid, gmlp, gv, rows2 = run_feed_back(
-        dch, patches, middle, raw1, act, slope, cprob, cprob0, z, aux, vectors, wcls, wmlp
-    )
-    gattn, gpix, gpos, rows3 = run_self_back(
-        dmid, pixels, embed, q, k, v, prob, ho, raw0, vectors, wattn, t1row, t1col, t2row
+        group, local, cards, vectors, wcls, wmlp_cls, head
+    )
+    dmid, gfeed, rows2 = run_feed_back(
+        n_dp, dch, patches, middle, raw1, act, slope, cprob, cprob0, z, aux, vectors, wcls, wmlp
+    )
+    gattn, gpix, gpos, rows3, chunk = run_self_back(
+        n_dp, n_mp, dmid, pixel_rows, embed, q, k, v, prob, ho, raw0, vectors, wattn,
+        t1row, t1col, t2row, gfeed,
     )
 
     block, shared, block_sq = run_reduce(
-        n_dp, n_mp, gattn, gmlp, gv.reshape(n_mp, hs, D), gpix, gpos, rows2, rows3
-    )
-    sharded = block.astype(F32)
-    shared = shared[: PIX + 256].astype(F32)
-    gpix = shared[:PIX]
-    gpos = shared[PIX : PIX + P_SIZE]
-    rows2 = shared[PIX + 208 : PIX + 224]
-    rows3 = shared[PIX + 224 : PIX + 248]
-
-    dkeys = rows2[8:16]
-    token = aux[8:9]
-    query = aux[16]
-    wq1 = wcls[:, :hs].reshape(D, D)
-    wk1 = wcls[:, hs : 2 * hs].reshape(D, D)
-    dquery = SCALE * jnp.sum(wk1.astype(F32) * jnp.repeat(dkeys, HEAD, axis=0), 1)
-    gq1 = dquery[:, None] * token
-    gk1 = (SCALE * query)[:, None] * jnp.repeat(dkeys, HEAD, axis=0)
-    dtoken = rows2[6] + jnp.sum(dquery[:, None] * wq1.astype(F32), 0)
-    unit, inverse = normalize(vectors[17])
-    grad_class_token = rows1[8] + normalize_back(unit, inverse, vectors[8], dtoken)
-    grad_vectors = jnp.stack(
-        [
-            rows3[0], rows3[1], rows3[2], rows3[3], rows2[0], rows2[1], rows2[2], rows2[3],
-            rows2[4] + dtoken * unit, rows2[5] + dtoken, rows1[2], rows1[3],
-            rows1[4], rows1[5], rows1[6], rows1[7],
-            jnp.sum(gpos, 0), grad_class_token, rows1[9], rows1[10],
-        ]
-    )
-    by_head = rows3[8:24].reshape(2, HEADS, HEADS, HEAD).sum(-1)
-    grad_talking = jnp.stack([by_head[0] * SCALE, by_head[1].T])
-
-    def mine(rows, size):
-        return lax.dynamic_slice_in_dim(rows, place_mp * size, size, 0)
-
-    def unpack(rows):
-        return rows.reshape(3, hs, D).transpose(2, 0, 1)
-
-    class_rows = jnp.concatenate([mine(gq1, hs), mine(gk1, hs), sharded[4 * hs + 2 * fs : 5 * hs + 2 * fs]], 0)
-    grads = (
-        jnp.stack([unpack(sharded[: 3 * hs]), unpack(class_rows)]),
-        jnp.stack([sharded[3 * hs : 4 * hs], mine(gout1, hs)]),
-        jnp.stack([sharded[4 * hs : 4 * hs + fs].T, mine(gup1, fs).T]),
-        jnp.stack([sharded[4 * hs + fs : 4 * hs + 2 * fs], mine(gdown1, fs)]),
-    )
-    grad_tables = jnp.concatenate([gpix, gpos, ghead], 0)
-
-    weights = (attn_in, attn_out, mlp_in, mlp_out)
-    means = (attn_in_mean, attn_out_mean, mlp_in_mean, mlp_out_mean)
-    squares = (attn_in_square, attn_out_square, mlp_in_square, mlp_out_square)
-    grad_norm = jnp.sqrt(
-        jnp.sum(block_sq[0])
-        + sum(jnp.sum(item * item) for item in (gq1, gk1, gout1, gup1, gdown1))
-        + jnp.sum(grad_tables * grad_tables)
-        + jnp.sum(grad_vectors * grad_vectors)
-        + jnp.sum(grad_talking * grad_talking)
-    )
-    factor = CLIP / jnp.maximum(grad_norm, CLIP)
-    moved = [adam_parts(grads[i], means[i], squares[i], factor) for i in range(4)]
-    updates = [moved[i][2] + DECAY * weights[i] for i in range(4)]
-    weight_sq, update_sq = lax.psum(
-        (
-            jnp.concatenate([layer_squares(item) for item in weights]),
-            jnp.concatenate([layer_squares(item) for item in updates]),
-        ),
-        "mp",
-    )
-    trust = trust_of(weight_sq, update_sq)
-    renewed = [
-        weights[i] - RATE * per_layer(trust[2 * i : 2 * i + 2], weights[i]) * updates[i]
-        for i in range(4)
-    ]
-
-    table_mean, table_square, table_direction = adam_parts(
-        grad_tables, tables_mean, tables_square, factor
-    )
-    table_update = table_direction + DECAY * tables
-    bounds = ((0, PIX), (PIX, PIX + P_SIZE), (PIX + P_SIZE, tables.shape[0]))
-
-    def segments(values):
-        by_row = jnp.sum(values * values, 1)
-        return jnp.stack([jnp.sum(by_row[low:high]) for low, high in bounds])
-
-    table_weight_sq = segments(tables)
-    table_update_sq = segments(table_update)
-    table_trust = trust_of(table_weight_sq, table_update_sq)
-    row = jnp.arange(tables.shape[0])[:, None]
-    row_trust = jnp.where(
-        row < PIX, table_trust[0], jnp.where(row < PIX + P_SIZE, table_trust[1], table_trust[2])
-    )
-    tables_new = tables - RATE * row_trust * table_update
-
-    vector_mean, vector_square, vector_direction = adam_parts(
-        grad_vectors, vectors_mean, vectors_square, factor
-    )
-    vectors_new = vectors - RATE_VECTOR * vector_direction
-    mixing_mean, mixing_square, mixing_direction = adam_parts(
-        grad_talking, talking_mean, talking_square, factor
-    )
-    mixing_update = mixing_direction + DECAY * talking
-    mixing_weight_sq = layer_squares(talking)
-    mixing_update_sq = layer_squares(mixing_update)
-    talking_new = talking - RATE * per_layer(
-        trust_of(mixing_weight_sq, mixing_update_sq), talking
-    ) * mixing_update
-    norms = jnp.stack(
-        [
-            jnp.sqrt(jnp.concatenate([weight_sq, table_weight_sq, mixing_weight_sq])),
-            jnp.sqrt(jnp.concatenate([update_sq, table_update_sq, mixing_update_sq])),
-        ]
-    )
-    statistics = stat[0, :12]
+        n_dp, n_mp, gattn, chunk, gpix, gpos, rows2, rows3
+    )
+    state = (
+        attn_in, attn_in_mean, attn_in_square, attn_out, attn_out_mean, attn_out_square,
+        mlp_in, mlp_in_mean, mlp_in_square, mlp_out, mlp_out_mean, mlp_out_square,
+        tables, tables_mean, tables_square,
+    )
+    smalls = (vectors, vectors_mean, vectors_square, talking, talking_mean, talking_square)
+    moved = run_moments(
+        n_dp, (block, shared, block_sq, gout1, gup1, gdown1, ghead, rows1, stat, aux, wcls),
+        smalls, state,
+    )
+    sums = run_sums(n_mp, moved[22])
+    renewed = run_renew(sums, moved[21], state[0:12:3], moved[0:12:3])
+    norms = renewed[8][:2, :13]
     return (
-        renewed[0],
-        moved[0][0],
-        moved[0][1],
+        from_rows(renewed[0]),
+        from_rows(moved[1]),
+        from_rows(moved[2]),
         renewed[1],
-        moved[1][0],
-        moved[1][1],
+        moved[4],
+        moved[5],
         renewed[2],
-        moved[2][0],
-        moved[2][1],
+        moved[7],
+        moved[8],
         renewed[3],
-        moved[3][0],
-        moved[3][1],
-        tables_new,
-        table_mean,
-        table_square,
-        vectors_new,
-        vector_mean,
-        vector_square,
-        talking_new,
-        mixing_mean,
-        mixing_square,
-        renewed[0].astype(BF),
-        renewed[1].astype(BF),
-        renewed[2].astype(BF),
-        renewed[3].astype(BF),
-        statistics,
-        grad_norm,
+        moved[10],
+        moved[11],
+        moved[12],
+        moved[13],
+        moved[14],
+        *moved[15:21],
+        from_rows(renewed[4]),
+        renewed[5],
+        renewed[6],
+        renewed[7],
+        stat[0, :12],
+        moved[21][0, 0],
         norms,
     )
 

time: 450 us -> 285 us (0.63); the launches traced: 441 us -> 285 us
  other arithmetic: 85.9 us -> 3.54 us
  local copies, waits for them, and re-layouts: 62.6 us -> 13.6 us
  between operations: 25.1 us -> 14.6 us
  blocking collectives: 7.36 us -> 0 us
  Pallas kernels: 260 us -> 253 us
    pallas_call x1, Pallas kernels: 102 us -> 51.5 us  [run_reduce(): pl.pallas_call(functools.partial(reduce_kernel, n_dp, n_mp), in_specs=[WH...]
    pallas_call x3 -> x6, Pallas kernels: 85.1 us -> 131 us  [the longest x1 52 us: run_self_back(): pl.pallas_call(functools.partial(self_back_kernel, n_dp, n_mp), grid=(cou...]
    reduce_sum x34 -> x0, other arithmetic: 41.2 us -> none  [the longest x1 9.67 us: segments(): by_row = jnp.sum(values * values, 1)]
    concatenate x4 -> x1, local copies, waits for them, and re-layouts: 17.5 us -> 0.06 us  [shards(): jnp.concatenate([mlp_in[b].T, mlp_out[b]], 0).astype(BF)]
    unnamed x112 -> x15, local copies, waits for them, and re-layouts: 13.4 us -> 0.57 us
    add x7 -> x0, other arithmetic: 12.7 us -> none  [the longest x4 10.5 us: shards(): updates = [moved[i][2] + DECAY * weights[i] for i in range(4)]]
    convert_element_type x6 -> x0, other arithmetic: 9.39 us -> none  [the longest x1 3.19 us: shards(): renewed[3].astype(BF)]
    psum x1 -> x0, blocking collectives: 7.36 us -> none  [shards(): lax.psum((jnp.concatenate([layer_squares(item) for item in weights]), jnp...]
  transfers between devices with their start and end apart: 3 -> 3, of which waited for: 0 -> 0; matrix products, arithmetic and copies ran while one was open for 8% -> 4% of each run, Pallas kernels for 17% -> 26%
where the time goes in v2:
time: 285 us
  Pallas kernels  253 us (89%)
  between operations  14.6 us (5%)
  local copies, waits for them, and re-layouts  13.6 us (5%)
  other arithmetic  3.54 us (1%)
    pallas_call x1, Pallas kernels, run_self_back(): pl.pallas_call(functools.partial(self_back_kernel, n_dp, n_mp), grid=(cou...  52 us
    pallas_call x1, Pallas kernels, run_reduce(): pl.pallas_call(functools.partial(reduce_kernel, n_dp, n_mp), in_specs=[WH...  51.5 us
    pallas_call x1, Pallas kernels, run_feed_back(): pl.pallas_call(feed_back_kernel, grid=(count,), in_specs=[constant(count,...  28.8 us
    pallas_call x1, Pallas kernels, run_feed(): pl.pallas_call(feed_kernel, grid=(count,), in_specs=[per_image(P_SIZE, D)...  24.4 us
    pallas_call x1, Pallas kernels, run_moments(): pl.pallas_call(functools.partial(moment_kernel, n_dp), in_specs=[WHOLE] *...  22.4 us
    pallas_call x1, Pallas kernels, run_self_attend(): pl.pallas_call(self_attend_kernel, grid=(count,), in_specs=[per_image(P_S...  22.3 us
    pallas_call x1, Pallas kernels, run_start(): pl.pallas_call(functools.partial(start_kernel, n_dp, n_mp), in_specs=[ANY...  16.7 us
    pallas_call x1, Pallas kernels, run_cards(): pl.pallas_call(functools.partial(card_kernel, n_dp, n_mp), in_specs=[WHOL...  11.9 us
  transfers between devices with their start and end apart: 3, of which 0 were waited for; matrix products, arithmetic and copies ran while one was open for 4% of the time, Pallas kernels for 26%

profile of v2, /device:TPU:0, one launch (start us, length us, event | category | flops | bytes accessed | tf_op | source)
XLA Modules:
  0.0 284.9 jit_solution(2949313770965202568)
XLA Ops:
  7.3 1.0 slice.73
  8.3 1.0 slice.72
  9.3 0.7 pad_maximum_fusion.2
  10.9 0.9 pad_maximum_fusion
  11.9 0.9 pad_maximum_fusion.1
  13.5 0.9 select_reduce_fusion
  15.8 0.7 copy.70.t1row
  16.5 0.8 copy.71.t2col
  17.4 2.4 slice.71.head
  19.8 1.2 copy.69.cols
  21.7 16.7 %start.1 = (bf16[4,384,384]{2,1,0:T(8,128)(2,1)}, f32[8,196,384]{2,1,0:T(8,128)}) custom-call(f32[2,288,384]{2,1,0:T(8,128)} %bitcast.69, f32[2,96,384]{2,1,0:T(8,128)} %rest_1_.1, bf16[1568,768]{1,0:T(8,128)(2,1)} %bitcast.66, f32[1964,384]{1,0:T(8,128)} %rest_12_.1, f32[20,384]{1,0:T(8,128)} %vec.13), custom_call_target="tpu_custom_call" | custom-call | tf_op jit(solution)/shard_map/start/pallas_call | solution.py:886
  38.4 22.3 %self_attend.1 = (bf16[8,196,384]{2,1,0:T(8,128)(2,1)}, bf16[8,196,384]{2,1,0:T(8,128)(2,1)}, bf16[8,196,384]{2,1,0:T(8,128)(2,1)}, bf16[8,8,196,196]{3,2,1,0:T(...) custom-call(f32[8,196,384]{2,1,0:T(8,128)} %get-tuple-element.97.emb, ...), custom_call_target="tpu_custom_call" | custom-call | tf_op jit(solution)/shard_map/self_attend/pallas_call | solution.py:613
  60.7 24.4 %feed.1 = (f32[8,196,384]{2,1,0:T(8,128)}, bf16[8,196,1536]{2,1,0:T(8,128)(2,1)}, bf16[8,196,1536]{2,1,0:T(8,128)(2,1)}, bf16[8,196,384]{2,1,0:T(8,128)(2,1)}, f...) custom-call(f32[8,196,384]{2,1,0:T(8,128)} %get-tuple-element.99.mid, ...), custom_call_target="tpu_custom_call" | custom-call | tf_op jit(solution)/shard_map/feed/pallas_call | solution.py:639
  85.1 11.9 %cards.1 = f32[1024,128]{1,0:T(8,128)} custom-call(f32[32,128]{1,0:T(8,128)} %get-tuple-element.101.card), custom_call_target="tpu_custom_call" | custom-call | tf_op jit(solution)/shard_map/cards/pallas_call | solution.py:788
  97.1 11.5 %token_net.1 = (f32[8,384]{1,0:T(8,128)}, f32[384,384]{1,0:T(8,128)}, f32[1536,384]{1,0:T(8,128)}, f32[1536,384]{1,0:T(8,128)}, f32[1008,384]{1,0:T(8,128)}, /*index=5*/f32[16,384]{1,0:T(8,128)}, f32[8,128]{1,0:T(8,128)}) custom-call(f32[1024,128]{1,0:T(8,128)} %cards.1, f32[20,384]{1,0:T(8,128)} %vec.13, ...), custom_call_target="tpu_custom_call" | custom-call | tf_op jit(solution)/shard_map/token_net/pallas_call | solution.py:665
  108.5 1.2 slice_bitcast_fusion.3
  109.7 28.8 %feed_back.1 = (f32[8,196,384]{2,1,0:T(8,128)}, bf16[4,896,384]{2,1,0:T(8,128)(2,1)}, f32[16,384]{1,0:T(8,128)}) custom-call(f32[8,384]{1,0:T(8,128)} %get-tuple-element.102.dch, f32[8,196,384]{2,1,0:T(8,128)} %get-tuple-element.103.patch, f32[8,196,384]{2,1,0:T(8,128)} %get-tuple-element.99.mid, bf16[8,196,384]{2,1,0:T(8,128)(2,1)} %get-tuple-element.104.raw, ...), custom_call_target="tpu_custom_call" | custom-call | tf_op jit(solution)/shard_map/feed_back/pallas_call | solution.py:683
  138.6 52.0 %self_back.1 = (f32[4,384,384]{2,1,0:T(8,128)}, f32[768,384]{1,0:T(8,128)}, f32[196,384]{1,0:T(8,128)}, f32[24,384]{1,0:T(8,128)}, bf16[112,384]{1,0:T(8,128)(2,1)}) custom-call(f32[8,196,384]{2,1,0:T(8,128)} %get-tuple-element.111.dmid, bf16[1568,768]{1,0:T(8,128)(2,1)} %bitcast.67, f32[8,196,384]{2,1,0:T(8,128)} %get-tuple-element.97.embed, ...), custom_call_target="tpu_custom_call" | custom-call | tf_op jit(solution)/shard_map/self_back/pallas_call | solution.py:707
  190.6 51.5 %reduce.1 = (bf16[1280,384]{1,0:T(8,128)(2,1)}, bf16[1024,384]{1,0:T(8,128)(2,1)}, f32[8,128]{1,0:T(8,128)}) custom-call(f32[4,384,384]{2,1,0:T(8,128)} %get-tuple-element.119.gattn, bf16[112,384]{1,0:T(8,128)(2,1)} %get-tuple-element.120.chunk, f32[768,384]{1,0:T(8,128)} %get-tuple-element.121.gpix, f32[196,384]{1,0:T(8,128)} %get-tuple-element.122.gpos, ...), custom_call_target="tpu_custom_call" | custom-call | tf_op jit(solution)/shard_map/reduce/pallas_call | solution.py:1061
  242.0 22.4 %moments.1 = (f32[2,288,384]{2,1,0:T(8,128)}, f32[2,288,384]{2,1,0:T(8,128)}, f32[2,288,384]{2,1,0:T(8,128)}, f32[2,96,384]{2,1,0:T(8,128)}, f32[2,96,384]{2,1,0...) custom-call(bf16[1280,384]{1,0:T(8,128)(2,1)} %get-tuple-element.125, ...), custom_call_target="tpu_custom_call" | custom-call | tf_op jit(solution)/shard_map/moments/pallas_call | solution.py:1365
  264.5 1.2 slice.54
  265.7 5.1 %sums.1 = f32[16,128]{1,0:T(8,128)} custom-call(f32[16,128]{1,0:T(8,128)} %get-tuple-element.134.sums), custom_call_target="tpu_custom_call" | custom-call | tf_op jit(solution)/shard_map/sums/pallas_call | solution.py:1412
  270.7 6.4 %renew.1 = (f32[2,288,384]{2,1,0:T(8,128)}, f32[2,96,384]{2,1,0:T(8,128)}, f32[2,384,384]{2,1,0:T(8,128)}, f32[2,384,384]{2,1,0:T(8,128)}, bf16[2,288,384]{2,1,0...) custom-call(f32[16,128]{1,0:T(8,128)} %sums.1, ...), custom_call_target="tpu_custom_call" | custom-call | tf_op jit(solution)/shard_map/renew/pallas_call | solution.py:1462
  277.2 1.2 slice.55
  (48 shorter events, 3.2 us)
Async XLA Ops:
  7.2 3.0 %copy-start.1 = (f32[2,384,384]{2,1,0:T(8,128)S(1)}, f32[2,384,384]{2,1,0:T(8,128)}, u32[]{:S(2)}) copy-start(f32[2,384,384]{2,1,0:T(8,128)} %rest_2_.1) | copy-start | bytes 3538948
  7.2 53.5 %all-gather.6.cloned.1.call-start = ((), (), s32[]{:S(2)}) async-start(), calls=%async_computation.1 | async-start | bytes 1474560 | tf_op jit(solution)/shard_map/all_gather | solution.py:1520
  9.3 1.4 copy-start
  10.1 50.6 %all-gather.4.cloned.1.call-start = ((), (), s32[]{:S(2)}) async-start(), calls=%async_computation | async-start | bytes 2949120 | tf_op jit(solution)/shard_map/all_gather | solution.py:1519
  11.8 2.7 copy-start.5
  11.8 2.8 copy-start.6
  11.8 3.0 %copy-start.4 = (f32[2,8,8]{2,1,0:T(8,128)S(1)}, f32[2,8,8]{2,1,0:T(8,128)}, u32[]{:S(2)}) copy-start(f32[2,8,8]{2,1,0:T(8,128)} %mix.1) | copy-start | bytes 1540
  11.8 85.2 %all-gather.8.cloned.1.call-start = ((), (), s32[]{:S(2)}) async-start(), calls=%async_computation.2 | async-start | bytes 2949120 | tf_op jit(solution)/shard_map/all_gather | solution.py:1521
  15.8 5.2 %copy-start.3 = (f32[8,384]{1,0:T(8,128)}, f32[8,384]{1,0:T(8,128)S(1)}, u32[]{:S(2)}) copy-start(f32[8,384]{1,0:T(8,128)S(1)} %reshape.181.t2row) | copy-start | bytes 36868
  15.8 5.2 %copy-start.2 = (f32[8,8,48]{0,2,1:T(8,128)}, f32[8,8,48]{0,2,1:T(8,128)S(1)}, u32[]{:S(2)}) copy-start(f32[8,8,48]{0,2,1:T(8,128)S(1)} %broadcast_in_dim.26) | copy-start | bytes 36868
Sparse Core Ops, SparseCore 0:
  10.2 20.8 all-gather.5
  33.3 23.6 all-gather.3
  59.1 24.0 all-gather.7

commit v3 on v2

v3 whole, which is shorter than its diff:
```python
import functools

import jax
import jax.numpy as jnp
from jax import lax
from jax.experimental import pallas as pl
from jax.experimental.pallas import tpu as pltpu
from jax.sharding import PartitionSpec as P

D = 384
HEADS = 8
HEAD = 48
PIX = 768
P_SIZE = 196
PAD = 208
WIDE = 256
STEP = 10
SCALE = HEAD**-0.5
BETA_ONE = 0.9
BETA_TWO = 0.999
ADAM_EPS = 1e-08
DECAY = 0.01
RATE = 0.5
RATE_VECTOR = 0.5
CLIP = 0.02
TEMP = 0.05
MASKED = -1000000000.0
NORM_EPS = 1e-06
F32 = jnp.float32
BF = jnp.bfloat16
VMEM_LIMIT = 58 * 2**20
ANY = pl.BlockSpec(memory_space=pl.ANY)
MESH = pl.DeviceIdType.MESH
WHOLE = pl.BlockSpec(memory_space=pltpu.VMEM)


def nn(left, right):
    return lax.dot_general(left, right, (((1,), (0,)), ((), ())), preferred_element_type=F32)


def nt(left, right):
    return lax.dot_general(left, right, (((1,), (1,)), ((), ())), preferred_element_type=F32)


def tn(left, right):
    return lax.dot_general(left, right, (((0,), (0,)), ((), ())), preferred_element_type=F32)


def colsum(values):
    return jnp.sum(values, 0, keepdims=True)


def normalize(inputs):
    center = inputs - jnp.mean(inputs, -1, keepdims=True)
    spread = jnp.mean(center * center, -1, keepdims=True)
    inverse = lax.rsqrt(spread + NORM_EPS)
    return center * inverse, inverse


def normalize_back(unit, inverse, gain, incoming):
    scaled = incoming * gain
    return inverse * (
        scaled
        - jnp.mean(scaled, -1, keepdims=True)
        - unit * jnp.mean(scaled * unit, -1, keepdims=True)
    )


def gelu_parts(inner):
    cumulative = 0.5 + 0.5 * lax.erf(inner * 0.5**0.5)
    bell = jnp.exp2(inner * inner * (-0.5 * 1.4426950408889634)) * 0.3989422804014327
    return inner * cumulative, cumulative + inner * bell


def head_mask(copies=1):
    row = lax.rem(lax.broadcasted_iota(jnp.int32, (copies * HEADS, D), 0), HEADS)
    column = lax.broadcasted_iota(jnp.int32, (copies * HEADS, D), 1)
    return ((column >= row * HEAD) & (column < row * HEAD + HEAD)).astype(F32)


def stat_lanes(parts, weight, first):
    lane = lax.broadcasted_iota(jnp.int32, (1, 128), 1)
    row = jnp.zeros((1, 128), F32)
    for place, values in enumerate(parts):
        total = jnp.sum(colsum(values * values * weight), keepdims=True)
        high = total.astype(BF).astype(F32)
        row = jnp.where(lane == first + 2 * place, high, row)
        row = jnp.where(lane == first + 2 * place + 1, total - high, row)
    return row


def part(ref, first, rows):
    shards_count = ref.shape[0]
    return ref[:, first : first + rows, :].reshape(shards_count * rows, ref.shape[2])


def pad_rows(rows, n_dp):
    return -(-rows // (16 * n_dp)) * 16 * n_dp


class Place:
    def __init__(self, n_dp, n_mp):
        self.n_dp, self.n_mp, self.n_y = n_dp, n_mp, n_mp // 2
        self.n_lo = 2 if n_dp < 16 else 4
        self.n_hi = n_dp // self.n_lo
        self.dp = lax.axis_index("dp")
        self.mp = lax.axis_index("mp")
        self.y = lax.div(self.mp, 2)
        self.core = lax.rem(self.mp, 2)
        self.high = lax.div(self.dp, self.n_lo)
        self.low = lax.rem(self.dp, self.n_lo)
        self.chunk = self.low * self.n_hi + self.high
        self.sibling = (self.dp, self.y * 2 + 1 - self.core)

    def along_y(self, step):
        return lax.rem(self.y + step, self.n_y)

    def along_lo(self, step):
        return lax.rem(self.low + step, self.n_lo)

    def along_hi(self, step):
        return lax.rem(self.high + step, self.n_hi)

    def at_lo(self, low):
        return (self.high * self.n_lo + low, self.mp)

    def at_hi(self, high):
        return (high * self.n_lo + self.low, self.mp)

    def near_partners(self):
        return [self.sibling] + [
            (self.dp, self.along_y(step) * 2 + self.core) for step in range(1, self.n_y)
        ]

    def low_partners(self):
        return [self.at_lo(self.along_lo(step)) for step in range(1, self.n_lo)]

    def dp_partners(self):
        return self.low_partners() + [self.at_hi(self.along_hi(step)) for step in range(1, self.n_hi)]


def greet(partners):
    barrier = pltpu.get_barrier_semaphore()
    for partner in partners:
        pl.semaphore_signal(barrier, inc=1, device_id=partner, device_id_type=MESH)
    return lambda: pl.semaphore_wait(barrier, len(partners))


def tile_rows(ref, first, rows):
    return ref.at[pl.ds(pl.multiple_of(first, 16), rows)]


class SpreadGather:
    def __init__(self, place, rows, out, far_sem, low_sem, near_sem):
        self.place, self.rows, self.out = place, rows, out
        self.far_sem, self.low_sem, self.near_sem = far_sem, low_sem, near_sem
        self.count = rows.shape[0] // place.n_lo

    def piece(self, ref, low):
        return tile_rows(ref, low * self.count, self.count)

    def far_copy(self, step, slot):
        p = self.place
        return remote(
            self.piece(self.rows, p.low), self.piece(self.out.at[slot], p.low),
            self.far_sem.at[0, step], self.far_sem.at[1, step],
            (p.dp, p.along_y(step) * 2 + p.core),
        )

    def low_copy(self, step, turn, low):
        p = self.place
        rows = self.piece(self.out.at[self.from_y(step) + p.core], low)
        at = (step - 1) * p.n_lo + turn
        return remote(
            rows, rows, self.low_sem.at[0, at], self.low_sem.at[1, at],
            p.at_lo(p.along_lo(turn)),
        )

    def near_copy(self, step, slot):
        return remote(
            self.rows if step == 0 else self.out.at[slot], self.out.at[slot],
            self.near_sem.at[0, step], self.near_sem.at[1, step], self.place.sibling,
        )

    def own_copy(self):
        return pltpu.make_async_copy(
            self.rows, self.out.at[self.place.mp], self.far_sem.at[0, 0]
        )

    def from_y(self, step):
        p = self.place
        return p.along_y(p.n_y - step) * 2

    def start(self):
        p = self.place
        for step in range(1, p.n_y):
            self.far_copy(step, p.mp).start()
        self.near_copy(0, p.mp).start()
        self.own_copy().start()

    def spread(self):
        p = self.place
        for step in range(1, p.n_y):
            self.far_copy(step, self.from_y(step) + p.core).wait_recv()
            for turn in range(1, p.n_lo):
                self.low_copy(step, turn, p.low).start()

    def forward(self):
        p = self.place
        for step in range(1, p.n_y):
            for turn in range(1, p.n_lo):
                self.low_copy(step, turn, p.along_lo(p.n_lo - turn)).wait_recv()
            self.near_copy(step, self.from_y(step) + p.core).start()

    def finish(self):
        p = self.place
        self.own_copy().wait()
        for step in range(1, p.n_y):
            self.far_copy(step, p.mp).wait_send()
            for turn in range(1, p.n_lo):
                self.low_copy(step, turn, p.low).wait_send()
        for step in range(p.n_y):
            self.near_copy(step, self.from_y(step) + p.core if step else p.mp).wait_send()
            self.near_copy(step, self.from_y(step) + 1 - p.core).wait_recv()


def spread_scratch(n_dp, n_mp):
    n_lo = 2 if n_dp < 16 else 4
    dma = pltpu.SemaphoreType.DMA
    return [dma((2, n_mp // 2)), dma((2, n_mp // 2 * n_lo)), dma((2, n_mp // 2))]


class Gather:
    def __init__(self, place, rows, out, far_sem, near_sem):
        self.place, self.rows, self.out = place, rows, out
        self.far_sem, self.near_sem = far_sem, near_sem

    def far_copy(self, step, slot):
        p = self.place
        return remote(
            self.rows, self.out.at[slot], self.far_sem.at[0, step], self.far_sem.at[1, step],
            (p.dp, p.along_y(step) * 2 + p.core),
        )

    def near_copy(self, step, slot):
        return remote(
            self.rows if step == 0 else self.out.at[slot], self.out.at[slot],
            self.near_sem.at[0, step], self.near_sem.at[1, step], self.place.sibling,
        )

    def own_copy(self):
        return pltpu.make_async_copy(
            self.rows, self.out.at[self.place.mp], self.far_sem.at[0, 0]
        )

    def from_y(self, step):
        p = self.place
        return p.along_y(p.n_y - step) * 2

    def start(self):
        p = self.place
        for step in range(1, p.n_y):
            self.far_copy(step, p.mp).start()
        self.near_copy(0, p.mp).start()
        self.own_copy().start()

    def forward(self):
        p = self.place
        for step in range(1, p.n_y):
            slot = self.from_y(step) + p.core
            self.far_copy(step, slot).wait_recv()
            self.near_copy(step, slot).start()

    def finish(self):
        p = self.place
        self.own_copy().wait()
        for step in range(1, p.n_y):
            self.far_copy(step, p.mp).wait_send()
        for step in range(p.n_y):
            self.near_copy(step, self.from_y(step) + p.core if step else p.mp).wait_send()
            self.near_copy(step, self.from_y(step) + 1 - p.core).wait_recv()


def gather_scratch(n_mp):
    dma = pltpu.SemaphoreType.DMA
    return [dma((2, n_mp // 2)), dma((2, n_mp // 2))]


class ShardSum:
    def __init__(
        self, place, rows, first, y_first, near, far, low, half, high,
        near_sem, far_sem, low_sem, high_sem,
    ):
        self.place, self.rows, self.first, self.y_first = place, rows, first, y_first
        self.near, self.far, self.low, self.half, self.high = near, far, low, half, high
        self.near_sem, self.far_sem = near_sem, far_sem
        self.low_sem, self.high_sem = low_sem, high_sem
        self.count = near.shape[1]
        self.wide = self.count // place.n_lo
        self.chunk = self.count // place.n_dp

    def near_copy(self, step):
        p = self.place
        y = p.along_y(step)
        return remote(
            self.rows.at[y * 2 + 1 - p.core, pl.ds(self.first, self.count)], self.near.at[y],
            self.near_sem.at[0, step], self.near_sem.at[1, step], p.sibling,
        )

    def far_copy(self, step):
        p = self.place
        y = p.along_y(step)
        rows = self.near.at[y]
        if not self.y_first:
            rows = tile_rows(rows, p.low * self.wide, self.wide)
        return remote(
            rows, self.far.at[step - 1],
            self.far_sem.at[0, step], self.far_sem.at[1, step], (p.dp, y * 2 + p.core),
        )

    def low_copy(self, step):
        p = self.place
        to = p.along_lo(step)
        at = pl.ds(pl.multiple_of(to * self.wide, 16), self.wide)
        rows = self.near.at[p.y, at] if self.y_first else self.near.at[:, at]
        return remote(
            rows, self.low.at[step - 1],
            self.low_sem.at[0, step], self.low_sem.at[1, step], p.at_lo(to),
        )

    def high_copy(self, step):
        p = self.place
        to = p.along_hi(step)
        return remote(
            tile_rows(self.half, to * self.chunk, self.chunk), self.high.at[step - 1],
            self.high_sem.at[0, step], self.high_sem.at[1, step], p.at_hi(to),
        )

    def start(self):
        for step in range(1, self.place.n_y + 1):
            self.near_copy(step).start()

    def second(self):
        p = self.place
        at = slice(self.first, self.first + self.count)
        for step in range(1, p.n_y + 1):
            y = p.along_y(step)
            self.near_copy(step).wait_recv()
            self.near[pl.ds(y, 1)] = (
                self.rows[pl.ds(y * 2 + p.core, 1), at, :].astype(F32)
                + self.near[pl.ds(y, 1)].astype(F32)
            ).astype(BF)
            if self.y_first and step < p.n_y:
                self.far_copy(step).start()
        if not self.y_first:
            for step in range(1, p.n_lo):
                self.low_copy(step).start()

    def third(self):
        p = self.place
        own = pl.ds(pl.multiple_of(p.low * self.wide, 16), self.wide)
        if self.y_first:
            sums = self.near[pl.ds(p.y, 1)].astype(F32)
            for step in range(1, p.n_y):
                self.far_copy(step).wait_recv()
                sums += self.far[step - 1].astype(F32)[None]
            self.near[pl.ds(p.y, 1)] = sums.astype(BF)
            for step in range(1, p.n_lo):
                self.low_copy(step).start()
        else:
            sums = self.near[:, own, :].astype(F32)
            for step in range(1, p.n_lo):
                self.low_copy(step).wait_recv()
                sums += self.low[step - 1].astype(F32)
            self.near[:, own, :] = sums.astype(BF)
            for step in range(1, p.n_y):
                self.far_copy(step).start()

    def fourth(self):
        p = self.place
        own = pl.ds(pl.multiple_of(p.low * self.wide, 16), self.wide)
        sums = self.near[pl.ds(p.y, 1), own, :][0].astype(F32)
        if self.y_first:
            for step in range(1, p.n_lo):
                self.low_copy(step).wait_recv()
                sums += self.low[step - 1].astype(F32)
        else:
            for step in range(1, p.n_y):
                self.far_copy(step).wait_recv()
                sums += self.far[step - 1].astype(F32)
        self.half[...] = sums.astype(BF)
        for step in range(1, p.n_hi):
            self.high_copy(step).start()

    def finish(self):
        p = self.place
        at = pl.ds(pl.multiple_of(p.high * self.chunk, 16), self.chunk)
        sums = self.half[at, :].astype(F32)
        for step in range(1, p.n_hi):
            self.high_copy(step).wait_recv()
            sums += self.high[step - 1].astype(F32)
        return sums.astype(BF)

    def wait_sends(self):
        p = self.place
        for step in range(1, p.n_y + 1):
            self.near_copy(step).wait_send()
            if step < p.n_y:
                self.far_copy(step).wait_send()
        for step in range(1, p.n_lo):
            self.low_copy(step).wait_send()
        for step in range(1, p.n_hi):
            self.high_copy(step).wait_send()


def sum_scratch(n_dp, n_mp, rows, y_first):
    n_y = n_mp // 2
    n_lo = 2 if n_dp < 16 else 4
    n_hi = n_dp // n_lo
    wide = rows // n_lo
    dma = pltpu.SemaphoreType.DMA
    far = (max(n_y - 1, 1), rows, D) if y_first else (max(n_y - 1, 1), wide, D)
    low = (n_lo - 1, wide, D) if y_first else (n_lo - 1, n_y, wide, D)
    return [
        pltpu.VMEM((n_y, rows, D), BF), pltpu.VMEM(far, BF), pltpu.VMEM(low, BF),
        pltpu.VMEM((wide, D), BF), pltpu.VMEM((n_hi - 1, rows // n_dp, D), BF),
        dma((2, n_y + 1)), dma((2, n_y + 1)), dma((2, n_lo)), dma((2, n_hi)),
    ]


SUM_BUFFERS = 9


def halves(rows, n_dp):
    unit = 16 * n_dp
    first = (rows // unit + 1) // 2 * unit
    return first, rows - first


class TableSum:
    def __init__(
        self, place, rows, out, near, low, part_rows, high, last, far, near_sem, low_sem, high_sem,
        far_sem, back_sem, hand_sem,
    ):
        self.place, self.rows, self.out = place, rows, out
        self.near, self.low, self.part, self.high = near, low, part_rows, high
        self.last, self.far = last, far
        self.near_sem, self.low_sem, self.high_sem = near_sem, low_sem, high_sem
        self.far_sem, self.back_sem, self.hand_sem = far_sem, back_sem, hand_sem
        self.chunk = high.shape[2]
        self.wide = low.shape[2]
        self.slab = place.core * place.n_y + place.y
        self.first = place.core * place.n_y

    def near_copy(self):
        p = self.place
        return remote(
            self.rows.at[pl.ds((1 - p.core) * p.n_y, p.n_y)], self.near,
            self.near_sem.at[0], self.near_sem.at[1], p.sibling,
        )

    def low_copy(self, step):
        p = self.place
        to = p.along_lo(step)
        return remote(
            self.near.at[:, pl.ds(pl.multiple_of(to * self.wide, 16), self.wide)],
            self.low.at[step - 1], self.low_sem.at[0, step], self.low_sem.at[1, step], p.at_lo(to),
        )

    def high_copy(self, step):
        p = self.place
        to = p.along_hi(step)
        return remote(
            self.part.at[:, pl.ds(pl.multiple_of(to * self.chunk, 16), self.chunk)],
            self.high.at[step - 1], self.high_sem.at[0, step], self.high_sem.at[1, step],
            p.at_hi(to),
        )

    def far_copy(self, step):
        p = self.place
        to = p.along_y(step)
        return remote(
            self.last.at[to], self.far.at[step - 1], self.far_sem.at[0, step],
            self.far_sem.at[1, step], (p.dp, to * 2 + p.core),
        )

    def start(self):
        self.near_copy().start()

    def near_to_low(self):
        p = self.place
        self.near_copy().wait_recv()
        self.near[...] = (
            self.rows[pl.ds(self.first, p.n_y)].astype(F32) + self.near[...].astype(F32)
        ).astype(BF)
        for step in range(1, p.n_lo):
            self.low_copy(step).start()

    def low_to_high(self):
        p = self.place
        at = pl.ds(pl.multiple_of(p.low * self.wide, 16), self.wide)
        sums = self.near[:, at, :].astype(F32)
        for step in range(1, p.n_lo):
            self.low_copy(step).wait_recv()
            sums += self.low[step - 1].astype(F32)
        self.part[...] = sums.astype(BF)
        for step in range(1, p.n_hi):
            self.high_copy(step).start()

    def high_to_far(self):
        p = self.place
        at = pl.ds(pl.multiple_of(p.high * self.chunk, 16), self.chunk)
        sums = self.part[:, at, :].astype(F32)
        for step in range(1, p.n_hi):
            self.high_copy(step).wait_recv()
            sums += self.high[step - 1].astype(F32)
        self.last[...] = sums.astype(BF)
        for step in range(1, p.n_y):
            self.far_copy(step).start()

    def chunk_at(self, slab, chunk):
        return self.out.at[slab, pl.ds(pl.multiple_of(chunk * self.chunk, 16), self.chunk)]

    def back_far(self, step, y):
        p = self.place
        rows = self.chunk_at(self.first + y, p.chunk)
        return remote(
            rows, rows, self.back_sem.at[0, step], self.back_sem.at[1, step],
            (p.dp, p.along_y(step) * 2 + p.core),
        )

    def back_high(self, step, chunk):
        p = self.place
        rows = self.chunk_at(pl.ds(self.first, p.n_y), chunk)
        return remote(
            rows, rows, self.back_sem.at[2, step], self.back_sem.at[3, step],
            p.at_hi(p.along_hi(step)),
        )

    def back_low(self, step, low):
        p = self.place
        rows = self.out.at[
            pl.ds(self.first, p.n_y), pl.ds(pl.multiple_of(low * self.wide, 16), self.wide)
        ]
        return remote(
            rows, rows, self.back_sem.at[4, step], self.back_sem.at[5, step],
            p.at_lo(p.along_lo(step)),
        )

    def hand_copy(self, core):
        p = self.place
        rows = self.out.at[pl.ds(core * p.n_y, p.n_y)]
        return remote(rows, rows, self.hand_sem.at[0], self.hand_sem.at[1], p.sibling)

    def turn(self):
        p = self.place
        sums = self.last[pl.ds(p.y, 1)][0].astype(F32)
        for step in range(1, p.n_y):
            self.far_copy(step).wait_recv()
            sums += self.far[step - 1].astype(F32)
        at = pl.ds(pl.multiple_of(p.chunk * self.chunk, 16), self.chunk)
        self.out[pl.ds(self.slab, 1), at, :] = sums.astype(BF)[None]
        for step in range(1, p.n_y):
            self.back_far(step, p.y).start()

    def far_to_high(self):
        p = self.place
        for step in range(1, p.n_y):
            self.back_far(step, p.along_y(p.n_y - step)).wait_recv()
        for step in range(1, p.n_hi):
            self.back_high(step, p.chunk).start()

    def high_to_low(self):
        p = self.place
        for step in range(1, p.n_hi):
            self.back_high(step, p.low * p.n_hi + p.along_hi(p.n_hi - step)).wait_recv()
        for step in range(1, p.n_lo):
            self.back_low(step, p.low).start()

    def low_to_near(self):
        p = self.place
        for step in range(1, p.n_lo):
            self.back_low(step, p.along_lo(p.n_lo - step)).wait_recv()
        self.hand_copy(p.core).start()

    def finish(self):
        p = self.place
        self.hand_copy(1 - p.core).wait_recv()
        self.near_copy().wait_send()
        self.hand_copy(p.core).wait_send()
        for step in range(1, p.n_lo):
            self.low_copy(step).wait_send()
            self.back_low(step, p.low).wait_send()
        for step in range(1, p.n_hi):
            self.high_copy(step).wait_send()
            self.back_high(step, p.chunk).wait_send()
        for step in range(1, p.n_y):
            self.far_copy(step).wait_send()
            self.back_far(step, p.y).wait_send()


def table_scratch(n_dp, n_mp, rows):
    n_y = n_mp // 2
    n_lo = 2 if n_dp < 16 else 4
    n_hi = n_dp // n_lo
    wide, chunk = rows // n_lo, rows // n_dp
    dma = pltpu.SemaphoreType.DMA
    return [
        pltpu.VMEM((n_y, rows, D), BF), pltpu.VMEM((n_lo - 1, n_y, wide, D), BF),
        pltpu.VMEM((n_y, wide, D), BF), pltpu.VMEM((n_hi - 1, n_y, chunk, D), BF),
        pltpu.VMEM((n_y, chunk, D), BF), pltpu.VMEM((max(n_y - 1, 1), chunk, D), BF),
        dma((2,)), dma((2, n_lo)), dma((2, n_hi)), dma((2, n_y)),
        dma((6, max(n_y, n_lo, n_hi))), dma((2,)),
    ]


class HandHigh:
    def __init__(self, place, rows, sems):
        self.place, self.rows, self.sems = place, rows, sems
        self.chunk = rows.shape[0] // place.n_hi

    def copy(self, step, source):
        p = self.place
        rows = tile_rows(self.rows, source * self.chunk, self.chunk)
        return remote(
            rows, rows, self.sems.at[0, step], self.sems.at[1, step], p.at_hi(p.along_hi(step))
        )

    def start(self, sums):
        p = self.place
        self.rows[pl.ds(pl.multiple_of(p.high * self.chunk, 16), self.chunk), :] = sums
        for step in range(1, p.n_hi):
            self.copy(step, p.high).start()

    def arrive(self):
        p = self.place
        for step in range(1, p.n_hi):
            self.copy(step, p.along_hi(p.n_hi - step)).wait_recv()

    def wait_sends(self):
        for step in range(1, self.place.n_hi):
            self.copy(step, self.place.high).wait_send()


class HandLow:
    def __init__(self, place, rows, first, count, sems):
        self.place, self.rows, self.first, self.sems = place, rows, first, sems
        self.run = count // place.n_lo

    def copy(self, step, source):
        p = self.place
        rows = tile_rows(self.rows, self.first + source * self.run, self.run)
        return remote(
            rows, rows, self.sems.at[0, step], self.sems.at[1, step], p.at_lo(p.along_lo(step))
        )

    def start(self, sums):
        p = self.place
        self.rows[pl.ds(pl.multiple_of(self.first + p.low * self.run, 16), self.run), :] = sums
        for step in range(1, p.n_lo):
            self.copy(step, p.low).start()

    def arrive(self):
        p = self.place
        for step in range(1, p.n_lo):
            self.copy(step, p.along_lo(p.n_lo - step)).wait_recv()

    def wait_sends(self):
        for step in range(1, self.place.n_lo):
            self.copy(step, self.place.low).wait_send()


def remote(src, dst, send_sem, recv_sem, device):
    return pltpu.make_async_remote_copy(
        src_ref=src, dst_ref=dst, send_sem=send_sem, recv_sem=recv_sem,
        device_id=device, device_id_type=MESH,
    )


def stack_heads(stack, rows, gains):
    for g in range(HEADS):
        stack[g * PAD : g * PAD + P_SIZE, :] = (rows * gains[g : g + 1, :]).astype(BF)


def column(cols, index):
    lane = lax.broadcasted_iota(jnp.int32, cols.shape, 1)
    return jnp.sum(jnp.where(lane == index, cols[...], 0.0), 1, keepdims=True)


def self_attend_kernel(
    n_dp, n_mp, embed, cols, vec, wattn, t1row, t2row, mlp_rows,
    q_out, k_out, v_out, prob_out, post_out, ho_out, raw_out, mid_out, stat_out, wmlp_out,
    stack, scores, *sems,
):
    shard = wattn.shape[1] // 4
    place = Place(n_dp, n_mp)
    gather = Gather(place, mlp_rows, wmlp_out, *sems)
    images = pl.num_programs(0)

    @pl.when(pl.program_id(0) == 0)
    def _():
        stack[...] = jnp.zeros_like(stack)
        greet(place.near_partners())()
        gather.start()

    @pl.when(pl.program_id(0) == images - 1)
    def _():
        gather.forward()

    x = embed[0]
    unit, _ = normalize(x)
    normed = (unit * vec[0:1, :] + vec[1:2, :]).astype(BF)
    q = nt(normed, part(wattn, 0, shard)).astype(BF)
    k = nt(normed, part(wattn, shard, shard)).astype(BF)
    v = nt(normed, part(wattn, 2 * shard, shard)).astype(BF)
    q_out[0] = q
    k_out[0] = k
    v_out[0] = v
    stack_heads(stack, q.astype(F32), t1row)
    scores[...] = nt(k, stack[...])
    bias = column(cols, pl.program_id(0))
    for first in range(0, HEADS * PAD, 128):
        mixed = scores[:, first : first + 128] + bias
        grown = jnp.exp(mixed - jnp.max(mixed, 0, keepdims=True))
        prob = grown * (1.0 / jnp.sum(grown, 0, keepdims=True))
        prob_out[0, :, first : first + 128] = prob.astype(BF)
    post = tn(prob_out[0], v)
    post_out[0] = post.astype(BF)
    heads_out = jnp.zeros(x.shape, F32)
    for g in range(HEADS):
        heads_out += post[g * PAD : g * PAD + P_SIZE, :] * t2row[g : g + 1, :]
    heads_out = heads_out.astype(BF)
    ho_out[0] = heads_out
    raw = nn(heads_out, part(wattn, 3 * shard, shard))
    raw_out[0] = raw.astype(BF)
    branch = vec[3:4, :] * (raw + vec[2:3, :])
    middle = x + branch
    mid_out[0] = middle
    weight = column(cols, pl.program_id(0) + cols.shape[1] // 2)
    stat_out[0] = stat_lanes((branch, middle), weight, 8)

    @pl.when(pl.program_id(0) == images - 1)
    def _():
        gather.finish()


def feed_kernel(
    n_dp, n_mp, mid, cols, bias_row, base, stat, vec, wmlp, cls_rows, up_rows, down_rows,
    patch_out, act_out, slope_out, raw_out, norm_out, cprob_out, cprob0_out, z_out, card_out,
    aux_out, wcls_out, wup_out, wdown_out, wcls, *sems,
):
    hidden = wmlp.shape[1] // 2
    shard = wcls.shape[1] // 4
    images = norm_out.shape[0]

    place = Place(n_dp, n_mp)
    gather_cls = SpreadGather(place, cls_rows, wcls, *sems[:3])
    gather_up = SpreadGather(place, up_rows, wup_out, *sems[3:6])
    gather_down = SpreadGather(place, down_rows, wdown_out, *sems[6:])

    def beside(step, *stages):
        @pl.when(pl.program_id(0) == step)
        def _():
            for stage in stages:
                stage()

    @pl.when(pl.program_id(0) == 0)
    def _():
        norm_out[...] = jnp.zeros_like(norm_out)
        greet(place.near_partners() + place.low_partners())()
        gather_cls.start()
        gather_up.start()
        gather_down.start()

    beside(images * 3 // 8, gather_cls.spread)
    beside(images // 2, gather_up.spread)
    beside(images * 5 // 8, gather_down.spread)
    beside(images * 3 // 4, gather_cls.forward)
    beside(images - 1, gather_up.forward, gather_cls.finish)

    middle = mid[0]
    unit, _ = normalize(middle)
    normed = (unit * vec[4:5, :] + vec[5:6, :]).astype(BF)
    inner = nt(normed, part(wmlp, 0, hidden))
    active, slope = gelu_parts(inner)
    active = active.astype(BF)
    act_out[0] = active
    slope_out[0] = slope.astype(BF)
    raw = nn(active, part(wmlp, hidden, hidden))
    raw_out[0] = raw.astype(BF)
    branch = vec[7:8, :] * (raw + vec[6:7, :])
    patches = middle + branch
    patch_out[0] = patches
    card_out[pl.ds(4 * pl.program_id(0) + 3, 1), :] = (
        base[pl.ds(pl.program_id(0), 1), :]
        + stat[0]
        + stat_lanes((branch, patches), column(cols, pl.program_id(0) + images), 12)
    )
    unit, _ = normalize(patches)
    norm_out[pl.ds(pl.program_id(0), 1), :P_SIZE, :] = (
        (unit * vec[8:9, :] + vec[9:10, :]).astype(BF)[None]
    )

    @pl.when(pl.program_id(0) == images - 1)
    def _():
        gather_down.forward()
        unit, _ = normalize(jnp.broadcast_to(vec[17:18, :], (HEADS, D)))
        token = (unit * vec[8:9, :] + vec[9:10, :]).astype(BF)
        query = nt(token, part(wcls, 0, shard)).astype(BF).astype(F32)
        keys = nn((query * head_mask()).astype(BF), part(wcls, shard, shard)) * SCALE
        token = token.astype(F32)
        aux_out[0:8, :] = keys
        aux_out[8:16, :] = token
        aux_out[16:24, :] = query
        scores = nt(keys.astype(BF), norm_out[...].reshape(images * WIDE, D)) + bias_row[...]
        score0 = jnp.sum(keys * token, -1, keepdims=True)
        for n in range(images):
            rows = slice(n * HEADS, (n + 1) * HEADS)
            mine = scores[:, n * WIDE : (n + 1) * WIDE]
            top = jnp.maximum(jnp.max(mine, -1, keepdims=True), score0)
            grown = jnp.exp(mine - top)
            grown0 = jnp.exp(score0 - top)
            scale = 1.0 / (jnp.sum(grown, -1, keepdims=True) + grown0)
            cprob = grown * scale
            cprob0 = grown0 * scale
            cprob_out[rows, :] = cprob
            cprob0_out[rows, :] = jnp.broadcast_to(cprob0, (HEADS, 128))
            z_out[rows, :] = nn(cprob.astype(BF), norm_out[n]) + cprob0 * token
        cheads = nt(z_out[...].astype(BF), part(wcls, 2 * shard, shard)) * head_mask(images)
        cheads = cheads.reshape(images, HEADS, D).sum(1)
        for piece in range(3):
            card_out[pl.ds(piece, images, stride=4), :] = cheads[:, 128 * piece : 128 * piece + 128]
        wcls_out[...] = wcls[...]
        gather_up.finish()
        gather_down.finish()


def card_token_kernel(n_dp, n_mp, group, card, vec, aux, *rest):
    far, outs, scratch = rest[:8], rest[8:18], rest[18:]
    dch_all, gout_all, gup_all, gdown_all, cards, slots, dp_sem, mp_sem, load_sem = scratch[:9]
    here = scratch[9:]
    loads = [
        pltpu.make_async_copy(far[i], here[i], load_sem.at[i]) for i in range(len(far))
    ]
    for copy in loads:
        copy.start()
    share_cards(n_dp, n_mp, card, cards, slots, dp_sem, mp_sem)
    for copy in loads:
        copy.wait()
    token_kernel(
        group, cards, vec, *here, aux, *outs, dch_all, gout_all, gup_all, gdown_all
    )


def token_kernel(
    group, cards, vec, wcls, wup_rows, wdown_rows, head, norm, cprob, cprob0, z, aux,
    left_out, right_out, gv_out, local_out, gout_out, gup_out, gdown_out, ghead_out, rows_out,
    stat_out, dch_all, gout_all, gup_all, gdown_all,
):
    hidden = wup_rows.shape[1]
    shard = wcls.shape[1] // 4
    images = cards.shape[0] // 4
    cheads = jnp.concatenate(
        [cards[pl.ds(piece, images, stride=4), :] for piece in range(3)], 1
    ).astype(BF)
    card = cards[pl.ds(3, images, stride=4), :]
    labels = (card[:, 0:1] * 32.0 + card[:, 1:2]).astype(jnp.int32)
    pairs = (card[:, 2:3] * 32.0 + card[:, 3:4]).astype(jnp.int32)
    column = lax.broadcasted_iota(jnp.int32, (images, images), 1)
    row = lax.broadcasted_iota(jnp.int32, (images, images), 0)
    slot = lax.rem(lax.broadcasted_iota(jnp.int32, (images, 1), 0), group).astype(F32)
    okay = (slot >= group - card[:, 4:5]).astype(F32)
    okay_row = colsum(jnp.where(row == column, okay, 0.0))
    wo = part(wcls, 3 * shard, shard)
    wup = part(wup_rows, 0, hidden)
    wdown = part(wdown_rows, 0, hidden)
    count = jnp.sum(okay, keepdims=True)
    raw = nn(cheads, wo) + vec[10:11, :]
    branch = vec[11:12, :] * raw
    middle = vec[17:18, :] + branch
    unit2, inverse2 = normalize(middle)
    normed = (unit2 * vec[12:13, :] + vec[13:14, :]).astype(BF)
    inner = nt(normed, wup)
    active, slope = gelu_parts(inner)
    active = active.astype(BF)
    down = nn(active, wdown) + vec[14:15, :]
    mlp_branch = vec[15:16, :] * down
    token = middle + mlp_branch
    unit3, inverse3 = normalize(token)
    feature = unit3 * vec[18:19, :] + vec[19:20, :]
    feature_low = feature.astype(BF)
    logits = nt(feature_low, head[...])
    top = jnp.max(logits, -1, keepdims=True)
    grown = jnp.exp(logits - top)
    total = jnp.sum(grown, -1, keepdims=True)
    hot = lax.broadcasted_iota(jnp.int32, logits.shape, 1) == labels
    cross = jnp.log(total) + top - jnp.sum(jnp.where(hot, logits, 0.0), -1, keepdims=True)
    share = okay / count
    dlogits = (share * (grown / total - hot.astype(F32))).astype(BF)
    classes = head.shape[0]
    ghead = tn(dlogits, feature_low)
    ghead_out[0:8, :] = jnp.zeros((8, D), F32)
    ghead_out[classes:, :] = jnp.zeros((8, D), F32)
    ghead_out[4 : classes + 4, :] = ghead
    replicated_sq = colsum(ghead * ghead)
    dfeature = nn(dlogits, head[...])

    length = lax.rsqrt(jnp.sum(feature * feature, -1, keepdims=True) + NORM_EPS)
    embed = (feature * length).astype(BF)
    sims = nt(embed, embed) / TEMP
    sims = jnp.where((okay_row > 0) & (row != column), sims, MASKED)
    top = jnp.max(sims, -1, keepdims=True)
    grown = jnp.exp(sims - top)
    total = jnp.sum(grown, -1, keepdims=True)
    hot = column == pairs
    contrast = jnp.log(total) + top - jnp.sum(jnp.where(hot, sims, 0.0), -1, keepdims=True)
    dsims = share * (grown / total - hot.astype(F32))
    high = dsims.astype(BF)
    low = (dsims - high.astype(F32)).astype(BF)
    dembed = (nn(high, embed) + nn(low, embed) + tn(high, embed) + tn(low, embed)) / TEMP
    dfeature += length * dembed - feature * (
        length * length * length * jnp.sum(dembed * feature, -1, keepdims=True)
    )

    dtoken = normalize_back(unit3, inverse3, vec[18:19, :], dfeature)
    rows_out[0:1, :] = jnp.zeros((1, D), F32)
    rows_out[1:2, :] = jnp.zeros((1, D), F32)
    rows_out[7:8, :] = colsum(dtoken * down)
    rows_out[6:7, :] = vec[15:16, :] * colsum(dtoken)
    ddown = (dtoken * vec[15:16, :]).astype(BF)
    gdown = tn(active, ddown)
    own_f = pl.multiple_of(lax.axis_index("mp") * hidden, hidden)
    gdown_all[...] = gdown
    gdown_out[...] = gdown_all[pl.ds(own_f, hidden), :]
    replicated_sq += colsum(gdown * gdown)
    dinner = (nt(ddown, wdown) * slope).astype(BF)
    gup = tn(dinner, normed)
    gup_all[...] = gup
    gup_out[...] = gup_all[pl.ds(own_f, hidden), :]
    replicated_sq += colsum(gup * gup)
    dnormed = nn(dinner, wup)
    rows_out[4:5, :] = colsum(dnormed * unit2)
    rows_out[5:6, :] = colsum(dnormed)
    dmiddle = dtoken + normalize_back(unit2, inverse2, vec[12:13, :], dnormed)
    rows_out[3:4, :] = colsum(dmiddle * raw)
    rows_out[2:3, :] = vec[11:12, :] * colsum(dmiddle)
    rows_out[8:9, :] = colsum(dmiddle)
    rows_out[9:10, :] = colsum(dfeature * unit3)
    rows_out[10:11, :] = colsum(dfeature)
    dbranch = (dmiddle * vec[11:12, :]).astype(BF)
    gout = tn(cheads, dbranch)
    gout_all[...] = gout
    own_h = pl.multiple_of(lax.axis_index("mp") * shard, shard)
    gout_out[...] = gout_all[pl.ds(own_h, shard), :]
    replicated_sq += colsum(gout * gout)
    dch_all[...] = nt(dbranch, wo)
    local = norm.shape[0]
    place = lax.axis_index("dp") * lax.axis_size("mp") + lax.axis_index("mp")
    if local % 8 == 0:
        dch = dch_all[pl.ds(pl.multiple_of(place * local, local), local), :]
    else:
        share_of = 8 // local
        start = pl.multiple_of(lax.div(place, share_of) * 8, 8)
        window = dch_all[pl.ds(start, 8), :]
        pick = lax.rem(place, share_of)
        dch = sum(
            jnp.where(pick == i, window[i * local : (i + 1) * local, :], 0.0)
            for i in range(share_of)
        )

    keys = aux[0:8, :]
    class_row = aux[8:16, :]
    mask = head_mask()
    spread = jnp.concatenate([mask * dch[n : n + 1, :] for n in range(local)], 0).astype(BF)
    dz = nn(spread, part(wcls, 2 * shard, shard))
    dz_low = dz.astype(BF)
    probs = cprob[...]
    prob0 = cprob0[...][:, 0:1]
    class_rows = jnp.concatenate([class_row] * local, 0)
    dprobs = jnp.concatenate(
        [nt(dz_low[n * HEADS : (n + 1) * HEADS, :], norm[n]) for n in range(local)], 0
    )
    dprob0 = jnp.sum(dz * class_rows, -1, keepdims=True)
    inside = jnp.sum(dprobs * probs, -1, keepdims=True) + dprob0 * prob0
    dscores = (probs * (dprobs - inside)).astype(BF)
    dscore0 = prob0 * (dprob0 - inside)
    gv_out[...] = tn(spread, z[...].astype(BF))
    local_out[0:8, :] = jnp.zeros((8, D), F32)
    dkeys = jnp.zeros((HEADS, D), F32)
    from_class = jnp.zeros((1, D), F32)
    for n in range(local):
        rows = slice(n * HEADS, (n + 1) * HEADS)
        dkeys += nn(dscores[rows, :], norm[n]) + dscore0[rows, :] * class_row
        from_class += colsum(prob0[rows, :] * dz[rows, :] + dscore0[rows, :] * keys)
        left_out[n] = jnp.concatenate([probs[rows, :].astype(BF), dscores[rows, :]], 0)
        right_out[n] = jnp.concatenate([dz_low[rows, :], keys.astype(BF)], 0)
    local_out[6:7, :] = from_class
    local_out[8:16, :] = dkeys
    lane = lax.broadcasted_iota(jnp.int32, (1, 128), 1)
    self_sums = colsum(card)
    count_tokens = self_sums[:, 5:6]

    def squares(values):
        return jnp.sum(colsum(values * values * okay), keepdims=True)

    entries = [jnp.sum(okay * cross, keepdims=True), jnp.sum(okay * contrast, keepdims=True)]
    entries += [count, count_tokens]
    entries += [
        jnp.sqrt((self_sums[:, i : i + 1] + self_sums[:, i + 1 : i + 2]) / D / count_tokens)
        for i in (8, 10, 12, 14)
    ]
    entries += [
        jnp.sqrt(squares(item) / D / count) for item in (branch, middle, mlp_branch, token)
    ]
    line = jnp.zeros((1, 128), F32)
    for i, entry in enumerate(entries):
        line = jnp.where(lane == i, entry, line)
    stat_out[0:1, :] = line
    stat_out[1:8, :] = jnp.broadcast_to(
        replicated_sq[:, 0:128] + replicated_sq[:, 128:256] + replicated_sq[:, 256:384], (7, 128)
    )


def feed_back_kernel(
    left, right, gv, local_rows, patch, mid, raw, act, slope, vec, wmlp,
    dmid_out, gfeed_out, rows_out, gmlp_out,
):
    hidden = wmlp.shape[1] // 2
    count = wmlp.shape[0]
    shard = D // count

    @pl.when(pl.program_id(0) == 0)
    def _():
        gmlp_out[...] = jnp.zeros_like(gmlp_out)
        rows_out[...] = local_rows[...]

    unit, inverse = normalize(patch[0])
    dnormed = tn(left[0], right[0])[:P_SIZE, :]
    rows_out[4:5, :] += colsum(dnormed * unit)
    rows_out[5:6, :] += colsum(dnormed)
    incoming = normalize_back(unit, inverse, vec[8:9, :], dnormed)

    unit, inverse = normalize(mid[0])
    normed = (unit * vec[4:5, :] + vec[5:6, :]).astype(BF)
    rows_out[3:4, :] += colsum(incoming * (raw[0].astype(F32) + vec[6:7, :]))
    rows_out[2:3, :] += vec[7:8, :] * colsum(incoming)
    ddown = (incoming * vec[7:8, :]).astype(BF)
    gmlp_out[:, hidden:, :] += tn(act[0], ddown).reshape(count, hidden, D)
    dinner = (nt(ddown, part(wmlp, hidden, hidden)) * slope[0].astype(F32)).astype(BF)
    gmlp_out[:, :hidden, :] += tn(dinner, normed).reshape(count, hidden, D)
    dnormed = nn(dinner, part(wmlp, 0, hidden))
    rows_out[0:1, :] += colsum(dnormed * unit)
    rows_out[1:2, :] += colsum(dnormed)
    dmid_out[0] = incoming + normalize_back(unit, inverse, vec[4:5, :], dnormed)

    @pl.when(pl.program_id(0) == pl.num_programs(0) - 1)
    def _():
        used = 2 * hidden + shard
        gfeed_out[:, : 2 * hidden, :] = gmlp_out[...].astype(BF)
        gfeed_out[:, 2 * hidden : used, :] = gv[...].astype(BF).reshape(count, shard, D)
        if used < gfeed_out.shape[1]:
            gfeed_out[:, used:, :] = jnp.zeros((count, gfeed_out.shape[1] - used, D), BF)


def self_back_kernel(
    n_dp, n_mp, dmid, pixels, embed, q, k, v, prob, post, ho, raw, vec, wattn, t1row, t2row, gfeed,
    gattn_out, gpix_out, gpos_out, rows_out, run_a_out, run_b_out,
    dx_all, dx_rows, stack_q, stack_h, slopes, run_a, run_b, hand_sem_a, hand_sem_b, *sum_buffers,
):
    shard = wattn.shape[1] // 4
    count = wattn.shape[0]
    images = dx_all.shape[0]
    place = Place(n_dp, n_mp)
    rows_a, _ = halves(gfeed.shape[1], n_dp)
    sum_a = ShardSum(place, gfeed, 0, True, *sum_buffers[:SUM_BUFFERS])
    sum_b = ShardSum(place, gfeed, rows_a, False, *sum_buffers[SUM_BUFFERS:])
    hand_a = HandHigh(place, run_a, hand_sem_a)
    hand_b = HandHigh(place, run_b, hand_sem_b)

    def beside(step, *stages):
        @pl.when(pl.program_id(0) == step)
        def _():
            for stage in stages:
                stage()

    @pl.when(pl.program_id(0) == 0)
    def _():
        gattn_out[...] = jnp.zeros_like(gattn_out)
        gpos_out[...] = jnp.zeros_like(gpos_out)
        rows_out[...] = jnp.zeros_like(rows_out)
        stack_q[...] = jnp.zeros_like(stack_q)
        stack_h[...] = jnp.zeros_like(stack_h)
        greet(place.near_partners() + place.dp_partners())()
        sum_a.start()
        sum_b.start()

    beside(1, sum_a.second, sum_b.second)
    beside(images * 3 // 8, sum_a.third, sum_b.third)
    beside(images // 2, sum_a.fourth, sum_b.fourth)

    wq = part(wattn, 0, shard)
    wk = part(wattn, shard, shard)
    wv = part(wattn, 2 * shard, shard)
    wo = part(wattn, 3 * shard, shard)
    incoming = dmid[0]
    rows_out[3:4, :] += colsum(incoming * (raw[0].astype(F32) + vec[2:3, :]))
    rows_out[2:3, :] += vec[3:4, :] * colsum(incoming)
    dbranch = (incoming * vec[3:4, :]).astype(BF)
    gattn_out[:, 3 * shard :, :] += tn(ho[0], dbranch).reshape(count, shard, D)
    dheads = nt(dbranch, wo).astype(BF).astype(F32)

    unit, inverse = normalize(embed[0])
    normed = (unit * vec[0:1, :] + vec[1:2, :]).astype(BF)
    beside(
        images * 3 // 4,
        lambda: hand_a.start(sum_a.finish()),
        lambda: hand_b.start(sum_b.finish()),
    )

    q_wide = q[0].astype(F32)
    stack_heads(stack_q, q_wide, t1row)
    stack_heads(stack_h, dheads, t2row)
    slopes[...] = nt(v[0], stack_h[...])
    dv = nn(prob[0], stack_h[...]).astype(BF)
    for first in range(0, HEADS * PAD, 128):
        at = slice(first, first + 128)
        chance = prob[0, :, at].astype(F32)
        dprob = slopes[:, at]
        slopes[:, at] = chance * (dprob - colsum(dprob * chance))
    dmixed = slopes[...].astype(BF)
    dk = nn(dmixed, stack_q[...]).astype(BF)
    dpre = tn(dmixed, k[0])
    dq = jnp.zeros(q_wide.shape, F32)
    for g in range(HEADS):
        rows = slice(g * PAD, g * PAD + P_SIZE)
        dq += dpre[rows, :] * t1row[g : g + 1, :]
        rows_out[8 + g : 9 + g, :] += colsum(q_wide * dpre[rows, :])
        rows_out[16 + g : 17 + g, :] += colsum(dheads * post[0, rows, :].astype(F32))
    dq = dq.astype(BF)
    gattn_out[:, :shard, :] += tn(dq, normed).reshape(count, shard, D)
    gattn_out[:, shard : 2 * shard, :] += tn(dk, normed).reshape(count, shard, D)
    gattn_out[:, 2 * shard : 3 * shard, :] += tn(dv, normed).reshape(count, shard, D)
    dnormed = nn(dq, wq) + nn(dk, wk) + nn(dv, wv)
    rows_out[0:1, :] += colsum(dnormed * unit)
    rows_out[1:2, :] += colsum(dnormed)
    dx = incoming + normalize_back(unit, inverse, vec[0:1, :], dnormed)
    gpos_out[...] += dx
    dx_all[pl.program_id(0)] = dx

    @pl.when(pl.program_id(0) == pl.num_programs(0) - 1)
    def _():
        for n in range(images):
            dx_rows[:, n, :] = dx_all[n]
        gpix_out[...] = tn(pixels[...], dx_rows[...].reshape(pixels.shape[0], D).astype(BF))
        for item in (hand_a, hand_b):
            item.arrive()
        run_a_out[...] = run_a[...]
        run_b_out[...] = run_b[...]
        for item in (sum_a, sum_b, hand_a, hand_b):
            item.wait_sends()


def per_image(*tail):
    return pl.BlockSpec((1, *tail), lambda n: (n, *(0 for _ in tail)))


def constant(*shape):
    return pl.BlockSpec(shape, lambda n: tuple(0 for _ in shape))


def shaped(*shape, dtype=F32):
    return jax.ShapeDtypeStruct(shape, dtype)


def params():
    return pltpu.CompilerParams(vmem_limit_bytes=VMEM_LIMIT, dimension_semantics=("arbitrary",))


def remote_params(collective_id):
    return pltpu.CompilerParams(
        vmem_limit_bytes=VMEM_LIMIT, dimension_semantics=("arbitrary",),
        collective_id=collective_id, has_side_effects=True,
    )


def run_self_attend(n_dp, n_mp, embed, cols, vec, wattn, t1row, t2row, mlp_rows):
    count = embed.shape[0]
    rows = per_image(P_SIZE, D)
    low = shaped(count, P_SIZE, D, dtype=BF)
    return pl.pallas_call(
        functools.partial(self_attend_kernel, n_dp, n_mp),
        grid=(count,),
        in_specs=[
            rows, constant(*cols.shape), constant(*vec.shape),
            constant(*wattn.shape), constant(HEADS, D), constant(HEADS, D),
            constant(*mlp_rows.shape),
        ],
        out_specs=[
            rows, rows, rows, per_image(P_SIZE, HEADS * PAD), per_image(HEADS * PAD, D),
            rows, rows, rows, per_image(1, 128), ANY,
        ],
        out_shape=[
            low, low, low, shaped(count, P_SIZE, HEADS * PAD, dtype=BF),
            shaped(count, HEADS * PAD, D, dtype=BF), low, low,
            shaped(count, P_SIZE, D), shaped(count, 1, 128),
            shaped(n_mp, *mlp_rows.shape, dtype=BF),
        ],
        scratch_shapes=[pltpu.VMEM((HEADS * PAD, D), BF), pltpu.VMEM((P_SIZE, HEADS * PAD), F32)]
        + gather_scratch(n_mp),
        compiler_params=remote_params(6),
        name="self_attend",
    )(embed, cols, vec, wattn, t1row, t2row, mlp_rows)


def run_feed(n_dp, n_mp, mid, cols, bias_row, base, stat, vec, wmlp, cls_rows, up_rows, down_rows):
    count = mid.shape[0]
    wide = 2 * wmlp.shape[0] * wmlp.shape[1] // 4
    return pl.pallas_call(
        functools.partial(feed_kernel, n_dp, n_mp),
        grid=(count,),
        in_specs=[
            per_image(P_SIZE, D), constant(*cols.shape), constant(1, count * WIDE),
            constant(*base.shape), per_image(1, 128), constant(*vec.shape), constant(*wmlp.shape),
            constant(*cls_rows.shape), constant(*up_rows.shape), constant(*down_rows.shape),
        ],
        out_specs=[
            per_image(P_SIZE, D), per_image(P_SIZE, wide), per_image(P_SIZE, wide),
            per_image(P_SIZE, D), constant(count, WIDE, D), constant(count * HEADS, WIDE),
            constant(count * HEADS, 128), constant(count * HEADS, D), constant(4 * count, 128),
            constant(24, D), constant(n_mp, *cls_rows.shape), ANY, ANY,
        ],
        out_shape=[
            shaped(count, P_SIZE, D), shaped(count, P_SIZE, wide, dtype=BF),
            shaped(count, P_SIZE, wide, dtype=BF), shaped(count, P_SIZE, D, dtype=BF),
            shaped(count, WIDE, D, dtype=BF), shaped(count * HEADS, WIDE),
            shaped(count * HEADS, 128), shaped(count * HEADS, D), shaped(4 * count, 128),
            shaped(24, D), shaped(n_mp, *cls_rows.shape, dtype=BF),
            shaped(n_mp, *up_rows.shape, dtype=BF), shaped(n_mp, *down_rows.shape, dtype=BF),
        ],
        scratch_shapes=[pltpu.VMEM((n_mp, *cls_rows.shape), BF)] + spread_scratch(n_dp, n_mp) * 3,
        compiler_params=remote_params(7),
        name="feed",
    )(mid, cols, bias_row, base, stat, vec, wmlp, cls_rows, up_rows, down_rows)


def run_token(n_dp, n_mp, group, card, vec, aux, wcls, wup, wdown, head, norm, cprob, cprob0, z):
    rows = card.shape[0]
    local = norm.shape[0]
    images = n_dp * n_mp * local
    hidden = wup.shape[1]
    shard = wcls.shape[1] // 4
    wide = wup.shape[0] * hidden
    dma = pltpu.SemaphoreType.DMA
    far = (wcls, wup, wdown, head, norm, cprob, cprob0, z)
    return pl.pallas_call(
        functools.partial(card_token_kernel, n_dp, n_mp, group),
        in_specs=[WHOLE] * 3 + [ANY] * 8,
        out_specs=[WHOLE] * 10,
        out_shape=[
            shaped(local, 2 * HEADS, WIDE, dtype=BF), shaped(local, 2 * HEADS, D, dtype=BF),
            shaped(D, D), shaped(16, D), shaped(shard, D), shaped(hidden, D), shaped(hidden, D),
            shaped(head.shape[0] + 8, D), shaped(16, D), shaped(8, 128),
        ],
        scratch_shapes=[
            pltpu.VMEM((images, D), F32), pltpu.VMEM((D, D), F32), pltpu.VMEM((wide, D), F32),
            pltpu.VMEM((wide, D), F32), pltpu.VMEM((n_dp * n_mp * rows, 128), F32),
            pltpu.VMEM((n_dp * n_mp * rows, 128), BF), dma((2, n_dp)), dma((2, n_mp)), dma((8,)),
        ]
        + [pltpu.VMEM(item.shape, item.dtype) for item in far],
        compiler_params=pltpu.CompilerParams(
            vmem_limit_bytes=VMEM_LIMIT, collective_id=1, has_side_effects=True
        ),
        name="token_net",
    )(card, vec, aux, *far)


def run_feed_back(n_dp, left, right, gv, local_rows, patch, mid, raw, act, slope, vec, wmlp):
    count = mid.shape[0]
    wide = act.shape[2]
    feed = (wmlp.shape[0], pad_rows(wmlp.shape[1] + D // wmlp.shape[0], n_dp), D)
    return pl.pallas_call(
        feed_back_kernel,
        grid=(count,),
        in_specs=[
            per_image(2 * HEADS, WIDE), per_image(2 * HEADS, D), constant(D, D), constant(16, D),
            per_image(P_SIZE, D), per_image(P_SIZE, D), per_image(P_SIZE, D),
            per_image(P_SIZE, wide), per_image(P_SIZE, wide), constant(*vec.shape),
            constant(*wmlp.shape),
        ],
        out_specs=[per_image(P_SIZE, D), constant(*feed), constant(16, D)],
        out_shape=[shaped(count, P_SIZE, D), shaped(*feed, dtype=BF), shaped(16, D)],
        scratch_shapes=[pltpu.VMEM(wmlp.shape, F32)],
        compiler_params=params(),
        name="feed_back",
    )(left, right, gv, local_rows, patch, mid, raw, act, slope, vec, wmlp)


def run_self_back(
    n_dp, n_mp, dmid, pixels, embed, q, k, v, prob, post, ho, raw, vec, wattn, t1row, t2row, gfeed
):
    count = dmid.shape[0]
    rows_a, rows_b = halves(gfeed.shape[1], n_dp)
    n_lo = 2 if n_dp < 16 else 4
    return pl.pallas_call(
        functools.partial(self_back_kernel, n_dp, n_mp),
        grid=(count,),
        in_specs=[
            per_image(P_SIZE, D), constant(*pixels.shape), per_image(P_SIZE, D),
            per_image(P_SIZE, D), per_image(P_SIZE, D), per_image(P_SIZE, D),
            per_image(P_SIZE, HEADS * PAD), per_image(HEADS * PAD, D), per_image(P_SIZE, D),
            per_image(P_SIZE, D), constant(*vec.shape), constant(*wattn.shape), constant(HEADS, D),
            constant(HEADS, D), constant(*gfeed.shape),
        ],
        out_specs=[
            constant(*wattn.shape), constant(PIX, D), constant(P_SIZE, D), constant(24, D),
            constant(rows_a // n_lo, D), constant(rows_b // n_lo, D),
        ],
        out_shape=[
            shaped(*wattn.shape), shaped(PIX, D), shaped(P_SIZE, D), shaped(24, D),
            shaped(rows_a // n_lo, D, dtype=BF), shaped(rows_b // n_lo, D, dtype=BF),
        ],
        scratch_shapes=[
            pltpu.VMEM((count, P_SIZE, D), F32), pltpu.VMEM((P_SIZE, count, D), F32),
            pltpu.VMEM((HEADS * PAD, D), BF), pltpu.VMEM((HEADS * PAD, D), BF),
            pltpu.VMEM((P_SIZE, HEADS * PAD), F32),
            pltpu.VMEM((rows_a // n_lo, D), BF), pltpu.VMEM((rows_b // n_lo, D), BF),
            pltpu.SemaphoreType.DMA((2, n_dp // n_lo)), pltpu.SemaphoreType.DMA((2, n_dp // n_lo)),
        ]
        + sum_scratch(n_dp, n_mp, rows_a, True)
        + sum_scratch(n_dp, n_mp, rows_b, False),
        compiler_params=pltpu.CompilerParams(
            vmem_limit_bytes=VMEM_LIMIT, dimension_semantics=("arbitrary",), collective_id=5,
            has_side_effects=True,
        ),
        name="self_back",
    )(dmid, pixels, embed, q, k, v, prob, post, ho, raw, vec, wattn, t1row, t2row, gfeed)


def share_cards(n_dp, n_mp, card, out, slots, dp_sem, mp_sem):
    dp = lax.axis_index("dp")
    mp = lax.axis_index("mp")
    rows = card.shape[0]
    barrier = pltpu.get_barrier_semaphore()
    others_dp = [(lax.rem(dp + step, n_dp), mp) for step in range(1, n_dp)]
    others_mp = [(dp, lax.rem(mp + step, n_mp)) for step in range(1, n_mp)]
    for partner in others_dp + others_mp:
        pl.semaphore_signal(barrier, inc=1, device_id=partner, device_id_type=MESH)
    own = tile_rows(slots, (mp * n_dp + dp) * rows, rows)
    slots[pl.ds(pl.multiple_of((mp * n_dp + dp) * rows, 16), rows), :] = card[...].astype(BF)
    pl.semaphore_wait(barrier, n_dp + n_mp - 2)
    sends = [
        remote(own, own, dp_sem.at[0, step], dp_sem.at[1, step], others_dp[step - 1])
        for step in range(1, n_dp)
    ]
    for copy in sends:
        copy.start()
    for step in range(1, n_dp):
        source = lax.rem(dp + n_dp - step, n_dp)
        theirs = tile_rows(slots, (mp * n_dp + source) * rows, rows)
        remote(own, theirs, dp_sem.at[0, step], dp_sem.at[1, step], (source, mp)).wait_recv()
    slab = tile_rows(slots, mp * n_dp * rows, n_dp * rows)
    for step in range(1, n_mp):
        sends.append(
            remote(slab, slab, mp_sem.at[0, step], mp_sem.at[1, step], others_mp[step - 1])
        )
        sends[-1].start()
    for step in range(1, n_mp):
        source = lax.rem(mp + n_mp - step, n_mp)
        theirs = tile_rows(slots, source * n_dp * rows, n_dp * rows)
        remote(slab, theirs, mp_sem.at[0, step], mp_sem.at[1, step], (dp, source)).wait_recv()
    for i in range(n_dp):
        for j in range(n_mp):
            to, source = (i * n_mp + j) * rows, (j * n_dp + i) * rows
            out[to : to + rows, :] = slots[source : source + rows, :].astype(F32)
    for copy in sends:
        copy.wait_send()


def start_kernel(
    n_dp, n_mp, group, attn_in, attn_out, mlp_in, mlp_out, pixels, tables, vec, mix, mask,
    counts, labels, pairs,
    out, mlp_rows, cls_rows, up_rows, down_rows, embed_out, head_out, t1_out, t2_out, cols_out, bias_out, base_out,
    head_rows, wide_up, wide_down, shard, wide_in, wide_out, patch_rows, pos_rows, by_patch, near_send, near_recv, far_send, far_recv, load_sem,
):
    dp = lax.axis_index("dp")
    mp = lax.axis_index("mp")
    n_y = n_mp // 2
    y = lax.div(mp, 2)
    core = lax.rem(mp, 2)
    sibling = (dp, y * 2 + 1 - core)
    load_patch = pltpu.make_async_copy(tables.at[pl.ds(0, PIX)], patch_rows, load_sem.at[0])
    load_pos = pltpu.make_async_copy(tables.at[pl.ds(PIX, 200)], pos_rows, load_sem.at[1])
    load_in = pltpu.make_async_copy(attn_in, wide_in, load_sem.at[2])
    load_out = pltpu.make_async_copy(attn_out, wide_out, load_sem.at[3])
    load_up = pltpu.make_async_copy(mlp_in, wide_up, load_sem.at[5])
    load_down = pltpu.make_async_copy(mlp_out, wide_down, load_sem.at[6])
    load_in.start()
    load_out.start()
    load_patch.start()
    load_pos.start()
    classes = head_out.shape[0]
    load_head = pltpu.make_async_copy(
        tables.at[pl.ds(PIX + P_SIZE - 4, classes + 4)], head_rows, load_sem.at[4]
    )
    load_up.start()
    load_down.start()
    load_head.start()
    barrier = pltpu.get_barrier_semaphore()
    pl.semaphore_signal(barrier, inc=1, device_id=sibling, device_id_type=MESH)
    for step in range(1, n_y):
        pl.semaphore_signal(
            barrier, inc=1, device_id=(dp, lax.rem(y + step, n_y) * 2 + core), device_id_type=MESH
        )
    third = attn_in.shape[1]
    load_in.wait()
    load_out.wait()
    shard[:third, :] = wide_in[0].astype(BF)
    shard[third:, :] = wide_out[0].astype(BF)
    pl.semaphore_wait(barrier, n_y)
    far = [
        remote(
            shard, out.at[mp], far_send.at[step], far_recv.at[step],
            (dp, lax.rem(y + step, n_y) * 2 + core),
        )
        for step in range(1, n_y)
    ]
    for copy in far:
        copy.start()
    near = [remote(shard, out.at[mp], near_send.at[0], near_recv.at[0], sibling)]
    near[0].start()
    out[pl.ds(mp, 1)] = shard[...][None]

    cls_rows[:third, :] = wide_in[1].astype(BF)
    cls_rows[third:, :] = wide_out[1].astype(BF)
    hidden = mlp_rows.shape[0] // 2
    load_up.wait()
    load_down.wait()
    mlp_rows[:hidden, :] = wide_up[0].T.astype(BF)
    mlp_rows[hidden:, :] = wide_down[0].astype(BF)
    up_rows[...] = wide_up[1].T.astype(BF)
    down_rows[...] = wide_down[1].astype(BF)

    images = mask.shape[0]
    lane = lax.broadcasted_iota(jnp.int32, (1, 128), 1)
    keep = (mask[...] > 0).astype(F32)
    bias = (1.0 - keep) * MASKED
    count = counts[0]
    okays = []
    bias_out[...] = jnp.full(bias_out.shape, MASKED, F32)
    for n in range(images):
        okays.append((jnp.full((1, 1), mp * images + n, jnp.int32) >= group - count).astype(F32))
        bias_out[:, n * WIDE : n * WIDE + P_SIZE] = bias[n : n + 1, :]
        tokens = jnp.sum(keep[n : n + 1, :], 1, keepdims=True) * okays[n]
        entries = (
            lax.div(labels[n], 32), lax.rem(labels[n], 32), lax.div(pairs[n], 32),
            lax.rem(pairs[n], 32), count,
        )
        line = jnp.where(lane == len(entries), tokens, 0.0)
        for place, entry in enumerate(entries):
            line = jnp.where(lane == place, entry.astype(F32), line)
        base_out[n : n + 1, :] = line
    cols_out[...] = jnp.concatenate([bias, keep * jnp.concatenate(okays, 0)], 0).T
    heads = head_mask()
    exact = functools.partial(
        lax.dot_general, preferred_element_type=F32, precision=lax.Precision.HIGHEST
    )
    t1_out[...] = exact(mix[0], heads, (((1,), (0,)), ((), ()))) * SCALE
    t2_out[...] = exact(mix[1], heads, (((0,), (0,)), ((), ())))

    load_patch.wait()
    wp = patch_rows[...].astype(BF)
    local = embed_out.shape[0]
    half = P_SIZE // 2
    for place in range(2):
        rows = slice(place * half * local, (place + 1) * half * local)
        by_patch[place * half : (place + 1) * half] = nn(pixels[rows, :], wp).reshape(half, local, D)

    for step in range(1, n_y):
        source = lax.rem(y + n_y - step, n_y) * 2
        slot = source + core
        remote(
            shard, out.at[slot], far_send.at[step], far_recv.at[step], (dp, slot)
        ).wait_recv()
        copy = remote(
            out.at[slot], out.at[slot], near_send.at[step], near_recv.at[step], sibling
        )
        copy.start()
        near.append(copy)
    load_pos.wait()
    offset = pos_rows[:P_SIZE, :] + vec[16:17, :]
    for n in range(local):
        embed_out[n] = by_patch[:, n, :] + offset
    load_head.wait()
    head_out[...] = head_rows[4:, :].astype(BF)
    for copy in far:
        copy.wait_send()
    for step in range(n_y):
        slot = lax.rem(y + n_y - step, n_y) * 2 + 1 - core
        near[step].wait_send()
        remote(
            out.at[slot], out.at[slot], near_send.at[step], near_recv.at[step], sibling
        ).wait_recv()


def run_start(
    n_dp, n_mp, group, attn_in, attn_out, mlp_in, mlp_out, pixels, tables, vec, mix, mask, counts,
    labels, pairs,
):
    local = labels.shape[0]
    classes = tables.shape[0] - PIX - P_SIZE
    scalars = pl.BlockSpec(memory_space=pltpu.SMEM)
    n_y = n_mp // 2
    rows = attn_in.shape[1] + attn_out.shape[1]
    hidden = mlp_in.shape[2]
    dma = pltpu.SemaphoreType.DMA
    return pl.pallas_call(
        functools.partial(start_kernel, n_dp, n_mp, group),
        in_specs=[ANY] * 4 + [WHOLE, ANY, WHOLE, WHOLE, WHOLE, scalars, scalars, scalars],
        out_specs=[WHOLE] * 12,
        out_shape=[
            shaped(n_mp, rows, D, dtype=BF), shaped(2 * hidden, D, dtype=BF),
            shaped(rows, D, dtype=BF), shaped(hidden, D, dtype=BF), shaped(hidden, D, dtype=BF),
            shaped(local, P_SIZE, D),
            shaped(classes, D, dtype=BF), shaped(HEADS, D), shaped(HEADS, D),
            shaped(P_SIZE, 2 * local), shaped(1, local * WIDE), shaped(local, 128),
        ],
        scratch_shapes=[
            pltpu.VMEM((classes + 4, D), F32), pltpu.VMEM(mlp_in.shape, F32),
            pltpu.VMEM(mlp_out.shape, F32),
            pltpu.VMEM((rows, D), BF), pltpu.VMEM(attn_in.shape, F32),
            pltpu.VMEM(attn_out.shape, F32), pltpu.VMEM((PIX, D), F32),
            pltpu.VMEM((200, D), F32),
            pltpu.VMEM((P_SIZE, local, D), F32),
            dma((n_y,)), dma((n_y,)), dma((n_y,)), dma((n_y,)), dma((7,)),
        ],
        compiler_params=pltpu.CompilerParams(
            vmem_limit_bytes=VMEM_LIMIT, collective_id=2, has_side_effects=True
        ),
        name="start",
    )(
        attn_in, attn_out, mlp_in, mlp_out, pixels, tables, vec, mix, mask, counts, labels, pairs
    )


def reduce_kernel(
    n_dp, n_mp, gattn, run_a, run_b, gpix, gpos, rows2, rows3,
    block_out, shared_out, square_out,
    blocks, commons, squares, attn_run, sem_a, sem_b, high_sem, low_sem, square_sem, *sum_buffers,
):
    p = Place(n_dp, n_mp)
    attn = ShardSum(p, blocks, 0, True, *sum_buffers[:SUM_BUFFERS])
    table = TableSum(p, commons, shared_out, *sum_buffers[SUM_BUFFERS:])
    rows_a = blocks.shape[1]
    wide = commons.shape[1]
    greeted = greet(p.near_partners() + p.dp_partners())

    used = gattn.shape[1]
    blocks[:, :used, :] = gattn[...].astype(BF)
    if used < rows_a:
        blocks[:, used:, :] = jnp.zeros((n_mp, rows_a - used, D), BF)
    commons[:3] = gpix[...].astype(BF).reshape(3, wide, D)
    commons[3] = jnp.concatenate(
        [
            gpos[...], jnp.zeros((12, D), F32), rows2[...], rows3[...], jnp.zeros((8, D), F32),
        ],
        0,
    ).astype(BF)
    if n_mp > 4:
        commons[4:] = jnp.zeros((n_mp - 4, wide, D), BF)

    rows_feed = p.n_lo * run_a.shape[0]
    hand_a = HandLow(p, block_out, rows_a, rows_feed, sem_a)
    hand_b = HandLow(p, block_out, rows_a + rows_feed, p.n_lo * run_b.shape[0], sem_b)
    hand_high = HandHigh(p, attn_run, high_sem)
    hand_low = HandLow(p, block_out, 0, rows_a, low_sem)

    greeted()
    attn.start()
    table.start()
    attn.second()
    table.near_to_low()
    hand_a.start(run_a[...])
    hand_b.start(run_b[...])
    table.low_to_high()
    attn.third()
    table.high_to_far()
    attn.fourth()
    table.turn()
    table.far_to_high()
    hand_high.start(attn.finish())
    table.high_to_low()
    hand_high.arrive()
    hand_low.start(attn_run[...])
    table.low_to_near()
    sends = []

    for item in (hand_a, hand_b, hand_low):
        item.arrive()
    sums = block_out[...].astype(F32)
    sums = colsum(sums * sums)
    squares[pl.ds(p.mp, 1)] = jnp.broadcast_to(
        sums[:, 0:128] + sums[:, 128:256] + sums[:, 256:384], (8, 128)
    )[None]

    for step in range(1, p.n_y):
        sends.append(
            remote(
                squares.at[p.mp], squares.at[p.mp], square_sem.at[0, step],
                square_sem.at[1, step], (p.dp, p.along_y(step) * 2 + p.core),
            )
        )
        sends[-1].start()
    for step in range(1, p.n_y):
        source = p.along_y(p.n_y - step) * 2 + p.core
        remote(
            squares.at[p.mp], squares.at[source], square_sem.at[0, step], square_sem.at[1, step],
            (p.dp, source),
        ).wait_recv()
    mine = squares[pl.ds(p.core, 1)]
    for y in range(1, p.n_y):
        mine += squares[pl.ds(2 * y + p.core, 1)]
    squares[pl.ds(n_mp + p.core, 1)] = mine
    sends.append(
        remote(
            squares.at[n_mp + p.core], squares.at[n_mp + p.core], square_sem.at[0, 0],
            square_sem.at[1, 0], p.sibling,
        )
    )
    sends[-1].start()
    table.finish()
    remote(
        squares.at[n_mp + p.core], squares.at[n_mp + 1 - p.core], square_sem.at[0, 0],
        square_sem.at[1, 0], p.sibling,
    ).wait_recv()
    square_out[...] = squares[n_mp] + squares[n_mp + 1]
    for copy in sends:
        copy.wait_send()
    for item in (attn, hand_a, hand_b, hand_high, hand_low):
        item.wait_sends()


def run_reduce(n_dp, n_mp, gattn, run_a, run_b, gpix, gpos, rows2, rows3):
    n = n_dp * n_mp
    rows_a = pad_rows(gattn.shape[1], n_dp)
    chunk_s = -(-(PIX + 256) // (16 * n)) * 16
    wide = chunk_s * n_dp
    assert wide == 256
    n_lo = 2 if n_dp < 16 else 4
    dma = pltpu.SemaphoreType.DMA
    return pl.pallas_call(
        functools.partial(reduce_kernel, n_dp, n_mp),
        in_specs=[WHOLE] * 7,
        out_specs=[WHOLE] * 3,
        out_shape=[
            shaped(rows_a + n_lo * (run_a.shape[0] + run_b.shape[0]), D, dtype=BF),
            shaped(n_mp, wide, D, dtype=BF), shaped(8, 128),
        ],
        scratch_shapes=[
            pltpu.VMEM((n_mp, rows_a, D), BF), pltpu.VMEM((n_mp, wide, D), BF),
            pltpu.VMEM((n_mp + 2, 8, 128), F32),
            pltpu.VMEM((rows_a // n_lo, D), BF),
            dma((2, n_lo)), dma((2, n_lo)), dma((2, n_dp // n_lo)), dma((2, n_lo)), dma((2, n_mp)),
        ]
        + sum_scratch(n_dp, n_mp, rows_a, True)
        + table_scratch(n_dp, n_mp, wide),
        compiler_params=pltpu.CompilerParams(
            vmem_limit_bytes=VMEM_LIMIT, collective_id=3, has_side_effects=True
        ),
        name="reduce",
    )(gattn, run_a, run_b, gpix, gpos, rows2, rows3)


def root(values):
    return values * lax.rsqrt(values)


def adam_parts(gradient, mean, square, factor):
    clipped = gradient * factor
    mean_new = BETA_ONE * mean + (1.0 - BETA_ONE) * clipped
    square_new = BETA_TWO * square + (1.0 - BETA_TWO) * clipped * clipped
    direction = (
        mean_new
        * (1.0 / (1.0 - BETA_ONE**STEP))
        / (root(square_new * (1.0 / (1.0 - BETA_TWO**STEP))) + ADAM_EPS)
    )
    return (mean_new, square_new, direction)


def fold(values):
    squares = (values * values).reshape(values.shape[0] // 8, 8, values.shape[1]).sum(0)
    width = values.shape[1]
    if width % 128:
        return jnp.broadcast_to(jnp.sum(squares, 1, keepdims=True), (8, 128)) * (1.0 / 128)
    return sum(squares[:, i : i + 128] for i in range(0, width, 128))


def total(values):
    return jnp.sum(jnp.sum(values, 0, keepdims=True), 1, keepdims=True)


def moment_sweep(factor, grad, w, m, s, u, rows):
    chunk = 32 if rows % 32 == 0 else 16

    def step(i, kept):
        at = pl.ds(pl.multiple_of(i * chunk, chunk), chunk)
        weight = w[at, :]
        mean, second, direction = adam_parts(grad(i, chunk), m[at, :], s[at, :], factor)
        m[at, :] = mean
        s[at, :] = second
        update = direction + DECAY * weight
        u[at, :] = update
        return (kept[0] + fold(weight), kept[1] + fold(update))

    zero = jnp.zeros((8, 128), F32)
    return lax.fori_loop(0, rows // chunk, step, (zero, zero))


def rows_from(ref, first):
    def read(i, chunk):
        at = pl.ds(pl.multiple_of(first + i * chunk, 16), chunk)
        return ref[at, :].astype(F32)

    return read


def moment_kernel(
    n_dp, block, shared, block_sq, gout1, gup1, gdown1, rows1, stat, aux, wcls,
    vec, vec_mean, vec_square, mix, mix_mean, mix_square, *rest,
):
    state = rest[:12]
    outs = rest[12:24]
    (
        vec_out, vec_mean_out, vec_square_out, mix_out, mix_mean_out, mix_square_out,
        misc_out, sums_out,
    ) = rest[24:32]
    held = rest[32:44]
    updates = rest[44:48]
    grad_q, grad_k, grad_flip, load_sem, save_sem = rest[48:]
    loads = [pltpu.make_async_copy(state[i], held[i], load_sem.at[i]) for i in range(12)]
    for copy in loads:
        copy.start()
    mp = lax.axis_index("mp")
    hs = state[3].shape[1]
    fs = state[9].shape[1]
    feed = pad_rows(4 * hs, n_dp)

    rows2 = shared[PIX + 208 : PIX + 224, :].astype(F32)
    rows3 = shared[PIX + 224 : PIX + 256, :].astype(F32)
    token = aux[8:9, :]
    wq = part(wcls, 0, hs)
    wk = part(wcls, hs, hs).astype(F32)
    query = nt(wq, aux[8:16, :].astype(BF))[:, 0:1].astype(BF).astype(F32)
    dkeys = jnp.concatenate(
        [jnp.broadcast_to(rows2[8 + h : 9 + h, :], (HEAD, D)) for h in range(HEADS)], 0
    )
    dquery = SCALE * jnp.sum(wk * dkeys, 1, keepdims=True)
    gq = dquery * token
    gk = (SCALE * query) * dkeys
    grad_q[...] = gq
    grad_k[...] = gk
    dtoken = rows2[6:7, :] + colsum(dquery * wq.astype(F32))
    unit, inverse = normalize(jnp.broadcast_to(vec[17:18, :], (8, D)))
    dcls = normalize_back(unit, inverse, vec[8:9, :], jnp.broadcast_to(dtoken, (8, D)))[0:1, :]
    dgain = rows2[4:5, :] + dtoken * unit[0:1, :]
    last = rows1[...]
    positions = shared[PIX : PIX + 208, :].astype(F32)
    grad_vec = jnp.concatenate(
        [
            rows3[0:4, :], rows2[0:4, :], dgain, rows2[5:6, :] + dtoken, last[2:8, :],
            colsum(positions), last[8:9, :] + dcls, last[9:11, :],
        ],
        0,
    )
    mask = head_mask()
    exact = functools.partial(
        lax.dot_general, dimension_numbers=(((1,), (1,)), ((), ())),
        preferred_element_type=F32, precision=lax.Precision.HIGHEST,
    )
    grad_mix = (exact(rows3[8:16, :], mask) * SCALE, exact(mask, rows3[16:24, :]))

    square = total(block_sq[0:1, :]) + total(stat[1:2, :]) + total(colsum(gq * gq + gk * gk))
    square += total(grad_vec * grad_vec)
    square += total(grad_mix[0] * grad_mix[0]) + total(grad_mix[1] * grad_mix[1])

    def square_rows(i, kept):
        rows = shared[pl.ds(pl.multiple_of(i * 16, 16), 16), :].astype(F32)
        return kept + fold(rows)

    square += total(lax.fori_loop(0, (PIX + 208) // 16, square_rows, jnp.zeros((8, 128), F32)))
    norm = jnp.sqrt(square)
    factor = CLIP / jnp.maximum(norm, CLIP)

    mean, second, direction = adam_parts(grad_vec, vec_mean[...], vec_square[...], factor)
    vec_mean_out[...] = mean
    vec_square_out[...] = second
    vec_out[...] = vec[...] - RATE_VECTOR * direction
    misc = []
    weight_sums = []
    for b in range(2):
        mean, second, direction = adam_parts(grad_mix[b], mix_mean[b], mix_square[b], factor)
        mix_mean_out[b] = mean
        mix_square_out[b] = second
        update = direction + DECAY * mix[b]
        weight_sq = total(mix[b] * mix[b])
        update_sq = total(update * update)
        mix_out[b] = mix[b] - RATE * jnp.sqrt(weight_sq / (update_sq + 1e-12)) * update
        weight_sums.append(weight_sq)
        misc.append(update_sq)

    def sweep(grad, w, m, s, u, rows):
        return moment_sweep(factor, grad, w, m, s, u, rows)

    saves = []

    def save(i, source):
        saves.append(pltpu.make_async_copy(source, outs[i], save_sem.at[i]))
        saves[-1].start()

    sums = []
    own_h = pl.multiple_of(mp * hs, hs)
    for kind in range(4):
        for copy in loads[3 * kind : 3 * kind + 3]:
            copy.wait()
        w, m, s = held[3 * kind : 3 * kind + 3]
        u = updates[kind]
        for b in range(2):
            views = (w.at[b], m.at[b], s.at[b], u.at[b])
            if kind == 0 and b == 0:
                sums.append(sweep(rows_from(block, 0), *views, 3 * hs))
            elif kind == 0:
                pieces = []
                for third, source in enumerate(
                    (
                        rows_from(grad_q, own_h),
                        rows_from(grad_k, own_h),
                        rows_from(block, feed + 2 * fs),
                    )
                ):
                    pieces.append(
                        sweep(
                            source, *(view.at[pl.ds(third * hs, hs)] for view in views), hs
                        )
                    )
                sums.append(
                    tuple(pieces[0][i] + pieces[1][i] + pieces[2][i] for i in range(2))
                )
            elif kind == 1:
                source = rows_from(gout1, 0) if b else rows_from(block, 3 * hs)
                sums.append(sweep(source, *views, hs))
            elif kind == 2:
                if b:
                    grad_flip[...] = gup1[...].T
                else:
                    grad_flip[...] = block[feed : feed + fs, :].astype(F32).T
                sums.append(sweep(rows_from(grad_flip, 0), *views, D))
            else:
                source = rows_from(gdown1, 0) if b else rows_from(block, feed + fs)
                sums.append(sweep(source, *views, fs))
        save(3 * kind, u)
        save(3 * kind + 1, m)
        save(3 * kind + 2, s)
    for place, pair in enumerate(sums):
        sums_out[place : place + 1, :] = colsum(pair[1])
        sums_out[8 + place : 9 + place, :] = colsum(pair[0])

    lane = lax.broadcasted_iota(jnp.int32, (1, 128), 1)
    misc_out[0:1, :] = jnp.broadcast_to(norm, (1, 128))
    weight_line = jnp.zeros((1, 128), F32)
    update_line = jnp.zeros((1, 128), F32)
    for b in range(2):
        weight_line = jnp.where(lane == 11 + b, weight_sums[b], weight_line)
        update_line = jnp.where(lane == 11 + b, misc[b], update_line)
    misc_out[1:2, :] = weight_line
    misc_out[2:3, :] = update_line
    misc_out[3:8, :] = jnp.zeros((5, 128), F32)
    for copy in saves:
        copy.wait()


def table_kernel(misc, shared, ghead, *rest):
    state, outs, misc_out = rest[:3], rest[3:6], rest[6]
    w, m, s, table_update, load_sem, save_sem = rest[7:]
    rows_all = w.shape[0]
    edge = PIX + P_SIZE - 4
    body = (rows_all - edge - 16) // 64 * 32
    middle = edge + 16 + body
    cuts = (0, PIX // 2, PIX, middle, rows_all)
    slabs = [pl.ds(low, high - low) for low, high in zip(cuts, cuts[1:])]
    loads = [
        [
            pltpu.make_async_copy(state[i].at[at], (w, m, s)[i].at[at], load_sem.at[i, place])
            for i in range(3)
        ]
        for place, at in enumerate(slabs)
    ]
    for group in loads:
        for copy in group:
            copy.start()
    factor = CLIP / jnp.maximum(misc[0:1, 0:1], CLIP)
    saves = []

    def arrive(place):
        for copy in loads[place]:
            copy.wait()

    def save(i, place):
        at = slabs[place]
        saves.append(
            pltpu.make_async_copy((w, m, s)[i].at[at], outs[i].at[at], save_sem.at[i, place])
        )
        saves[-1].start()

    def slab(first, count, grad):
        at = slice(first, first + count)
        weight = w[at, :]
        mean, second, direction = adam_parts(grad, m[at, :], s[at, :], factor)
        m[at, :] = mean
        s[at, :] = second
        update = direction + DECAY * weight
        table_update[at, :] = update
        return weight, update

    def run(first, count, source, offset):
        def at(ref, start):
            return ref.at[pl.ds(start, count)]

        return moment_sweep(
            factor, rows_from(source, offset), at(w, first), at(m, first), at(s, first),
            at(table_update, first), count,
        )

    def renew(first, count, rate):
        def step(i, _):
            at = pl.ds(pl.multiple_of(first + i * 32, 16), 32)
            w[at, :] = w[at, :] - rate * table_update[at, :]
            return 0

        lax.fori_loop(0, count // 32, step, 0)

    def rate_of(weight_sq, update_sq):
        return RATE * jnp.sqrt(weight_sq / (update_sq + 1e-12))

    def masked(values, mask):
        return total(jnp.where(mask, values * values, 0.0))

    arrive(0)
    first_half = run(0, PIX // 2, shared, 0)
    save(1, 0)
    save(2, 0)
    arrive(1)
    second_half = run(PIX // 2, PIX // 2, shared, PIX // 2)
    save(1, 1)
    save(2, 1)
    sq_w = [total(first_half[0] + second_half[0])]
    sq_u = [total(first_half[1] + second_half[1])]
    rates = [rate_of(sq_w[0], sq_u[0])]
    renew(0, PIX, rates[0])
    save(0, 0)
    save(0, 1)
    arrive(2)
    place_rows = run(PIX, P_SIZE - 4, shared, PIX)
    tile = lax.broadcasted_iota(jnp.int32, (16, 1), 0) < 4
    weight, update = slab(edge, 16, shared[edge : edge + 16, :].astype(F32) + ghead[0:16, :])
    heads = run(edge + 16, body, ghead, 16)
    save(1, 2)
    save(2, 2)
    arrive(3)
    rest_rows = (rows_all - middle) // 32 * 32
    more_heads = run(middle, rest_rows, ghead, 16 + body)
    left = middle + rest_rows
    tail_weight, tail_update = slab(
        left, rows_all - left, ghead[16 + left - edge - 16 : 16 + rows_all - edge - 16, :]
    )
    save(1, 3)
    save(2, 3)
    sq_w += [
        total(place_rows[0]) + masked(weight, tile),
        total(heads[0] + more_heads[0]) + masked(weight, ~tile) + total(tail_weight * tail_weight),
    ]
    sq_u += [
        total(place_rows[1]) + masked(update, tile),
        total(heads[1] + more_heads[1]) + masked(update, ~tile) + total(tail_update * tail_update),
    ]
    rates += [rate_of(sq_w[i], sq_u[i]) for i in (1, 2)]
    renew(PIX, P_SIZE - 4, rates[1])
    w[edge : edge + 16, :] = weight - jnp.where(tile, rates[1], rates[2]) * update
    renew(edge + 16, body, rates[2])
    save(0, 2)
    renew(middle, rest_rows, rates[2])
    w[left:rows_all, :] = tail_weight - rates[2] * tail_update
    save(0, 3)

    lane = lax.broadcasted_iota(jnp.int32, (1, 128), 1)
    weight_line = misc[1:2, :]
    update_line = misc[2:3, :]
    for place in range(3):
        weight_line = jnp.where(lane == 8 + place, sq_w[place], weight_line)
        update_line = jnp.where(lane == 8 + place, sq_u[place], update_line)
    misc_out[...] = misc[...]
    misc_out[1:2, :] = weight_line
    misc_out[2:3, :] = update_line
    for copy in saves:
        copy.wait()


def run_moments(n_dp, grads, smalls, state):
    outs = [jax.ShapeDtypeStruct(item.shape, F32) for item in state]
    fs = state[9].shape[1]
    dma = pltpu.SemaphoreType.DMA
    return pl.pallas_call(
        functools.partial(moment_kernel, n_dp),
        in_specs=[WHOLE] * (len(grads) + len(smalls)) + [ANY] * 12,
        out_specs=[ANY] * 12 + [WHOLE] * 8,
        out_shape=outs
        + [jax.ShapeDtypeStruct(item.shape, F32) for item in smalls]
        + [shaped(8, 128), shaped(16, 128)],
        scratch_shapes=[pltpu.VMEM(item.shape, F32) for item in state]
        + [pltpu.VMEM(state[3 * kind].shape, F32) for kind in range(4)]
        + [
            pltpu.VMEM((D, D), F32), pltpu.VMEM((D, D), F32), pltpu.VMEM((D, fs), F32),
            dma((12,)), dma((12,)),
        ],
        compiler_params=pltpu.CompilerParams(vmem_limit_bytes=VMEM_LIMIT),
        name="moments",
    )(*grads, *smalls, *state)


def run_tables(misc, shared, ghead, state):
    shape = state[0].shape
    dma = pltpu.SemaphoreType.DMA
    return pl.pallas_call(
        table_kernel,
        in_specs=[WHOLE] * 3 + [ANY] * 3,
        out_specs=[ANY] * 3 + [WHOLE],
        out_shape=[shaped(*shape)] * 3 + [shaped(8, 128)],
        scratch_shapes=[pltpu.VMEM(shape, F32)] * 4 + [dma((3, 4)), dma((3, 4))],
        cost_estimate=pl.CostEstimate(
            flops=40 * shape[0] * shape[1], bytes_accessed=28 * shape[0] * shape[1],
            transcendentals=2 * shape[0] * shape[1],
        ),
        compiler_params=pltpu.CompilerParams(vmem_limit_bytes=VMEM_LIMIT),
        name="tables",
    )(misc, shared, ghead, *state)


def renew_kernel(n_mp, misc, stat, *rest):
    theirs, rest = rest[:n_mp], rest[n_mp:]
    weights, updates = rest[:4], rest[4:8]
    new, copies = rest[8:12], rest[12:16]
    norms, norm_out, stat_out, slots = rest[16:]
    mp = lax.axis_index("mp")
    for step in range(n_mp):
        slots[pl.ds(lax.rem(mp + n_mp - step, n_mp), 1)] = theirs[step][...][None]
    sums = jnp.sum(slots[...], 0)
    rates = []
    lane = lax.broadcasted_iota(jnp.int32, (1, 128), 1)
    weight_line, update_line = misc[1:2, :], misc[2:3, :]
    for place in range(8):
        update_sq = total(sums[place : place + 1, :])
        weight_sq = total(sums[8 + place : 9 + place, :])
        rates.append(RATE * jnp.sqrt(weight_sq / (update_sq + 1e-12)))
        weight_line = jnp.where(lane == place, weight_sq, weight_line)
        update_line = jnp.where(lane == place, update_sq, update_line)
    norms[...] = jnp.sqrt(jnp.concatenate([weight_line, update_line], 0))[:, :13]
    norm_out[...] = misc[0:1, 0:1]
    stat_out[...] = stat[0:1, :12]
    for kind in range(4):
        rows = weights[kind].shape[1]
        chunk = 32 if rows % 32 == 0 else 16
        for b in range(2):
            w, u, out, low = weights[kind], updates[kind], new[kind], copies[kind]
            rate = rates[2 * kind + b]

            def step(i, _, b=b, w=w, u=u, out=out, low=low, rate=rate, chunk=chunk):
                at = pl.ds(pl.multiple_of(i * chunk, chunk), chunk)
                values = w[b, at, :] - rate * u[b, at, :]
                out[b, at, :] = values
                low[b, at, :] = values.astype(BF)
                return 0

            lax.fori_loop(0, rows // chunk, step, 0)


def run_renew(n_mp, misc, stat, sums, weights, updates):
    return pl.pallas_call(
        functools.partial(renew_kernel, n_mp),
        in_specs=[WHOLE] * (10 + n_mp),
        out_specs=[WHOLE] * 11,
        out_shape=[shaped(*item.shape) for item in weights]
        + [shaped(*item.shape, dtype=BF) for item in weights]
        + [shaped(2, 13), shaped(1, 1), shaped(1, 12)],
        scratch_shapes=[pltpu.VMEM((n_mp, 16, 128), F32)],
        compiler_params=pltpu.CompilerParams(vmem_limit_bytes=VMEM_LIMIT),
        name="renew",
    )(misc, stat, *sums, *weights, *updates)


def shards(
    pixels,
    token_mask,
    counts,
    labels,
    pairs,
    attn_in,
    attn_in_mean,
    attn_in_square,
    attn_out,
    attn_out_mean,
    attn_out_square,
    mlp_in,
    mlp_in_mean,
    mlp_in_square,
    mlp_out,
    mlp_out_mean,
    mlp_out_square,
    tables,
    tables_mean,
    tables_square,
    vectors,
    vectors_mean,
    vectors_square,
    talking,
    talking_mean,
    talking_square,
):
    local = pixels.shape[0]
    group = token_mask.shape[0]
    place_mp = lax.axis_index("mp")
    n_mp = lax.axis_size("mp")
    n_dp = lax.axis_size("dp")
    hs = attn_in.shape[3]
    fs = mlp_in.shape[2]

    def as_rows(item):
        return item.transpose(0, 2, 3, 1).reshape(2, 3 * hs, D)

    def from_rows(item):
        return item.reshape(2, 3, hs, D).transpose(0, 3, 1, 2)

    attn_in, attn_in_mean, attn_in_square = map(as_rows, (attn_in, attn_in_mean, attn_in_square))
    pixel_rows = pixels.transpose(1, 0, 2).reshape(P_SIZE * local, PIX)
    mask = lax.dynamic_slice_in_dim(token_mask, place_mp * local, local, 0)
    (
        wattn, mlp_rows, cls_rows, up_rows, down_rows, embed, head, t1row, t2row, cols, bias_row,
        base,
    ) = run_start(
        n_dp, n_mp, group, attn_in, attn_out, mlp_in, mlp_out, pixel_rows, tables, vectors,
        talking, mask, counts, labels, pairs,
    )
    q, k, v, prob, post, ho, raw0, middle, stat_a, wmlp = run_self_attend(
        n_dp, n_mp, embed, cols, vectors, wattn, t1row, t2row, mlp_rows
    )
    patches, act, slope, raw1, norm, cprob, cprob0, z, card, aux, wcls, wup, wdown = run_feed(
        n_dp, n_mp, middle, cols, bias_row, base, stat_a, vectors, wmlp, cls_rows, up_rows,
        down_rows,
    )
    left, right, gv, local_rows, gout1, gup1, gdown1, ghead, rows1, stat = run_token(
        n_dp, n_mp, group, card, vectors, aux, wcls, wup, wdown, head, norm, cprob, cprob0, z
    )
    dmid, gfeed, rows2 = run_feed_back(
        n_dp, left, right, gv, local_rows, patches, middle, raw1, act, slope, vectors, wmlp
    )
    gattn, gpix, gpos, rows3, run_a, run_b = run_self_back(
        n_dp, n_mp, dmid, pixel_rows, embed, q, k, v, prob, post, ho, raw0, vectors, wattn,
        t1row, t2row, gfeed,
    )

    block, shared, block_sq = run_reduce(
        n_dp, n_mp, gattn, run_a, run_b, gpix, gpos, rows2, rows3
    )
    shared = shared.reshape(-1, D)
    state = (
        attn_in, attn_in_mean, attn_in_square, attn_out, attn_out_mean, attn_out_square,
        mlp_in, mlp_in_mean, mlp_in_square, mlp_out, mlp_out_mean, mlp_out_square,
    )
    smalls = (vectors, vectors_mean, vectors_square, talking, talking_mean, talking_square)
    moved = run_moments(
        n_dp, (block, shared, block_sq, gout1, gup1, gdown1, rows1, stat, aux, wcls),
        smalls, state,
    )
    sums = [moved[19]]
    for step in range(1, n_mp):
        sums.append(lax.ppermute(moved[19], "mp", [(i, (i + step) % n_mp) for i in range(n_mp)]))
    table = run_tables(moved[18], shared, ghead, (tables, tables_mean, tables_square))
    renewed = run_renew(n_mp, table[3], stat, sums, state[0:12:3], moved[0:12:3])
    return (
        from_rows(renewed[0]),
        from_rows(moved[1]),
        from_rows(moved[2]),
        renewed[1],
        moved[4],
        moved[5],
        renewed[2],
        moved[7],
        moved[8],
        renewed[3],
        moved[10],
        moved[11],
        *table[:3],
        *moved[12:18],
        from_rows(renewed[4]),
        renewed[5],
        renewed[6],
        renewed[7],
        renewed[10].reshape(12),
        renewed[9].reshape(()),
        renewed[8],
    )


def solution(mesh):
    return jax.shard_map(
        shards,
        mesh=mesh,
        in_specs=(
            P(("dp", "mp"), None, None),
            P("dp", None),
            P("dp"),
            P(("dp", "mp")),
            P(("dp", "mp")),
            P(None, None, None, "mp"),
            P(None, None, None, "mp"),
            P(None, None, None, "mp"),
            P(None, "mp", None),
            P(None, "mp", None),
            P(None, "mp", None),
            P(None, None, "mp"),
            P(None, None, "mp"),
            P(None, None, "mp"),
            P(None, "mp", None),
            P(None, "mp", None),
            P(None, "mp", None),
            P(),
            P(),
            P(),
            P(),
            P(),
            P(),
            P(),
            P(),
            P(),
        ),
        out_specs=(
            P(None, None, None, "mp"),
            P(None, None, None, "mp"),
            P(None, None, None, "mp"),
            P(None, "mp", None),
            P(None, "mp", None),
            P(None, "mp", None),
            P(None, None, "mp"),
            P(None, None, "mp"),
            P(None, None, "mp"),
            P(None, "mp", None),
            P(None, "mp", None),
            P(None, "mp", None),
            P(),
            P(),
            P(),
            P(),
            P(),
            P(),
            P(),
            P(),
            P(),
            P(None, None, None, "mp"),
            P(None, "mp", None),
            P(None, None, "mp"),
            P(None, "mp", None),
            P(),
            P(),
            P(),
        ),
        check_vma=False,
    )
```

time: 285 us -> 237 us (0.83)
  Pallas kernels: 253 us -> 229 us
  between operations: 14.6 us -> 1.64 us
  local copies, waits for them, and re-layouts: 13.6 us -> 1.29 us
  other arithmetic: 3.54 us -> 0 us
    pallas_call x1, Pallas kernels: 22.4 us -> 11.5 us  [run_moments(): pl.pallas_call(functools.partial(moment_kernel, n_dp), in_specs=[WHOLE] *...]
    slice x6 -> x0, local copies, waits for them, and re-layouts: 6.97 us -> none  [the longest x1 2.42 us: shards(): head = tables[PIX + P_SIZE:].astype(BF)]
    pallas_call x1, Pallas kernels: 51.5 us -> 44.6 us  [run_reduce(): pl.pallas_call(functools.partial(reduce_kernel, n_dp, n_mp), in_specs=[WH...]
    pallas_call x1, Pallas kernels: 52 us -> 48.7 us  [run_self_back(): pl.pallas_call(functools.partial(self_back_kernel, n_dp, n_mp), grid=(cou...]
    pallas_call x8 -> x7, Pallas kernels: 127 us -> 124 us  [the longest x1 24.8 us: run_feed(): pl.pallas_call(functools.partial(feed_kernel, n_dp, n_mp), grid=(count,),...]
  transfers between devices with their start and end apart: 3 -> 3, of which waited for: 0 -> 0; matrix products, arithmetic and copies ran while one was open for 4% -> 0% of each run, Pallas kernels for 26% -> 4%
where the time goes in v3:
time: 237 us; the launch traced here: 234 us
  Pallas kernels  229 us (97%)
  starting transfers between devices  2.41 us (1%)
    pallas_call x1, Pallas kernels, run_self_back(): pl.pallas_call(functools.partial(self_back_kernel, n_dp, n_mp), grid=(cou...  48.7 us
    pallas_call x1, Pallas kernels, run_reduce(): pl.pallas_call(functools.partial(reduce_kernel, n_dp, n_mp), in_specs=[WH...  44.6 us
    pallas_call x1, Pallas kernels, run_feed(): pl.pallas_call(functools.partial(feed_kernel, n_dp, n_mp), grid=(count,),...  24.8 us
    pallas_call x1, Pallas kernels, run_feed_back(): pl.pallas_call(feed_back_kernel, grid=(count,), in_specs=[per_image(2 * H...  23.6 us
    pallas_call x1, Pallas kernels, run_self_attend(): pl.pallas_call(functools.partial(self_attend_kernel, n_dp, n_mp), grid=(c...  21.7 us
    pallas_call x1, Pallas kernels, run_token(): pl.pallas_call(functools.partial(card_token_kernel, n_dp, n_mp, group), i...  21.5 us
    pallas_call x1, Pallas kernels, run_start(): pl.pallas_call(functools.partial(start_kernel, n_dp, n_mp, group), in_spe...  17 us
    pallas_call x1, Pallas kernels, run_moments(): pl.pallas_call(functools.partial(moment_kernel, n_dp), in_specs=[WHOLE] *...  11.5 us
  transfers between devices with their start and end apart: 3, of which 0 were waited for; matrix products, arithmetic and copies ran while one was open for 0% of the time, Pallas kernels for 4%

profile of v3, /device:TPU:0, one launch (start us, length us, event | category | flops | bytes accessed | tf_op | source)
XLA Modules:
  0.0 234.5 jit_solution(2144280414797724307)
XLA Ops:
  0.7 0.0 copy-start
  1.3 0.1 copy-done
  1.4 0.6 constant_dynamic-slice_fusion.mask
  2.0 17.0 %start.1 = (bf16[4,384,384]{2,1,0:T(8,128)(2,1)}, bf16[768,384]{1,0:T(8,128)(2,1)}, bf16[384,384]{1,0:T(8,128)(2,1)}, bf16[384,384]{1,0:T(8,128)(2,1)}, bf16[384...) custom-call(f32[2,288,384]{2,1,0:T(8,128)} %bitcast.29, ...), custom_call_target="tpu_custom_call" | custom-call | tf_op jit(solution)/shard_map/start/pallas_call | solution.py:1516
  19.0 21.7 %self_attend.1 = (bf16[8,196,384]{2,1,0:T(8,128)(2,1)}, bf16[8,196,384]{2,1,0:T(8,128)(2,1)}, bf16[8,196,384]{2,1,0:T(8,128)(2,1)}, bf16[8,196,1664]{2,1,0:T(8,1...) custom-call(f32[8,196,384]{2,1,0:T(8,128)} %get-tuple-element.120.em, ...), custom_call_target="tpu_custom_call" | custom-call | tf_op jit(solution)/shard_map/self_attend/pallas_call | solution.py:1190
  40.7 24.8 %feed.1 = (f32[8,196,384]{2,1,0:T(8,128)}, bf16[8,196,1536]{2,1,0:T(8,128)(2,1)}, bf16[8,196,1536]{2,1,0:T(8,128)(2,1)}, bf16[8,196,384]{2,1,0:T(8,128)(2,1)}, b...) custom-call(f32[8,196,384]{2,1,0:T(8,128)} %get-tuple-element.126.mi, ...), custom_call_target="tpu_custom_call" | custom-call | tf_op jit(solution)/shard_map/feed/pallas_call | solution.py:1218
  65.5 21.5 %token_net.1 = (bf16[8,16,256]{2,1,0:T(8,128)(2,1)}, bf16[8,16,384]{2,1,0:T(8,128)(2,1)}, f32[384,384]{1,0:T(8,128)}, f32[16,384]{1,0:T(8,128)}, f32[96,384]{1,0...) custom-call(f32[32,128]{1,0:T(8,128)} %get-tuple-element.134.card, ...), custom_call_target="tpu_custom_call" | custom-call | tf_op jit(solution)/shard_map/token_net/pallas_call | solution.py:1255
  87.0 23.6 %feed_back.1 = (f32[8,196,384]{2,1,0:T(8,128)}, bf16[4,896,384]{2,1,0:T(8,128)(2,1)}, f32[16,384]{1,0:T(8,128)}) custom-call(bf16[8,16,256]{2,1,0:T(8,128)(2,1)} %get-tuple-element.144.left, bf16[8,16,384]{2,1,0:T(8,128)(2,1)} %get-tuple-element.145.right, f32[384,384]{1,0:T(8,128)} %get-tuple-element.146.gv, f32[16,384]{1,0:T(8,128)} %get-tuple-element.147.local_rows, ...), custom_call_target="tpu_custom_call" | custom-call | tf_op jit(solution)/shard_map/feed_back/pallas_call | solution.py:1281
  110.6 48.7 %self_back.1 = (f32[4,384,384]{2,1,0:T(8,128)}, f32[768,384]{1,0:T(8,128)}, f32[196,384]{1,0:T(8,128)}, f32[24,384]{1,0:T(8,128)}, bf16[256,384]{1,0:T(8,128)(2,1)}, /*index=5*/bf16[192,384]{1,0:T(8,128)(2,1)}) custom-call(f32[8,196,384]{2,1,0:T(8,128)} %get-tuple-element.152.dmid, bf16[1568,768]{1,0:T(8,128)(2,1)} %bitcast.28, ...), custom_call_target="tpu_custom_call" | custom-call | tf_op jit(solution)/shard_map/self_back/pallas_call | solution.py:1304
  159.2 44.6 %reduce.1 = (bf16[1280,384]{1,0:T(8,128)(2,1)}, bf16[4,256,384]{2,1,0:T(8,128)(2,1)}, f32[8,128]{1,0:T(8,128)}) custom-call(f32[4,384,384]{2,1,0:T(8,128)} %get-tuple-element.161.gattn, bf16[256,384]{1,0:T(8,128)(2,1)} %get-tuple-element.162.run_a, bf16[192,384]{1,0:T(8,128)(2,1)} %get-tuple-element.163.run_b, f32[768,384]{1,0:T(8,128)} %get-tuple-element.164.gpix, ...), custom_call_target="tpu_custom_call" | custom-call | tf_op jit(solution)/shard_map/reduce/pallas_call | solution.py:1650
  203.9 11.5 %moments.1 = (f32[2,288,384]{2,1,0:T(8,128)}, f32[2,288,384]{2,1,0:T(8,128)}, f32[2,288,384]{2,1,0:T(8,128)}, f32[2,96,384]{2,1,0:T(8,128)}, f32[2,96,384]{2,1,0...) custom-call(bf16[1280,384]{1,0:T(8,128)(2,1)} %get-tuple-element.168, ...), custom_call_target="tpu_custom_call" | custom-call | tf_op jit(solution)/shard_map/moments/pallas_call | solution.py:2010
  215.4 2.1 collective-permute-start.2
  217.5 0.1 collective-permute-start.1
  217.6 0.2 collective-permute-start
  217.8 9.4 %tables.3 = (f32[1964,384]{1,0:T(8,128)}, f32[1964,384]{1,0:T(8,128)}, f32[1964,384]{1,0:T(8,128)}, f32[8,128]{1,0:T(8,128)}) custom-call(f32[8,128]{1,0:T(8,128)} %get-tuple-element.176.misc, bf16[1024,384]{1,0:T(8,128)(2,1)} %bitcast.33, f32[1008,384]{1,0:T(8,128)} %get-tuple-element.177.ghead, f32[1964,384]{1,0:T(8,128)} %rest_0_.1, f32[1964,384]{1,0:T(8,128)} %rest_1_.1, ...), custom_call_target="tpu_custom_call" | custom-call | flops 30167040 | bytes 21116928 | tf_op jit(solution)/shard_map/tables/pallas_call | solution.py:2031
  227.2 0.0 collective-permute-done.2.rest_3_
  227.2 0.0 collective-permute-done.1.rest_2_
  227.2 0.0 collective-permute-done.rest_1_
  227.2 0.0 copy-start.4
  227.3 0.6 copy-done.2
  227.8 0.0 copy-done.3
  227.8 0.0 copy-done.4
  227.8 6.5 %renew.1 = (f32[2,288,384]{2,1,0:T(8,128)}, f32[2,96,384]{2,1,0:T(8,128)}, f32[2,384,384]{2,1,0:T(8,128)}, f32[2,384,384]{2,1,0:T(8,128)}, bf16[2,288,384]{2,1,0...) custom-call(f32[8,128]{1,0:T(8,128)} %get-tuple-element.178.misc, ...), custom_call_target="tpu_custom_call" | custom-call | tf_op jit(solution)/shard_map/renew/pallas_call | solution.py:2085
  234.3 0.0 copy-done.1
  (3 shorter events, 0.0 us)
Async XLA Ops:
  0.7 0.8 copy-start
  215.4 11.8 %collective-permute-start.2 = (f32[16,128]{1,0:T(8,128)}, f32[16,128]{1,0:T(8,128)S(1)}, u32[]{:S(2)}, u32[]{:S(2)}) collective-permute-start(f32[16,128]{1,0:T(8,128)} %get-tuple-element.179.rest_0_), channel_id=1, source_target_pairs={{0,3},{1,0},{2,1},{3,2},{4,7},{5,4},{6,5},{7,6},{8,11},{9,8},{10,9... | collective-permute-start | bytes 24584 | tf_op jit(solution)/shard_map/ppermute | solution.py:2183
  217.5 9.7 %collective-permute-start.1 = (f32[16,128]{1,0:T(8,128)}, f32[16,128]{1,0:T(8,128)S(1)}, u32[]{:S(2)}, u32[]{:S(2)}) collective-permute-start(f32[16,128]{1,0:T(8,128)} %get-tuple-element.179.rest_0_), channel_id=1, source_target_pairs={{0,2},{1,3},{2,0},{3,1},{4,6},{5,7},{6,4},{7,5},{8,10},{9,11},{10,... | collective-permute-start | bytes 24584 | tf_op jit(solution)/shard_map/ppermute | solution.py:2183
  217.6 9.6 %collective-permute-start = (f32[16,128]{1,0:T(8,128)}, f32[16,128]{1,0:T(8,128)S(1)}, u32[]{:S(2)}, u32[]{:S(2)}) collective-permute-start(f32[16,128]{1,0:T(8,128)} %get-tuple-element.179.rest_0_), channel_id=1, source_target_pairs={{0,1},{1,2},{2,3},{3,0},{4,5},{5,6},{6,7},{7,4},{8,9},{9,10},{10,1... | collective-permute-start | bytes 24584 | tf_op jit(solution)/shard_map/ppermute | solution.py:2183
  227.2 0.6 copy-start.2
  227.2 0.6 copy-start.3
  227.2 0.6 copy-start.4
  227.8 6.5 %copy-start.1 = (s32[32,196]{1,0:T(8,128)S(1)}, s32[32,196]{1,0:T(8,128)}, u32[]{:S(2)}) copy-start(s32[32,196]{1,0:T(8,128)} %param.27) | copy-start | bytes 75268

commit v4 on v3

--- a/solution.py
+++ b/solution.py
@@ -1064,8 +1064,9 @@
 
 def self_back_kernel(
     n_dp, n_mp, dmid, pixels, embed, q, k, v, prob, post, ho, raw, vec, wattn, t1row, t2row, gfeed,
-    gattn_out, gpix_out, gpos_out, rows_out, run_a_out, run_b_out,
-    dx_all, dx_rows, stack_q, stack_h, slopes, run_a, run_b, hand_sem_a, hand_sem_b, *sum_buffers,
+    rows_feed, block_far, shared_far, square_out,
+    gattn_out, gpos_out, rows_out, dx_all, dx_rows, stack_q, stack_h, slopes,
+    blocks_out, commons_out, block_here, shared_here, save_sem, *sum_buffers,
 ):
     shard = wattn.shape[1] // 4
     count = wattn.shape[0]
@@ -1073,9 +1074,9 @@
     place = Place(n_dp, n_mp)
     rows_a, _ = halves(gfeed.shape[1], n_dp)
     sum_a = ShardSum(place, gfeed, 0, True, *sum_buffers[:SUM_BUFFERS])
-    sum_b = ShardSum(place, gfeed, rows_a, False, *sum_buffers[SUM_BUFFERS:])
-    hand_a = HandHigh(place, run_a, hand_sem_a)
-    hand_b = HandHigh(place, run_b, hand_sem_b)
+    sum_b = ShardSum(
+        place, gfeed, rows_a, False, *sum_buffers[SUM_BUFFERS : 2 * SUM_BUFFERS]
+    )
 
     def beside(step, *stages):
         @pl.when(pl.program_id(0) == step)
@@ -1096,7 +1097,7 @@
 
     beside(1, sum_a.second, sum_b.second)
     beside(images * 3 // 8, sum_a.third, sum_b.third)
-    beside(images // 2, sum_a.fourth, sum_b.fourth)
+    beside(images * 5 // 8, sum_a.fourth, sum_b.fourth)
 
     wq = part(wattn, 0, shard)
     wk = part(wattn, shard, shard)
@@ -1111,12 +1112,6 @@
 
     unit, inverse = normalize(embed[0])
     normed = (unit * vec[0:1, :] + vec[1:2, :]).astype(BF)
-    beside(
-        images * 3 // 4,
-        lambda: hand_a.start(sum_a.finish()),
-        lambda: hand_b.start(sum_b.finish()),
-    )
-
     q_wide = q[0].astype(F32)
     stack_heads(stack_q, q_wide, t1row)
     stack_heads(stack_h, dheads, t2row)
@@ -1151,13 +1146,40 @@
     def _():
         for n in range(images):
             dx_rows[:, n, :] = dx_all[n]
-        gpix_out[...] = tn(pixels[...], dx_rows[...].reshape(pixels.shape[0], D).astype(BF))
-        for item in (hand_a, hand_b):
-            item.arrive()
-        run_a_out[...] = run_a[...]
-        run_b_out[...] = run_b[...]
-        for item in (sum_a, sum_b, hand_a, hand_b):
-            item.wait_sends()
+        gpix = tn(pixels[...], dx_rows[...].reshape(pixels.shape[0], D).astype(BF))
+        used = gattn_out.shape[1]
+        blocks_out[:, :used, :] = gattn_out[...].astype(BF)
+        if used < blocks_out.shape[1]:
+            blocks_out[:, used:, :] = jnp.zeros((count, blocks_out.shape[1] - used, D), BF)
+        wide = commons_out.shape[1]
+        commons_out[:3] = gpix.astype(BF).reshape(3, wide, D)
+        commons_out[3] = jnp.concatenate(
+            [
+                gpos_out[...], jnp.zeros((12, D), F32), rows_feed[...], rows_out[...],
+                jnp.zeros((8, D), F32),
+            ],
+            0,
+        ).astype(BF)
+        if count > 4:
+            commons_out[4:] = jnp.zeros((count - 4, wide, D), BF)
+        reduce_rows(
+            place, blocks_out, commons_out, sum_a.finish(), sum_b.finish(), block_here,
+            shared_here, square_out, *sum_buffers[2 * SUM_BUFFERS :],
+        )
+        saves = [
+            pltpu.make_async_copy(block_here, block_far, save_sem.at[0]),
+            pltpu.make_async_copy(shared_here, shared_far, save_sem.at[1]),
+        ]
+        for copy in saves:
+            copy.start()
+        sum_a.wait_sends()
+        sum_b.wait_sends()
+        for copy in saves:
+            copy.wait()
+
+
+def table_rows(n_dp, n_mp):
+    return -(-(PIX + 256) // (16 * n_dp * n_mp)) * 16 * n_dp
 
 
 def per_image(*tail):
@@ -1296,10 +1318,14 @@
 
 
 def run_self_back(
-    n_dp, n_mp, dmid, pixels, embed, q, k, v, prob, post, ho, raw, vec, wattn, t1row, t2row, gfeed
+    n_dp, n_mp, dmid, pixels, embed, q, k, v, prob, post, ho, raw, vec, wattn, t1row, t2row, gfeed,
+    rows_feed,
 ):
     count = dmid.shape[0]
     rows_a, rows_b = halves(gfeed.shape[1], n_dp)
+    blocks = (n_mp, pad_rows(wattn.shape[1], n_dp), D)
+    commons = (n_mp, table_rows(n_dp, n_mp), D)
+    rows = blocks[1] + rows_a + rows_b
     n_lo = 2 if n_dp < 16 else 4
     return pl.pallas_call(
         functools.partial(self_back_kernel, n_dp, n_mp),
@@ -1309,31 +1335,33 @@
             per_image(P_SIZE, D), per_image(P_SIZE, D), per_image(P_SIZE, D),
             per_image(P_SIZE, HEADS * PAD), per_image(HEADS * PAD, D), per_image(P_SIZE, D),
             per_image(P_SIZE, D), constant(*vec.shape), constant(*wattn.shape), constant(HEADS, D),
-            constant(HEADS, D), constant(*gfeed.shape),
+            constant(HEADS, D), constant(*gfeed.shape), constant(16, D),
         ],
         out_specs=[
-            constant(*wattn.shape), constant(PIX, D), constant(P_SIZE, D), constant(24, D),
-            constant(rows_a // n_lo, D), constant(rows_b // n_lo, D),
+            ANY, ANY, constant(8, 128),
         ],
         out_shape=[
-            shaped(*wattn.shape), shaped(PIX, D), shaped(P_SIZE, D), shaped(24, D),
-            shaped(rows_a // n_lo, D, dtype=BF), shaped(rows_b // n_lo, D, dtype=BF),
+            shaped(rows, D, dtype=BF), shaped(*commons, dtype=BF), shaped(8, 128),
         ],
         scratch_shapes=[
+            pltpu.VMEM(wattn.shape, F32), pltpu.VMEM((P_SIZE, D), F32), pltpu.VMEM((24, D), F32),
             pltpu.VMEM((count, P_SIZE, D), F32), pltpu.VMEM((P_SIZE, count, D), F32),
             pltpu.VMEM((HEADS * PAD, D), BF), pltpu.VMEM((HEADS * PAD, D), BF),
             pltpu.VMEM((P_SIZE, HEADS * PAD), F32),
-            pltpu.VMEM((rows_a // n_lo, D), BF), pltpu.VMEM((rows_b // n_lo, D), BF),
-            pltpu.SemaphoreType.DMA((2, n_dp // n_lo)), pltpu.SemaphoreType.DMA((2, n_dp // n_lo)),
+            pltpu.VMEM(blocks, BF), pltpu.VMEM(commons, BF), pltpu.VMEM((rows, D), BF),
+            pltpu.VMEM(commons, BF), pltpu.SemaphoreType.DMA((2,)),
         ]
         + sum_scratch(n_dp, n_mp, rows_a, True)
-        + sum_scratch(n_dp, n_mp, rows_b, False),
+        + sum_scratch(n_dp, n_mp, rows_b, False)
+        + reduce_scratch(
+            n_dp, n_mp, blocks[1], commons[1], (rows_a // n_lo, rows_b // n_lo)
+        ),
         compiler_params=pltpu.CompilerParams(
             vmem_limit_bytes=VMEM_LIMIT, dimension_semantics=("arbitrary",), collective_id=5,
             has_side_effects=True,
         ),
         name="self_back",
-    )(dmid, pixels, embed, q, k, v, prob, post, ho, raw, vec, wattn, t1row, t2row, gfeed)
+    )(dmid, pixels, embed, q, k, v, prob, post, ho, raw, vec, wattn, t1row, t2row, gfeed, rows_feed)
 
 
 def share_cards(n_dp, n_mp, card, out, slots, dp_sem, mp_sem):
@@ -1379,8 +1407,8 @@
 def start_kernel(
     n_dp, n_mp, group, attn_in, attn_out, mlp_in, mlp_out, pixels, tables, vec, mix, mask,
     counts, labels, pairs,
-    out, mlp_rows, cls_rows, up_rows, down_rows, embed_out, head_out, t1_out, t2_out, cols_out, bias_out, base_out,
-    head_rows, wide_up, wide_down, shard, wide_in, wide_out, patch_rows, pos_rows, by_patch, near_send, near_recv, far_send, far_recv, load_sem,
+    out, mlp_rows, cls_rows, up_rows, down_rows, embed_far, head_out, t1_out, t2_out, cols_out, bias_out, base_out,
+    embed_out, head_rows, wide_up, wide_down, shard, wide_in, wide_out, patch_rows, pos_rows, by_patch, near_send, near_recv, far_send, far_recv, load_sem,
 ):
     dp = lax.axis_index("dp")
     mp = lax.axis_index("mp")
@@ -1490,8 +1518,11 @@
     offset = pos_rows[:P_SIZE, :] + vec[16:17, :]
     for n in range(local):
         embed_out[n] = by_patch[:, n, :] + offset
+    save_embed = pltpu.make_async_copy(embed_out, embed_far, load_sem.at[7])
+    save_embed.start()
     load_head.wait()
     head_out[...] = head_rows[4:, :].astype(BF)
+    save_embed.wait()
     for copy in far:
         copy.wait_send()
     for step in range(n_y):
@@ -1516,7 +1547,7 @@
     return pl.pallas_call(
         functools.partial(start_kernel, n_dp, n_mp, group),
         in_specs=[ANY] * 4 + [WHOLE, ANY, WHOLE, WHOLE, WHOLE, scalars, scalars, scalars],
-        out_specs=[WHOLE] * 12,
+        out_specs=[WHOLE] * 5 + [ANY] + [WHOLE] * 6,
         out_shape=[
             shaped(n_mp, rows, D, dtype=BF), shaped(2 * hidden, D, dtype=BF),
             shaped(rows, D, dtype=BF), shaped(hidden, D, dtype=BF), shaped(hidden, D, dtype=BF),
@@ -1525,13 +1556,14 @@
             shaped(P_SIZE, 2 * local), shaped(1, local * WIDE), shaped(local, 128),
         ],
         scratch_shapes=[
+            pltpu.VMEM((local, P_SIZE, D), F32),
             pltpu.VMEM((classes + 4, D), F32), pltpu.VMEM(mlp_in.shape, F32),
             pltpu.VMEM(mlp_out.shape, F32),
             pltpu.VMEM((rows, D), BF), pltpu.VMEM(attn_in.shape, F32),
             pltpu.VMEM(attn_out.shape, F32), pltpu.VMEM((PIX, D), F32),
             pltpu.VMEM((200, D), F32),
             pltpu.VMEM((P_SIZE, local, D), F32),
-            dma((n_y,)), dma((n_y,)), dma((n_y,)), dma((n_y,)), dma((7,)),
+            dma((n_y,)), dma((n_y,)), dma((n_y,)), dma((n_y,)), dma((8,)),
         ],
         compiler_params=pltpu.CompilerParams(
             vmem_limit_bytes=VMEM_LIMIT, collective_id=2, has_side_effects=True
@@ -1542,47 +1574,36 @@
     )
 
 
-def reduce_kernel(
-    n_dp, n_mp, gattn, run_a, run_b, gpix, gpos, rows2, rows3,
+def reduce_rows(
+    p, blocks, commons, chunk_a, chunk_b,
     block_out, shared_out, square_out,
-    blocks, commons, squares, attn_run, sem_a, sem_b, high_sem, low_sem, square_sem, *sum_buffers,
+    squares, attn_run, run_a, run_b, sem_a, sem_b, high_a, high_b, high_sem, low_sem, square_sem,
+    *sum_buffers,
 ):
-    p = Place(n_dp, n_mp)
+    n_mp = p.n_mp
     attn = ShardSum(p, blocks, 0, True, *sum_buffers[:SUM_BUFFERS])
     table = TableSum(p, commons, shared_out, *sum_buffers[SUM_BUFFERS:])
     rows_a = blocks.shape[1]
-    wide = commons.shape[1]
-    greeted = greet(p.near_partners() + p.dp_partners())
-
-    used = gattn.shape[1]
-    blocks[:, :used, :] = gattn[...].astype(BF)
-    if used < rows_a:
-        blocks[:, used:, :] = jnp.zeros((n_mp, rows_a - used, D), BF)
-    commons[:3] = gpix[...].astype(BF).reshape(3, wide, D)
-    commons[3] = jnp.concatenate(
-        [
-            gpos[...], jnp.zeros((12, D), F32), rows2[...], rows3[...], jnp.zeros((8, D), F32),
-        ],
-        0,
-    ).astype(BF)
-    if n_mp > 4:
-        commons[4:] = jnp.zeros((n_mp - 4, wide, D), BF)
-
     rows_feed = p.n_lo * run_a.shape[0]
     hand_a = HandLow(p, block_out, rows_a, rows_feed, sem_a)
     hand_b = HandLow(p, block_out, rows_a + rows_feed, p.n_lo * run_b.shape[0], sem_b)
+    wide_a = HandHigh(p, run_a, high_a)
+    wide_b = HandHigh(p, run_b, high_b)
     hand_high = HandHigh(p, attn_run, high_sem)
     hand_low = HandLow(p, block_out, 0, rows_a, low_sem)
 
-    greeted()
     attn.start()
     table.start()
+    wide_a.start(chunk_a)
+    wide_b.start(chunk_b)
     attn.second()
     table.near_to_low()
-    hand_a.start(run_a[...])
-    hand_b.start(run_b[...])
     table.low_to_high()
     attn.third()
+    wide_a.arrive()
+    hand_a.start(run_a[...])
+    wide_b.arrive()
+    hand_b.start(run_b[...])
     table.high_to_far()
     attn.fourth()
     table.turn()
@@ -1635,39 +1656,25 @@
     square_out[...] = squares[n_mp] + squares[n_mp + 1]
     for copy in sends:
         copy.wait_send()
-    for item in (attn, hand_a, hand_b, hand_high, hand_low):
+    for item in (attn, wide_a, wide_b, hand_a, hand_b, hand_high, hand_low):
         item.wait_sends()
 
 
-def run_reduce(n_dp, n_mp, gattn, run_a, run_b, gpix, gpos, rows2, rows3):
-    n = n_dp * n_mp
-    rows_a = pad_rows(gattn.shape[1], n_dp)
-    chunk_s = -(-(PIX + 256) // (16 * n)) * 16
-    wide = chunk_s * n_dp
+def reduce_scratch(n_dp, n_mp, rows_a, wide, feed):
     assert wide == 256
     n_lo = 2 if n_dp < 16 else 4
+    n_hi = n_dp // n_lo
     dma = pltpu.SemaphoreType.DMA
-    return pl.pallas_call(
-        functools.partial(reduce_kernel, n_dp, n_mp),
-        in_specs=[WHOLE] * 7,
-        out_specs=[WHOLE] * 3,
-        out_shape=[
-            shaped(rows_a + n_lo * (run_a.shape[0] + run_b.shape[0]), D, dtype=BF),
-            shaped(n_mp, wide, D, dtype=BF), shaped(8, 128),
-        ],
-        scratch_shapes=[
-            pltpu.VMEM((n_mp, rows_a, D), BF), pltpu.VMEM((n_mp, wide, D), BF),
-            pltpu.VMEM((n_mp + 2, 8, 128), F32),
-            pltpu.VMEM((rows_a // n_lo, D), BF),
-            dma((2, n_lo)), dma((2, n_lo)), dma((2, n_dp // n_lo)), dma((2, n_lo)), dma((2, n_mp)),
+    return (
+        [
+            pltpu.VMEM((n_mp + 2, 8, 128), F32), pltpu.VMEM((rows_a // n_lo, D), BF),
+            pltpu.VMEM((feed[0], D), BF), pltpu.VMEM((feed[1], D), BF),
+            dma((2, n_lo)), dma((2, n_lo)), dma((2, n_hi)), dma((2, n_hi)), dma((2, n_hi)),
+            dma((2, n_lo)), dma((2, n_mp)),
         ]
         + sum_scratch(n_dp, n_mp, rows_a, True)
-        + table_scratch(n_dp, n_mp, wide),
-        compiler_params=pltpu.CompilerParams(
-            vmem_limit_bytes=VMEM_LIMIT, collective_id=3, has_side_effects=True
-        ),
-        name="reduce",
-    )(gattn, run_a, run_b, gpix, gpos, rows2, rows3)
+        + table_scratch(n_dp, n_mp, wide)
+    )
 
 
 def root(values):
@@ -1724,9 +1731,10 @@
 
 
 def moment_kernel(
-    n_dp, block, shared, block_sq, gout1, gup1, gdown1, rows1, stat, aux, wcls,
-    vec, vec_mean, vec_square, mix, mix_mean, mix_square, *rest,
+    n_dp, block_sq, gout1, rows1, stat, aux, vec, vec_mean, vec_square, mix, mix_mean, mix_square,
+    *rest,
 ):
+    large, rest = rest[:5], rest[5:]
     state = rest[:12]
     outs = rest[12:24]
     (
@@ -1735,10 +1743,17 @@
     ) = rest[24:32]
     held = rest[32:44]
     updates = rest[44:48]
-    grad_q, grad_k, grad_flip, load_sem, save_sem = rest[48:]
+    grad_q, grad_k, grad_flip, load_sem, save_sem = rest[48:53]
+    large_here = rest[53:]
+    first_loads = [
+        pltpu.make_async_copy(large[i], large_here[i], load_sem.at[12 + i]) for i in range(5)
+    ]
     loads = [pltpu.make_async_copy(state[i], held[i], load_sem.at[i]) for i in range(12)]
-    for copy in loads:
+    for copy in first_loads + loads:
         copy.start()
+    for copy in first_loads:
+        copy.wait()
+    block, shared, wcls, gup1, gdown1 = large_here
     mp = lax.axis_index("mp")
     hs = state[3].shape[1]
     fs = state[9].shape[1]
@@ -2003,13 +2018,13 @@
         copy.wait()
 
 
-def run_moments(n_dp, grads, smalls, state):
+def run_moments(n_dp, grads, smalls, large, state):
     outs = [jax.ShapeDtypeStruct(item.shape, F32) for item in state]
     fs = state[9].shape[1]
     dma = pltpu.SemaphoreType.DMA
     return pl.pallas_call(
         functools.partial(moment_kernel, n_dp),
-        in_specs=[WHOLE] * (len(grads) + len(smalls)) + [ANY] * 12,
+        in_specs=[WHOLE] * (len(grads) + len(smalls)) + [ANY] * 17,
         out_specs=[ANY] * 12 + [WHOLE] * 8,
         out_shape=outs
         + [jax.ShapeDtypeStruct(item.shape, F32) for item in smalls]
@@ -2018,11 +2033,12 @@
         + [pltpu.VMEM(state[3 * kind].shape, F32) for kind in range(4)]
         + [
             pltpu.VMEM((D, D), F32), pltpu.VMEM((D, D), F32), pltpu.VMEM((D, fs), F32),
-            dma((12,)), dma((12,)),
-        ],
+            dma((17,)), dma((12,)),
+        ]
+        + [pltpu.VMEM(item.shape, item.dtype) for item in large],
         compiler_params=pltpu.CompilerParams(vmem_limit_bytes=VMEM_LIMIT),
         name="moments",
-    )(*grads, *smalls, *state)
+    )(*grads, *smalls, *large, *state)
 
 
 def run_tables(misc, shared, ghead, state):
@@ -2047,7 +2063,19 @@
     theirs, rest = rest[:n_mp], rest[n_mp:]
     weights, updates = rest[:4], rest[4:8]
     new, copies = rest[8:12], rest[12:16]
-    norms, norm_out, stat_out, slots = rest[16:]
+    norms, norm_out, stat_out = rest[16:19]
+    here, changes, lows = rest[19:23], rest[23:27], rest[27:31]
+    slots, load_sem, save_sem = rest[31:]
+    loads = [
+        (
+            pltpu.make_async_copy(weights[kind], here[kind], load_sem.at[0, kind]),
+            pltpu.make_async_copy(updates[kind], changes[kind], load_sem.at[1, kind]),
+        )
+        for kind in range(4)
+    ]
+    for pair in loads[::-1]:
+        for copy in pair:
+            copy.start()
     mp = lax.axis_index("mp")
     for step in range(n_mp):
         slots[pl.ds(lax.rem(mp + n_mp - step, n_mp), 1)] = theirs[step][...][None]
@@ -2064,32 +2092,45 @@
     norms[...] = jnp.sqrt(jnp.concatenate([weight_line, update_line], 0))[:, :13]
     norm_out[...] = misc[0:1, 0:1]
     stat_out[...] = stat[0:1, :12]
-    for kind in range(4):
-        rows = weights[kind].shape[1]
+    saves = []
+    for kind in (3, 2, 1, 0):
+        w, u, low = here[kind], changes[kind], lows[kind]
+        rows = w.shape[1]
         chunk = 32 if rows % 32 == 0 else 16
+        for copy in loads[kind]:
+            copy.wait()
         for b in range(2):
-            w, u, out, low = weights[kind], updates[kind], new[kind], copies[kind]
             rate = rates[2 * kind + b]
 
-            def step(i, _, b=b, w=w, u=u, out=out, low=low, rate=rate, chunk=chunk):
+            def step(i, _, b=b, w=w, u=u, low=low, rate=rate, chunk=chunk):
                 at = pl.ds(pl.multiple_of(i * chunk, chunk), chunk)
                 values = w[b, at, :] - rate * u[b, at, :]
-                out[b, at, :] = values
+                w[b, at, :] = values
                 low[b, at, :] = values.astype(BF)
                 return 0
 
             lax.fori_loop(0, rows // chunk, step, 0)
+        saves.append(pltpu.make_async_copy(w, new[kind], save_sem.at[0, kind]))
+        saves.append(pltpu.make_async_copy(low, copies[kind], save_sem.at[1, kind]))
+        for copy in saves[-2:]:
+            copy.start()
+    for copy in saves:
+        copy.wait()
 
 
 def run_renew(n_mp, misc, stat, sums, weights, updates):
+    dma = pltpu.SemaphoreType.DMA
     return pl.pallas_call(
         functools.partial(renew_kernel, n_mp),
-        in_specs=[WHOLE] * (10 + n_mp),
-        out_specs=[WHOLE] * 11,
+        in_specs=[WHOLE] * (2 + n_mp) + [ANY] * 8,
+        out_specs=[ANY] * 8 + [WHOLE] * 3,
         out_shape=[shaped(*item.shape) for item in weights]
         + [shaped(*item.shape, dtype=BF) for item in weights]
         + [shaped(2, 13), shaped(1, 1), shaped(1, 12)],
-        scratch_shapes=[pltpu.VMEM((n_mp, 16, 128), F32)],
+        scratch_shapes=[pltpu.VMEM(item.shape, F32) for item in weights]
+        + [pltpu.VMEM(item.shape, F32) for item in weights]
+        + [pltpu.VMEM(item.shape, BF) for item in weights]
+        + [pltpu.VMEM((n_mp, 16, 128), F32), dma((2, 4)), dma((2, 4))],
         compiler_params=pltpu.CompilerParams(vmem_limit_bytes=VMEM_LIMIT),
         name="renew",
     )(misc, stat, *sums, *weights, *updates)
@@ -2160,14 +2201,11 @@
     dmid, gfeed, rows2 = run_feed_back(
         n_dp, left, right, gv, local_rows, patches, middle, raw1, act, slope, vectors, wmlp
     )
-    gattn, gpix, gpos, rows3, run_a, run_b = run_self_back(
+    block, shared, block_sq = run_self_back(
         n_dp, n_mp, dmid, pixel_rows, embed, q, k, v, prob, post, ho, raw0, vectors, wattn,
-        t1row, t2row, gfeed,
-    )
-
-    block, shared, block_sq = run_reduce(
-        n_dp, n_mp, gattn, run_a, run_b, gpix, gpos, rows2, rows3
-    )
+        t1row, t2row, gfeed, rows2,
+    )
+
     shared = shared.reshape(-1, D)
     state = (
         attn_in, attn_in_mean, attn_in_square, attn_out, attn_out_mean, attn_out_square,
@@ -2175,8 +2213,8 @@
     )
     smalls = (vectors, vectors_mean, vectors_square, talking, talking_mean, talking_square)
     moved = run_moments(
-        n_dp, (block, shared, block_sq, gout1, gup1, gdown1, rows1, stat, aux, wcls),
-        smalls, state,
+        n_dp, (block_sq, gout1, rows1, stat, aux), smalls, (block, shared, wcls, gup1, gdown1),
+        state,
     )
     sums = [moved[19]]
     for step in range(1, n_mp):

time: 237 us -> 223 us (0.941)
  Pallas kernels: 229 us -> 216 us
    pallas_call x1 -> x0, Pallas kernels: 44.6 us -> none  [run_reduce(): pl.pallas_call(functools.partial(reduce_kernel, n_dp, n_mp), in_specs=[WH...]
    pallas_call x1, Pallas kernels: 48.7 us -> 81 us  [run_self_back(): pl.pallas_call(functools.partial(self_back_kernel, n_dp, n_mp), grid=(cou...]
where the time goes in v4:
time: 223 us; the launch traced here: 221 us
  Pallas kernels  216 us (97%)
    pallas_call x1, Pallas kernels, run_self_back(): pl.pallas_call(functools.partial(self_back_kernel, n_dp, n_mp), grid=(cou...  81 us
    pallas_call x1, Pallas kernels, run_feed(): pl.pallas_call(functools.partial(feed_kernel, n_dp, n_mp), grid=(count,),...  24.8 us
    pallas_call x1, Pallas kernels, run_feed_back(): pl.pallas_call(feed_back_kernel, grid=(count,), in_specs=[per_image(2 * H...  23.6 us
    pallas_call x1, Pallas kernels, run_self_attend(): pl.pallas_call(functools.partial(self_attend_kernel, n_dp, n_mp), grid=(c...  21.6 us
    pallas_call x1, Pallas kernels, run_token(): pl.pallas_call(functools.partial(card_token_kernel, n_dp, n_mp, group), i...  21.5 us
    pallas_call x1, Pallas kernels, run_start(): pl.pallas_call(functools.partial(start_kernel, n_dp, n_mp, group), in_spe...  17.2 us
    pallas_call x1, Pallas kernels, run_moments(): pl.pallas_call(functools.partial(moment_kernel, n_dp), in_specs=[WHOLE] *...  11 us
    pallas_call x1, Pallas kernels, run_tables(): pl.pallas_call(table_kernel, in_specs=[WHOLE] * 3 + [ANY] * 3, out_specs=...  9.41 us
  transfers between devices with their start and end apart: 3, of which 0 were waited for; matrix products, arithmetic and copies ran while one was open for 0% of the time, Pallas kernels for 4%

profile of v4, /device:TPU:0, one launch (start us, length us, event | category | flops | bytes accessed | tf_op | source)
XLA Modules:
  0.0 221.4 jit_solution(5063417169131965441)
XLA Ops:
  0.7 0.0 copy-start
  1.3 0.1 copy-done
  1.4 0.6 constant_dynamic-slice_fusion.mask
  2.0 17.2 %start.1 = (bf16[4,384,384]{2,1,0:T(8,128)(2,1)}, bf16[768,384]{1,0:T(8,128)(2,1)}, bf16[384,384]{1,0:T(8,128)(2,1)}, bf16[384,384]{1,0:T(8,128)(2,1)}, bf16[384...) custom-call(f32[2,288,384]{2,1,0:T(8,128)} %bitcast.29, ...), custom_call_target="tpu_custom_call" | custom-call | tf_op jit(solution)/shard_map/start/pallas_call | solution.py:1547
  19.3 21.6 %self_attend.1 = (bf16[8,196,384]{2,1,0:T(8,128)(2,1)}, bf16[8,196,384]{2,1,0:T(8,128)(2,1)}, bf16[8,196,384]{2,1,0:T(8,128)(2,1)}, bf16[8,196,1664]{2,1,0:T(8,1...) custom-call(f32[8,196,384]{2,1,0:T(8,128)} %get-tuple-element.114.em, ...), custom_call_target="tpu_custom_call" | custom-call | tf_op jit(solution)/shard_map/self_attend/pallas_call | solution.py:1212
  40.9 24.8 %feed.1 = (f32[8,196,384]{2,1,0:T(8,128)}, bf16[8,196,1536]{2,1,0:T(8,128)(2,1)}, bf16[8,196,1536]{2,1,0:T(8,128)(2,1)}, bf16[8,196,384]{2,1,0:T(8,128)(2,1)}, b...) custom-call(f32[8,196,384]{2,1,0:T(8,128)} %get-tuple-element.120.mi, ...), custom_call_target="tpu_custom_call" | custom-call | tf_op jit(solution)/shard_map/feed/pallas_call | solution.py:1240
  65.7 21.5 %token_net.1 = (bf16[8,16,256]{2,1,0:T(8,128)(2,1)}, bf16[8,16,384]{2,1,0:T(8,128)(2,1)}, f32[384,384]{1,0:T(8,128)}, f32[16,384]{1,0:T(8,128)}, f32[96,384]{1,0...) custom-call(f32[32,128]{1,0:T(8,128)} %get-tuple-element.128.card, ...), custom_call_target="tpu_custom_call" | custom-call | tf_op jit(solution)/shard_map/token_net/pallas_call | solution.py:1277
  87.2 23.6 %feed_back.1 = (f32[8,196,384]{2,1,0:T(8,128)}, bf16[4,896,384]{2,1,0:T(8,128)(2,1)}, f32[16,384]{1,0:T(8,128)}) custom-call(bf16[8,16,256]{2,1,0:T(8,128)(2,1)} %get-tuple-element.138.left, bf16[8,16,384]{2,1,0:T(8,128)(2,1)} %get-tuple-element.139.right, f32[384,384]{1,0:T(8,128)} %get-tuple-element.140.gv, f32[16,384]{1,0:T(8,128)} %get-tuple-element.141.local_rows, ...), custom_call_target="tpu_custom_call" | custom-call | tf_op jit(solution)/shard_map/feed_back/pallas_call | solution.py:1303
  110.8 81.0 %self_back.1 = (bf16[1280,384]{1,0:T(8,128)(2,1)}, bf16[4,256,384]{2,1,0:T(8,128)(2,1)}, f32[8,128]{1,0:T(8,128)}) custom-call(f32[8,196,384]{2,1,0:T(8,128)} %get-tuple-element.146.dmid, bf16[1568,768]{1,0:T(8,128)(2,1)} %bitcast.28, f32[8,196,384]{2,1,0:T(8,128)} %get-tuple-element.114.embed, bf16[8,196,384]{2,1,0:T(8,128)(2,1)} %get-tuple-element.147.q, ...), custom_call_target="tpu_custom_call" | custom-call | tf_op jit(solution)/shard_map/self_back/pallas_call | solution.py:1330
  191.8 11.0 %moments.1 = (f32[2,288,384]{2,1,0:T(8,128)}, f32[2,288,384]{2,1,0:T(8,128)}, f32[2,288,384]{2,1,0:T(8,128)}, f32[2,96,384]{2,1,0:T(8,128)}, f32[2,96,384]{2,1,0...) custom-call(f32[8,128]{1,0:T(8,128)} %get-tuple-element.156.block_sq, ...), custom_call_target="tpu_custom_call" | custom-call | tf_op jit(solution)/shard_map/moments/pallas_call | solution.py:2025
  202.9 0.8 collective-permute-start.2
  203.7 1.2 collective-permute-start.1
  204.9 0.0 collective-permute-start
  204.9 9.4 %tables.3 = (f32[1964,384]{1,0:T(8,128)}, f32[1964,384]{1,0:T(8,128)}, f32[1964,384]{1,0:T(8,128)}, f32[8,128]{1,0:T(8,128)}) custom-call(f32[8,128]{1,0:T(8,128)} %get-tuple-element.164.misc, bf16[1024,384]{1,0:T(8,128)(2,1)} %bitcast.33, f32[1008,384]{1,0:T(8,128)} %get-tuple-element.165.ghead, f32[1964,384]{1,0:T(8,128)} %rest_0_.1, f32[1964,384]{1,0:T(8,128)} %rest_1_.1, ...), custom_call_target="tpu_custom_call" | custom-call | flops 30167040 | bytes 21116928 | tf_op jit(solution)/shard_map/tables/pallas_call | solution.py:2047
  214.3 0.0 collective-permute-done.2.rest_3_
  214.3 0.0 copy-start.2
  214.3 0.0 collective-permute-done.1.rest_2_
  214.3 0.0 copy-start.3
  214.4 0.0 collective-permute-done.rest_1_
  214.4 0.0 copy-start.4
  214.4 0.5 copy-done.2
  214.9 0.0 copy-done.3
  214.9 0.0 copy-done.4
  215.0 6.2 %renew.1 = (f32[2,288,384]{2,1,0:T(8,128)}, f32[2,96,384]{2,1,0:T(8,128)}, f32[2,384,384]{2,1,0:T(8,128)}, f32[2,384,384]{2,1,0:T(8,128)}, bf16[2,288,384]{2,1,0...) custom-call(f32[8,128]{1,0:T(8,128)} %get-tuple-element.166.misc, ...), custom_call_target="tpu_custom_call" | custom-call | tf_op jit(solution)/shard_map/renew/pallas_call | solution.py:2123
  (2 shorter events, 0.0 us)
Async XLA Ops:
  0.7 0.8 copy-start
  202.9 11.5 %collective-permute-start.2 = (f32[16,128]{1,0:T(8,128)}, f32[16,128]{1,0:T(8,128)S(1)}, u32[]{:S(2)}, u32[]{:S(2)}) collective-permute-start(f32[16,128]{1,0:T(8,128)} %get-tuple-element.167.rest_0_), channel_id=1, source_target_pairs={{0,3},{1,0},{2,1},{3,2},{4,7},{5,4},{6,5},{7,6},{8,11},{9,8},{10,9... | collective-permute-start | bytes 24584 | tf_op jit(solution)/shard_map/ppermute | solution.py:2221
  203.7 10.7 %collective-permute-start.1 = (f32[16,128]{1,0:T(8,128)}, f32[16,128]{1,0:T(8,128)S(1)}, u32[]{:S(2)}, u32[]{:S(2)}) collective-permute-start(f32[16,128]{1,0:T(8,128)} %get-tuple-element.167.rest_0_), channel_id=1, source_target_pairs={{0,2},{1,3},{2,0},{3,1},{4,6},{5,7},{6,4},{7,5},{8,10},{9,11},{10,... | collective-permute-start | bytes 24584 | tf_op jit(solution)/shard_map/ppermute | solution.py:2221
  204.9 9.5 %collective-permute-start = (f32[16,128]{1,0:T(8,128)}, f32[16,128]{1,0:T(8,128)S(1)}, u32[]{:S(2)}, u32[]{:S(2)}) collective-permute-start(f32[16,128]{1,0:T(8,128)} %get-tuple-element.167.rest_0_), channel_id=1, source_target_pairs={{0,1},{1,2},{2,3},{3,0},{4,5},{5,6},{6,7},{7,4},{8,9},{9,10},{10,1... | collective-permute-start | bytes 24584 | tf_op jit(solution)/shard_map/ppermute | solution.py:2221
  214.3 0.6 copy-start.2
  214.3 0.6 copy-start.3
  214.4 0.6 copy-start.4
  215.0 6.2 %copy-start.1 = (s32[32,196]{1,0:T(8,128)S(1)}, s32[32,196]{1,0:T(8,128)}, u32[]{:S(2)}) copy-start(s32[32,196]{1,0:T(8,128)} %param.27) | copy-start | bytes 75268

commit v5 on v4

--- a/solution.py
+++ b/solution.py
@@ -130,6 +130,12 @@
     def near_partners(self):
         return [self.sibling] + [
             (self.dp, self.along_y(step) * 2 + self.core) for step in range(1, self.n_y)
+        ]
+
+    def all_partners(self):
+        partners = [(lax.rem(self.dp + step, self.n_dp), self.mp) for step in range(1, self.n_dp)]
+        return partners + [
+            (self.dp, lax.rem(self.mp + step, self.n_mp)) for step in range(1, self.n_mp)
         ]
 
     def low_partners(self):
@@ -745,15 +751,18 @@
 
 
 def feed_kernel(
-    n_dp, n_mp, mid, cols, bias_row, base, stat, vec, wmlp, cls_rows, up_rows, down_rows,
-    patch_out, act_out, slope_out, raw_out, norm_out, cprob_out, cprob0_out, z_out, card_out,
-    aux_out, wcls_out, wup_out, wdown_out, wcls, *sems,
+    n_dp, n_mp, group, mid, cols, bias_row, base, stat, vec, wmlp, cls_rows, up_rows, down_rows,
+    head_far,
+    patch_out, act_out, slope_out, raw_out, aux_out, wcls_out, *rest,
 ):
+    token_outs, rest = rest[:10], rest[10:]
+    norm_out, cprob_out, cprob0_out, z_out, card_out, wup_out, wdown_out, wcls, head = rest[:9]
+    token_scratch, (cards, slots, dp_sem, mp_sem, head_sem), sems = rest[9:13], rest[13:18], rest[18:]
     hidden = wmlp.shape[1] // 2
     shard = wcls.shape[1] // 4
     images = norm_out.shape[0]
-
     place = Place(n_dp, n_mp)
+    load_head = pltpu.make_async_copy(head_far, head, head_sem.at[0])
     gather_cls = SpreadGather(place, cls_rows, wcls, *sems[:3])
     gather_up = SpreadGather(place, up_rows, wup_out, *sems[3:6])
     gather_down = SpreadGather(place, down_rows, wdown_out, *sems[6:])
@@ -767,7 +776,8 @@
     @pl.when(pl.program_id(0) == 0)
     def _():
         norm_out[...] = jnp.zeros_like(norm_out)
-        greet(place.near_partners() + place.low_partners())()
+        load_head.start()
+        greet(place.all_partners())()
         gather_cls.start()
         gather_up.start()
         gather_down.start()
@@ -803,7 +813,6 @@
 
     @pl.when(pl.program_id(0) == images - 1)
     def _():
-        gather_down.forward()
         unit, _ = normalize(jnp.broadcast_to(vec[17:18, :], (HEADS, D)))
         token = (unit * vec[8:9, :] + vec[9:10, :]).astype(BF)
         query = nt(token, part(wcls, 0, shard)).astype(BF).astype(F32)
@@ -830,26 +839,16 @@
         cheads = cheads.reshape(images, HEADS, D).sum(1)
         for piece in range(3):
             card_out[pl.ds(piece, images, stride=4), :] = cheads[:, 128 * piece : 128 * piece + 128]
+        gather_down.forward()
+        share_cards(n_dp, n_mp, card_out, cards, slots, dp_sem, mp_sem)
         wcls_out[...] = wcls[...]
         gather_up.finish()
         gather_down.finish()
-
-
-def card_token_kernel(n_dp, n_mp, group, card, vec, aux, *rest):
-    far, outs, scratch = rest[:8], rest[8:18], rest[18:]
-    dch_all, gout_all, gup_all, gdown_all, cards, slots, dp_sem, mp_sem, load_sem = scratch[:9]
-    here = scratch[9:]
-    loads = [
-        pltpu.make_async_copy(far[i], here[i], load_sem.at[i]) for i in range(len(far))
-    ]
-    for copy in loads:
-        copy.start()
-    share_cards(n_dp, n_mp, card, cards, slots, dp_sem, mp_sem)
-    for copy in loads:
-        copy.wait()
-    token_kernel(
-        group, cards, vec, *here, aux, *outs, dch_all, gout_all, gup_all, gdown_all
-    )
+        load_head.wait()
+        token_kernel(
+            group, cards, vec, wcls, wup_out, wdown_out, head, norm_out, cprob_out, cprob0_out,
+            z_out, aux_out, *token_outs, *token_scratch,
+        )
 
 
 def token_kernel(
@@ -1234,66 +1233,56 @@
     )(embed, cols, vec, wattn, t1row, t2row, mlp_rows)
 
 
-def run_feed(n_dp, n_mp, mid, cols, bias_row, base, stat, vec, wmlp, cls_rows, up_rows, down_rows):
+def run_feed(
+    n_dp, n_mp, group, mid, cols, bias_row, base, stat, vec, wmlp, cls_rows, up_rows, down_rows, head
+):
     count = mid.shape[0]
-    wide = 2 * wmlp.shape[0] * wmlp.shape[1] // 4
+    shard, hidden = cls_rows.shape[0] // 4, up_rows.shape[0]
+    wide = n_mp * hidden
+    everyone = n_dp * n_mp * count
+    wcls = (n_mp, *cls_rows.shape)
+    half = (n_mp, *up_rows.shape)
+    dma = pltpu.SemaphoreType.DMA
+    token_outs = [
+        shaped(count, 2 * HEADS, WIDE, dtype=BF), shaped(count, 2 * HEADS, D, dtype=BF),
+        shaped(D, D), shaped(16, D), shaped(shard, D), shaped(hidden, D), shaped(hidden, D),
+        shaped(head.shape[0] + 8, D), shaped(16, D), shaped(8, 128),
+    ]
     return pl.pallas_call(
-        functools.partial(feed_kernel, n_dp, n_mp),
+        functools.partial(feed_kernel, n_dp, n_mp, group),
         grid=(count,),
         in_specs=[
             per_image(P_SIZE, D), constant(*cols.shape), constant(1, count * WIDE),
             constant(*base.shape), per_image(1, 128), constant(*vec.shape), constant(*wmlp.shape),
-            constant(*cls_rows.shape), constant(*up_rows.shape), constant(*down_rows.shape),
+            constant(*cls_rows.shape), constant(*up_rows.shape), constant(*down_rows.shape), ANY,
         ],
         out_specs=[
             per_image(P_SIZE, D), per_image(P_SIZE, wide), per_image(P_SIZE, wide),
-            per_image(P_SIZE, D), constant(count, WIDE, D), constant(count * HEADS, WIDE),
-            constant(count * HEADS, 128), constant(count * HEADS, D), constant(4 * count, 128),
-            constant(24, D), constant(n_mp, *cls_rows.shape), ANY, ANY,
-        ],
+            per_image(P_SIZE, D), constant(24, D), constant(*wcls),
+        ]
+        + [constant(*item.shape) for item in token_outs],
         out_shape=[
             shaped(count, P_SIZE, D), shaped(count, P_SIZE, wide, dtype=BF),
             shaped(count, P_SIZE, wide, dtype=BF), shaped(count, P_SIZE, D, dtype=BF),
-            shaped(count, WIDE, D, dtype=BF), shaped(count * HEADS, WIDE),
-            shaped(count * HEADS, 128), shaped(count * HEADS, D), shaped(4 * count, 128),
-            shaped(24, D), shaped(n_mp, *cls_rows.shape, dtype=BF),
-            shaped(n_mp, *up_rows.shape, dtype=BF), shaped(n_mp, *down_rows.shape, dtype=BF),
-        ],
-        scratch_shapes=[pltpu.VMEM((n_mp, *cls_rows.shape), BF)] + spread_scratch(n_dp, n_mp) * 3,
+            shaped(24, D), shaped(*wcls, dtype=BF),
+        ]
+        + token_outs,
+        scratch_shapes=[
+            pltpu.VMEM((count, WIDE, D), BF), pltpu.VMEM((count * HEADS, WIDE), F32),
+            pltpu.VMEM((count * HEADS, 128), F32), pltpu.VMEM((count * HEADS, D), F32),
+            pltpu.VMEM((4 * count, 128), F32), pltpu.VMEM(half, BF), pltpu.VMEM(half, BF),
+            pltpu.VMEM(wcls, BF), pltpu.VMEM(head.shape, BF),
+            pltpu.VMEM((everyone, D), F32), pltpu.VMEM((D, D), F32), pltpu.VMEM((wide, D), F32),
+            pltpu.VMEM((wide, D), F32),
+            pltpu.VMEM((4 * everyone, 128), F32), pltpu.VMEM((4 * everyone, 128), BF),
+            dma((2, n_dp)), dma((2, n_mp)), dma((1,)),
+        ]
+        + spread_scratch(n_dp, n_mp) * 3,
         compiler_params=remote_params(7),
         name="feed",
-    )(mid, cols, bias_row, base, stat, vec, wmlp, cls_rows, up_rows, down_rows)
-
-
-def run_token(n_dp, n_mp, group, card, vec, aux, wcls, wup, wdown, head, norm, cprob, cprob0, z):
-    rows = card.shape[0]
-    local = norm.shape[0]
-    images = n_dp * n_mp * local
-    hidden = wup.shape[1]
-    shard = wcls.shape[1] // 4
-    wide = wup.shape[0] * hidden
-    dma = pltpu.SemaphoreType.DMA
-    far = (wcls, wup, wdown, head, norm, cprob, cprob0, z)
-    return pl.pallas_call(
-        functools.partial(card_token_kernel, n_dp, n_mp, group),
-        in_specs=[WHOLE] * 3 + [ANY] * 8,
-        out_specs=[WHOLE] * 10,
-        out_shape=[
-            shaped(local, 2 * HEADS, WIDE, dtype=BF), shaped(local, 2 * HEADS, D, dtype=BF),
-            shaped(D, D), shaped(16, D), shaped(shard, D), shaped(hidden, D), shaped(hidden, D),
-            shaped(head.shape[0] + 8, D), shaped(16, D), shaped(8, 128),
-        ],
-        scratch_shapes=[
-            pltpu.VMEM((images, D), F32), pltpu.VMEM((D, D), F32), pltpu.VMEM((wide, D), F32),
-            pltpu.VMEM((wide, D), F32), pltpu.VMEM((n_dp * n_mp * rows, 128), F32),
-            pltpu.VMEM((n_dp * n_mp * rows, 128), BF), dma((2, n_dp)), dma((2, n_mp)), dma((8,)),
-        ]
-        + [pltpu.VMEM(item.shape, item.dtype) for item in far],
-        compiler_params=pltpu.CompilerParams(
-            vmem_limit_bytes=VMEM_LIMIT, collective_id=1, has_side_effects=True
-        ),
-        name="token_net",
-    )(card, vec, aux, *far)
+    )(
+        mid, cols, bias_row, base, stat, vec, wmlp, cls_rows, up_rows, down_rows, head
+    )
 
 
 def run_feed_back(n_dp, left, right, gv, local_rows, patch, mid, raw, act, slope, vec, wmlp):
@@ -1368,14 +1357,10 @@
     dp = lax.axis_index("dp")
     mp = lax.axis_index("mp")
     rows = card.shape[0]
-    barrier = pltpu.get_barrier_semaphore()
     others_dp = [(lax.rem(dp + step, n_dp), mp) for step in range(1, n_dp)]
     others_mp = [(dp, lax.rem(mp + step, n_mp)) for step in range(1, n_mp)]
-    for partner in others_dp + others_mp:
-        pl.semaphore_signal(barrier, inc=1, device_id=partner, device_id_type=MESH)
     own = tile_rows(slots, (mp * n_dp + dp) * rows, rows)
     slots[pl.ds(pl.multiple_of((mp * n_dp + dp) * rows, 16), rows), :] = card[...].astype(BF)
-    pl.semaphore_wait(barrier, n_dp + n_mp - 2)
     sends = [
         remote(own, own, dp_sem.at[0, step], dp_sem.at[1, step], others_dp[step - 1])
         for step in range(1, n_dp)
@@ -1715,7 +1700,7 @@
         m[at, :] = mean
         s[at, :] = second
         update = direction + DECAY * weight
-        u[at, :] = update
+        u[at, :] = update.astype(u.dtype)
         return (kept[0] + fold(weight), kept[1] + fold(update))
 
     zero = jnp.zeros((8, 128), F32)
@@ -2019,7 +2004,9 @@
 
 
 def run_moments(n_dp, grads, smalls, large, state):
-    outs = [jax.ShapeDtypeStruct(item.shape, F32) for item in state]
+    outs = [
+        jax.ShapeDtypeStruct(item.shape, F32 if i % 3 else BF) for i, item in enumerate(state)
+    ]
     fs = state[9].shape[1]
     dma = pltpu.SemaphoreType.DMA
     return pl.pallas_call(
@@ -2030,7 +2017,7 @@
         + [jax.ShapeDtypeStruct(item.shape, F32) for item in smalls]
         + [shaped(8, 128), shaped(16, 128)],
         scratch_shapes=[pltpu.VMEM(item.shape, F32) for item in state]
-        + [pltpu.VMEM(state[3 * kind].shape, F32) for kind in range(4)]
+        + [pltpu.VMEM(state[3 * kind].shape, BF) for kind in range(4)]
         + [
             pltpu.VMEM((D, D), F32), pltpu.VMEM((D, D), F32), pltpu.VMEM((D, fs), F32),
             dma((17,)), dma((12,)),
@@ -2104,7 +2091,7 @@
 
             def step(i, _, b=b, w=w, u=u, low=low, rate=rate, chunk=chunk):
                 at = pl.ds(pl.multiple_of(i * chunk, chunk), chunk)
-                values = w[b, at, :] - rate * u[b, at, :]
+                values = w[b, at, :] - rate * u[b, at, :].astype(F32)
                 w[b, at, :] = values
                 low[b, at, :] = values.astype(BF)
                 return 0
@@ -2128,8 +2115,7 @@
         + [shaped(*item.shape, dtype=BF) for item in weights]
         + [shaped(2, 13), shaped(1, 1), shaped(1, 12)],
         scratch_shapes=[pltpu.VMEM(item.shape, F32) for item in weights]
-        + [pltpu.VMEM(item.shape, F32) for item in weights]
-        + [pltpu.VMEM(item.shape, BF) for item in weights]
+        + [pltpu.VMEM(item.shape, BF) for item in weights] * 2
         + [pltpu.VMEM((n_mp, 16, 128), F32), dma((2, 4)), dma((2, 4))],
         compiler_params=pltpu.CompilerParams(vmem_limit_bytes=VMEM_LIMIT),
         name="renew",
@@ -2191,12 +2177,12 @@
     q, k, v, prob, post, ho, raw0, middle, stat_a, wmlp = run_self_attend(
         n_dp, n_mp, embed, cols, vectors, wattn, t1row, t2row, mlp_rows
     )
-    patches, act, slope, raw1, norm, cprob, cprob0, z, card, aux, wcls, wup, wdown = run_feed(
-        n_dp, n_mp, middle, cols, bias_row, base, stat_a, vectors, wmlp, cls_rows, up_rows,
-        down_rows,
-    )
-    left, right, gv, local_rows, gout1, gup1, gdown1, ghead, rows1, stat = run_token(
-        n_dp, n_mp, group, card, vectors, aux, wcls, wup, wdown, head, norm, cprob, cprob0, z
+    (
+        patches, act, slope, raw1, aux, wcls, left, right, gv, local_rows, gout1, gup1, gdown1,
+        ghead, rows1, stat,
+    ) = run_feed(
+        n_dp, n_mp, group, middle, cols, bias_row, base, stat_a, vectors, wmlp, cls_rows, up_rows,
+        down_rows, head,
     )
     dmid, gfeed, rows2 = run_feed_back(
         n_dp, left, right, gv, local_rows, patches, middle, raw1, act, slope, vectors, wmlp

time: 223 us -> 218 us (0.978)
  Pallas kernels: 216 us -> 212 us
    pallas_call x2 -> x1, Pallas kernels: 46.3 us -> 42.4 us  [run_feed(): pl.pallas_call(functools.partial(feed_kernel, n_dp, n_mp, group), grid=(c...]
where the time goes in v5:
time: 218 us; the launch traced here: 217 us
  Pallas kernels  212 us (97%)
    pallas_call x1, Pallas kernels, run_self_back(): pl.pallas_call(functools.partial(self_back_kernel, n_dp, n_mp), grid=(cou...  80.9 us
    pallas_call x1, Pallas kernels, run_feed(): pl.pallas_call(functools.partial(feed_kernel, n_dp, n_mp, group), grid=(c...  42.4 us
    pallas_call x1, Pallas kernels, run_feed_back(): pl.pallas_call(feed_back_kernel, grid=(count,), in_specs=[per_image(2 * H...  23.6 us
    pallas_call x1, Pallas kernels, run_self_attend(): pl.pallas_call(functools.partial(self_attend_kernel, n_dp, n_mp), grid=(c...  21.7 us
    pallas_call x1, Pallas kernels, run_start(): pl.pallas_call(functools.partial(start_kernel, n_dp, n_mp, group), in_spe...  17.2 us
    pallas_call x1, Pallas kernels, run_moments(): pl.pallas_call(functools.partial(moment_kernel, n_dp), in_specs=[WHOLE] *...  10.8 us
    pallas_call x1, Pallas kernels, run_tables(): pl.pallas_call(table_kernel, in_specs=[WHOLE] * 3 + [ANY] * 3, out_specs=...  9.41 us
    pallas_call x1, Pallas kernels, run_renew(): pl.pallas_call(functools.partial(renew_kernel, n_mp), in_specs=[WHOLE] *...  5.56 us
  transfers between devices with their start and end apart: 3, of which 0 were waited for; matrix products, arithmetic and copies ran while one was open for 0% of the time, Pallas kernels for 4%

profile of v5, /device:TPU:0, one launch (start us, length us, event | category | flops | bytes accessed | tf_op | source)
XLA Modules:
  0.0 216.6 jit_solution(11529111338549583244)
XLA Ops:
  0.7 0.0 copy-start
  1.3 0.1 copy-done
  1.4 0.6 constant_dynamic-slice_fusion.mask
  2.0 17.2 %start.1 = (bf16[4,384,384]{2,1,0:T(8,128)(2,1)}, bf16[768,384]{1,0:T(8,128)(2,1)}, bf16[384,384]{1,0:T(8,128)(2,1)}, bf16[384,384]{1,0:T(8,128)(2,1)}, bf16[384...) custom-call(f32[2,288,384]{2,1,0:T(8,128)} %bitcast.29, ...), custom_call_target="tpu_custom_call" | custom-call | tf_op jit(solution)/shard_map/start/pallas_call | solution.py:1532
  19.3 21.7 %self_attend.1 = (bf16[8,196,384]{2,1,0:T(8,128)(2,1)}, bf16[8,196,384]{2,1,0:T(8,128)(2,1)}, bf16[8,196,384]{2,1,0:T(8,128)(2,1)}, bf16[8,196,1664]{2,1,0:T(8,1...) custom-call(f32[8,196,384]{2,1,0:T(8,128)} %get-tuple-element.107.em, ...), custom_call_target="tpu_custom_call" | custom-call | tf_op jit(solution)/shard_map/self_attend/pallas_call | solution.py:1211
  41.0 42.4 %feed.1 = (f32[8,196,384]{2,1,0:T(8,128)}, bf16[8,196,1536]{2,1,0:T(8,128)(2,1)}, bf16[8,196,1536]{2,1,0:T(8,128)(2,1)}, bf16[8,196,384]{2,1,0:T(8,128)(2,1)}, f...) custom-call(f32[8,196,384]{2,1,0:T(8,128)} %get-tuple-element.113.mi, ...), custom_call_target="tpu_custom_call" | custom-call | tf_op jit(solution)/shard_map/feed/pallas_call | solution.py:1251
  83.4 23.6 %feed_back.1 = (f32[8,196,384]{2,1,0:T(8,128)}, bf16[4,896,384]{2,1,0:T(8,128)(2,1)}, f32[16,384]{1,0:T(8,128)}) custom-call(bf16[8,16,256]{2,1,0:T(8,128)(2,1)} %get-tuple-element.122.left, bf16[8,16,384]{2,1,0:T(8,128)(2,1)} %get-tuple-element.123.right, f32[384,384]{1,0:T(8,128)} %get-tuple-element.124.gv, f32[16,384]{1,0:T(8,128)} %get-tuple-element.125.local_rows, ...), custom_call_target="tpu_custom_call" | custom-call | tf_op jit(solution)/shard_map/feed_back/pallas_call | solution.py:1292
  107.0 80.9 %self_back.1 = (bf16[1280,384]{1,0:T(8,128)(2,1)}, bf16[4,256,384]{2,1,0:T(8,128)(2,1)}, f32[8,128]{1,0:T(8,128)}) custom-call(f32[8,196,384]{2,1,0:T(8,128)} %get-tuple-element.130.dmid, bf16[1568,768]{1,0:T(8,128)(2,1)} %bitcast.28, f32[8,196,384]{2,1,0:T(8,128)} %get-tuple-element.107.embed, bf16[8,196,384]{2,1,0:T(8,128)(2,1)} %get-tuple-element.131.q, ...), custom_call_target="tpu_custom_call" | custom-call | tf_op jit(solution)/shard_map/self_back/pallas_call | solution.py:1319
  187.9 10.8 %moments.1 = (bf16[2,288,384]{2,1,0:T(8,128)(2,1)}, f32[2,288,384]{2,1,0:T(8,128)}, f32[2,288,384]{2,1,0:T(8,128)}, bf16[2,96,384]{2,1,0:T(8,128)(2,1)}, f32[2,9...) custom-call(f32[8,128]{1,0:T(8,128)} %get-tuple-element.140.block_sq, ...), custom_call_target="tpu_custom_call" | custom-call | tf_op jit(solution)/shard_map/moments/pallas_call | solution.py:2012
  198.8 1.1 collective-permute-start.2
  199.9 0.9 collective-permute-start.1
  200.8 0.0 collective-permute-start
  200.8 9.4 %tables.3 = (f32[1964,384]{1,0:T(8,128)}, f32[1964,384]{1,0:T(8,128)}, f32[1964,384]{1,0:T(8,128)}, f32[8,128]{1,0:T(8,128)}) custom-call(f32[8,128]{1,0:T(8,128)} %get-tuple-element.150.misc, bf16[1024,384]{1,0:T(8,128)(2,1)} %bitcast.33, f32[1008,384]{1,0:T(8,128)} %get-tuple-element.151.ghead, f32[1964,384]{1,0:T(8,128)} %rest_0_.1, f32[1964,384]{1,0:T(8,128)} %rest_1_.1, ...), custom_call_target="tpu_custom_call" | custom-call | flops 30167040 | bytes 21116928 | tf_op jit(solution)/shard_map/tables/pallas_call | solution.py:2034
  210.2 0.0 collective-permute-done.2.rest_3_
  210.2 0.0 copy-start.2
  210.3 0.0 collective-permute-done.1.rest_2_
  210.3 0.0 copy-start.3
  210.3 0.0 collective-permute-done.rest_1_
  210.3 0.0 copy-start.4
  210.3 0.5 copy-done.2
  210.8 0.0 copy-done.3
  210.9 0.0 copy-done.4
  210.9 5.6 %renew.1 = (f32[2,288,384]{2,1,0:T(8,128)}, f32[2,96,384]{2,1,0:T(8,128)}, f32[2,384,384]{2,1,0:T(8,128)}, f32[2,384,384]{2,1,0:T(8,128)}, bf16[2,288,384]{2,1,0...) custom-call(f32[8,128]{1,0:T(8,128)} %get-tuple-element.152.misc, ...), custom_call_target="tpu_custom_call" | custom-call | tf_op jit(solution)/shard_map/renew/pallas_call | solution.py:2110
  216.4 0.0 copy-done.1
  (1 shorter events, 0.0 us)
Async XLA Ops:
  0.7 0.8 copy-start
  198.8 11.5 %collective-permute-start.2 = (f32[16,128]{1,0:T(8,128)}, f32[16,128]{1,0:T(8,128)S(1)}, u32[]{:S(2)}, u32[]{:S(2)}) collective-permute-start(f32[16,128]{1,0:T(8,128)} %get-tuple-element.153.rest_0_), channel_id=1, source_target_pairs={{0,3},{1,0},{2,1},{3,2},{4,7},{5,4},{6,5},{7,6},{8,11},{9,8},{10,9... | collective-permute-start | bytes 24584 | tf_op jit(solution)/shard_map/ppermute | solution.py:2207
  199.9 10.3 %collective-permute-start.1 = (f32[16,128]{1,0:T(8,128)}, f32[16,128]{1,0:T(8,128)S(1)}, u32[]{:S(2)}, u32[]{:S(2)}) collective-permute-start(f32[16,128]{1,0:T(8,128)} %get-tuple-element.153.rest_0_), channel_id=1, source_target_pairs={{0,2},{1,3},{2,0},{3,1},{4,6},{5,7},{6,4},{7,5},{8,10},{9,11},{10,... | collective-permute-start | bytes 24584 | tf_op jit(solution)/shard_map/ppermute | solution.py:2207
  200.8 9.5 %collective-permute-start = (f32[16,128]{1,0:T(8,128)}, f32[16,128]{1,0:T(8,128)S(1)}, u32[]{:S(2)}, u32[]{:S(2)}) collective-permute-start(f32[16,128]{1,0:T(8,128)} %get-tuple-element.153.rest_0_), channel_id=1, source_target_pairs={{0,1},{1,2},{2,3},{3,0},{4,5},{5,6},{6,7},{7,4},{8,9},{9,10},{10,1... | collective-permute-start | bytes 24584 | tf_op jit(solution)/shard_map/ppermute | solution.py:2207
  210.2 0.6 copy-start.2
  210.3 0.6 copy-start.3
  210.3 0.6 copy-start.4
  210.9 5.6 %copy-start.1 = (s32[32,196]{1,0:T(8,128)S(1)}, s32[32,196]{1,0:T(8,128)}, u32[]{:S(2)}) copy-start(s32[32,196]{1,0:T(8,128)} %param.27) | copy-start | bytes 75268

commit v6 on v5

--- a/solution.py
+++ b/solution.py
@@ -694,26 +694,37 @@
 
 
 def self_attend_kernel(
-    n_dp, n_mp, embed, cols, vec, wattn, t1row, t2row, mlp_rows,
-    q_out, k_out, v_out, prob_out, post_out, ho_out, raw_out, mid_out, stat_out, wmlp_out,
-    stack, scores, *sems,
+    n_dp, n_mp, group, attn_in, attn_out, mlp_in, mlp_out, pixels, tables, vec, mix, mask,
+    counts, labels, pairs,
+    q_out, k_out, v_out, prob_out, post_out, ho_out, raw_out, mid_out, stat_out,
+    wmlp_out, wattn_far, embed_far, cls_rows, up_rows, down_rows, head_out, t1row, t2row, cols,
+    bias_out, base_out,
+    stack, scores, embed, wattn, mlp_rows, save_sem, *rest,
 ):
+    start_scratch, sems = rest[:-2], rest[-2:]
     shard = wattn.shape[1] // 4
-    place = Place(n_dp, n_mp)
-    gather = Gather(place, mlp_rows, wmlp_out, *sems)
+    gather = Gather(Place(n_dp, n_mp), mlp_rows, wmlp_out, *sems)
+    save = pltpu.make_async_copy(wattn, wattn_far, save_sem.at[0])
     images = pl.num_programs(0)
-
-    @pl.when(pl.program_id(0) == 0)
+    n = pl.program_id(0)
+
+    @pl.when(n == 0)
     def _():
         stack[...] = jnp.zeros_like(stack)
-        greet(place.near_partners())()
+        start_part(
+            n_dp, n_mp, group, attn_in, attn_out, mlp_in, mlp_out, pixels, tables, vec, mix, mask,
+            counts, labels, pairs,
+            wattn, mlp_rows, cls_rows, up_rows, down_rows, embed_far, head_out, t1row, t2row, cols,
+            bias_out, base_out, embed, *start_scratch,
+        )
         gather.start()
-
-    @pl.when(pl.program_id(0) == images - 1)
+        save.start()
+
+    @pl.when(n == images * 3 // 4)
     def _():
         gather.forward()
 
-    x = embed[0]
+    x = embed[pl.ds(n, 1)][0]
     unit, _ = normalize(x)
     normed = (unit * vec[0:1, :] + vec[1:2, :]).astype(BF)
     q = nt(normed, part(wattn, 0, shard)).astype(BF)
@@ -745,9 +756,10 @@
     weight = column(cols, pl.program_id(0) + cols.shape[1] // 2)
     stat_out[0] = stat_lanes((branch, middle), weight, 8)
 
-    @pl.when(pl.program_id(0) == images - 1)
+    @pl.when(n == images - 1)
     def _():
         gather.finish()
+        save.wait()
 
 
 def feed_kernel(
@@ -1204,33 +1216,60 @@
     )
 
 
-def run_self_attend(n_dp, n_mp, embed, cols, vec, wattn, t1row, t2row, mlp_rows):
-    count = embed.shape[0]
+def run_self_attend(
+    n_dp, n_mp, group, attn_in, attn_out, mlp_in, mlp_out, pixels, tables, vec, mix, mask, counts,
+    labels, pairs,
+):
+    count = labels.shape[0]
+    classes = tables.shape[0] - PIX - P_SIZE
+    n_y = n_mp // 2
+    shard = attn_in.shape[1] + attn_out.shape[1]
+    hidden = mlp_in.shape[2]
     rows = per_image(P_SIZE, D)
     low = shaped(count, P_SIZE, D, dtype=BF)
+    scalars = pl.BlockSpec(memory_space=pltpu.SMEM)
+    dma = pltpu.SemaphoreType.DMA
+    shared = [
+        shaped(shard, D, dtype=BF), shaped(hidden, D, dtype=BF), shaped(hidden, D, dtype=BF),
+        shaped(classes, D, dtype=BF), shaped(HEADS, D), shaped(HEADS, D),
+        shaped(P_SIZE, 2 * count), shaped(1, count * WIDE), shaped(count, 128),
+    ]
     return pl.pallas_call(
-        functools.partial(self_attend_kernel, n_dp, n_mp),
+        functools.partial(self_attend_kernel, n_dp, n_mp, group),
         grid=(count,),
         in_specs=[
-            rows, constant(*cols.shape), constant(*vec.shape),
-            constant(*wattn.shape), constant(HEADS, D), constant(HEADS, D),
-            constant(*mlp_rows.shape),
+            ANY, ANY, ANY, ANY, constant(*pixels.shape), ANY, constant(*vec.shape),
+            constant(*mix.shape), constant(*mask.shape), scalars, scalars, scalars,
         ],
         out_specs=[
             rows, rows, rows, per_image(P_SIZE, HEADS * PAD), per_image(HEADS * PAD, D),
-            rows, rows, rows, per_image(1, 128), ANY,
-        ],
+            rows, rows, rows, per_image(1, 128), ANY, ANY, ANY,
+        ]
+        + [constant(*item.shape) for item in shared],
         out_shape=[
             low, low, low, shaped(count, P_SIZE, HEADS * PAD, dtype=BF),
             shaped(count, HEADS * PAD, D, dtype=BF), low, low,
             shaped(count, P_SIZE, D), shaped(count, 1, 128),
-            shaped(n_mp, *mlp_rows.shape, dtype=BF),
-        ],
-        scratch_shapes=[pltpu.VMEM((HEADS * PAD, D), BF), pltpu.VMEM((P_SIZE, HEADS * PAD), F32)]
+            shaped(n_mp, 2 * hidden, D, dtype=BF), shaped(n_mp, shard, D, dtype=BF),
+            shaped(count, P_SIZE, D),
+        ]
+        + shared,
+        scratch_shapes=[
+            pltpu.VMEM((HEADS * PAD, D), BF), pltpu.VMEM((P_SIZE, HEADS * PAD), F32),
+            pltpu.VMEM((count, P_SIZE, D), F32), pltpu.VMEM((n_mp, shard, D), BF),
+            pltpu.VMEM((2 * hidden, D), BF), dma((1,)),
+            pltpu.VMEM((classes + 4, D), F32), pltpu.VMEM(mlp_in.shape, F32),
+            pltpu.VMEM(mlp_out.shape, F32),
+            pltpu.VMEM((shard, D), BF), pltpu.VMEM(attn_in.shape, F32),
+            pltpu.VMEM(attn_out.shape, F32), pltpu.VMEM((PIX, D), F32),
+            pltpu.VMEM((200, D), F32),
+            pltpu.VMEM((P_SIZE, count, D), F32),
+            dma((n_y,)), dma((n_y,)), dma((n_y,)), dma((n_y,)), dma((8,)),
+        ]
         + gather_scratch(n_mp),
         compiler_params=remote_params(6),
         name="self_attend",
-    )(embed, cols, vec, wattn, t1row, t2row, mlp_rows)
+    )(attn_in, attn_out, mlp_in, mlp_out, pixels, tables, vec, mix, mask, counts, labels, pairs)
 
 
 def run_feed(
@@ -1389,7 +1428,7 @@
         copy.wait_send()
 
 
-def start_kernel(
+def start_part(
     n_dp, n_mp, group, attn_in, attn_out, mlp_in, mlp_out, pixels, tables, vec, mix, mask,
     counts, labels, pairs,
     out, mlp_rows, cls_rows, up_rows, down_rows, embed_far, head_out, t1_out, t2_out, cols_out, bias_out, base_out,
@@ -1516,47 +1555,6 @@
         remote(
             out.at[slot], out.at[slot], near_send.at[step], near_recv.at[step], sibling
         ).wait_recv()
-
-
-def run_start(
-    n_dp, n_mp, group, attn_in, attn_out, mlp_in, mlp_out, pixels, tables, vec, mix, mask, counts,
-    labels, pairs,
-):
-    local = labels.shape[0]
-    classes = tables.shape[0] - PIX - P_SIZE
-    scalars = pl.BlockSpec(memory_space=pltpu.SMEM)
-    n_y = n_mp // 2
-    rows = attn_in.shape[1] + attn_out.shape[1]
-    hidden = mlp_in.shape[2]
-    dma = pltpu.SemaphoreType.DMA
-    return pl.pallas_call(
-        functools.partial(start_kernel, n_dp, n_mp, group),
-        in_specs=[ANY] * 4 + [WHOLE, ANY, WHOLE, WHOLE, WHOLE, scalars, scalars, scalars],
-        out_specs=[WHOLE] * 5 + [ANY] + [WHOLE] * 6,
-        out_shape=[
-            shaped(n_mp, rows, D, dtype=BF), shaped(2 * hidden, D, dtype=BF),
-            shaped(rows, D, dtype=BF), shaped(hidden, D, dtype=BF), shaped(hidden, D, dtype=BF),
-            shaped(local, P_SIZE, D),
-            shaped(classes, D, dtype=BF), shaped(HEADS, D), shaped(HEADS, D),
-            shaped(P_SIZE, 2 * local), shaped(1, local * WIDE), shaped(local, 128),
-        ],
-        scratch_shapes=[
-            pltpu.VMEM((local, P_SIZE, D), F32),
-            pltpu.VMEM((classes + 4, D), F32), pltpu.VMEM(mlp_in.shape, F32),
-            pltpu.VMEM(mlp_out.shape, F32),
-            pltpu.VMEM((rows, D), BF), pltpu.VMEM(attn_in.shape, F32),
-            pltpu.VMEM(attn_out.shape, F32), pltpu.VMEM((PIX, D), F32),
-            pltpu.VMEM((200, D), F32),
-            pltpu.VMEM((P_SIZE, local, D), F32),
-            dma((n_y,)), dma((n_y,)), dma((n_y,)), dma((n_y,)), dma((8,)),
-        ],
-        compiler_params=pltpu.CompilerParams(
-            vmem_limit_bytes=VMEM_LIMIT, collective_id=2, has_side_effects=True
-        ),
-        name="start",
-    )(
-        attn_in, attn_out, mlp_in, mlp_out, pixels, tables, vec, mix, mask, counts, labels, pairs
-    )
 
 
 def reduce_rows(
@@ -2168,14 +2166,11 @@
     pixel_rows = pixels.transpose(1, 0, 2).reshape(P_SIZE * local, PIX)
     mask = lax.dynamic_slice_in_dim(token_mask, place_mp * local, local, 0)
     (
-        wattn, mlp_rows, cls_rows, up_rows, down_rows, embed, head, t1row, t2row, cols, bias_row,
-        base,
-    ) = run_start(
+        q, k, v, prob, post, ho, raw0, middle, stat_a, wmlp, wattn, embed, cls_rows, up_rows,
+        down_rows, head, t1row, t2row, cols, bias_row, base,
+    ) = run_self_attend(
         n_dp, n_mp, group, attn_in, attn_out, mlp_in, mlp_out, pixel_rows, tables, vectors,
         talking, mask, counts, labels, pairs,
-    )
-    q, k, v, prob, post, ho, raw0, middle, stat_a, wmlp = run_self_attend(
-        n_dp, n_mp, embed, cols, vectors, wattn, t1row, t2row, mlp_rows
     )
     (
         patches, act, slope, raw1, aux, wcls, left, right, gv, local_rows, gout1, gup1, gdown1,

time: 218 us -> 214 us (0.982)
  Pallas kernels: 212 us -> 208 us
    pallas_call x2 -> x1, Pallas kernels: 39 us -> 35.6 us  [run_self_attend(): pl.pallas_call(functools.partial(self_attend_kernel, n_dp, n_mp, group),...]
where the time goes in v6:
time: 214 us; the launch traced here: 213 us
  Pallas kernels  208 us (97%)
    pallas_call x1, Pallas kernels, run_self_back(): pl.pallas_call(functools.partial(self_back_kernel, n_dp, n_mp), grid=(cou...  80.4 us
    pallas_call x1, Pallas kernels, run_feed(): pl.pallas_call(functools.partial(feed_kernel, n_dp, n_mp, group), grid=(c...  42.4 us
    pallas_call x1, Pallas kernels, run_self_attend(): pl.pallas_call(functools.partial(self_attend_kernel, n_dp, n_mp, group),...  35.6 us
    pallas_call x1, Pallas kernels, run_feed_back(): pl.pallas_call(feed_back_kernel, grid=(count,), in_specs=[per_image(2 * H...  23.6 us
    pallas_call x1, Pallas kernels, run_moments(): pl.pallas_call(functools.partial(moment_kernel, n_dp), in_specs=[WHOLE] *...  10.8 us
    pallas_call x1, Pallas kernels, run_tables(): pl.pallas_call(table_kernel, in_specs=[WHOLE] * 3 + [ANY] * 3, out_specs=...  9.39 us
    pallas_call x1, Pallas kernels, run_renew(): pl.pallas_call(functools.partial(renew_kernel, n_mp), in_specs=[WHOLE] *...  5.56 us
  transfers between devices with their start and end apart: 3, of which 0 were waited for; matrix products, arithmetic and copies ran while one was open for 0% of the time, Pallas kernels for 4%

profile of v6, /device:TPU:0, one launch (start us, length us, event | category | flops | bytes accessed | tf_op | source)
XLA Modules:
  0.0 212.7 jit_solution(6208592345612770832)
XLA Ops:
  0.7 0.0 copy-start
  1.3 0.1 copy-done
  1.4 0.6 constant_dynamic-slice_fusion.mask
  2.0 35.6 %self_attend.1 = (bf16[8,196,384]{2,1,0:T(8,128)(2,1)}, bf16[8,196,384]{2,1,0:T(8,128)(2,1)}, bf16[8,196,384]{2,1,0:T(8,128)(2,1)}, bf16[8,196,1664]{2,1,0:T(8,1...) custom-call(f32[2,288,384]{2,1,0:T(8,128)} %bitcast.29, ...), custom_call_target="tpu_custom_call" | custom-call | tf_op jit(solution)/shard_map/self_attend/pallas_call | solution.py:1237
  37.7 42.4 %feed.1 = (f32[8,196,384]{2,1,0:T(8,128)}, bf16[8,196,1536]{2,1,0:T(8,128)(2,1)}, bf16[8,196,1536]{2,1,0:T(8,128)(2,1)}, bf16[8,196,384]{2,1,0:T(8,128)(2,1)}, f...) custom-call(f32[8,196,384]{2,1,0:T(8,128)} %get-tuple-element.106.mi, ...), custom_call_target="tpu_custom_call" | custom-call | tf_op jit(solution)/shard_map/feed/pallas_call | solution.py:1290
  80.1 23.6 %feed_back.1 = (f32[8,196,384]{2,1,0:T(8,128)}, bf16[4,896,384]{2,1,0:T(8,128)(2,1)}, f32[16,384]{1,0:T(8,128)}) custom-call(bf16[8,16,256]{2,1,0:T(8,128)(2,1)} %get-tuple-element.116.left, bf16[8,16,384]{2,1,0:T(8,128)(2,1)} %get-tuple-element.117.right, f32[384,384]{1,0:T(8,128)} %get-tuple-element.118.gv, f32[16,384]{1,0:T(8,128)} %get-tuple-element.119.local_rows, ...), custom_call_target="tpu_custom_call" | custom-call | tf_op jit(solution)/shard_map/feed_back/pallas_call | solution.py:1331
  103.7 80.4 %self_back.1 = (bf16[1280,384]{1,0:T(8,128)(2,1)}, bf16[4,256,384]{2,1,0:T(8,128)(2,1)}, f32[8,128]{1,0:T(8,128)}) custom-call(f32[8,196,384]{2,1,0:T(8,128)} %get-tuple-element.124.dmid, bf16[1568,768]{1,0:T(8,128)(2,1)} %bitcast.28, f32[8,196,384]{2,1,0:T(8,128)} %get-tuple-element.125.embed, bf16[8,196,384]{2,1,0:T(8,128)(2,1)} %get-tuple-element.126.q, ...), custom_call_target="tpu_custom_call" | custom-call | tf_op jit(solution)/shard_map/self_back/pallas_call | solution.py:1358
  184.1 10.8 %moments.1 = (bf16[2,288,384]{2,1,0:T(8,128)(2,1)}, f32[2,288,384]{2,1,0:T(8,128)}, f32[2,288,384]{2,1,0:T(8,128)}, bf16[2,96,384]{2,1,0:T(8,128)(2,1)}, f32[2,9...) custom-call(f32[8,128]{1,0:T(8,128)} %get-tuple-element.138.block_sq, ...), custom_call_target="tpu_custom_call" | custom-call | tf_op jit(solution)/shard_map/moments/pallas_call | solution.py:2010
  194.9 1.0 collective-permute-start.2
  195.9 1.0 collective-permute-start.1
  196.9 0.0 collective-permute-start
  196.9 9.4 %tables.3 = (f32[1964,384]{1,0:T(8,128)}, f32[1964,384]{1,0:T(8,128)}, f32[1964,384]{1,0:T(8,128)}, f32[8,128]{1,0:T(8,128)}) custom-call(f32[8,128]{1,0:T(8,128)} %get-tuple-element.148.misc, bf16[1024,384]{1,0:T(8,128)(2,1)} %bitcast.33, f32[1008,384]{1,0:T(8,128)} %get-tuple-element.149.ghead, f32[1964,384]{1,0:T(8,128)} %rest_0_.1, f32[1964,384]{1,0:T(8,128)} %rest_1_.1, ...), custom_call_target="tpu_custom_call" | custom-call | flops 30167040 | bytes 21116928 | tf_op jit(solution)/shard_map/tables/pallas_call | solution.py:2032
  206.4 0.0 collective-permute-done.2.rest_3_
  206.4 0.0 copy-start.2
  206.4 0.0 collective-permute-done.1.rest_2_
  206.4 0.0 copy-start.3
  206.4 0.0 collective-permute-done.rest_1_
  206.4 0.0 copy-start.4
  206.4 0.5 copy-done.2
  207.0 0.0 copy-done.3
  207.0 0.0 copy-done.4
  207.0 0.0 copy-start.1
  207.0 5.6 %renew.1 = (f32[2,288,384]{2,1,0:T(8,128)}, f32[2,96,384]{2,1,0:T(8,128)}, f32[2,384,384]{2,1,0:T(8,128)}, f32[2,384,384]{2,1,0:T(8,128)}, bf16[2,288,384]{2,1,0...) custom-call(f32[8,128]{1,0:T(8,128)} %get-tuple-element.150.misc, ...), custom_call_target="tpu_custom_call" | custom-call | tf_op jit(solution)/shard_map/renew/pallas_call | solution.py:2108
  212.6 0.0 copy-done.1
Async XLA Ops:
  0.7 0.8 copy-start
  194.9 11.4 %collective-permute-start.2 = (f32[16,128]{1,0:T(8,128)}, f32[16,128]{1,0:T(8,128)S(1)}, u32[]{:S(2)}, u32[]{:S(2)}) collective-permute-start(f32[16,128]{1,0:T(8,128)} %get-tuple-element.151.rest_0_), channel_id=1, source_target_pairs={{0,3},{1,0},{2,1},{3,2},{4,7},{5,4},{6,5},{7,6},{8,11},{9,8},{10,9... | collective-permute-start | bytes 24584 | tf_op jit(solution)/shard_map/ppermute | solution.py:2202
  195.9 10.4 %collective-permute-start.1 = (f32[16,128]{1,0:T(8,128)}, f32[16,128]{1,0:T(8,128)S(1)}, u32[]{:S(2)}, u32[]{:S(2)}) collective-permute-start(f32[16,128]{1,0:T(8,128)} %get-tuple-element.151.rest_0_), channel_id=1, source_target_pairs={{0,2},{1,3},{2,0},{3,1},{4,6},{5,7},{6,4},{7,5},{8,10},{9,11},{10,... | collective-permute-start | bytes 24584 | tf_op jit(solution)/shard_map/ppermute | solution.py:2202
  196.9 9.4 %collective-permute-start = (f32[16,128]{1,0:T(8,128)}, f32[16,128]{1,0:T(8,128)S(1)}, u32[]{:S(2)}, u32[]{:S(2)}) collective-permute-start(f32[16,128]{1,0:T(8,128)} %get-tuple-element.151.rest_0_), channel_id=1, source_target_pairs={{0,1},{1,2},{2,3},{3,0},{4,5},{5,6},{6,7},{7,4},{8,9},{9,10},{10,1... | collective-permute-start | bytes 24584 | tf_op jit(solution)/shard_map/ppermute | solution.py:2202
  206.4 0.6 copy-start.2
  206.4 0.6 copy-start.3
  206.4 0.6 copy-start.4
  207.0 5.6 %copy-start.1 = (s32[32,196]{1,0:T(8,128)S(1)}, s32[32,196]{1,0:T(8,128)}, u32[]{:S(2)}) copy-start(s32[32,196]{1,0:T(8,128)} %param.27) | copy-start | bytes 75268

commit v7 on v6

--- a/solution.py
+++ b/solution.py
@@ -697,13 +697,14 @@
     n_dp, n_mp, group, attn_in, attn_out, mlp_in, mlp_out, pixels, tables, vec, mix, mask,
     counts, labels, pairs,
     q_out, k_out, v_out, prob_out, post_out, ho_out, raw_out, mid_out, stat_out,
-    wmlp_out, wattn_far, embed_far, cls_rows, up_rows, down_rows, head_out, t1row, t2row, cols,
+    wmlp_out, wattn_far, embed_far, wcls_out, up_rows, down_rows, head_out, t1row, t2row, cols,
     bias_out, base_out,
-    stack, scores, embed, wattn, mlp_rows, save_sem, *rest,
+    stack, scores, embed, wattn, mlp_rows, cls_rows, save_sem, *rest,
 ):
-    start_scratch, sems = rest[:-2], rest[-2:]
+    start_scratch, sems = rest[:-4], rest[-4:]
     shard = wattn.shape[1] // 4
-    gather = Gather(Place(n_dp, n_mp), mlp_rows, wmlp_out, *sems)
+    gather = Gather(Place(n_dp, n_mp), mlp_rows, wmlp_out, *sems[:2])
+    gather_cls = Gather(gather.place, cls_rows, wcls_out, *sems[2:])
     save = pltpu.make_async_copy(wattn, wattn_far, save_sem.at[0])
     images = pl.num_programs(0)
     n = pl.program_id(0)
@@ -711,18 +712,26 @@
     @pl.when(n == 0)
     def _():
         stack[...] = jnp.zeros_like(stack)
+
+        def begin():
+            gather.start()
+            gather_cls.start()
+
         start_part(
-            n_dp, n_mp, group, attn_in, attn_out, mlp_in, mlp_out, pixels, tables, vec, mix, mask,
+            begin, n_dp, n_mp, group, attn_in, attn_out, mlp_in, mlp_out, pixels, tables, vec, mix, mask,
             counts, labels, pairs,
             wattn, mlp_rows, cls_rows, up_rows, down_rows, embed_far, head_out, t1row, t2row, cols,
             bias_out, base_out, embed, *start_scratch,
         )
-        gather.start()
         save.start()
 
-    @pl.when(n == images * 3 // 4)
+    @pl.when(n == images * 5 // 8)
     def _():
         gather.forward()
+
+    @pl.when(n == images - 1)
+    def _():
+        gather_cls.forward()
 
     x = embed[pl.ds(n, 1)][0]
     unit, _ = normalize(x)
@@ -759,25 +768,25 @@
     @pl.when(n == images - 1)
     def _():
         gather.finish()
+        gather_cls.finish()
         save.wait()
 
 
 def feed_kernel(
-    n_dp, n_mp, group, mid, cols, bias_row, base, stat, vec, wmlp, cls_rows, up_rows, down_rows,
+    n_dp, n_mp, group, mid, cols, bias_row, base, stat, vec, wmlp, wcls, up_rows, down_rows,
     head_far,
-    patch_out, act_out, slope_out, raw_out, aux_out, wcls_out, *rest,
+    patch_out, act_out, slope_out, raw_out, aux_out, *rest,
 ):
     token_outs, rest = rest[:10], rest[10:]
-    norm_out, cprob_out, cprob0_out, z_out, card_out, wup_out, wdown_out, wcls, head = rest[:9]
-    token_scratch, (cards, slots, dp_sem, mp_sem, head_sem), sems = rest[9:13], rest[13:18], rest[18:]
+    norm_out, cprob_out, cprob0_out, z_out, card_out, wup_out, wdown_out, head = rest[:8]
+    token_scratch, (cards, slots, dp_sem, mp_sem, head_sem), sems = rest[8:12], rest[12:17], rest[17:]
     hidden = wmlp.shape[1] // 2
     shard = wcls.shape[1] // 4
     images = norm_out.shape[0]
     place = Place(n_dp, n_mp)
     load_head = pltpu.make_async_copy(head_far, head, head_sem.at[0])
-    gather_cls = SpreadGather(place, cls_rows, wcls, *sems[:3])
-    gather_up = SpreadGather(place, up_rows, wup_out, *sems[3:6])
-    gather_down = SpreadGather(place, down_rows, wdown_out, *sems[6:])
+    gather_up = SpreadGather(place, up_rows, wup_out, *sems[:3])
+    gather_down = SpreadGather(place, down_rows, wdown_out, *sems[3:])
 
     def beside(step, *stages):
         @pl.when(pl.program_id(0) == step)
@@ -790,15 +799,13 @@
         norm_out[...] = jnp.zeros_like(norm_out)
         load_head.start()
         greet(place.all_partners())()
-        gather_cls.start()
         gather_up.start()
         gather_down.start()
 
-    beside(images * 3 // 8, gather_cls.spread)
-    beside(images // 2, gather_up.spread)
-    beside(images * 5 // 8, gather_down.spread)
-    beside(images * 3 // 4, gather_cls.forward)
-    beside(images - 1, gather_up.forward, gather_cls.finish)
+    beside(images * 3 // 8, gather_up.spread)
+    beside(images // 2, gather_down.spread)
+    beside(images * 3 // 4, gather_up.forward)
+    beside(images - 1, gather_down.forward)
 
     middle = mid[0]
     unit, _ = normalize(middle)
@@ -851,9 +858,7 @@
         cheads = cheads.reshape(images, HEADS, D).sum(1)
         for piece in range(3):
             card_out[pl.ds(piece, images, stride=4), :] = cheads[:, 128 * piece : 128 * piece + 128]
-        gather_down.forward()
         share_cards(n_dp, n_mp, card_out, cards, slots, dp_sem, mp_sem)
-        wcls_out[...] = wcls[...]
         gather_up.finish()
         gather_down.finish()
         load_head.wait()
@@ -1230,7 +1235,7 @@
     scalars = pl.BlockSpec(memory_space=pltpu.SMEM)
     dma = pltpu.SemaphoreType.DMA
     shared = [
-        shaped(shard, D, dtype=BF), shaped(hidden, D, dtype=BF), shaped(hidden, D, dtype=BF),
+        shaped(hidden, D, dtype=BF), shaped(hidden, D, dtype=BF),
         shaped(classes, D, dtype=BF), shaped(HEADS, D), shaped(HEADS, D),
         shaped(P_SIZE, 2 * count), shaped(1, count * WIDE), shaped(count, 128),
     ]
@@ -1243,7 +1248,7 @@
         ],
         out_specs=[
             rows, rows, rows, per_image(P_SIZE, HEADS * PAD), per_image(HEADS * PAD, D),
-            rows, rows, rows, per_image(1, 128), ANY, ANY, ANY,
+            rows, rows, rows, per_image(1, 128), ANY, ANY, ANY, ANY,
         ]
         + [constant(*item.shape) for item in shared],
         out_shape=[
@@ -1251,13 +1256,13 @@
             shaped(count, HEADS * PAD, D, dtype=BF), low, low,
             shaped(count, P_SIZE, D), shaped(count, 1, 128),
             shaped(n_mp, 2 * hidden, D, dtype=BF), shaped(n_mp, shard, D, dtype=BF),
-            shaped(count, P_SIZE, D),
+            shaped(count, P_SIZE, D), shaped(n_mp, shard, D, dtype=BF),
         ]
         + shared,
         scratch_shapes=[
             pltpu.VMEM((HEADS * PAD, D), BF), pltpu.VMEM((P_SIZE, HEADS * PAD), F32),
             pltpu.VMEM((count, P_SIZE, D), F32), pltpu.VMEM((n_mp, shard, D), BF),
-            pltpu.VMEM((2 * hidden, D), BF), dma((1,)),
+            pltpu.VMEM((2 * hidden, D), BF), pltpu.VMEM((shard, D), BF), dma((1,)),
             pltpu.VMEM((classes + 4, D), F32), pltpu.VMEM(mlp_in.shape, F32),
             pltpu.VMEM(mlp_out.shape, F32),
             pltpu.VMEM((shard, D), BF), pltpu.VMEM(attn_in.shape, F32),
@@ -1266,20 +1271,19 @@
             pltpu.VMEM((P_SIZE, count, D), F32),
             dma((n_y,)), dma((n_y,)), dma((n_y,)), dma((n_y,)), dma((8,)),
         ]
-        + gather_scratch(n_mp),
+        + gather_scratch(n_mp) * 2,
         compiler_params=remote_params(6),
         name="self_attend",
     )(attn_in, attn_out, mlp_in, mlp_out, pixels, tables, vec, mix, mask, counts, labels, pairs)
 
 
 def run_feed(
-    n_dp, n_mp, group, mid, cols, bias_row, base, stat, vec, wmlp, cls_rows, up_rows, down_rows, head
+    n_dp, n_mp, group, mid, cols, bias_row, base, stat, vec, wmlp, wcls, up_rows, down_rows, head
 ):
     count = mid.shape[0]
-    shard, hidden = cls_rows.shape[0] // 4, up_rows.shape[0]
+    shard, hidden = wcls.shape[1] // 4, up_rows.shape[0]
     wide = n_mp * hidden
     everyone = n_dp * n_mp * count
-    wcls = (n_mp, *cls_rows.shape)
     half = (n_mp, *up_rows.shape)
     dma = pltpu.SemaphoreType.DMA
     token_outs = [
@@ -1293,34 +1297,34 @@
         in_specs=[
             per_image(P_SIZE, D), constant(*cols.shape), constant(1, count * WIDE),
             constant(*base.shape), per_image(1, 128), constant(*vec.shape), constant(*wmlp.shape),
-            constant(*cls_rows.shape), constant(*up_rows.shape), constant(*down_rows.shape), ANY,
+            constant(*wcls.shape), constant(*up_rows.shape), constant(*down_rows.shape), ANY,
         ],
         out_specs=[
             per_image(P_SIZE, D), per_image(P_SIZE, wide), per_image(P_SIZE, wide),
-            per_image(P_SIZE, D), constant(24, D), constant(*wcls),
+            per_image(P_SIZE, D), constant(24, D),
         ]
         + [constant(*item.shape) for item in token_outs],
         out_shape=[
             shaped(count, P_SIZE, D), shaped(count, P_SIZE, wide, dtype=BF),
             shaped(count, P_SIZE, wide, dtype=BF), shaped(count, P_SIZE, D, dtype=BF),
-            shaped(24, D), shaped(*wcls, dtype=BF),
+            shaped(24, D),
         ]
         + token_outs,
         scratch_shapes=[
             pltpu.VMEM((count, WIDE, D), BF), pltpu.VMEM((count * HEADS, WIDE), F32),
             pltpu.VMEM((count * HEADS, 128), F32), pltpu.VMEM((count * HEADS, D), F32),
             pltpu.VMEM((4 * count, 128), F32), pltpu.VMEM(half, BF), pltpu.VMEM(half, BF),
-            pltpu.VMEM(wcls, BF), pltpu.VMEM(head.shape, BF),
+            pltpu.VMEM(head.shape, BF),
             pltpu.VMEM((everyone, D), F32), pltpu.VMEM((D, D), F32), pltpu.VMEM((wide, D), F32),
             pltpu.VMEM((wide, D), F32),
             pltpu.VMEM((4 * everyone, 128), F32), pltpu.VMEM((4 * everyone, 128), BF),
             dma((2, n_dp)), dma((2, n_mp)), dma((1,)),
         ]
-        + spread_scratch(n_dp, n_mp) * 3,
+        + spread_scratch(n_dp, n_mp) * 2,
         compiler_params=remote_params(7),
         name="feed",
     )(
-        mid, cols, bias_row, base, stat, vec, wmlp, cls_rows, up_rows, down_rows, head
+        mid, cols, bias_row, base, stat, vec, wmlp, wcls, up_rows, down_rows, head
     )
 
 
@@ -1429,7 +1433,7 @@
 
 
 def start_part(
-    n_dp, n_mp, group, attn_in, attn_out, mlp_in, mlp_out, pixels, tables, vec, mix, mask,
+    begin, n_dp, n_mp, group, attn_in, attn_out, mlp_in, mlp_out, pixels, tables, vec, mix, mask,
     counts, labels, pairs,
     out, mlp_rows, cls_rows, up_rows, down_rows, embed_far, head_out, t1_out, t2_out, cols_out, bias_out, base_out,
     embed_out, head_rows, wide_up, wide_down, shard, wide_in, wide_out, patch_rows, pos_rows, by_patch, near_send, near_recv, far_send, far_recv, load_sem,
@@ -1489,6 +1493,7 @@
     load_down.wait()
     mlp_rows[:hidden, :] = wide_up[0].T.astype(BF)
     mlp_rows[hidden:, :] = wide_down[0].astype(BF)
+    begin()
     up_rows[...] = wide_up[1].T.astype(BF)
     down_rows[...] = wide_down[1].astype(BF)
 
@@ -2166,17 +2171,17 @@
     pixel_rows = pixels.transpose(1, 0, 2).reshape(P_SIZE * local, PIX)
     mask = lax.dynamic_slice_in_dim(token_mask, place_mp * local, local, 0)
     (
-        q, k, v, prob, post, ho, raw0, middle, stat_a, wmlp, wattn, embed, cls_rows, up_rows,
+        q, k, v, prob, post, ho, raw0, middle, stat_a, wmlp, wattn, embed, wcls, up_rows,
         down_rows, head, t1row, t2row, cols, bias_row, base,
     ) = run_self_attend(
         n_dp, n_mp, group, attn_in, attn_out, mlp_in, mlp_out, pixel_rows, tables, vectors,
         talking, mask, counts, labels, pairs,
     )
     (
-        patches, act, slope, raw1, aux, wcls, left, right, gv, local_rows, gout1, gup1, gdown1,
+        patches, act, slope, raw1, aux, left, right, gv, local_rows, gout1, gup1, gdown1,
         ghead, rows1, stat,
     ) = run_feed(
-        n_dp, n_mp, group, middle, cols, bias_row, base, stat_a, vectors, wmlp, cls_rows, up_rows,
+        n_dp, n_mp, group, middle, cols, bias_row, base, stat_a, vectors, wmlp, wcls, up_rows,
         down_rows, head,
     )
     dmid, gfeed, rows2 = run_feed_back(

time: 214 us -> 214 us (level)
    pallas_call x1, Pallas kernels: 42.4 us -> 40.2 us  [run_feed(): pl.pallas_call(functools.partial(feed_kernel, n_dp, n_mp, group), grid=(c...]
where the time goes in v7:
time: 214 us; the launch traced here: 213 us
  Pallas kernels  208 us (97%)
    pallas_call x1, Pallas kernels, run_self_back(): pl.pallas_call(functools.partial(self_back_kernel, n_dp, n_mp), grid=(cou...  81.3 us
    pallas_call x1, Pallas kernels, run_feed(): pl.pallas_call(functools.partial(feed_kernel, n_dp, n_mp, group), grid=(c...  40.2 us
    pallas_call x1, Pallas kernels, run_self_attend(): pl.pallas_call(functools.partial(self_attend_kernel, n_dp, n_mp, group),...  36.7 us
    pallas_call x1, Pallas kernels, run_feed_back(): pl.pallas_call(feed_back_kernel, grid=(count,), in_specs=[per_image(2 * H...  23.6 us
    pallas_call x1, Pallas kernels, run_moments(): pl.pallas_call(functools.partial(moment_kernel, n_dp), in_specs=[WHOLE] *...  10.8 us
    pallas_call x1, Pallas kernels, run_tables(): pl.pallas_call(table_kernel, in_specs=[WHOLE] * 3 + [ANY] * 3, out_specs=...  9.41 us
    pallas_call x1, Pallas kernels, run_renew(): pl.pallas_call(functools.partial(renew_kernel, n_mp), in_specs=[WHOLE] *...  5.56 us
  transfers between devices with their start and end apart: 3, of which 0 were waited for; matrix products, arithmetic and copies ran while one was open for 0% of the time, Pallas kernels for 4%

profile of v7, /device:TPU:0, one launch (start us, length us, event | category | flops | bytes accessed | tf_op | source)
XLA Modules:
  0.0 212.5 jit_solution(11620326861905400884)
XLA Ops:
  0.7 0.0 copy-start
  1.3 0.1 copy-done
  1.4 0.6 constant_dynamic-slice_fusion.mask
  2.0 36.7 %self_attend.1 = (bf16[8,196,384]{2,1,0:T(8,128)(2,1)}, bf16[8,196,384]{2,1,0:T(8,128)(2,1)}, bf16[8,196,384]{2,1,0:T(8,128)(2,1)}, bf16[8,196,1664]{2,1,0:T(8,1...) custom-call(f32[2,288,384]{2,1,0:T(8,128)} %bitcast.29, ...), custom_call_target="tpu_custom_call" | custom-call | tf_op jit(solution)/shard_map/self_attend/pallas_call | solution.py:1242
  38.7 40.2 %feed.1 = (f32[8,196,384]{2,1,0:T(8,128)}, bf16[8,196,1536]{2,1,0:T(8,128)(2,1)}, bf16[8,196,1536]{2,1,0:T(8,128)(2,1)}, bf16[8,196,384]{2,1,0:T(8,128)(2,1)}, f...) custom-call(f32[8,196,384]{2,1,0:T(8,128)} %get-tuple-element.105.mi, ...), custom_call_target="tpu_custom_call" | custom-call | tf_op jit(solution)/shard_map/feed/pallas_call | solution.py:1294
  78.9 23.6 %feed_back.1 = (f32[8,196,384]{2,1,0:T(8,128)}, bf16[4,896,384]{2,1,0:T(8,128)(2,1)}, f32[16,384]{1,0:T(8,128)}) custom-call(bf16[8,16,256]{2,1,0:T(8,128)(2,1)} %get-tuple-element.115.left, bf16[8,16,384]{2,1,0:T(8,128)(2,1)} %get-tuple-element.116.right, f32[384,384]{1,0:T(8,128)} %get-tuple-element.117.gv, f32[16,384]{1,0:T(8,128)} %get-tuple-element.118.local_rows, ...), custom_call_target="tpu_custom_call" | custom-call | tf_op jit(solution)/shard_map/feed_back/pallas_call | solution.py:1335
  102.5 81.3 %self_back.1 = (bf16[1280,384]{1,0:T(8,128)(2,1)}, bf16[4,256,384]{2,1,0:T(8,128)(2,1)}, f32[8,128]{1,0:T(8,128)}) custom-call(f32[8,196,384]{2,1,0:T(8,128)} %get-tuple-element.123.dmid, bf16[1568,768]{1,0:T(8,128)(2,1)} %bitcast.28, f32[8,196,384]{2,1,0:T(8,128)} %get-tuple-element.124.embed, bf16[8,196,384]{2,1,0:T(8,128)(2,1)} %get-tuple-element.125.q, ...), custom_call_target="tpu_custom_call" | custom-call | tf_op jit(solution)/shard_map/self_back/pallas_call | solution.py:1362
  183.8 10.8 %moments.1 = (bf16[2,288,384]{2,1,0:T(8,128)(2,1)}, f32[2,288,384]{2,1,0:T(8,128)}, f32[2,288,384]{2,1,0:T(8,128)}, bf16[2,96,384]{2,1,0:T(8,128)(2,1)}, f32[2,9...) custom-call(f32[8,128]{1,0:T(8,128)} %get-tuple-element.137.block_sq, ...), custom_call_target="tpu_custom_call" | custom-call | tf_op jit(solution)/shard_map/moments/pallas_call | solution.py:2015
  194.7 0.8 collective-permute-start.2
  195.5 1.2 collective-permute-start.1
  196.7 0.0 collective-permute-start
  196.7 9.4 %tables.3 = (f32[1964,384]{1,0:T(8,128)}, f32[1964,384]{1,0:T(8,128)}, f32[1964,384]{1,0:T(8,128)}, f32[8,128]{1,0:T(8,128)}) custom-call(f32[8,128]{1,0:T(8,128)} %get-tuple-element.146.misc, bf16[1024,384]{1,0:T(8,128)(2,1)} %bitcast.33, f32[1008,384]{1,0:T(8,128)} %get-tuple-element.147.ghead, f32[1964,384]{1,0:T(8,128)} %rest_0_.1, f32[1964,384]{1,0:T(8,128)} %rest_1_.1, ...), custom_call_target="tpu_custom_call" | custom-call | flops 30167040 | bytes 21116928 | tf_op jit(solution)/shard_map/tables/pallas_call | solution.py:2037
  206.1 0.0 collective-permute-done.2.rest_3_
  206.1 0.0 copy-start.2
  206.2 0.0 collective-permute-done.1.rest_2_
  206.2 0.0 copy-start.3
  206.2 0.0 collective-permute-done.rest_1_
  206.2 0.0 copy-start.4
  206.2 0.5 copy-done.2
  206.7 0.0 copy-done.3
  206.8 0.0 copy-done.4
  206.8 0.0 copy-start.1
  206.8 5.6 %renew.1 = (f32[2,288,384]{2,1,0:T(8,128)}, f32[2,96,384]{2,1,0:T(8,128)}, f32[2,384,384]{2,1,0:T(8,128)}, f32[2,384,384]{2,1,0:T(8,128)}, bf16[2,288,384]{2,1,0...) custom-call(f32[8,128]{1,0:T(8,128)} %get-tuple-element.148.misc, ...), custom_call_target="tpu_custom_call" | custom-call | tf_op jit(solution)/shard_map/renew/pallas_call | solution.py:2113
  212.3 0.0 copy-done.1
Async XLA Ops:
  0.7 0.8 copy-start
  194.7 11.5 %collective-permute-start.2 = (f32[16,128]{1,0:T(8,128)}, f32[16,128]{1,0:T(8,128)S(1)}, u32[]{:S(2)}, u32[]{:S(2)}) collective-permute-start(f32[16,128]{1,0:T(8,128)} %get-tuple-element.149.rest_0_), channel_id=1, source_target_pairs={{0,3},{1,0},{2,1},{3,2},{4,7},{5,4},{6,5},{7,6},{8,11},{9,8},{10,9... | collective-permute-start | bytes 24584 | tf_op jit(solution)/shard_map/ppermute | solution.py:2207
  195.5 10.7 %collective-permute-start.1 = (f32[16,128]{1,0:T(8,128)}, f32[16,128]{1,0:T(8,128)S(1)}, u32[]{:S(2)}, u32[]{:S(2)}) collective-permute-start(f32[16,128]{1,0:T(8,128)} %get-tuple-element.149.rest_0_), channel_id=1, source_target_pairs={{0,2},{1,3},{2,0},{3,1},{4,6},{5,7},{6,4},{7,5},{8,10},{9,11},{10,... | collective-permute-start | bytes 24584 | tf_op jit(solution)/shard_map/ppermute | solution.py:2207
  196.7 9.5 %collective-permute-start = (f32[16,128]{1,0:T(8,128)}, f32[16,128]{1,0:T(8,128)S(1)}, u32[]{:S(2)}, u32[]{:S(2)}) collective-permute-start(f32[16,128]{1,0:T(8,128)} %get-tuple-element.149.rest_0_), channel_id=1, source_target_pairs={{0,1},{1,2},{2,3},{3,0},{4,5},{5,6},{6,7},{7,4},{8,9},{9,10},{10,1... | collective-permute-start | bytes 24584 | tf_op jit(solution)/shard_map/ppermute | solution.py:2207
  206.1 0.6 copy-start.2
  206.2 0.6 copy-start.3
  206.2 0.6 copy-start.4
  206.8 5.6 %copy-start.1 = (s32[32,196]{1,0:T(8,128)S(1)}, s32[32,196]{1,0:T(8,128)}, u32[]{:S(2)}) copy-start(s32[32,196]{1,0:T(8,128)} %param.27) | copy-start | bytes 75268
